TPU v7x, 256 devices: a whole 4x4x8 slice. The times are simulated.
256 devices in a mesh: dp: 64 (over z, y_hi, x), ctx: 4 (over y_lo, core).
Axes of the slice: x: 4, y: 4 (y_hi: 2, y_lo: 2; y = y_hi * 2 + y_lo), z: 8, core: 2. Of those that a mesh axis runs over, the one named last changes fastest.
Arguments:
- gated_hidden_input: bfloat16 [64, 2, 256, 29568], P('dp', None, 'ctx'), may hold values from -16 to 16
- frozen: bfloat16 [64, 2, 256, 8192], P('dp', None, 'ctx'), may hold values from -25 to 25
- head_gradient_rows: bfloat16 [64, 2, 256, 8192], P('dp', None, 'ctx'), may hold values from -0.875 to 0.875
- down_factor_weight: bfloat16 [29568, 64], P('dp'), may hold values from -0.03125 to 0.03125
- up_factor_weight: bfloat16 [64, 8192], P(None, 'dp'), may hold values from -0.1875 to 0.1875
- final_norm_gain: bfloat16 [8192], P('dp'), may hold values from 0.5 to 1.5
- logratio: float32 [64, 2, 256], P('dp', None, 'ctx'), may hold values from -8 to 8
- starts: int32 [64, 2], P('dp'), may hold values from 0 to 127
Outputs:
- preference_pair_loss: float32 [64], P('dp')
- gradient_down_factor: float32 [29568, 64], P('dp')
- gradient_up_factor: float32 [64, 8192], P(None, 'dp')
All inputs are finite; a program needn't handle non-finite values.
Results may differ from a plain program's by a relative error of at most 0.007.
Values may be sent and summed in bfloat16 or wider, within the bound.
No kernel may reach another device: no remote copies, remote signals or barrier semaphores. Data moves between devices by JAX's collectives and lax.ppermute only.
A program may use at most 128 MiB of HBM per device.

v0:
```python
import jax
import jax.numpy as jnp
from jax import lax
from jax.sharding import PartitionSpec as P

ADAPTER_SCALING = 2.0
DPO_BETA = 0.1
NORM_EPSILON = 1e-06


def token_contract(left_rows, values):
    upper_part = values.astype(jnp.bfloat16)
    lower_part = (values - upper_part.astype(jnp.float32)).astype(jnp.bfloat16)
    first_operand = jnp.einsum(
        "tf,tk->fk", left_rows, upper_part, preferred_element_type=jnp.float32
    )
    return first_operand + jnp.einsum(
        "tf,tk->fk", left_rows, lower_part, preferred_element_type=jnp.float32
    )


def local(
    gated_hidden_input,
    frozen,
    head_gradient_rows,
    down_factor_weight,
    up_factor_weight,
    final_norm_gain,
    logratio,
    starts,
):
    precise_result = lax.Precision.HIGHEST
    row_block = frozen.shape[2]
    model_width = frozen.shape[3]
    own_hidden = gated_hidden_input.reshape(-1, gated_hidden_input.shape[3])
    position_shape = (1, 1, row_block)
    positions = lax.axis_index("ctx") * row_block + lax.broadcasted_iota(
        jnp.int32, position_shape, 2
    )
    keep_mask = (positions >= starts[:, :, None]).astype(jnp.float32)
    seq_sum = lax.psum(jnp.sum(keep_mask * logratio, axis=2), "ctx")
    margin = DPO_BETA * (seq_sum[:, 0] - seq_sum[:, 1])
    preference_pair_loss = jnp.logaddexp(0.0, -margin)
    sides = jnp.array([1.0, -1.0], jnp.float32)
    row_gradient_slope = (
        (-DPO_BETA * jax.nn.sigmoid(-margin))[:, None, None] * sides[None, :, None] * keep_mask
    ).reshape(-1)
    up_complete_matrix, gain_full = (
        lax.all_gather(up_factor_weight, "dp", axis=1, tiled=True),
        lax.all_gather(final_norm_gain, "dp", axis=0, tiled=True),
    )
    gain_f32 = gain_full.astype(jnp.float32)
    columns = own_hidden
    adapter_bfloat_copy = jnp.dot(
        columns,
        lax.all_gather(down_factor_weight, "dp", axis=0, tiled=True),
        preferred_element_type=jnp.float32,
    ).astype(jnp.bfloat16)
    residual_row_block = frozen.reshape(-1, model_width).astype(jnp.float32)
    policy_hidden_state = residual_row_block + ADAPTER_SCALING * jnp.dot(
        adapter_bfloat_copy, up_complete_matrix, preferred_element_type=jnp.float32
    )
    policy_rms = jnp.sqrt(
        jnp.mean(policy_hidden_state * policy_hidden_state, axis=1) + NORM_EPSILON
    )
    gained = (
        row_gradient_slope[:, None]
        * head_gradient_rows.reshape(-1, model_width).astype(jnp.float32)
        * gain_f32[None, :]
    )
    inner = jnp.sum(gained * policy_hidden_state, axis=1)
    gradient_state_rows = (
        gained / policy_rms[:, None]
        - policy_hidden_state
        * (inner / (model_width * policy_rms * policy_rms * policy_rms))[:, None]
    )
    gradient_reduced_precision = ADAPTER_SCALING * jnp.dot(
        gradient_state_rows, up_complete_matrix.astype(jnp.float32).T, precision=precise_result
    )
    columns = own_hidden
    down_factor_portion = lax.psum_scatter(
        token_contract(columns, gradient_reduced_precision), "dp", scatter_dimension=0, tiled=True
    )
    upper_part = gradient_state_rows.astype(jnp.bfloat16)
    lower_part = (gradient_state_rows - upper_part.astype(jnp.float32)).astype(jnp.bfloat16)
    first_operand = jnp.einsum(
        "td,tk->dk", upper_part, adapter_bfloat_copy, preferred_element_type=jnp.float32
    )
    second_operand = jnp.einsum(
        "td,tk->dk", lower_part, adapter_bfloat_copy, preferred_element_type=jnp.float32
    )
    up_factor_portion = lax.psum_scatter(
        ADAPTER_SCALING * (first_operand + second_operand), "dp", scatter_dimension=0, tiled=True
    )
    gradient_down_factor, gradient_up_transposed = lax.psum(
        (down_factor_portion, up_factor_portion), "ctx"
    )
    return (preference_pair_loss, gradient_down_factor, gradient_up_transposed.T)


def solution(mesh):
    return jax.shard_map(
        local,
        mesh=mesh,
        in_specs=(
            P("dp", None, "ctx", None),
            P("dp", None, "ctx", None),
            P("dp", None, "ctx", None),
            P("dp", None),
            P(None, "dp"),
            P("dp"),
            P("dp", None, "ctx"),
            P("dp", None),
        ),
        out_specs=(P("dp"), P("dp", None), P(None, "dp")),
        check_vma=False,
    )
```

profile of v0, /device:TPU:1, one launch (start us, length us, event | category | flops | bytes accessed | tf_op | source)
XLA Modules:
  0.0 1384.5 jit_solution(7279494489921872206)
XLA Ops:
  7.2 0.0 all-gather.7.cloned.1.call-start
  7.2 0.7 all-gather.7.cloned.1.call-update
  7.9 0.0 all-gather.5.cloned.1.call-start
  7.9 0.7 all-gather.5.cloned.1.call-update
  8.6 0.0 all-reduce.6.cloned.1.call-start
  8.7 0.9 fusion.14
  9.6 8.3 psum.21
  17.8 0.6 fusion.16
  19.8 0.7 broadcast_multiply_fusion
  20.5 0.1 mul.110
  20.5 0.1 mul.111
  20.6 0.1 ge.40
  20.7 0.7 ge.41
  21.4 0.1 ge.42
  21.5 154.2 %all-gather = bf16[64,1,128]{2,1,0:T(2,128)(2,1)S(1)} all-gather(bf16[1,1,128]{2,1,0:T(2,128)(2,1)} %bitcast.45), channel_id=1, replica_groups=mesh['dp'=64,'ctx'=4] {'dp'}, dimensions={0}, use_global_device_ids=true | all-gather | bytes 16640 | tf_op jit(solution)/shard_map/all_gather | solution.py:50
  175.7 0.0 all-gather.7.cloned.1.call-done
  175.8 6.5 copy.13
  182.3 8.3 reshape.143
  190.6 7.1 convolution_convert_fusion
  197.7 36.5 %all-gather.5.cloned.1.call-done = bf16[64,8192]{1,0:T(8,128)(2,1)} async-done(((bf16[64,128]{1,0:T(8,128)(2,1)}), bf16[64,8192]{1,0:T(8,128)(2,1)}) %all-gather.5.cloned.1.call-update) | async-done | bytes 1048592 | tf_op jit(solution)/shard_map/all_gather | solution.py:49
  234.2 0.0 copy-done.2
  234.2 3.9 multiply_reduce_fusion
  238.1 0.0 copy-start.3
  238.1 0.0 slice-start.1
  238.1 1.1 fusion.6
  239.2 0.1 copy-done.3
  239.4 2.6 convolution_multiply_fusion.1
  241.9 0.0 slice-done
  241.9 0.0 slice-done.1
  242.0 1.1 fusion.12
  243.1 0.0 copy-done
  243.1 4.6 fusion
  247.7 0.0 all-reduce.6.cloned.1.call-update
  247.8 0.0 reduce-scatter.3.cloned.1.call-start
  247.8 0.0 copy-start.1
  247.8 2.8 fusion.9
  250.6 0.7 copy-done.1
  251.3 1.8 fusion.2
  253.1 0.0 reduce-scatter.3.cloned.1.call-update
  253.1 0.0 all-reduce.4.cloned.1.call-start
  253.2 0.6 dynamic-slice
  254.4 678.2 %all-reduce.6.cloned.1.call-done = f32[29568,64]{0,1:T(8,128)} async-done(((f32[29568,64]{0,1:T(8,128)}), f32[29568,64]{0,1:T(8,128)}) %all-reduce.6.cloned.1.call-update) | async-done | bytes 7569424
  932.6 1.7 constant_dynamic-slice_fusion
  934.3 0.0 all-reduce.4.cloned.1.call-update
  934.4 349.7 %reduce-scatter.3.cloned.1.call-done = f32[128,64]{0,1:T(8,128)} async-done(((f32[8192,64]{0,1:T(8,128)}), f32[128,64]{0,1:T(8,128)}) %reduce-scatter.3.cloned.1.call-update) | async-done | bytes 32784 | tf_op jit(solution)/shard_map/reduce_scatter | solution.py:92
  1284.2 63.0 %psum.23 = f32[64,128]{1,0:T(8,128)} all-reduce(f32[64,128]{1,0:T(8,128)} %bitcast.44), channel_id=1, replica_groups=mesh['dp'=64,'ctx'=4] {'ctx'}, use_global_device_ids=true, to_apply=%region_7.0 | all-reduce | flops 8192 | bytes 65536 | tf_op jit(solution)/shard_map/psum | solution.py:95
  1347.1 28.1 %all-reduce.4.cloned.1.call-done = f32[462,64]{0,1:T(8,128)} async-done(((f32[462,64]{0,1:T(8,128)}), f32[462,64]{0,1:T(8,128)}) %all-reduce.4.cloned.1.call-update) | async-done | bytes 118288 | tf_op jit(solution)/shard_map/psum | solution.py:95
  1375.2 1.6 copy.18
  (11 shorter events, 0.1 us)
Async XLA Ops:
  7.2 168.6 %all-gather.7.cloned.1.call-start = ((), (), s32[]{:S(2)}) async-start(), calls=%async_computation.4 | async-start | bytes 4259840 | tf_op jit(solution)/shard_map/all_gather | solution.py:56
  7.9 226.3 %all-gather.5.cloned.1.call-start = ((), (), s32[]{:S(2)}) async-start(), calls=%async_computation.1 | async-start | bytes 1064960 | tf_op jit(solution)/shard_map/all_gather | solution.py:49
  8.6 924.0 %all-reduce.6.cloned.1.call-start = ((), (), s32[]{:S(2)}) async-start(), calls=%async_computation.5 | async-start | bytes 15138816
  190.6 43.6 %copy-start.2 = (bf16[1,2,64,8192]{3,2,1,0:T(8,128)(2,1)S(1)}, bf16[1,2,64,8192]{3,2,1,0:T(8,128)(2,1)}, u32[]{:S(2)}) copy-start(bf16[1,2,64,8192]{3,2,1,0:T(8,128)(2,1)} %param.11) | copy-start | bytes 6291460
  234.2 7.7 slice-start
  238.1 1.2 copy-start.3
  238.1 3.8 slice-start.1
  239.4 3.8 copy-start
  247.8 1036.4 %reduce-scatter.3.cloned.1.call-start = ((), (), s32[]{:S(2)}) async-start(), calls=%async_computation.3 | async-start | bytes 2129920 | tf_op jit(solution)/shard_map/reduce_scatter | solution.py:92
  247.8 3.5 copy-start.1
  251.3 1.9 copy-start.4
  253.1 1122.1 %all-reduce.4.cloned.1.call-start = ((), (), s32[]{:S(2)}) async-start(), calls=%async_computation.2 | async-start | bytes 262144 | tf_op jit(solution)/shard_map/psum | solution.py:95
Sparse Core Ops, SparseCore 0:
  11.6 128.1 all-gather.6
  143.3 90.8 all-gather.4
  247.9 684.7 all-reduce.5
  935.1 348.9 reduce-scatter.2
  1287.2 87.9 all-reduce.3
where the time goes:
time: 1380 us
  waiting for transfers between devices  1090 us (79%)
  blocking collectives  225 us (16%)
  matrix products  23.9 us (2%)
  local copies, waits for them, and re-layouts  21.1 us (2%)
  between operations  17.2 us (1%)
    unnamed x6, waiting for transfers between devices  680 us
    reduce_scatter x1, waiting for transfers between devices, local(): lax.psum_scatter(ADAPTER_SCALING * (first_operand + second_operand), 'dp'...  350 us
    all_gather x1, blocking collectives, local(): lax.all_gather(final_norm_gain, 'dp', axis=0, tiled=True)  154 us
    psum x1, blocking collectives, local(): lax.psum((down_factor_portion, up_factor_portion), 'ctx')  63 us
    all_gather x1, waiting for transfers between devices, local(): lax.all_gather(up_factor_weight, 'dp', axis=1, tiled=True)  36.5 us
    psum x1, waiting for transfers between devices, local(): lax.psum((down_factor_portion, up_factor_portion), 'ctx')  28.1 us
  transfers between devices with their start and end apart: 5, of which 4 were waited for; matrix products, arithmetic and copies ran while one was open for 2% of the time, Pallas kernels for 0%

commit v1 on v0

v1 whole, which is shorter than its diff:
```python
import jax
import jax.numpy as jnp
from jax import lax
from jax.sharding import Mesh, PartitionSpec as P

ADAPTER_SCALING = 2.0
DPO_BETA = 0.1
NORM_EPSILON = 1e-06

FINE_AXES = ("z", "yh", "x", "yl", "c")
FINE_SHAPE = (8, 2, 4, 2, 2)
DP = ("z", "yh", "x")
CTX = ("yl", "c")
LANES = 640


def spread(values, axes, count):
    copies = jnp.broadcast_to(values[None], (count,) + values.shape)
    return lax.all_to_all(copies, axes, 0, 0, tiled=True)


def exchange_sum(values, axes):
    moved = lax.all_to_all(values, axes, 0, 0, tiled=True)
    return jnp.sum(moved.astype(jnp.float32), axis=0)


def token_contract(values, left_rows):
    upper_part = values.astype(jnp.bfloat16)
    return jnp.einsum("tk,tf->kf", upper_part, left_rows, preferred_element_type=jnp.float32)


def local(
    gated_hidden_input,
    frozen,
    head_gradient_rows,
    down_factor_weight,
    up_factor_weight,
    final_norm_gain,
    logratio,
    starts,
):
    row_block = frozen.shape[2]
    model_width = frozen.shape[3]
    own_hidden = gated_hidden_input.reshape(-1, gated_hidden_input.shape[3])
    down_rows, order = down_factor_weight.shape
    up_columns = up_factor_weight.shape[1]
    used = down_rows + up_columns
    yl, core = lax.axis_index("yl"), lax.axis_index("c")

    gain_columns = final_norm_gain.reshape(-1, order).T
    block = jnp.concatenate([down_factor_weight.T, up_factor_weight, gain_columns], axis=1)
    block = jnp.pad(block, ((0, 0), (0, LANES - block.shape[1])))
    quarter = lax.dynamic_slice_in_dim(block, core * 32 + yl * 16, 16, axis=0)
    held = spread(quarter, "z", 8)
    held = spread(held, ("yh", "yl"), 4)
    held = spread(held, "x", 4)
    held = spread(held, "c", 2)
    held = held.reshape(2, 4, 2, 2, 8, 16, LANES).transpose(0, 3, 5, 4, 2, 1, 6)
    held = held.reshape(order, 64, LANES)
    down_t = held[:, :, :down_rows].reshape(order, -1)
    up_full = held[:, :, down_rows:used].reshape(order, -1)
    gain_full = held[:, :, used : used + gain_columns.shape[1]].transpose(1, 2, 0).reshape(-1)
    gain_f32 = gain_full.astype(jnp.float32)

    position_shape = (1, 1, row_block)
    positions = (yl * 2 + core) * row_block + lax.broadcasted_iota(jnp.int32, position_shape, 2)
    keep_mask = (positions >= starts[:, :, None]).astype(jnp.float32)
    seq_sum = lax.psum(jnp.sum(keep_mask * logratio, axis=2), CTX)
    margin = DPO_BETA * (seq_sum[:, 0] - seq_sum[:, 1])
    preference_pair_loss = jnp.logaddexp(0.0, -margin)
    sides = jnp.array([1.0, -1.0], jnp.float32)
    row_gradient_slope = (
        (-DPO_BETA * jax.nn.sigmoid(-margin))[:, None, None] * sides[None, :, None] * keep_mask
    ).reshape(-1)

    adapter_bfloat_copy = jnp.einsum(
        "tf,kf->tk", own_hidden, down_t, preferred_element_type=jnp.float32
    ).astype(jnp.bfloat16)
    residual_row_block = frozen.reshape(-1, model_width).astype(jnp.float32)
    policy_hidden_state = residual_row_block + ADAPTER_SCALING * jnp.dot(
        adapter_bfloat_copy, up_full, preferred_element_type=jnp.float32
    )
    policy_rms = jnp.sqrt(
        jnp.mean(policy_hidden_state * policy_hidden_state, axis=1) + NORM_EPSILON
    )
    gained = (
        row_gradient_slope[:, None]
        * head_gradient_rows.reshape(-1, model_width).astype(jnp.float32)
        * gain_f32[None, :]
    )
    inner = jnp.sum(gained * policy_hidden_state, axis=1)
    gradient_state_rows = (
        gained / policy_rms[:, None]
        - policy_hidden_state
        * (inner / (model_width * policy_rms * policy_rms * policy_rms))[:, None]
    )
    gradient_low = ADAPTER_SCALING * lax.dot_general(
        gradient_state_rows,
        up_full.astype(jnp.float32),
        (((1,), (1,)), ((), ())),
        precision=lax.Precision.HIGHEST,
    )
    down_gradient = token_contract(gradient_low, own_hidden)
    up_gradient = ADAPTER_SCALING * jnp.einsum(
        "tk,td->kd",
        adapter_bfloat_copy,
        gradient_state_rows.astype(jnp.bfloat16),
        preferred_element_type=jnp.float32,
    )
    packed = jnp.concatenate(
        [
            down_gradient.reshape(order, 64, down_rows).astype(jnp.bfloat16),
            up_gradient.reshape(order, 64, up_columns).astype(jnp.bfloat16),
        ],
        axis=2,
    )
    packed = jnp.pad(packed, ((0, 0), (0, 0), (0, LANES - used)))
    packed = packed.reshape(2, 2, 16, 8, 2, 4, LANES).transpose(0, 5, 3, 4, 1, 2, 6)
    share = exchange_sum(packed, "c").astype(jnp.bfloat16)
    share = exchange_sum(share, "x").astype(jnp.bfloat16)
    share = share.reshape(32, 16, LANES)
    share = exchange_sum(share, ("z", "yh", "yl"))
    whole = spread(share, CTX, 4).reshape(2, 2, 16, LANES).transpose(1, 0, 2, 3)
    whole = whole.reshape(order, LANES)
    return (
        preference_pair_loss,
        whole[:, :down_rows].T,
        whole[:, down_rows:used],
    )


def solution(mesh):
    fine = Mesh(mesh.devices.reshape(FINE_SHAPE), FINE_AXES)
    return jax.shard_map(
        local,
        mesh=fine,
        in_specs=(
            P(DP, None, CTX, None),
            P(DP, None, CTX, None),
            P(DP, None, CTX, None),
            P(DP, None),
            P(None, DP),
            P(DP),
            P(DP, None, CTX),
            P(DP, None),
        ),
        out_specs=(P(DP), P(DP, None), P(None, DP)),
        check_vma=False,
    )
```

time: 1380 us -> 208 us (0.15)
  waiting for transfers between devices: 1090 us -> 3.77 us
  blocking collectives: 225 us -> 113 us
  local copies, waits for them, and re-layouts: 21.1 us -> 48.3 us
    unnamed x6 -> x0, waiting for transfers between devices: 680 us -> none
    reduce_scatter x1 -> x0, waiting for transfers between devices: 350 us -> none  [local(): lax.psum_scatter(ADAPTER_SCALING * (first_operand + second_operand), 'dp'...]
    all_gather x1 -> x0, blocking collectives: 154 us -> none  [local(): lax.all_gather(final_norm_gain, 'dp', axis=0, tiled=True)]
    all_to_all x0 -> x6, blocking collectives: none -> 104 us  [the longest x3 66.1 us: exchange_sum(): moved = lax.all_to_all(values, axes, 0, 0, tiled=True)]
    psum x2 -> x1, blocking collectives: 71.2 us -> 9.36 us  [local(): seq_sum = lax.psum(jnp.sum(keep_mask * logratio, axis=2), CTX)]
    all_gather x2 -> x0, waiting for transfers between devices: 36.6 us -> none  [the longest x1 36.5 us: local(): lax.all_gather(up_factor_weight, 'dp', axis=1, tiled=True)]
    psum x1 -> x0, waiting for transfers between devices: 28.1 us -> none  [local(): lax.psum((down_factor_portion, up_factor_portion), 'ctx')]
    reshape x0 -> x4, local copies, waits for them, and re-layouts: none -> 20.4 us  [the longest x1 10.5 us: local(): own_hidden = gated_hidden_input.reshape(-1, gated_hidden_input.shape[3])]
  transfers between devices with their start and end apart: 5 -> 2, of which waited for: 4 -> 1; matrix products, arithmetic and copies ran while one was open for 2% -> 10% of each run, Pallas kernels for 0% -> 0%
where the time goes in v1:
time: 208 us; the launch traced here: 206 us
  blocking collectives  113 us (54%)
  local copies, waits for them, and re-layouts  48.3 us (23%)
  matrix products  18.7 us (9%)
  starting transfers between devices  10.8 us (5%)
  other arithmetic  8.35 us (4%)
  waiting for transfers between devices  3.77 us (2%)
  between operations  3.49 us (2%)
    all_to_all x3, blocking collectives, exchange_sum(): moved = lax.all_to_all(values, axes, 0, 0, tiled=True)  66.1 us
    all_to_all x3, blocking collectives, spread(): return lax.all_to_all(copies, axes, 0, 0, tiled=True)  37.6 us
    all_to_all x2, starting transfers between devices, spread(): return lax.all_to_all(copies, axes, 0, 0, tiled=True)  10.8 us
    reshape x1, local copies, waits for them, and re-layouts, local(): own_hidden = gated_hidden_input.reshape(-1, gated_hidden_input.shape[3])  10.5 us
    psum x1, blocking collectives, local(): seq_sum = lax.psum(jnp.sum(keep_mask * logratio, axis=2), CTX)  9.36 us
    dot_general x1, local copies, waits for them, and re-layouts, token_contract(): jnp.einsum('tk,tf->kf', upper_part, left_rows, preferred_element_type=jnp...  9.12 us
    slice x2, local copies, waits for them, and re-layouts, local(): down_t = held[:, :, :down_rows].reshape(order, -1)  8.79 us
    reshape x1, local copies, waits for them, and re-layouts, local(): down_t = held[:, :, :down_rows].reshape(order, -1)  8.32 us
  transfers between devices with their start and end apart: 2, of which 1 were waited for; matrix products, arithmetic and copies ran while one was open for 10% of the time, Pallas kernels for 0%

profile of v1, /device:TPU:1, one launch (start us, length us, event | category | flops | bytes accessed | tf_op | source)
XLA Modules:
  0.0 206.5 jit_solution(839864016568825967)
XLA Ops:
  0.6 0.7 reshape.175
  1.4 0.1 copy.47
  1.5 0.8 fusion.24
  2.3 17.0 %all_to_all.40 = bf16[8,16,640]{2,1,0:T(8,128)(2,1)S(1)} all-to-all(bf16[8,16,640]{2,1,0:T(8,128)(2,1)S(1)} %broadcast_in_dim.10), channel_id=1, replica_groups=mesh['z'=8,'yh'=2,'x'=4,'yl'=2,'c'=2] {'z'}, dimensions={0} | all-to-all | bytes 327680 | tf_op jit(solution)/shard_map/all_to_all | solution.py:19
  19.3 11.7 %all_to_all.41 = bf16[4,8,16,640]{3,2,1,0:T(8,128)(2,1)S(1)} all-to-all(bf16[4,8,16,640]{3,2,1,0:T(8,128)(2,1)S(1)} %broadcast_in_dim.11), channel_id=1, replica_groups=mesh['z'=8,'yh'=2,'x'=4,'yl'=2,'c'=2] {'yh','yl'}, dimensions={0} | all-to-all | bytes 1310720 | tf_op jit(solution)/shard_map/all_to_all | solution.py:19
  31.1 1.8 broadcast_in_dim.12
  32.9 4.0 %all-to-all-start.2 = ((bf16[4,4,8,16,640]{4,3,2,1,0:T(8,128)(2,1)}), bf16[4,4,8,16,640]{4,3,2,1,0:T(8,128)(2,1)S(1)}, u32[]{:S(2)}, u32[]{:S(2)}) async-start(bf16[4,4,8,16,640]{4,3,2,1,0:T(8,128)(2,1)} %broadcast_in_dim.12), calls=%async_computation.2 | async-start | bytes 5242880 | tf_op jit(solution)/shard_map/all_to_all | solution.py:19
  36.9 0.2 fusion.25
  37.1 9.4 %psum.7 = f32[1,2]{1,0:T(1,128)S(1)} all-reduce(f32[1,2]{1,0:T(1,128)S(1)} %bitcast.83), channel_id=1, replica_groups=mesh['z'=8,'yh'=2,'x'=4,'yl'=2,'c'=2] {'yl','c'}, use_global_device_ids=true, to_apply=%region_1.2 | all-reduce | flops 2 | bytes 16 | tf_op jit(solution)/shard_map/psum | solution.py:68
  46.4 0.1 ge.40
  46.5 0.6 fusion.27
  48.5 0.1 mul.120
  48.6 0.1 mul.121
  48.7 0.1 ge.41
  48.7 0.1 ge.42
  48.8 10.5 %copy.52 = bf16[128,29568]{0,1:T(8,128)(2,1)} copy(bf16[128,29568]{1,0:T(8,128)(2,1)} %bitcast.64) | data formatting | bytes 15138816 | tf_op jit(solution)/shard_map/reshape | solution.py:44
  59.3 9.1 %dot_general.23 = bf16[64,462,128]{2,1,0:T(8,128)(2,1)} reshape(bf16[29568,128]{1,0:T(8,128)(2,1)} %bitcast.66) | data formatting | bytes 15138816 | tf_op jit(solution)/shard_map/tk,tf->kf/dot_general | solution.py:29
  68.4 0.7 broadcast_in_dim.13
  69.2 8.9 %all_to_all.42 = bf16[2,4,4,8,16,640]{5,4,3,2,1,0:T(8,128)(2,1)S(1)} all-to-all(bf16[2,4,4,8,16,640]{5,4,3,2,1,0:T(8,128)(2,1)S(1)} %broadcast_in_dim.13), channel_id=1, replica_groups=mesh['z'=8,'yh'=2,'x'=4,'yl'=2,'c'=2] {'c'}, dimensions={0} | all-to-all | bytes 10485760 | tf_op jit(solution)/shard_map/all_to_all | solution.py:19
  78.1 0.9 copy.48
  79.0 0.4 convert_bitcast_fusion
  79.3 1.9 copy-done
  81.2 2.3 %slice.29 = bf16[64,64,462]{2,0,1:T(8,128)(2,1)} slice(bf16[64,64,640]{2,0,1:T(8,128)(2,1)S(1)} %bitcast.68), slice={[0:64], [0:64], [0:462]} | slice | bytes 7569408 | tf_op jit(solution)/shard_map/slice | solution.py:60
  83.6 0.7 copy.49
  84.2 0.1 reshape.188
  84.4 6.5 %copy.50 = bf16[64,64,462]{2,1,0:T(8,128)(2,1)} copy(bf16[64,64,462]{2,0,1:T(8,128)(2,1)} %slice.29) | data formatting | bytes 7569408 | tf_op jit(solution)/shard_map/slice | solution.py:60
  90.8 8.3 %reshape.178 = bf16[64,29568]{1,0:T(8,128)(2,1)} reshape(bf16[64,64,462]{2,1,0:T(8,128)(2,1)} %copy.50) | data formatting | bytes 7569408 | tf_op jit(solution)/shard_map/reshape | solution.py:60
  99.1 7.1 %convolution_convert_fusion.1 = bf16[64,128]{1,0:T(8,128)(2,1)S(1)} fusion(bf16[64,29568]{1,0:T(8,128)(2,1)} %reshape.178, bf16[128,29568]{1,0:T(8,128)(2,1)} %bitcast.65), kind=kOutput, calls=%fused_computation.23 | convolution fusion | flops 484450304 | bytes 11370496 | tf_op jit(solution)/shard_map/tf,kf->tk/dot_general | solution.py:76
  106.3 3.5 %multiply_reduce_fusion = (f32[128]{0:T(128)S(1)}, f32[128]{0:T(128)S(1)}, f32[128,8192]{1,0:T(8,128)S(1)}) fusion(f32[8192]{0:T(1024)S(1)} %reshape.188, bf16[1,2,64,8192]{3,2,1,0:T(8,128)(2,1)S(1)} %copy-done.1, f32[128]{0:T(128)S(1)} %compare_select_fusion, bf16[64,128]{1,0:T(8,128)(2,1)S(1)} %convolution_convert_fusion.1, ...), kind=kOutput, calls=%fused_computation.15 | convolution fusion | flops 144703232 | bytes 9487872 | tf_op jit(solution)/shard_map/dot_general | solution.py:80
  109.9 1.1 fusion.8
  111.0 4.5 %fusion.15 = bf16[128,64,1]{0,1,2:T(8,128)(2,1)S(1)} fusion(f32[128,8192]{1,0:T(8,128)S(1)} %fusion.8, bf16[64,64,640]{2,0,1:T(8,128)(2,1)} %bitcast.70), kind=kOutput, calls=%fused_computation.24 | convolution fusion | flops 805322752 | bytes 5259264 | tf_op jit(solution)/shard_map/dot_general | solution.py:97
  115.5 0.4 fusion.11
  115.9 0.3 copy.74
  116.2 3.2 %convolution_convert_fusion = bf16[64,64,462]{2,0,1:T(8,128)(2,1)S(1)} fusion(bf16[128,64,1]{0,1,2:T(8,128)(2,1)S(1)} %fusion.15, bf16[64,462,128]{2,1,0:T(8,128)(2,1)S(1)} %bitcast.63), kind=kOutput, calls=%fused_computation.16 | convolution fusion | flops 486334464 | bytes 11370496 | tf_op jit(solution)/shard_map/tk,tf->kf/dot_general | solution.py:29
  119.4 1.4 fusion.4
  120.8 0.9 copy.73
  121.7 9.2 %all_to_all.43 = bf16[2,4,8,2,2,16,640]{6,5,4,1,3,2,0:T(8,128)(2,1)} all-to-all(bf16[2,4,8,2,2,16,640]{6,5,4,1,3,2,0:T(8,128)(2,1)S(1)} %bitcast.73), channel_id=1, replica_groups=mesh['z'=8,'yh'=2,'x'=4,'yl'=2,'c'=2] {'c'}, dimensions={0} | all-to-all | bytes 10485760 | tf_op jit(solution)/shard_map/all_to_all | solution.py:23
  130.9 3.8 %reduce_sum.66 = bf16[4,8,2,2,16,640]{5,4,3,0,2,1:T(8,128)(2,1)S(1)} reduce(bf16[2,4,8,2,2,16,640]{6,5,4,1,3,2,0:T(8,128)(2,1)} %all_to_all.43, bf16[]{:T(256)} %constant.39.clone.1), dimensions={0}, to_apply=%region_4.5 | reduce | flops 1310720 | bytes 7864322 | tf_op jit(solution)/shard_map/reduce_sum | solution.py:24
  134.7 0.4 copy.56
  135.1 35.4 %all_to_all.44 = bf16[4,8,2,2,16,640]{5,4,3,2,1,0:T(8,128)(2,1)S(1)} all-to-all(bf16[4,8,2,2,16,640]{5,4,3,2,1,0:T(8,128)(2,1)S(1)} %copy.56), channel_id=1, replica_groups=mesh['z'=8,'yh'=2,'x'=4,'yl'=2,'c'=2] {'x'}, dimensions={0} | all-to-all | bytes 5242880 | tf_op jit(solution)/shard_map/all_to_all | solution.py:23
  170.5 0.5 reduce_sum.67
  171.1 21.5 %all_to_all.45 = bf16[32,16,640]{2,1,0:T(8,128)(2,1)S(1)} all-to-all(bf16[32,16,640]{2,1,0:T(8,128)(2,1)S(1)} %bitcast.75), channel_id=1, replica_groups=mesh['z'=8,'yh'=2,'x'=4,'yl'=2,'c'=2] {'z','yh','yl'}, dimensions={0} | all-to-all | bytes 1310720 | tf_op jit(solution)/shard_map/all_to_all | solution.py:23
  192.6 0.1 convert_reduce_fusion
  192.7 0.7 broadcast_in_dim.14
  193.3 6.8 %all-to-all-start.7 = ((f32[4,16,640]{2,1,0:T(8,128)}), f32[4,16,640]{2,1,0:T(8,128)S(1)}, u32[]{:S(2)}, u32[]{:S(2)}) async-start(f32[4,16,640]{2,1,0:T(8,128)} %broadcast_in_dim.14), calls=%async_computation.7 | async-start | bytes 327680 | tf_op jit(solution)/shard_map/all_to_all | solution.py:19
  200.2 3.8 %all-to-all-done.7 = f32[4,16,640]{2,1,0:T(8,128)S(1)} async-done(((f32[4,16,640]{2,1,0:T(8,128)}), f32[4,16,640]{2,1,0:T(8,128)S(1)}, u32[]{:S(2)}, u32[]{:S(2)}) %all-to-all-start.7) | async-done | bytes 163872 | tf_op jit(solution)/shard_map/all_to_all | solution.py:19
  204.0 0.7 slice.32
  204.7 0.7 slice_bitcast_fusion.1
  (25 shorter events, 0.1 us)
Async XLA Ops:
  31.1 5.8 %copy-start.2 = (f32[1,2,64]{2,1,0:T(2,128)S(1)}, f32[1,2,64]{2,1,0:T(2,128)}, u32[]{:S(2)}) copy-start(f32[1,2,64]{2,1,0:T(2,128)} %param.15) | copy-start | bytes 1540
  31.1 5.8 %copy-start.3 = (s32[1,2]{1,0:T(1,128)S(1)}, s32[1,2]{1,0:T(1,128)}, u32[]{:S(2)}) copy-start(s32[1,2]{1,0:T(1,128)} %param.16) | copy-start | bytes 28
  31.1 17.4 %copy-start.5 = (f32[2]{0:T(128)S(1)}, f32[2]{0:T(128)}, u32[]{:S(2)}) copy-start(f32[2]{0:T(128)} %constant.47.clone) | copy-start | bytes 28
  32.9 35.6 %all-to-all-start.2 = ((bf16[4,4,8,16,640]{4,3,2,1,0:T(8,128)(2,1)}), bf16[4,4,8,16,640]{4,3,2,1,0:T(8,128)(2,1)S(1)}, u32[]{:S(2)}, u32[]{:S(2)}) async-start(bf16[4,4,8,16,640]{4,3,2,1,0:T(8,128)(2,1)} %broadcast_in_dim.12), calls=%async_computation.2 | async-start | bytes 5242880 | tf_op jit(solution)/shard_map/all_to_all | solution.py:19
  78.9 2.3 %copy-start = (bf16[2,2,16,8,2,4,640]{6,2,1,0,5,4,3:T(8,128)(2,1)}, bf16[2,2,16,8,2,4,640]{6,2,1,0,5,4,3:T(8,128)(2,1)S(1)}, u32[]{:S(2)}) copy-start(bf16[2,2,16,8,2,4,640]{6,2,1,0,5,4,3:T(8,128)(2,1)S(1)} %copy.48) | copy-start | bytes 15728644
  99.1 7.1 %copy-start.1 = (bf16[1,2,64,8192]{3,2,1,0:T(8,128)(2,1)S(1)}, bf16[1,2,64,8192]{3,2,1,0:T(8,128)(2,1)}, u32[]{:S(2)}) copy-start(bf16[1,2,64,8192]{3,2,1,0:T(8,128)(2,1)} %param.11) | copy-start | bytes 6291460
  99.1 7.1 %copy-start.4 = (bf16[1,2,64,8192]{3,2,1,0:T(8,128)(2,1)S(1)}, bf16[1,2,64,8192]{3,2,1,0:T(8,128)(2,1)}, u32[]{:S(2)}) copy-start(bf16[1,2,64,8192]{3,2,1,0:T(8,128)(2,1)} %param.10) | copy-start | bytes 6291460
  109.9 6.3 %slice-start = ((s8[7602176]{0:T(1024)(128)(4,1)}), s8[4194304]{0:T(1024)(128)(4,1)S(1)}, s32[]{:S(2)}) async-start(s8[7602176]{0:T(1024)(128)(4,1)} %bitcast.62), calls=%async_computation.8 | async-start | bytes 8388608
  111.0 5.2 %slice-start.1 = ((s8[7602176]{0:T(1024)(128)(4,1)}), s8[3407872]{0:T(1024)(128)(4,1)S(1)}, s32[]{:S(2)}) async-start(s8[7602176]{0:T(1024)(128)(4,1)} %bitcast.62), calls=%async_computation.9 | async-start | bytes 6815744
  193.3 10.6 %all-to-all-start.7 = ((f32[4,16,640]{2,1,0:T(8,128)}), f32[4,16,640]{2,1,0:T(8,128)S(1)}, u32[]{:S(2)}, u32[]{:S(2)}) async-start(f32[4,16,640]{2,1,0:T(8,128)} %broadcast_in_dim.14), calls=%async_computation.7 | async-start | bytes 327680 | tf_op jit(solution)/shard_map/all_to_all | solution.py:19

commit v2 on v1

v2 whole, which is shorter than its diff:
```python
import jax
import jax.numpy as jnp
from jax import lax
from jax.experimental import pallas as pl
from jax.experimental.pallas import tpu as pltpu
from jax.sharding import Mesh, PartitionSpec as P

SCALE = 2.0
BETA = 0.1
EPS = 1e-06

FINE_AXES = ("z", "yh", "x", "yl", "c")
FINE_SHAPE = (8, 2, 4, 2, 2)
DP = ("z", "yh", "x")
CTX = ("yl", "c")
Y = ("yh", "yl")

LANES = 640
UP = 128
DOWN = 462
GAIN_AT = UP + DOWN
SUMS_AT = GAIN_AT + 32
CHUNKS = 64
ORDER = 64
BF, F32 = jnp.bfloat16, jnp.float32
NT = (((1,), (1,)), ((), ()))
NN = (((1,), (0,)), ((), ()))


def dot(a, b, dims):
    return lax.dot_general(a, b, dims, preferred_element_type=F32)


def slots(place, sign):
    py, px, pc = place[1], place[2], place[3]
    dxs = [(sign * (px - x)) & 3 for x in range(4)]
    dys = [(sign * (py - y)) & 3 for y in range(4)]
    cores = [((pc + c) & 1) * 128 for c in range(2)]

    def flat(chunk, q):
        z, yh, x = chunk // 8, chunk // 4 % 2, chunk % 4
        c, y = q // 2, yh * 2 + q % 2
        if z < 4:
            return cores[c] + dys[y] * 4 + (x * 16 + z)
        return cores[c] + dys[y] * 16 + dxs[x] * 4 + (60 + z)

    return flat


def kernel(place_ref, starts_ref, *refs):
    parts, (hidden_hbm, frozen_hbm, head_hbm) = refs[:10], refs[10:13]
    outs, margin_ref = refs[13:23], refs[23]
    hid, fro, hea, wt, up, gains, gain, pol, block, sems = refs[24:]
    width = fro.shape[1]

    def ranges():
        begin = 0
        for i in range(10):
            size = 64 if i % 5 == 0 else 16
            yield pl.ds(begin, size)
            begin += size

    loads = [
        pltpu.make_async_copy(parts[i], block.at[at], sems.at[i]) for i, at in enumerate(ranges())
    ]
    loads.append(pltpu.make_async_copy(hidden_hbm, hid, sems.at[10]))
    loads.append(pltpu.make_async_copy(frozen_hbm, fro, sems.at[11]))
    loads.append(pltpu.make_async_copy(head_hbm, hea, sems.at[12]))
    for copy in loads:
        copy.start()
    for copy in loads[:10]:
        copy.wait()

    pz, py, px, pc = (place_ref[i] for i in range(4))
    sums = jnp.zeros((1, 128), F32)
    for c in range(2):
        for yl in range(2):
            dy = (py - ((py & 2) + yl)) & 3
            inside = jnp.where(pz < 4, px * 16 + dy * 4 + pz, 60 + dy * 16 + pz)
            held = block[((pc + c) & 1) * 128 + inside]
            sums += held[0:1, LANES - 128 :].astype(F32)
    lane = SUMS_AT - (LANES - 128)
    sides = [sum(sums[:, lane + 3 * s + j : lane + 3 * s + j + 1] for j in range(3)) for s in (0, 1)]
    margin = BETA * (sides[0] - sides[1])
    margin_ref[...] = jnp.broadcast_to(margin, margin_ref.shape)
    row = lax.broadcasted_iota(jnp.int32, (128, 1), 0)
    position = (row & 63) + ((py & 1) * 2 + pc) * 64
    start = jnp.where(row < 64, starts_ref[0, 0], starts_ref[0, 1])
    weight = jnp.where(row < 64, -BETA, BETA)
    slope = jnp.where(position >= start, weight, 0.0) / (1.0 + jnp.exp(margin))

    source = slots(place_ref, 1)
    for chunk in range(CHUNKS):
        for q in range(4):
            held = block[source(chunk, q)]
            rows = slice(16 * q, 16 * q + 16)
            up[rows, chunk * UP : (chunk + 1) * UP] = held[:, :UP]
            wt[rows, chunk * DOWN : (chunk + 1) * DOWN] = held[:, UP : UP + DOWN]
            gains[q, chunk : chunk + 1, :] = held[0:1, LANES - 128 :].astype(F32)
    lane = GAIN_AT - (LANES - 128)
    gain[...] = jnp.concatenate([gains[q][:, lane : lane + 32] for q in range(4)], axis=1)

    loads[10].wait()
    tile = 2688

    def low_step(i, total):
        at = pl.ds(pl.multiple_of(i * tile, 128), tile)
        return total + dot(hid[:, at], wt[:, at], NT)

    low = lax.fori_loop(0, wt.shape[1] // tile, low_step, jnp.zeros((128, ORDER), F32)).astype(BF)
    low_t = low.astype(F32).T.astype(BF)

    loads[11].wait()
    loads[12].wait()
    step = 512

    def gained(i):
        pieces = []
        for j in range(step // 128):
            at = pl.ds(pl.multiple_of(i * step + j * 128, 128), 128)
            pieces.append(hea[:, at].astype(F32) * gain[pl.ds(i * (step // 128) + j, 1), :])
        return jnp.concatenate(pieces, axis=1)

    def fold(v):
        return sum(v[:, 128 * j : 128 * j + 128] for j in range(step // 128))

    def state_step(i, carry):
        squares, inner = carry
        at = pl.ds(pl.multiple_of(i * step, 128), step)
        state = fro[:, at].astype(F32) + SCALE * dot(low, up[:, at], NN)
        pol[:, at] = state
        return squares + fold(state * state), inner + fold(gained(i) * state)

    zero = jnp.zeros((128, 128), F32)
    squares, inner = lax.fori_loop(0, width // step, state_step, (zero, zero))
    rms = jnp.sqrt(jnp.sum(squares, axis=1, keepdims=True) / width + EPS)
    inner = slope * jnp.sum(inner, axis=1, keepdims=True)
    first = slope / rms
    second = inner / (width * rms * rms * rms)

    target = slots(place_ref, -1)
    total = jnp.zeros((128, ORDER), F32)
    for i in range(width // step):
        at = slice(i * step, (i + 1) * step)
        grad = gained(i) * first - pol[:, at] * second
        high = grad.astype(BF)
        rest = (grad - high.astype(F32)).astype(BF)
        total += dot(high, up[:, at], NT) + dot(rest, up[:, at], NT)
        share = (SCALE * dot(low_t, high, NN)).astype(BF)
        for j in range(step // 128):
            for q in range(4):
                block[target(i * (step // 128) + j, q), :, :UP] = share[
                    16 * q : 16 * q + 16, 128 * j : 128 * j + 128
                ]
    grad_low = (SCALE * total).T.astype(BF)

    for chunk in range(CHUNKS):
        begin = chunk * DOWN // 128 * 128
        shift = chunk * DOWN - begin
        span = 512 if shift + DOWN <= 512 else 640
        share = dot(grad_low, hid[:, begin : begin + span], NN)
        if shift:
            share = pltpu.roll(share, span - shift, 1)
        share = share[:, :512].astype(BF)
        for q in range(4):
            block[target(chunk, q), :, UP:] = share[16 * q : 16 * q + 16]

    stores = [
        pltpu.make_async_copy(block.at[at], outs[i], sems.at[i]) for i, at in enumerate(ranges())
    ]
    for copy in stores:
        copy.start()
    for copy in stores:
        copy.wait()


def shares(place, starts, parts, hidden, frozen, head):
    rows, units = hidden.shape
    width = frozen.shape[1]
    any_space = pl.BlockSpec(memory_space=pl.ANY)
    smem = pl.BlockSpec(memory_space=pltpu.SMEM)
    sizes = ([64] + [16] * 4) * 2
    outs = pl.pallas_call(
        kernel,
        out_shape=[jax.ShapeDtypeStruct((n, 16, LANES), BF) for n in sizes]
        + [jax.ShapeDtypeStruct((8, 128), F32)],
        in_specs=[smem, smem] + [any_space] * 13,
        out_specs=[any_space] * 10 + [pl.BlockSpec(memory_space=pltpu.VMEM)],
        scratch_shapes=[
            pltpu.VMEM((rows, units), BF),
            pltpu.VMEM((rows, width), BF),
            pltpu.VMEM((rows, width), BF),
            pltpu.VMEM((ORDER, units), BF),
            pltpu.VMEM((ORDER, width), BF),
            pltpu.VMEM((4, CHUNKS, 128), F32),
            pltpu.VMEM((CHUNKS, 128), F32),
            pltpu.VMEM((rows, width), F32),
            pltpu.VMEM((256, 16, LANES), BF),
            pltpu.SemaphoreType.DMA((13,)),
        ],
        compiler_params=pltpu.CompilerParams(vmem_limit_bytes=40 * 1024 * 1024),
        cost_estimate=pl.CostEstimate(
            flops=2 * rows * ORDER * (2 * units + 4 * width),
            bytes_accessed=2 * rows * (units + 2 * width) + 4 * 256 * 16 * LANES,
            transcendentals=0,
        ),
    )(place, starts, *parts, hidden, frozen, head)
    return outs[:5], outs[5:10], outs[10][0, 0:1]


def ring(values, axes, count, step):
    return lax.ppermute(values, axes, [(i, (i + step) % count) for i in range(count)])


def spread(values, axes, count):
    copies = jnp.broadcast_to(values[None], (count,) + values.shape)
    return lax.all_to_all(copies, axes, 0, 0, tiled=True)


def together(*values):
    return lax.optimization_barrier(tuple(values))


def total_of(*values):
    return sum(v.astype(F32) for v in values)


def local(
    gated_hidden_input,
    frozen,
    head_gradient_rows,
    down_factor_weight,
    up_factor_weight,
    final_norm_gain,
    logratio,
    starts,
):
    row_block = frozen.shape[2]
    yh, yl, core = lax.axis_index("yh"), lax.axis_index("yl"), lax.axis_index("c")
    place = jnp.stack([lax.axis_index("z"), yh * 2 + yl, lax.axis_index("x"), core])

    positions = (yl * 2 + core) * row_block + lax.broadcasted_iota(
        jnp.int32, (1, 1, row_block), 2
    )
    partial = jnp.sum(jnp.where(positions >= starts[:, :, None], logratio, 0.0), axis=2)[0]
    high = lax.reduce_precision(partial, 8, 7)
    middle = lax.reduce_precision(partial - high, 8, 7)
    low = partial - high - middle
    sums = jnp.stack([high, middle, low], axis=1).reshape(1, 6).astype(BF)

    begin = core * 32 + yl * 16
    rows_of_down = lax.dynamic_slice_in_dim(down_factor_weight.T, begin, 16, axis=0)
    rows_of_up = lax.dynamic_slice_in_dim(up_factor_weight, begin, 16, axis=0)
    gain_part = lax.dynamic_slice_in_dim(final_norm_gain, (core * 2 + yl) * 32, 32)
    tail = jnp.concatenate([gain_part[None], sums, jnp.zeros((1, LANES - SUMS_AT - 6), BF)], axis=1)
    quarter = jnp.concatenate(
        [rows_of_up, rows_of_down, jnp.broadcast_to(tail, (16, tail.shape[1]))], axis=1
    )
    by_z = spread(quarter, "z", 8)
    near, far = together(by_z[:4], by_z[4:])
    near_parts = [ring(near, Y, 4, s) for s in (1, 2, 3)]
    far_parts = [ring(far, "x", 4, s) for s in (1, 2, 3)]
    moved = together(near, far, *near_parts, *far_parts)
    near = jnp.stack([moved[0], *moved[2:5]]).reshape(16, 16, LANES)
    far = jnp.stack([moved[1], *moved[5:8]]).reshape(16, 16, LANES)
    near, far = together(near, far)
    far_rows = [far] + [ring(far, Y, 4, s) for s in (1, 2, 3)]
    near_all = spread(near, "x", 4).reshape(64, 16, LANES)
    own = [near_all, *far_rows]
    other = [ring(v, "c", 2, 1) for v in own]

    own, other, margin = shares(
        place,
        starts,
        [*own, *other],
        gated_hidden_input.reshape(-1, gated_hidden_input.shape[3]),
        frozen.reshape(-1, frozen.shape[3]),
        head_gradient_rows.reshape(-1, frozen.shape[3]),
    )

    came = [ring(v, "c", 2, 1) for v in other]
    chip = [total_of(a, b).astype(BF) for a, b in zip(own, came)]
    far_rows = [ring(chip[1 + s], Y, 4, s) for s in (1, 2, 3)]
    near_all = lax.all_to_all(chip[0].reshape(4, 16, 16, LANES), "x", 0, 0, tiled=True)
    near = jnp.sum(near_all.astype(F32), axis=0).astype(BF).reshape(4, 4, 16, LANES)
    far = total_of(chip[1], *far_rows).astype(BF).reshape(4, 4, 16, LANES)
    near, far = together(near, far)
    near_parts = [ring(near[s], Y, 4, s) for s in (1, 2, 3)]
    far_parts = [ring(far[s], "x", 4, s) for s in (1, 2, 3)]
    moved = together(*near_parts, *far_parts)
    near = total_of(near[0], *moved[:3]).astype(BF)
    far = total_of(far[0], *moved[3:]).astype(BF)
    by_z = lax.all_to_all(jnp.concatenate([near, far]), "z", 0, 0, tiled=True)
    share = jnp.sum(by_z.astype(F32), axis=0)
    whole = spread(share, CTX, 4).reshape(2, 2, 16, LANES).transpose(1, 0, 2, 3)
    whole = whole.reshape(ORDER, LANES)
    return (
        jnp.logaddexp(0.0, -margin),
        whole[:, UP : UP + DOWN].T,
        whole[:, :UP],
    )


def solution(mesh):
    fine = Mesh(mesh.devices.reshape(FINE_SHAPE), FINE_AXES)
    return jax.shard_map(
        local,
        mesh=fine,
        in_specs=(
            P(DP, None, CTX, None),
            P(DP, None, CTX, None),
            P(DP, None, CTX, None),
            P(DP, None),
            P(None, DP),
            P(DP),
            P(DP, None, CTX),
            P(DP, None),
        ),
        out_specs=(P(DP), P(DP, None), P(None, DP)),
        check_vma=False,
    )
```

time: 208 us -> 164 us (0.79)
  blocking collectives: 113 us -> 43.3 us
  local copies, waits for them, and re-layouts: 48.3 us -> 4.4 us
  starting transfers between devices: 10.8 us -> 50 us
  waiting for transfers between devices: 3.77 us -> 38.9 us
  Pallas kernels: 0 us -> 19.1 us
  matrix products: 18.7 us -> 0 us
  other arithmetic: 8.35 us -> 5.31 us
    all_to_all x3 -> x1, blocking collectives: 66.1 us -> 10.9 us  [local(): by_z = lax.all_to_all(jnp.concatenate([near, far]), 'z', 0, 0, tiled=True)]
    ppermute x0 -> x28, starting transfers between devices: none -> 38.7 us  [ring(): lax.ppermute(values, axes, [(i, (i + step) % count) for i in range(count)])]
    ppermute x0 -> x28, waiting for transfers between devices: none -> 36.3 us  [ring(): lax.ppermute(values, axes, [(i, (i + step) % count) for i in range(count)])]
    reshape x4 -> x0, local copies, waits for them, and re-layouts: 20.4 us -> none  [the longest x1 10.5 us: local(): own_hidden = gated_hidden_input.reshape(-1, gated_hidden_input.shape[3])]
    pallas_call x0 -> x1, Pallas kernels: none -> 19.1 us  [shares(): pl.pallas_call(kernel, out_shape=[jax.ShapeDtypeStruct((n, 16, LANES), BF...]
    dot_general x5 -> x0, matrix products: 18.7 us -> none  [the longest x1 7.12 us: local(): jnp.einsum('tf,kf->tk', own_hidden, down_t, preferred_element_type=jnp.fl...]
    psum x1 -> x0, blocking collectives: 9.36 us -> none  [local(): seq_sum = lax.psum(jnp.sum(keep_mask * logratio, axis=2), CTX)]
    dot_general x1 -> x0, local copies, waits for them, and re-layouts: 9.12 us -> none  [token_contract(): jnp.einsum('tk,tf->kf', upper_part, left_rows, preferred_element_type=jnp...]
  transfers between devices with their start and end apart: 2 -> 30, of which waited for: 1 -> 16; matrix products, arithmetic and copies ran while one was open for 10% -> 2% of each run, Pallas kernels for 0% -> 0%
where the time goes in v2:
time: 164 us
  starting transfers between devices  50 us (30%)
  blocking collectives  43.3 us (26%)
  waiting for transfers between devices  38.9 us (24%)
  Pallas kernels  19.1 us (12%)
  other arithmetic  5.31 us (3%)
  local copies, waits for them, and re-layouts  4.4 us (3%)
  between operations  2.77 us (2%)
    ppermute x28, starting transfers between devices, ring(): lax.ppermute(values, axes, [(i, (i + step) % count) for i in range(count)])  38.7 us
    ppermute x28, waiting for transfers between devices, ring(): lax.ppermute(values, axes, [(i, (i + step) % count) for i in range(count)])  36.3 us
    all_to_all x2, blocking collectives, spread(): return lax.all_to_all(copies, axes, 0, 0, tiled=True)  32.4 us
    pallas_call x1, Pallas kernels, shares(): pl.pallas_call(kernel, out_shape=[jax.ShapeDtypeStruct((n, 16, LANES), BF...  19.1 us
    all_to_all x1, blocking collectives, local(): by_z = lax.all_to_all(jnp.concatenate([near, far]), 'z', 0, 0, tiled=True)  10.9 us
    all_to_all x1, starting transfers between devices, spread(): return lax.all_to_all(copies, axes, 0, 0, tiled=True)  7.61 us
    all_to_all x1, starting transfers between devices, local(): lax.all_to_all(chip[0].reshape(4, 16, 16, LANES), 'x', 0, 0, tiled=True)  3.68 us
  transfers between devices with their start and end apart: 30, of which 16 were waited for; matrix products, arithmetic and copies ran while one was open for 2% of the time, Pallas kernels for 0%

profile of v2, /device:TPU:1, one launch (start us, length us, event | category | flops | bytes accessed | tf_op | source)
XLA Modules:
  0.0 163.7 jit_solution(10215616360766632990)
XLA Ops:
  0.7 0.9 fusion.6
  1.8 0.7 constant_dynamic-slice_fusion
  2.5 0.7 dynamic-slice_bitcast_fusion.1
  3.4 17.0 %all_to_all.25 = bf16[8,16,640]{2,1,0:T(8,128)(2,1)S(1)} all-to-all(bf16[8,16,640]{2,1,0:T(8,128)(2,1)S(1)} %broadcast_in_dim.37), channel_id=1, replica_groups=mesh['z'=8,'yh'=2,'x'=4,'yl'=2,'c'=2] {'z'}, dimensions={0} | all-to-all | bytes 327680 | tf_op jit(solution)/shard_map/all_to_all | solution.py:217
  20.4 2.8 %collective-permute-start.2 = (bf16[4,16,640]{2,1,0:T(8,128)(2,1)S(1)}, bf16[4,16,640]{2,1,0:T(8,128)(2,1)S(1)}, u32[]{:S(2)}, u32[]{:S(2)}) collective-permute-start(bf16[4,16,640]{2,1,0:T(8,128)(2,1)S(1)} %get-tuple-element.36), channel_id=1, source_target_pairs={{0,18},{2,0},{16,2},{18,16},{1,19},{3,1},{17,3},{19,17},{4,22},{6,... | collective-permute-start | bytes 245768 | tf_op jit(solution)/shard_map/ppermute | solution.py:212
  23.5 0.7 collective-permute-start
  24.2 2.5 %collective-permute-start.5 = (bf16[4,16,640]{2,1,0:T(8,128)(2,1)S(1)}, bf16[4,16,640]{2,1,0:T(8,128)(2,1)S(1)}, u32[]{:S(2)}, u32[]{:S(2)}) collective-permute-start(bf16[4,16,640]{2,1,0:T(8,128)(2,1)S(1)} %get-tuple-element.40), channel_id=1, source_target_pairs={{0,12},{4,0},{8,4},{12,8},{1,13},{5,1},{9,5},{13,9},{2,14},{6,2},{... | collective-permute-start | bytes 245768 | tf_op jit(solution)/shard_map/ppermute | solution.py:212
  26.7 0.5 collective-permute-start.4
  27.2 0.6 collective-permute-start.3
  28.1 0.8 collective-permute-done
  28.8 2.7 %collective-permute-done.4 = bf16[4,16,640]{2,1,0:T(8,128)(2,1)S(1)} collective-permute-done((bf16[4,16,640]{2,1,0:T(8,128)(2,1)S(1)}, bf16[4,16,640]{2,1,0:T(8,128)(2,1)S(1)}, u32[]{:S(2)}, u32[]{:S(2)}) %collective-permute-start.4) | collective-permute-done | bytes 81952 | tf_op jit(solution)/shard_map/ppermute | solution.py:212
  31.6 0.9 collective-permute-done.3
  32.5 0.8 pad_maximum_fusion.1
  33.4 15.5 %all_to_all.26 = bf16[4,16,16,640]{3,2,1,0:T(8,128)(2,1)S(1)} all-to-all(bf16[4,16,16,640]{3,2,1,0:T(8,128)(2,1)S(1)} %broadcast_in_dim.38), channel_id=1, replica_groups=mesh['z'=8,'yh'=2,'x'=4,'yl'=2,'c'=2] {'x'}, dimensions={0} | all-to-all | bytes 2621440 | tf_op jit(solution)/shard_map/all_to_all | solution.py:217
  48.9 6.0 %collective-permute-start.9 = (bf16[64,16,640]{2,1,0:T(8,128)(2,1)S(1)}, bf16[64,16,640]{2,1,0:T(8,128)(2,1)}, u32[]{:S(2)}, u32[]{:S(2)}) collective-permute-start(bf16[64,16,640]{2,1,0:T(8,128)(2,1)S(1)} %bitcast.64), channel_id=1, source_target_pairs={{0,1},{1,0},{2,3},{3,2},{4,5},{5,4},{6,7},{7,6},{8,9},{9,8},{10,11... | collective-permute-start | bytes 3932168 | tf_op jit(solution)/shard_map/ppermute | solution.py:212
  54.9 1.9 %collective-permute-start.8 = (bf16[16,16,640]{2,1,0:T(8,128)(2,1)}, bf16[16,16,640]{2,1,0:T(8,128)(2,1)}, u32[]{:S(2)}, u32[]{:S(2)}) collective-permute-start(bf16[16,16,640]{2,1,0:T(8,128)(2,1)} %bitcast.18.refs_1_), channel_id=1, source_target_pairs={{0,18},{2,0},{16,2},{18,16},{1,19},{3,1},{17,3},{19,17},{4,22},{6,... | collective-permute-start | bytes 983048 | tf_op jit(solution)/shard_map/ppermute | solution.py:212
  56.8 1.4 collective-permute-start.7
  58.2 0.6 collective-permute-start.10
  58.7 5.9 %collective-permute-done.8.refs_4_ = bf16[16,16,640]{2,1,0:T(8,128)(2,1)} collective-permute-done((bf16[16,16,640]{2,1,0:T(8,128)(2,1)}, bf16[16,16,640]{2,1,0:T(8,128)(2,1)}, u32[]{:S(2)}, u32[]{:S(2)}) %collective-permute-start.8) | collective-permute-done | bytes 327712 | tf_op jit(solution)/shard_map/ppermute | solution.py:212
  64.6 7.4 %collective-permute-start.13 = (bf16[16,16,640]{2,1,0:T(8,128)(2,1)}, bf16[16,16,640]{2,1,0:T(8,128)(2,1)}, u32[]{:S(2)}, u32[]{:S(2)}) collective-permute-start(bf16[16,16,640]{2,1,0:T(8,128)(2,1)} %collective-permute-done.8.refs_4_), channel_id=1, source_target_pairs={{0,1},{1,0},{2,3},{3,2},{4,5},{5,4},{6,7},{7,6},{8,9},{9,8},{10,11... | collective-permute-start | bytes 983048 | tf_op jit(solution)/shard_map/ppermute | solution.py:212
  72.1 3.2 %collective-permute-done.6.refs_2_ = bf16[16,16,640]{2,1,0:T(8,128)(2,1)} collective-permute-done((bf16[16,16,640]{2,1,0:T(8,128)(2,1)}, bf16[16,16,640]{2,1,0:T(8,128)(2,1)}, u32[]{:S(2)}, u32[]{:S(2)}) %collective-permute-start.6) | collective-permute-done | bytes 327712 | tf_op jit(solution)/shard_map/ppermute | solution.py:212
  75.2 0.5 collective-permute-start.11
  75.8 1.5 collective-permute-done.11.refs_7_
  77.3 19.1 %shard_map.106 = (bf16[64,16,640]{2,1,0:T(8,128)(2,1)S(1)}, bf16[16,16,640]{2,1,0:T(8,128)(2,1)S(1)}, bf16[16,16,640]{2,1,0:T(8,128)(2,1)S(1)}, bf16[16,16,640]{...) custom-call(s32[4]{0:T(128)S(1)} %pad_add_fusion.place_ref, ...), custom_call_target="tpu_custom_call" | custom-call | flops 1505755136 | bytes 22249472 | tf_op jit(solution)/shard_map/pallas_call | solution.py:183
  97.9 3.0 %collective-permute-done.16 = bf16[16,16,640]{2,1,0:T(8,128)(2,1)S(1)} collective-permute-done((bf16[16,16,640]{2,1,0:T(8,128)(2,1)S(1)}, bf16[16,16,640]{2,1,0:T(8,128)(2,1)S(1)}, u32[]{:S(2)}, u32[]{:S(2)}) %collective-permute-start.16) | collective-permute-done | bytes 327712 | tf_op jit(solution)/shard_map/ppermute | solution.py:212
  101.2 1.4 add_convert_fusion
  102.6 3.7 %all-to-all-start.2 = ((bf16[4,16,16,640]{3,2,1,0:T(8,128)(2,1)}), bf16[4,16,16,640]{3,2,1,0:T(8,128)(2,1)S(1)}, u32[]{:S(2)}, u32[]{:S(2)}) async-start(bf16[4,16,16,640]{3,2,1,0:T(8,128)(2,1)} %bitcast.24), calls=%async_computation.2 | async-start | bytes 2621440 | tf_op jit(solution)/shard_map/all_to_all | solution.py:284
  106.4 1.9 %collective-permute-start.19 = (bf16[16,16,640]{2,1,0:T(8,128)(2,1)S(1)}, bf16[16,16,640]{2,1,0:T(8,128)(2,1)S(1)}, u32[]{:S(2)}, u32[]{:S(2)}) collective-permute-start(bf16[16,16,640]{2,1,0:T(8,128)(2,1)S(1)} %add_convert_fusion.3), channel_id=1, source_target_pairs={{0,16},{2,18},{16,0},{18,2},{1,17},{3,19},{17,1},{19,3},{4,20},{6,... | collective-permute-start | bytes 983048 | tf_op jit(solution)/shard_map/ppermute | solution.py:212
  108.4 1.9 %collective-permute-start.21 = (bf16[16,16,640]{2,1,0:T(8,128)(2,1)S(1)}, bf16[16,16,640]{2,1,0:T(8,128)(2,1)S(1)}, u32[]{:S(2)}, u32[]{:S(2)}) collective-permute-start(bf16[16,16,640]{2,1,0:T(8,128)(2,1)S(1)} %add_convert_fusion.2), channel_id=1, source_target_pairs={{0,18},{2,0},{16,2},{18,16},{1,19},{3,1},{17,3},{19,17},{4,22},{6,... | collective-permute-start | bytes 983048 | tf_op jit(solution)/shard_map/ppermute | solution.py:212
  110.4 1.4 collective-permute-done.17
  111.8 5.9 %collective-permute-done.19 = bf16[16,16,640]{2,1,0:T(8,128)(2,1)S(1)} collective-permute-done((bf16[16,16,640]{2,1,0:T(8,128)(2,1)S(1)}, bf16[16,16,640]{2,1,0:T(8,128)(2,1)S(1)}, u32[]{:S(2)}, u32[]{:S(2)}) %collective-permute-start.19) | collective-permute-done | bytes 327712 | tf_op jit(solution)/shard_map/ppermute | solution.py:212
  117.7 6.2 %collective-permute-done.21 = bf16[16,16,640]{2,1,0:T(8,128)(2,1)S(1)} collective-permute-done((bf16[16,16,640]{2,1,0:T(8,128)(2,1)S(1)}, bf16[16,16,640]{2,1,0:T(8,128)(2,1)S(1)}, u32[]{:S(2)}, u32[]{:S(2)}) %collective-permute-start.21) | collective-permute-done | bytes 327712 | tf_op jit(solution)/shard_map/ppermute | solution.py:212
  124.0 1.3 add_convert_fusion.1
  125.6 3.5 %collective-permute-start.24 = (bf16[4,16,640]{2,1,0:T(8,128)(2,1)S(1)}, bf16[4,16,640]{2,1,0:T(8,128)(2,1)S(1)}, u32[]{:S(2)}, u32[]{:S(2)}) collective-permute-start(bf16[4,16,640]{2,1,0:T(8,128)(2,1)S(1)} %get-tuple-element.68), channel_id=1, source_target_pairs={{0,18},{2,0},{16,2},{18,16},{1,19},{3,1},{17,3},{19,17},{4,22},{6,... | collective-permute-start | bytes 245768 | tf_op jit(solution)/shard_map/ppermute | solution.py:212
  129.3 0.5 collective-permute-start.22
  129.8 2.7 %collective-permute-start.27 = (bf16[4,16,640]{2,1,0:T(8,128)(2,1)S(1)}, bf16[4,16,640]{2,1,0:T(8,128)(2,1)S(1)}, u32[]{:S(2)}, u32[]{:S(2)}) collective-permute-start(bf16[4,16,640]{2,1,0:T(8,128)(2,1)S(1)} %get-tuple-element.65), channel_id=1, source_target_pairs={{0,12},{4,0},{8,4},{12,8},{1,13},{5,1},{9,5},{13,9},{2,14},{6,2},{... | collective-permute-start | bytes 245768 | tf_op jit(solution)/shard_map/ppermute | solution.py:212
  132.5 0.6 collective-permute-start.26
  133.0 0.7 collective-permute-start.25
  134.0 2.1 %collective-permute-done.22 = bf16[4,16,640]{2,1,0:T(8,128)(2,1)S(1)} collective-permute-done((bf16[4,16,640]{2,1,0:T(8,128)(2,1)S(1)}, bf16[4,16,640]{2,1,0:T(8,128)(2,1)S(1)}, u32[]{:S(2)}, u32[]{:S(2)}) %collective-permute-start.22) | collective-permute-done | bytes 81952 | tf_op jit(solution)/shard_map/ppermute | solution.py:212
  136.1 1.3 collective-permute-done.26
  137.3 0.8 collective-permute-done.25
  138.3 10.9 %all_to_all.27 = bf16[8,16,640]{2,1,0:T(8,128)(2,1)S(1)} all-to-all(bf16[8,16,640]{2,1,0:T(8,128)(2,1)S(1)} %pad_maximum_fusion.2), channel_id=1, replica_groups=mesh['z'=8,'yh'=2,'x'=4,'yl'=2,'c'=2] {'z'}, dimensions={0} | all-to-all | bytes 327680 | tf_op jit(solution)/shard_map/all_to_all | solution.py:293
  149.1 0.7 broadcast_in_dim.39
  149.8 7.6 %all-to-all-start.4 = ((f32[4,16,640]{2,1,0:T(8,128)}), f32[4,16,640]{2,1,0:T(8,128)S(1)}, u32[]{:S(2)}, u32[]{:S(2)}) async-start(f32[4,16,640]{2,1,0:T(8,128)} %broadcast_in_dim.39), calls=%async_computation.4 | async-start | bytes 327680 | tf_op jit(solution)/shard_map/all_to_all | solution.py:217
  157.4 0.5 slice.41
  158.7 2.6 %all-to-all-done.4 = f32[4,16,640]{2,1,0:T(8,128)S(1)} async-done(((f32[4,16,640]{2,1,0:T(8,128)}), f32[4,16,640]{2,1,0:T(8,128)S(1)}, u32[]{:S(2)}, u32[]{:S(2)}) %all-to-all-start.4) | async-done | bytes 163872 | tf_op jit(solution)/shard_map/all_to_all | solution.py:217
  161.3 0.6 slice.55
  161.9 0.7 slice_bitcast_fusion
  (69 shorter events, 4.1 us)
Async XLA Ops:
  0.6 1.8 %copy-start = (bf16[462,64]{0,1:T(8,128)(2,1)S(1)}, bf16[462,64]{0,1:T(8,128)(2,1)}, u32[]{:S(2)}) copy-start(bf16[462,64]{0,1:T(8,128)(2,1)} %param.11) | copy-start | bytes 177412
  20.4 6.9 %collective-permute-start.2 = (bf16[4,16,640]{2,1,0:T(8,128)(2,1)S(1)}, bf16[4,16,640]{2,1,0:T(8,128)(2,1)S(1)}, u32[]{:S(2)}, u32[]{:S(2)}) collective-permute-start(bf16[4,16,640]{2,1,0:T(8,128)(2,1)S(1)} %get-tuple-element.36), channel_id=1, source_target_pairs={{0,18},{2,0},{16,2},{18,16},{1,19},{3,1},{17,3},{19,17},{4,22},{6,... | collective-permute-start | bytes 245768 | tf_op jit(solution)/shard_map/ppermute | solution.py:212
  23.2 4.9 %collective-permute-start.1 = (bf16[4,16,640]{2,1,0:T(8,128)(2,1)S(1)}, bf16[4,16,640]{2,1,0:T(8,128)(2,1)S(1)}, u32[]{:S(2)}, u32[]{:S(2)}) collective-permute-start(bf16[4,16,640]{2,1,0:T(8,128)(2,1)S(1)} %get-tuple-element.36), channel_id=1, source_target_pairs={{0,16},{2,18},{16,0},{18,2},{1,17},{3,19},{17,1},{19,3},{4,20},{6,... | collective-permute-start | bytes 245768 | tf_op jit(solution)/shard_map/ppermute | solution.py:212
  23.5 5.3 %collective-permute-start = (bf16[4,16,640]{2,1,0:T(8,128)(2,1)S(1)}, bf16[4,16,640]{2,1,0:T(8,128)(2,1)S(1)}, u32[]{:S(2)}, u32[]{:S(2)}) collective-permute-start(bf16[4,16,640]{2,1,0:T(8,128)(2,1)S(1)} %get-tuple-element.36), channel_id=1, source_target_pairs={{0,2},{2,16},{16,18},{18,0},{1,3},{3,17},{17,19},{19,1},{4,6},{6,2... | collective-permute-start | bytes 245768 | tf_op jit(solution)/shard_map/ppermute | solution.py:212
  24.2 4.6 %collective-permute-start.5 = (bf16[4,16,640]{2,1,0:T(8,128)(2,1)S(1)}, bf16[4,16,640]{2,1,0:T(8,128)(2,1)S(1)}, u32[]{:S(2)}, u32[]{:S(2)}) collective-permute-start(bf16[4,16,640]{2,1,0:T(8,128)(2,1)S(1)} %get-tuple-element.40), channel_id=1, source_target_pairs={{0,12},{4,0},{8,4},{12,8},{1,13},{5,1},{9,5},{13,9},{2,14},{6,2},{... | collective-permute-start | bytes 245768 | tf_op jit(solution)/shard_map/ppermute | solution.py:212
  26.7 4.9 %collective-permute-start.4 = (bf16[4,16,640]{2,1,0:T(8,128)(2,1)S(1)}, bf16[4,16,640]{2,1,0:T(8,128)(2,1)S(1)}, u32[]{:S(2)}, u32[]{:S(2)}) collective-permute-start(bf16[4,16,640]{2,1,0:T(8,128)(2,1)S(1)} %get-tuple-element.40), channel_id=1, source_target_pairs={{0,8},{4,12},{8,0},{12,4},{1,9},{5,13},{9,1},{13,5},{2,10},{6,14},... | collective-permute-start | bytes 245768 | tf_op jit(solution)/shard_map/ppermute | solution.py:212
  27.2 5.2 %collective-permute-start.3 = (bf16[4,16,640]{2,1,0:T(8,128)(2,1)S(1)}, bf16[4,16,640]{2,1,0:T(8,128)(2,1)S(1)}, u32[]{:S(2)}, u32[]{:S(2)}) collective-permute-start(bf16[4,16,640]{2,1,0:T(8,128)(2,1)S(1)} %get-tuple-element.40), channel_id=1, source_target_pairs={{0,4},{4,8},{8,12},{12,0},{1,5},{5,9},{9,13},{13,1},{2,6},{6,10},{... | collective-permute-start | bytes 245768 | tf_op jit(solution)/shard_map/ppermute | solution.py:212
  33.4 43.9 %copy-start.1 = (bf16[1,2,64,8192]{3,2,1,0:T(8,128)(2,1)S(1)}, bf16[1,2,64,8192]{3,2,1,0:T(8,128)(2,1)}, u32[]{:S(2)}) copy-start(bf16[1,2,64,8192]{3,2,1,0:T(8,128)(2,1)} %param.9) | copy-start | bytes 6291460
  33.4 43.9 %copy-start.8 = (s32[1,2]{1,0:T(1,128)S(1)}, s32[1,2]{1,0:T(1,128)}, u32[]{:S(2)}) copy-start(s32[1,2]{1,0:T(1,128)} %starts_ref.1) | copy-start | bytes 28
  48.9 28.4 %collective-permute-start.9 = (bf16[64,16,640]{2,1,0:T(8,128)(2,1)S(1)}, bf16[64,16,640]{2,1,0:T(8,128)(2,1)}, u32[]{:S(2)}, u32[]{:S(2)}) collective-permute-start(bf16[64,16,640]{2,1,0:T(8,128)(2,1)S(1)} %bitcast.64), channel_id=1, source_target_pairs={{0,1},{1,0},{2,3},{3,2},{4,5},{5,4},{6,7},{7,6},{8,9},{9,8},{10,11... | collective-permute-start | bytes 3932168 | tf_op jit(solution)/shard_map/ppermute | solution.py:212
  54.9 9.8 %collective-permute-start.8 = (bf16[16,16,640]{2,1,0:T(8,128)(2,1)}, bf16[16,16,640]{2,1,0:T(8,128)(2,1)}, u32[]{:S(2)}, u32[]{:S(2)}) collective-permute-start(bf16[16,16,640]{2,1,0:T(8,128)(2,1)} %bitcast.18.refs_1_), channel_id=1, source_target_pairs={{0,18},{2,0},{16,2},{18,16},{1,19},{3,1},{17,3},{19,17},{4,22},{6,... | collective-permute-start | bytes 983048 | tf_op jit(solution)/shard_map/ppermute | solution.py:212
  56.8 15.3 %collective-permute-start.7 = (bf16[16,16,640]{2,1,0:T(8,128)(2,1)}, bf16[16,16,640]{2,1,0:T(8,128)(2,1)}, u32[]{:S(2)}, u32[]{:S(2)}) collective-permute-start(bf16[16,16,640]{2,1,0:T(8,128)(2,1)} %bitcast.18.refs_1_), channel_id=1, source_target_pairs={{0,16},{2,18},{16,0},{18,2},{1,17},{3,19},{17,1},{19,3},{4,20},{6,... | collective-permute-start | bytes 983048 | tf_op jit(solution)/shard_map/ppermute | solution.py:212
  58.2 17.1 %collective-permute-start.6 = (bf16[16,16,640]{2,1,0:T(8,128)(2,1)}, bf16[16,16,640]{2,1,0:T(8,128)(2,1)}, u32[]{:S(2)}, u32[]{:S(2)}) collective-permute-start(bf16[16,16,640]{2,1,0:T(8,128)(2,1)} %bitcast.18.refs_1_), channel_id=1, source_target_pairs={{0,2},{2,16},{16,18},{18,0},{1,3},{3,17},{17,19},{19,1},{4,6},{6,2... | collective-permute-start | bytes 983048 | tf_op jit(solution)/shard_map/ppermute | solution.py:212
  58.2 17.6 %collective-permute-start.10 = (bf16[16,16,640]{2,1,0:T(8,128)(2,1)}, bf16[16,16,640]{2,1,0:T(8,128)(2,1)}, u32[]{:S(2)}, u32[]{:S(2)}) collective-permute-start(bf16[16,16,640]{2,1,0:T(8,128)(2,1)} %bitcast.18.refs_1_), channel_id=1, source_target_pairs={{0,1},{1,0},{2,3},{3,2},{4,5},{5,4},{6,7},{7,6},{8,9},{9,8},{10,11... | collective-permute-start | bytes 983048 | tf_op jit(solution)/shard_map/ppermute | solution.py:212
  64.6 11.2 %collective-permute-start.13 = (bf16[16,16,640]{2,1,0:T(8,128)(2,1)}, bf16[16,16,640]{2,1,0:T(8,128)(2,1)}, u32[]{:S(2)}, u32[]{:S(2)}) collective-permute-start(bf16[16,16,640]{2,1,0:T(8,128)(2,1)} %collective-permute-done.8.refs_4_), channel_id=1, source_target_pairs={{0,1},{1,0},{2,3},{3,2},{4,5},{5,4},{6,7},{7,6},{8,9},{9,8},{10,11... | collective-permute-start | bytes 983048 | tf_op jit(solution)/shard_map/ppermute | solution.py:212
  72.1 3.8 %collective-permute-start.12 = (bf16[16,16,640]{2,1,0:T(8,128)(2,1)}, bf16[16,16,640]{2,1,0:T(8,128)(2,1)}, u32[]{:S(2)}, u32[]{:S(2)}) collective-permute-start(bf16[16,16,640]{2,1,0:T(8,128)(2,1)} %collective-permute-done.7.refs_3_), channel_id=1, source_target_pairs={{0,1},{1,0},{2,3},{3,2},{4,5},{5,4},{6,7},{7,6},{8,9},{9,8},{10,11... | collective-permute-start | bytes 983048 | tf_op jit(solution)/shard_map/ppermute | solution.py:212
  75.2 2.1 %collective-permute-start.11 = (bf16[16,16,640]{2,1,0:T(8,128)(2,1)}, bf16[16,16,640]{2,1,0:T(8,128)(2,1)}, u32[]{:S(2)}, u32[]{:S(2)}) collective-permute-start(bf16[16,16,640]{2,1,0:T(8,128)(2,1)} %collective-permute-done.6.refs_2_), channel_id=1, source_target_pairs={{0,1},{1,0},{2,3},{3,2},{4,5},{5,4},{6,7},{7,6},{8,9},{9,8},{10,11... | collective-permute-start | bytes 983048 | tf_op jit(solution)/shard_map/ppermute | solution.py:212
  96.4 6.2 %copy-start.2 = (bf16[16,16,640]{2,1,0:T(8,128)(2,1)}, bf16[16,16,640]{2,1,0:T(8,128)(2,1)S(1)}, u32[]{:S(2)}) copy-start(bf16[16,16,640]{2,1,0:T(8,128)(2,1)S(1)} %get-tuple-element.55) | copy-start | bytes 983044
  96.4 6.2 %copy-start.4 = (bf16[16,16,640]{2,1,0:T(8,128)(2,1)}, bf16[16,16,640]{2,1,0:T(8,128)(2,1)S(1)}, u32[]{:S(2)}) copy-start(bf16[16,16,640]{2,1,0:T(8,128)(2,1)S(1)} %get-tuple-element.53) | copy-start | bytes 983044
  96.4 6.2 %copy-start.6 = (bf16[16,16,640]{2,1,0:T(8,128)(2,1)}, bf16[16,16,640]{2,1,0:T(8,128)(2,1)S(1)}, u32[]{:S(2)}) copy-start(bf16[16,16,640]{2,1,0:T(8,128)(2,1)S(1)} %get-tuple-element.49) | copy-start | bytes 983044
  96.5 4.7 %collective-permute-start.14 = (bf16[64,16,640]{2,1,0:T(8,128)(2,1)S(1)}, bf16[64,16,640]{2,1,0:T(8,128)(2,1)S(1)}, u32[]{:S(2)}, u32[]{:S(2)}) collective-permute-start(bf16[64,16,640]{2,1,0:T(8,128)(2,1)S(1)} %get-tuple-element.48), channel_id=1, source_target_pairs={{0,1},{1,0},{2,3},{3,2},{4,5},{5,4},{6,7},{7,6},{8,9},{9,8},{10,11... | collective-permute-start | bytes 3932168 | tf_op jit(solution)/shard_map/ppermute | solution.py:212
  96.9 4.1 %collective-permute-start.16 = (bf16[16,16,640]{2,1,0:T(8,128)(2,1)S(1)}, bf16[16,16,640]{2,1,0:T(8,128)(2,1)S(1)}, u32[]{:S(2)}, u32[]{:S(2)}) collective-permute-start(bf16[16,16,640]{2,1,0:T(8,128)(2,1)S(1)} %get-tuple-element.52), channel_id=1, source_target_pairs={{0,1},{1,0},{2,3},{3,2},{4,5},{5,4},{6,7},{7,6},{8,9},{9,8},{10,11... | collective-permute-start | bytes 983048 | tf_op jit(solution)/shard_map/ppermute | solution.py:212
  97.0 13.3 %collective-permute-start.15 = (bf16[16,16,640]{2,1,0:T(8,128)(2,1)}, bf16[16,16,640]{2,1,0:T(8,128)(2,1)}, u32[]{:S(2)}, u32[]{:S(2)}) collective-permute-start(bf16[16,16,640]{2,1,0:T(8,128)(2,1)} %get-tuple-element.50), channel_id=1, source_target_pairs={{0,1},{1,0},{2,3},{3,2},{4,5},{5,4},{6,7},{7,6},{8,9},{9,8},{10,11... | collective-permute-start | bytes 983048 | tf_op jit(solution)/shard_map/ppermute | solution.py:212
  97.4 8.9 %collective-permute-start.18 = (bf16[16,16,640]{2,1,0:T(8,128)(2,1)}, bf16[16,16,640]{2,1,0:T(8,128)(2,1)S(1)}, u32[]{:S(2)}, u32[]{:S(2)}) collective-permute-start(bf16[16,16,640]{2,1,0:T(8,128)(2,1)} %get-tuple-element.54), channel_id=1, source_target_pairs={{0,1},{1,0},{2,3},{3,2},{4,5},{5,4},{6,7},{7,6},{8,9},{9,8},{10,11... | collective-permute-start | bytes 983048 | tf_op jit(solution)/shard_map/ppermute | solution.py:212
  97.6 10.8 %collective-permute-start.20 = (bf16[16,16,640]{2,1,0:T(8,128)(2,1)}, bf16[16,16,640]{2,1,0:T(8,128)(2,1)S(1)}, u32[]{:S(2)}, u32[]{:S(2)}) collective-permute-start(bf16[16,16,640]{2,1,0:T(8,128)(2,1)} %get-tuple-element.56), channel_id=1, source_target_pairs={{0,1},{1,0},{2,3},{3,2},{4,5},{5,4},{6,7},{7,6},{8,9},{9,8},{10,11... | collective-permute-start | bytes 983048 | tf_op jit(solution)/shard_map/ppermute | solution.py:212
  101.1 10.8 %collective-permute-start.17 = (bf16[16,16,640]{2,1,0:T(8,128)(2,1)S(1)}, bf16[16,16,640]{2,1,0:T(8,128)(2,1)}, u32[]{:S(2)}, u32[]{:S(2)}) collective-permute-start(bf16[16,16,640]{2,1,0:T(8,128)(2,1)S(1)} %add_convert_fusion.4), channel_id=1, source_target_pairs={{0,2},{2,16},{16,18},{18,0},{1,3},{3,17},{17,19},{19,1},{4,6},{6,2... | collective-permute-start | bytes 983048 | tf_op jit(solution)/shard_map/ppermute | solution.py:212
  102.6 3.7 %copy-start.5 = (bf16[16,16,640]{2,1,0:T(8,128)(2,1)S(1)}, bf16[16,16,640]{2,1,0:T(8,128)(2,1)}, u32[]{:S(2)}) copy-start(bf16[16,16,640]{2,1,0:T(8,128)(2,1)} %copy-done.4) | copy-start | bytes 983044
  102.6 5.7 %copy-start.3 = (bf16[16,16,640]{2,1,0:T(8,128)(2,1)S(1)}, bf16[16,16,640]{2,1,0:T(8,128)(2,1)}, u32[]{:S(2)}) copy-start(bf16[16,16,640]{2,1,0:T(8,128)(2,1)} %copy-done.2) | copy-start | bytes 983044
  102.6 22.6 %all-to-all-start.2 = ((bf16[4,16,16,640]{3,2,1,0:T(8,128)(2,1)}), bf16[4,16,16,640]{3,2,1,0:T(8,128)(2,1)S(1)}, u32[]{:S(2)}, u32[]{:S(2)}) async-start(bf16[4,16,16,640]{3,2,1,0:T(8,128)(2,1)} %bitcast.24), calls=%async_computation.2 | async-start | bytes 2621440 | tf_op jit(solution)/shard_map/all_to_all | solution.py:284
  106.3 17.6 %copy-start.7 = (bf16[16,16,640]{2,1,0:T(8,128)(2,1)S(1)}, bf16[16,16,640]{2,1,0:T(8,128)(2,1)}, u32[]{:S(2)}) copy-start(bf16[16,16,640]{2,1,0:T(8,128)(2,1)} %copy-done.6) | copy-start | bytes 983044
  106.4 11.3 %collective-permute-start.19 = (bf16[16,16,640]{2,1,0:T(8,128)(2,1)S(1)}, bf16[16,16,640]{2,1,0:T(8,128)(2,1)S(1)}, u32[]{:S(2)}, u32[]{:S(2)}) collective-permute-start(bf16[16,16,640]{2,1,0:T(8,128)(2,1)S(1)} %add_convert_fusion.3), channel_id=1, source_target_pairs={{0,16},{2,18},{16,0},{18,2},{1,17},{3,19},{17,1},{19,3},{4,20},{6,... | collective-permute-start | bytes 983048 | tf_op jit(solution)/shard_map/ppermute | solution.py:212
  108.4 15.5 %collective-permute-start.21 = (bf16[16,16,640]{2,1,0:T(8,128)(2,1)S(1)}, bf16[16,16,640]{2,1,0:T(8,128)(2,1)S(1)}, u32[]{:S(2)}, u32[]{:S(2)}) collective-permute-start(bf16[16,16,640]{2,1,0:T(8,128)(2,1)S(1)} %add_convert_fusion.2), channel_id=1, source_target_pairs={{0,18},{2,0},{16,2},{18,16},{1,19},{3,1},{17,3},{19,17},{4,22},{6,... | collective-permute-start | bytes 983048 | tf_op jit(solution)/shard_map/ppermute | solution.py:212
  125.6 7.4 %collective-permute-start.24 = (bf16[4,16,640]{2,1,0:T(8,128)(2,1)S(1)}, bf16[4,16,640]{2,1,0:T(8,128)(2,1)S(1)}, u32[]{:S(2)}, u32[]{:S(2)}) collective-permute-start(bf16[4,16,640]{2,1,0:T(8,128)(2,1)S(1)} %get-tuple-element.68), channel_id=1, source_target_pairs={{0,18},{2,0},{16,2},{18,16},{1,19},{3,1},{17,3},{19,17},{4,22},{6,... | collective-permute-start | bytes 245768 | tf_op jit(solution)/shard_map/ppermute | solution.py:212
  129.1 4.9 %collective-permute-start.23 = (bf16[4,16,640]{2,1,0:T(8,128)(2,1)S(1)}, bf16[4,16,640]{2,1,0:T(8,128)(2,1)S(1)}, u32[]{:S(2)}, u32[]{:S(2)}) collective-permute-start(bf16[4,16,640]{2,1,0:T(8,128)(2,1)S(1)} %get-tuple-element.69), channel_id=1, source_target_pairs={{0,16},{2,18},{16,0},{18,2},{1,17},{3,19},{17,1},{19,3},{4,20},{6,... | collective-permute-start | bytes 245768 | tf_op jit(solution)/shard_map/ppermute | solution.py:212
  129.3 6.8 %collective-permute-start.22 = (bf16[4,16,640]{2,1,0:T(8,128)(2,1)S(1)}, bf16[4,16,640]{2,1,0:T(8,128)(2,1)S(1)}, u32[]{:S(2)}, u32[]{:S(2)}) collective-permute-start(bf16[4,16,640]{2,1,0:T(8,128)(2,1)S(1)} %get-tuple-element.70), channel_id=1, source_target_pairs={{0,2},{2,16},{16,18},{18,0},{1,3},{3,17},{17,19},{19,1},{4,6},{6,2... | collective-permute-start | bytes 245768 | tf_op jit(solution)/shard_map/ppermute | solution.py:212
  129.8 6.3 %collective-permute-start.27 = (bf16[4,16,640]{2,1,0:T(8,128)(2,1)S(1)}, bf16[4,16,640]{2,1,0:T(8,128)(2,1)S(1)}, u32[]{:S(2)}, u32[]{:S(2)}) collective-permute-start(bf16[4,16,640]{2,1,0:T(8,128)(2,1)S(1)} %get-tuple-element.65), channel_id=1, source_target_pairs={{0,12},{4,0},{8,4},{12,8},{1,13},{5,1},{9,5},{13,9},{2,14},{6,2},{... | collective-permute-start | bytes 245768 | tf_op jit(solution)/shard_map/ppermute | solution.py:212
  132.5 4.9 %collective-permute-start.26 = (bf16[4,16,640]{2,1,0:T(8,128)(2,1)S(1)}, bf16[4,16,640]{2,1,0:T(8,128)(2,1)S(1)}, u32[]{:S(2)}, u32[]{:S(2)}) collective-permute-start(bf16[4,16,640]{2,1,0:T(8,128)(2,1)S(1)} %get-tuple-element.66), channel_id=1, source_target_pairs={{0,8},{4,12},{8,0},{12,4},{1,9},{5,13},{9,1},{13,5},{2,10},{6,14},... | collective-permute-start | bytes 245768 | tf_op jit(solution)/shard_map/ppermute | solution.py:212
  133.0 5.1 %collective-permute-start.25 = (bf16[4,16,640]{2,1,0:T(8,128)(2,1)S(1)}, bf16[4,16,640]{2,1,0:T(8,128)(2,1)S(1)}, u32[]{:S(2)}, u32[]{:S(2)}) collective-permute-start(bf16[4,16,640]{2,1,0:T(8,128)(2,1)S(1)} %get-tuple-element.67), channel_id=1, source_target_pairs={{0,4},{4,8},{8,12},{12,0},{1,5},{5,9},{9,13},{13,1},{2,6},{6,10},{... | collective-permute-start | bytes 245768 | tf_op jit(solution)/shard_map/ppermute | solution.py:212
  149.8 11.5 %all-to-all-start.4 = ((f32[4,16,640]{2,1,0:T(8,128)}), f32[4,16,640]{2,1,0:T(8,128)S(1)}, u32[]{:S(2)}, u32[]{:S(2)}) async-start(f32[4,16,640]{2,1,0:T(8,128)} %broadcast_in_dim.39), calls=%async_computation.4 | async-start | bytes 327680 | tf_op jit(solution)/shard_map/all_to_all | solution.py:217

commit v3 on v2

--- a/solution.py
+++ b/solution.py
@@ -1,3 +1,5 @@
+import itertools
+
 import jax
 import jax.numpy as jnp
 from jax import lax
@@ -13,7 +15,6 @@
 FINE_SHAPE = (8, 2, 4, 2, 2)
 DP = ("z", "yh", "x")
 CTX = ("yl", "c")
-Y = ("yh", "yl")
 
 LANES = 640
 UP = 128
@@ -33,50 +34,43 @@
 
 def slots(place, sign):
     py, px, pc = place[1], place[2], place[3]
-    dxs = [(sign * (px - x)) & 3 for x in range(4)]
-    dys = [(sign * (py - y)) & 3 for y in range(4)]
+    dxs = [((sign * (px - x)) & 3) * 32 for x in range(4)]
+    dys = [((sign * (py - y)) & 3) * 32 for y in range(4)]
     cores = [((pc + c) & 1) * 128 for c in range(2)]
 
     def flat(chunk, q):
         z, yh, x = chunk // 8, chunk // 4 % 2, chunk % 4
         c, y = q // 2, yh * 2 + q % 2
-        if z < 4:
-            return cores[c] + dys[y] * 4 + (x * 16 + z)
-        return cores[c] + dys[y] * 16 + dxs[x] * 4 + (60 + z)
+        if c == 0:
+            return cores[0] + dxs[x] + (z * 4 + y)
+        return cores[1] + dys[y] + (z * 4 + x)
 
     return flat
 
 
 def kernel(place_ref, starts_ref, *refs):
-    parts, (hidden_hbm, frozen_hbm, head_hbm) = refs[:10], refs[10:13]
-    outs, margin_ref = refs[13:23], refs[23]
-    hid, fro, hea, wt, up, gains, gain, pol, block, sems = refs[24:]
+    parts, (hidden_hbm, frozen_hbm, head_hbm) = refs[:8], refs[8:11]
+    outs, margin_ref = refs[11:19], refs[19]
+    hid, fro, hea, wt, up, gains, gain, pol, block, sems = refs[20:]
     width = fro.shape[1]
 
-    def ranges():
-        begin = 0
-        for i in range(10):
-            size = 64 if i % 5 == 0 else 16
-            yield pl.ds(begin, size)
-            begin += size
-
     loads = [
-        pltpu.make_async_copy(parts[i], block.at[at], sems.at[i]) for i, at in enumerate(ranges())
+        pltpu.make_async_copy(parts[i], block.at[pl.ds(32 * i, 32)], sems.at[i]) for i in range(8)
     ]
-    loads.append(pltpu.make_async_copy(hidden_hbm, hid, sems.at[10]))
-    loads.append(pltpu.make_async_copy(frozen_hbm, fro, sems.at[11]))
-    loads.append(pltpu.make_async_copy(head_hbm, hea, sems.at[12]))
+    loads.append(pltpu.make_async_copy(hidden_hbm, hid, sems.at[8]))
+    loads.append(pltpu.make_async_copy(frozen_hbm, fro, sems.at[9]))
+    loads.append(pltpu.make_async_copy(head_hbm, hea, sems.at[10]))
     for copy in loads:
         copy.start()
-    for copy in loads[:10]:
+    for copy in loads[:8]:
         copy.wait()
 
     pz, py, px, pc = (place_ref[i] for i in range(4))
     sums = jnp.zeros((1, 128), F32)
     for c in range(2):
         for yl in range(2):
-            dy = (py - ((py & 2) + yl)) & 3
-            inside = jnp.where(pz < 4, px * 16 + dy * 4 + pz, 60 + dy * 16 + pz)
+            y = (py & 2) + yl
+            inside = pz * 4 + px + ((py - y) & 3) * 32 if c else pz * 4 + y
             held = block[((pc + c) & 1) * 128 + inside]
             sums += held[0:1, LANES - 128 :].astype(F32)
     lane = SUMS_AT - (LANES - 128)
@@ -100,7 +94,7 @@
     lane = GAIN_AT - (LANES - 128)
     gain[...] = jnp.concatenate([gains[q][:, lane : lane + 32] for q in range(4)], axis=1)
 
-    loads[10].wait()
+    loads[8].wait()
     tile = 2688
 
     def low_step(i, total):
@@ -110,8 +104,8 @@
     low = lax.fori_loop(0, wt.shape[1] // tile, low_step, jnp.zeros((128, ORDER), F32)).astype(BF)
     low_t = low.astype(F32).T.astype(BF)
 
-    loads[11].wait()
-    loads[12].wait()
+    loads[9].wait()
+    loads[10].wait()
     step = 512
 
     def gained(i):
@@ -166,7 +160,7 @@
             block[target(chunk, q), :, UP:] = share[16 * q : 16 * q + 16]
 
     stores = [
-        pltpu.make_async_copy(block.at[at], outs[i], sems.at[i]) for i, at in enumerate(ranges())
+        pltpu.make_async_copy(block.at[pl.ds(32 * i, 32)], outs[i], sems.at[i]) for i in range(8)
     ]
     for copy in stores:
         copy.start()
@@ -179,13 +173,12 @@
     width = frozen.shape[1]
     any_space = pl.BlockSpec(memory_space=pl.ANY)
     smem = pl.BlockSpec(memory_space=pltpu.SMEM)
-    sizes = ([64] + [16] * 4) * 2
     outs = pl.pallas_call(
         kernel,
-        out_shape=[jax.ShapeDtypeStruct((n, 16, LANES), BF) for n in sizes]
+        out_shape=[jax.ShapeDtypeStruct((32, 16, LANES), BF)] * 8
         + [jax.ShapeDtypeStruct((8, 128), F32)],
-        in_specs=[smem, smem] + [any_space] * 13,
-        out_specs=[any_space] * 10 + [pl.BlockSpec(memory_space=pltpu.VMEM)],
+        in_specs=[smem, smem] + [any_space] * 11,
+        out_specs=[any_space] * 8 + [pl.BlockSpec(memory_space=pltpu.VMEM)],
         scratch_shapes=[
             pltpu.VMEM((rows, units), BF),
             pltpu.VMEM((rows, width), BF),
@@ -196,7 +189,7 @@
             pltpu.VMEM((CHUNKS, 128), F32),
             pltpu.VMEM((rows, width), F32),
             pltpu.VMEM((256, 16, LANES), BF),
-            pltpu.SemaphoreType.DMA((13,)),
+            pltpu.SemaphoreType.DMA((11,)),
         ],
         compiler_params=pltpu.CompilerParams(vmem_limit_bytes=40 * 1024 * 1024),
         cost_estimate=pl.CostEstimate(
@@ -205,20 +198,29 @@
             transcendentals=0,
         ),
     )(place, starts, *parts, hidden, frozen, head)
-    return outs[:5], outs[5:10], outs[10][0, 0:1]
-
-
-def ring(values, axes, count, step):
-    return lax.ppermute(values, axes, [(i, (i + step) % count) for i in range(count)])
-
-
-def spread(values, axes, count):
-    copies = jnp.broadcast_to(values[None], (count,) + values.shape)
-    return lax.all_to_all(copies, axes, 0, 0, tiled=True)
-
-
-def together(*values):
-    return lax.optimization_barrier(tuple(values))
+    return outs[:4], outs[4:8], outs[8][0, 0:1]
+
+
+def device(z, y, x, c):
+    return (((z * 2 + y // 2) * 4 + x) * 2 + y % 2) * 2 + c
+
+
+def ring(values, step):
+    pairs = [
+        (device(z, y, x, c), device(z, (y + step * c) % 4, (x + step * (1 - c)) % 4, c))
+        for z, y, x, c in itertools.product(range(8), range(4), range(4), range(2))
+    ]
+    return lax.ppermute(values, FINE_AXES, pairs)
+
+
+def crosswise(values):
+    groups = [[device(z, y, x, 0) for z in range(8) for y in range(4)] for x in range(4)]
+    groups += [[device(z, y, x, 1) for z in range(8) for x in range(4)] for y in range(4)]
+    return lax.all_to_all(values, FINE_AXES, 0, 0, axis_index_groups=groups, tiled=True)
+
+
+def other_core(values):
+    return lax.ppermute(values, "c", [(0, 1), (1, 0)])
 
 
 def total_of(*values):
@@ -256,18 +258,9 @@
     quarter = jnp.concatenate(
         [rows_of_up, rows_of_down, jnp.broadcast_to(tail, (16, tail.shape[1]))], axis=1
     )
-    by_z = spread(quarter, "z", 8)
-    near, far = together(by_z[:4], by_z[4:])
-    near_parts = [ring(near, Y, 4, s) for s in (1, 2, 3)]
-    far_parts = [ring(far, "x", 4, s) for s in (1, 2, 3)]
-    moved = together(near, far, *near_parts, *far_parts)
-    near = jnp.stack([moved[0], *moved[2:5]]).reshape(16, 16, LANES)
-    far = jnp.stack([moved[1], *moved[5:8]]).reshape(16, 16, LANES)
-    near, far = together(near, far)
-    far_rows = [far] + [ring(far, Y, 4, s) for s in (1, 2, 3)]
-    near_all = spread(near, "x", 4).reshape(64, 16, LANES)
-    own = [near_all, *far_rows]
-    other = [ring(v, "c", 2, 1) for v in own]
+    held = crosswise(jnp.broadcast_to(quarter[None], (32, 16, LANES)))
+    own = [held] + [ring(held, step) for step in (1, 2, 3)]
+    other = [other_core(v) for v in own]
 
     own, other, margin = shares(
         place,
@@ -278,21 +271,13 @@
         head_gradient_rows.reshape(-1, frozen.shape[3]),
     )
 
-    came = [ring(v, "c", 2, 1) for v in other]
-    chip = [total_of(a, b).astype(BF) for a, b in zip(own, came)]
-    far_rows = [ring(chip[1 + s], Y, 4, s) for s in (1, 2, 3)]
-    near_all = lax.all_to_all(chip[0].reshape(4, 16, 16, LANES), "x", 0, 0, tiled=True)
-    near = jnp.sum(near_all.astype(F32), axis=0).astype(BF).reshape(4, 4, 16, LANES)
-    far = total_of(chip[1], *far_rows).astype(BF).reshape(4, 4, 16, LANES)
-    near, far = together(near, far)
-    near_parts = [ring(near[s], Y, 4, s) for s in (1, 2, 3)]
-    far_parts = [ring(far[s], "x", 4, s) for s in (1, 2, 3)]
-    moved = together(*near_parts, *far_parts)
-    near = total_of(near[0], *moved[:3]).astype(BF)
-    far = total_of(far[0], *moved[3:]).astype(BF)
-    by_z = lax.all_to_all(jnp.concatenate([near, far]), "z", 0, 0, tiled=True)
-    share = jnp.sum(by_z.astype(F32), axis=0)
-    whole = spread(share, CTX, 4).reshape(2, 2, 16, LANES).transpose(1, 0, 2, 3)
+    chip = [total_of(a, other_core(b)).astype(BF) for a, b in zip(own, other)]
+    came = [ring(chip[step], step) for step in (1, 2, 3)]
+    line = total_of(chip[0], *came).astype(BF)
+    share = jnp.sum(crosswise(line).astype(F32), axis=0)
+    copies = jnp.broadcast_to(share[None], (4, 16, LANES))
+    whole = lax.all_to_all(copies, CTX, 0, 0, tiled=True)
+    whole = whole.reshape(2, 2, 16, LANES).transpose(1, 0, 2, 3)
     whole = whole.reshape(ORDER, LANES)
     return (
         jnp.logaddexp(0.0, -margin),

time: 164 us -> 139 us (0.85)
  starting transfers between devices: 50 us -> 28.5 us
  waiting for transfers between devices: 38.9 us -> 29.9 us
  blocking collectives: 43.3 us -> 51.4 us
  other arithmetic: 5.31 us -> 2.29 us
    ppermute x28 -> x14, starting transfers between devices: 38.7 us -> 21 us  [the longest x8 12.1 us: other_core(): return lax.ppermute(values, 'c', [(0, 1), (1, 0)])]
    ppermute x28 -> x14, waiting for transfers between devices: 36.3 us -> 27.3 us  [the longest x6 24.2 us: ring(): return lax.ppermute(values, FINE_AXES, pairs)]
    all_to_all x3 -> x2, blocking collectives: 43.3 us -> 51.4 us  [crosswise(): lax.all_to_all(values, FINE_AXES, 0, 0, axis_index_groups=groups, tiled=T...]
    all_to_all x2 -> x1, starting transfers between devices: 11.3 us -> 7.46 us  [local(): whole = lax.all_to_all(copies, CTX, 0, 0, tiled=True)]
    convert_element_type x6 -> x4, other arithmetic: 3.04 us -> 0.98 us  [the longest x3 0.54 us: local(): chip = [total_of(a, other_core(b)).astype(BF) for a, b in zip(own, other)]]
  transfers between devices with their start and end apart: 30 -> 15, of which waited for: 16 -> 8; matrix products, arithmetic and copies ran while one was open for 2% -> 1% of each run, Pallas kernels for 0% -> 0%
where the time goes in v3:
time: 139 us; the launch traced here: 138 us
  blocking collectives  51.4 us (37%)
  waiting for transfers between devices  29.9 us (22%)
  starting transfers between devices  28.5 us (21%)
  Pallas kernels  19.5 us (14%)
  local copies, waits for them, and re-layouts  4.25 us (3%)
  between operations  2.61 us (2%)
  other arithmetic  2.29 us (2%)
    all_to_all x2, blocking collectives, crosswise(): lax.all_to_all(values, FINE_AXES, 0, 0, axis_index_groups=groups, tiled=T...  51.4 us
    ppermute x6, waiting for transfers between devices, ring(): return lax.ppermute(values, FINE_AXES, pairs)  24.2 us
    pallas_call x1, Pallas kernels, shares(): pl.pallas_call(kernel, out_shape=[jax.ShapeDtypeStruct((32, 16, LANES), B...  19.5 us
    ppermute x8, starting transfers between devices, other_core(): return lax.ppermute(values, 'c', [(0, 1), (1, 0)])  12.1 us
    ppermute x6, starting transfers between devices, ring(): return lax.ppermute(values, FINE_AXES, pairs)  8.89 us
    all_to_all x1, starting transfers between devices, local(): whole = lax.all_to_all(copies, CTX, 0, 0, tiled=True)  7.46 us
    ppermute x8, waiting for transfers between devices, other_core(): return lax.ppermute(values, 'c', [(0, 1), (1, 0)])  3.08 us
  transfers between devices with their start and end apart: 15, of which 8 were waited for; matrix products, arithmetic and copies ran while one was open for 1% of the time, Pallas kernels for 0%

profile of v3, /device:TPU:1, one launch (start us, length us, event | category | flops | bytes accessed | tf_op | source)
XLA Modules:
  0.0 138.4 jit_solution(12062039968928392478)
XLA Ops:
  0.6 0.0 copy-start
  0.6 0.0 copy-start.2
  0.7 1.0 fusion
  1.7 0.1 copy.13
  1.8 0.1 convert_element_type.66
  1.9 0.7 constant_dynamic-slice_fusion
  2.6 0.7 dynamic-slice_bitcast_fusion.1
  3.4 0.1 fusion.2
  3.4 0.1 pad.2.clone
  3.5 0.1 broadcast_in_dim.31
  3.6 29.6 %all_to_all.15.refs_0_ = bf16[32,16,640]{2,1,0:T(8,128)(2,1)S(1)} all-to-all(bf16[32,16,640]{2,1,0:T(8,128)(2,1)S(1)} %broadcast_in_dim.31), channel_id=1, replica_groups={{0,2,16,18,32,34,48,50,64,66,80,82,96,98,112,114,128,130,144,146,160,16..., dimensions={0} | all-to-all | bytes 1310720 | tf_op jit(solution)/shard_map/all_to_all | solution.py:219
  33.2 3.6 %collective-permute-start.2 = (bf16[32,16,640]{2,1,0:T(8,128)(2,1)S(1)}, bf16[32,16,640]{2,1,0:T(8,128)(2,1)S(1)}, u32[]{:S(2)}, u32[]{:S(2)}) collective-permute-start(bf16[32,16,640]{2,1,0:T(8,128)(2,1)S(1)} %all_to_all.15.refs_0_), channel_id=1, source_target_pairs={{0,12},{1,19},{4,0},{5,23},{8,4},{9,27},{12,8},{13,31},{2,14},{3,1... | collective-permute-start | bytes 1966088 | tf_op jit(solution)/shard_map/ppermute | solution.py:213
  36.9 0.0 collective-permute-start.1
  36.9 0.7 collective-permute-start
  37.5 4.0 %collective-permute-start.3 = (bf16[32,16,640]{2,1,0:T(8,128)(2,1)S(1)}, bf16[32,16,640]{2,1,0:T(8,128)(2,1)}, u32[]{:S(2)}, u32[]{:S(2)}) collective-permute-start(bf16[32,16,640]{2,1,0:T(8,128)(2,1)S(1)} %all_to_all.15.refs_0_), channel_id=1, source_target_pairs={{0,1},{1,0},{2,3},{3,2},{4,5},{5,4},{6,7},{7,6},{8,9},{9,8},{10,11... | collective-permute-start | bytes 1966088 | tf_op jit(solution)/shard_map/ppermute | solution.py:223
  41.6 9.9 %collective-permute-done.2.refs_3_ = bf16[32,16,640]{2,1,0:T(8,128)(2,1)S(1)} collective-permute-done((bf16[32,16,640]{2,1,0:T(8,128)(2,1)S(1)}, bf16[32,16,640]{2,1,0:T(8,128)(2,1)S(1)}, u32[]{:S(2)}, u32[]{:S(2)}) %collective-permute-start.2) | collective-permute-done | bytes 655392 | tf_op jit(solution)/shard_map/ppermute | solution.py:213
  51.4 3.2 %collective-permute-start.6 = (bf16[32,16,640]{2,1,0:T(8,128)(2,1)S(1)}, bf16[32,16,640]{2,1,0:T(8,128)(2,1)}, u32[]{:S(2)}, u32[]{:S(2)}) collective-permute-start(bf16[32,16,640]{2,1,0:T(8,128)(2,1)S(1)} %collective-permute-done.2.refs_3_), channel_id=1, source_target_pairs={{0,1},{1,0},{2,3},{3,2},{4,5},{5,4},{6,7},{7,6},{8,9},{9,8},{10,11... | collective-permute-start | bytes 1966088 | tf_op jit(solution)/shard_map/ppermute | solution.py:223
  54.6 0.0 collective-permute-start.5
  54.7 0.3 collective-permute-done.refs_1_
  54.9 3.8 %collective-permute-start.4 = (bf16[32,16,640]{2,1,0:T(8,128)(2,1)}, bf16[32,16,640]{2,1,0:T(8,128)(2,1)}, u32[]{:S(2)}, u32[]{:S(2)}) collective-permute-start(bf16[32,16,640]{2,1,0:T(8,128)(2,1)} %collective-permute-done.refs_1_), channel_id=1, source_target_pairs={{0,1},{1,0},{2,3},{3,2},{4,5},{5,4},{6,7},{7,6},{8,9},{9,8},{10,11... | collective-permute-start | bytes 1966088 | tf_op jit(solution)/shard_map/ppermute | solution.py:223
  58.7 0.1 pad_add_fusion.place_ref
  58.8 0.0 collective-permute-done.3.refs_4_
  58.8 2.0 %collective-permute-done.4.refs_5_ = bf16[32,16,640]{2,1,0:T(8,128)(2,1)} collective-permute-done((bf16[32,16,640]{2,1,0:T(8,128)(2,1)}, bf16[32,16,640]{2,1,0:T(8,128)(2,1)}, u32[]{:S(2)}, u32[]{:S(2)}) %collective-permute-start.4) | collective-permute-done | bytes 655392 | tf_op jit(solution)/shard_map/ppermute | solution.py:223
  60.8 19.5 %shard_map.106 = (bf16[32,16,640]{2,1,0:T(8,128)(2,1)S(1)}, bf16[32,16,640]{2,1,0:T(8,128)(2,1)S(1)}, bf16[32,16,640]{2,1,0:T(8,128)(2,1)S(1)}, bf16[32,16,640]{...) custom-call(s32[4]{0:T(128)S(1)} %pad_add_fusion.place_ref, ...), custom_call_target="tpu_custom_call" | custom-call | flops 1505755136 | bytes 22249472 | tf_op jit(solution)/shard_map/pallas_call | solution.py:176
  80.3 0.5 collective-permute-start.8
  80.8 0.1 collective-permute-start.10
  80.9 0.4 collective-permute-start.12
  81.3 0.1 collective-permute-start.7
  81.4 1.1 collective-permute-done.8
  82.5 0.2 add_convert_fusion.3
  82.7 0.7 collective-permute-start.9
  83.4 0.0 collective-permute-done.10
  83.4 0.2 add_convert_fusion.2
  83.6 2.7 %collective-permute-start.11 = (bf16[32,16,640]{2,1,0:T(8,128)(2,1)S(1)}, bf16[32,16,640]{2,1,0:T(8,128)(2,1)S(1)}, u32[]{:S(2)}, u32[]{:S(2)}) collective-permute-start(bf16[32,16,640]{2,1,0:T(8,128)(2,1)S(1)} %add_convert_fusion.2), channel_id=1, source_target_pairs={{0,8},{1,17},{4,12},{5,21},{8,0},{9,25},{12,4},{13,29},{2,10},{3,1... | collective-permute-start | bytes 1966088 | tf_op jit(solution)/shard_map/ppermute | solution.py:213
  86.3 0.2 add_convert_fusion.1
  86.5 1.1 collective-permute-start.13
  87.6 6.1 %collective-permute-done.9 = bf16[32,16,640]{2,1,0:T(8,128)(2,1)S(1)} collective-permute-done((bf16[32,16,640]{2,1,0:T(8,128)(2,1)S(1)}, bf16[32,16,640]{2,1,0:T(8,128)(2,1)S(1)}, u32[]{:S(2)}, u32[]{:S(2)}) %collective-permute-start.9) | collective-permute-done | bytes 655392 | tf_op jit(solution)/shard_map/ppermute | solution.py:213
  93.7 7.6 %collective-permute-done.11 = bf16[32,16,640]{2,1,0:T(8,128)(2,1)S(1)} collective-permute-done((bf16[32,16,640]{2,1,0:T(8,128)(2,1)S(1)}, bf16[32,16,640]{2,1,0:T(8,128)(2,1)S(1)}, u32[]{:S(2)}, u32[]{:S(2)}) %collective-permute-start.11) | collective-permute-done | bytes 655392 | tf_op jit(solution)/shard_map/ppermute | solution.py:213
  101.3 0.4 collective-permute-done.13
  101.7 0.4 add_convert_fusion
  102.1 21.7 %all_to_all.16 = bf16[32,16,640]{2,1,0:T(8,128)(2,1)S(1)} all-to-all(bf16[32,16,640]{2,1,0:T(8,128)(2,1)S(1)} %add_convert_fusion), channel_id=1, replica_groups={{0,2,16,18,32,34,48,50,64,66,80,82,96,98,112,114,128,130,144,146,160,16..., dimensions={0} | all-to-all | bytes 1310720 | tf_op jit(solution)/shard_map/all_to_all | solution.py:219
  123.9 0.1 convert_reduce_fusion
  124.0 0.7 broadcast_in_dim.32
  124.7 7.5 %all-to-all-start.2 = ((f32[4,16,640]{2,1,0:T(8,128)}), f32[4,16,640]{2,1,0:T(8,128)S(1)}, u32[]{:S(2)}, u32[]{:S(2)}) async-start(f32[4,16,640]{2,1,0:T(8,128)} %broadcast_in_dim.32), calls=%async_computation.2 | async-start | bytes 327680 | tf_op jit(solution)/shard_map/all_to_all | solution.py:279
  132.1 0.5 slice.9
  133.4 2.6 %all-to-all-done.2 = f32[4,16,640]{2,1,0:T(8,128)S(1)} async-done(((f32[4,16,640]{2,1,0:T(8,128)}), f32[4,16,640]{2,1,0:T(8,128)S(1)}, u32[]{:S(2)}, u32[]{:S(2)}) %all-to-all-start.2) | async-done | bytes 163872 | tf_op jit(solution)/shard_map/all_to_all | solution.py:279
  136.0 0.6 slice.13
  136.6 0.7 slice_bitcast_fusion
  (16 shorter events, 0.1 us)
Async XLA Ops:
  0.6 2.0 %copy-start = (bf16[462,64]{0,1:T(8,128)(2,1)S(1)}, bf16[462,64]{0,1:T(8,128)(2,1)}, u32[]{:S(2)}) copy-start(bf16[462,64]{0,1:T(8,128)(2,1)} %param.11) | copy-start | bytes 177412
  0.6 60.1 %copy-start.2 = (s32[1,2]{1,0:T(1,128)S(1)}, s32[1,2]{1,0:T(1,128)}, u32[]{:S(2)}) copy-start(s32[1,2]{1,0:T(1,128)} %starts_ref.1) | copy-start | bytes 28
  0.7 60.1 %copy-start.1 = (bf16[1,2,64,8192]{3,2,1,0:T(8,128)(2,1)S(1)}, bf16[1,2,64,8192]{3,2,1,0:T(8,128)(2,1)}, u32[]{:S(2)}) copy-start(bf16[1,2,64,8192]{3,2,1,0:T(8,128)(2,1)} %param.9) | copy-start | bytes 6291460
  33.2 18.2 %collective-permute-start.2 = (bf16[32,16,640]{2,1,0:T(8,128)(2,1)S(1)}, bf16[32,16,640]{2,1,0:T(8,128)(2,1)S(1)}, u32[]{:S(2)}, u32[]{:S(2)}) collective-permute-start(bf16[32,16,640]{2,1,0:T(8,128)(2,1)S(1)} %all_to_all.15.refs_0_), channel_id=1, source_target_pairs={{0,12},{1,19},{4,0},{5,23},{8,4},{9,27},{12,8},{13,31},{2,14},{3,1... | collective-permute-start | bytes 1966088 | tf_op jit(solution)/shard_map/ppermute | solution.py:213
  36.9 17.8 %collective-permute-start.1 = (bf16[32,16,640]{2,1,0:T(8,128)(2,1)S(1)}, bf16[32,16,640]{2,1,0:T(8,128)(2,1)}, u32[]{:S(2)}, u32[]{:S(2)}) collective-permute-start(bf16[32,16,640]{2,1,0:T(8,128)(2,1)S(1)} %all_to_all.15.refs_0_), channel_id=1, source_target_pairs={{0,8},{1,17},{4,12},{5,21},{8,0},{9,25},{12,4},{13,29},{2,10},{3,1... | collective-permute-start | bytes 1966088 | tf_op jit(solution)/shard_map/ppermute | solution.py:213
  36.9 18.1 %collective-permute-start = (bf16[32,16,640]{2,1,0:T(8,128)(2,1)S(1)}, bf16[32,16,640]{2,1,0:T(8,128)(2,1)}, u32[]{:S(2)}, u32[]{:S(2)}) collective-permute-start(bf16[32,16,640]{2,1,0:T(8,128)(2,1)S(1)} %all_to_all.15.refs_0_), channel_id=1, source_target_pairs={{0,4},{1,3},{4,8},{5,7},{8,12},{9,11},{12,0},{13,15},{2,6},{3,17},... | collective-permute-start | bytes 1966088 | tf_op jit(solution)/shard_map/ppermute | solution.py:213
  37.5 21.2 %collective-permute-start.3 = (bf16[32,16,640]{2,1,0:T(8,128)(2,1)S(1)}, bf16[32,16,640]{2,1,0:T(8,128)(2,1)}, u32[]{:S(2)}, u32[]{:S(2)}) collective-permute-start(bf16[32,16,640]{2,1,0:T(8,128)(2,1)S(1)} %all_to_all.15.refs_0_), channel_id=1, source_target_pairs={{0,1},{1,0},{2,3},{3,2},{4,5},{5,4},{6,7},{7,6},{8,9},{9,8},{10,11... | collective-permute-start | bytes 1966088 | tf_op jit(solution)/shard_map/ppermute | solution.py:223
  51.4 7.4 %collective-permute-start.6 = (bf16[32,16,640]{2,1,0:T(8,128)(2,1)S(1)}, bf16[32,16,640]{2,1,0:T(8,128)(2,1)}, u32[]{:S(2)}, u32[]{:S(2)}) collective-permute-start(bf16[32,16,640]{2,1,0:T(8,128)(2,1)S(1)} %collective-permute-done.2.refs_3_), channel_id=1, source_target_pairs={{0,1},{1,0},{2,3},{3,2},{4,5},{5,4},{6,7},{7,6},{8,9},{9,8},{10,11... | collective-permute-start | bytes 1966088 | tf_op jit(solution)/shard_map/ppermute | solution.py:223
  54.6 4.1 %collective-permute-start.5 = (bf16[32,16,640]{2,1,0:T(8,128)(2,1)}, bf16[32,16,640]{2,1,0:T(8,128)(2,1)}, u32[]{:S(2)}, u32[]{:S(2)}) collective-permute-start(bf16[32,16,640]{2,1,0:T(8,128)(2,1)} %collective-permute-done.1.refs_2_), channel_id=1, source_target_pairs={{0,1},{1,0},{2,3},{3,2},{4,5},{5,4},{6,7},{7,6},{8,9},{9,8},{10,11... | collective-permute-start | bytes 1966088 | tf_op jit(solution)/shard_map/ppermute | solution.py:223
  54.9 5.8 %collective-permute-start.4 = (bf16[32,16,640]{2,1,0:T(8,128)(2,1)}, bf16[32,16,640]{2,1,0:T(8,128)(2,1)}, u32[]{:S(2)}, u32[]{:S(2)}) collective-permute-start(bf16[32,16,640]{2,1,0:T(8,128)(2,1)} %collective-permute-done.refs_1_), channel_id=1, source_target_pairs={{0,1},{1,0},{2,3},{3,2},{4,5},{5,4},{6,7},{7,6},{8,9},{9,8},{10,11... | collective-permute-start | bytes 1966088 | tf_op jit(solution)/shard_map/ppermute | solution.py:223
  80.3 2.2 %collective-permute-start.8 = (bf16[32,16,640]{2,1,0:T(8,128)(2,1)S(1)}, bf16[32,16,640]{2,1,0:T(8,128)(2,1)S(1)}, u32[]{:S(2)}, u32[]{:S(2)}) collective-permute-start(bf16[32,16,640]{2,1,0:T(8,128)(2,1)S(1)} %get-tuple-element.16), channel_id=1, source_target_pairs={{0,1},{1,0},{2,3},{3,2},{4,5},{5,4},{6,7},{7,6},{8,9},{9,8},{10,11... | collective-permute-start | bytes 1966088 | tf_op jit(solution)/shard_map/ppermute | solution.py:223
  80.8 2.7 %collective-permute-start.10 = (bf16[32,16,640]{2,1,0:T(8,128)(2,1)S(1)}, bf16[32,16,640]{2,1,0:T(8,128)(2,1)S(1)}, u32[]{:S(2)}, u32[]{:S(2)}) collective-permute-start(bf16[32,16,640]{2,1,0:T(8,128)(2,1)S(1)} %get-tuple-element.18), channel_id=1, source_target_pairs={{0,1},{1,0},{2,3},{3,2},{4,5},{5,4},{6,7},{7,6},{8,9},{9,8},{10,11... | collective-permute-start | bytes 1966088 | tf_op jit(solution)/shard_map/ppermute | solution.py:223
  80.9 5.4 %collective-permute-start.12 = (bf16[32,16,640]{2,1,0:T(8,128)(2,1)S(1)}, bf16[32,16,640]{2,1,0:T(8,128)(2,1)S(1)}, u32[]{:S(2)}, u32[]{:S(2)}) collective-permute-start(bf16[32,16,640]{2,1,0:T(8,128)(2,1)S(1)} %get-tuple-element.20), channel_id=1, source_target_pairs={{0,1},{1,0},{2,3},{3,2},{4,5},{5,4},{6,7},{7,6},{8,9},{9,8},{10,11... | collective-permute-start | bytes 1966088 | tf_op jit(solution)/shard_map/ppermute | solution.py:223
  81.3 6.4 %collective-permute-start.7 = (bf16[32,16,640]{2,1,0:T(8,128)(2,1)S(1)}, bf16[32,16,640]{2,1,0:T(8,128)(2,1)S(1)}, u32[]{:S(2)}, u32[]{:S(2)}) collective-permute-start(bf16[32,16,640]{2,1,0:T(8,128)(2,1)S(1)} %get-tuple-element.14), channel_id=1, source_target_pairs={{0,1},{1,0},{2,3},{3,2},{4,5},{5,4},{6,7},{7,6},{8,9},{9,8},{10,11... | collective-permute-start | bytes 1966088 | tf_op jit(solution)/shard_map/ppermute | solution.py:223
  82.7 11.0 %collective-permute-start.9 = (bf16[32,16,640]{2,1,0:T(8,128)(2,1)S(1)}, bf16[32,16,640]{2,1,0:T(8,128)(2,1)S(1)}, u32[]{:S(2)}, u32[]{:S(2)}) collective-permute-start(bf16[32,16,640]{2,1,0:T(8,128)(2,1)S(1)} %add_convert_fusion.3), channel_id=1, source_target_pairs={{0,4},{1,3},{4,8},{5,7},{8,12},{9,11},{12,0},{13,15},{2,6},{3,17},... | collective-permute-start | bytes 1966088 | tf_op jit(solution)/shard_map/ppermute | solution.py:213
  83.6 17.7 %collective-permute-start.11 = (bf16[32,16,640]{2,1,0:T(8,128)(2,1)S(1)}, bf16[32,16,640]{2,1,0:T(8,128)(2,1)S(1)}, u32[]{:S(2)}, u32[]{:S(2)}) collective-permute-start(bf16[32,16,640]{2,1,0:T(8,128)(2,1)S(1)} %add_convert_fusion.2), channel_id=1, source_target_pairs={{0,8},{1,17},{4,12},{5,21},{8,0},{9,25},{12,4},{13,29},{2,10},{3,1... | collective-permute-start | bytes 1966088 | tf_op jit(solution)/shard_map/ppermute | solution.py:213
  86.5 15.2 %collective-permute-start.13 = (bf16[32,16,640]{2,1,0:T(8,128)(2,1)S(1)}, bf16[32,16,640]{2,1,0:T(8,128)(2,1)S(1)}, u32[]{:S(2)}, u32[]{:S(2)}) collective-permute-start(bf16[32,16,640]{2,1,0:T(8,128)(2,1)S(1)} %add_convert_fusion.1), channel_id=1, source_target_pairs={{0,12},{1,19},{4,0},{5,23},{8,4},{9,27},{12,8},{13,31},{2,14},{3,1... | collective-permute-start | bytes 1966088 | tf_op jit(solution)/shard_map/ppermute | solution.py:213
  124.7 11.3 %all-to-all-start.2 = ((f32[4,16,640]{2,1,0:T(8,128)}), f32[4,16,640]{2,1,0:T(8,128)S(1)}, u32[]{:S(2)}, u32[]{:S(2)}) async-start(f32[4,16,640]{2,1,0:T(8,128)} %broadcast_in_dim.32), calls=%async_computation.2 | async-start | bytes 327680 | tf_op jit(solution)/shard_map/all_to_all | solution.py:279

commit v4 on v3

--- a/solution.py
+++ b/solution.py
@@ -36,42 +36,37 @@
     py, px, pc = place[1], place[2], place[3]
     dxs = [((sign * (px - x)) & 3) * 32 for x in range(4)]
     dys = [((sign * (py - y)) & 3) * 32 for y in range(4)]
-    cores = [((pc + c) & 1) * 128 for c in range(2)]
-
-    def flat(chunk, q):
+
+    def flat(chunk, other, yl):
         z, yh, x = chunk // 8, chunk // 4 % 2, chunk % 4
-        c, y = q // 2, yh * 2 + q % 2
-        if c == 0:
-            return cores[0] + dxs[x] + (z * 4 + y)
-        return cores[1] + dys[y] + (z * 4 + x)
+        y = yh * 2 + yl
+        first = pc == other
+        return jnp.where(first, dxs[x] + (z * 4 + y), dys[y] + (z * 4 + x))
 
     return flat
 
 
 def kernel(place_ref, starts_ref, *refs):
-    parts, (hidden_hbm, frozen_hbm, head_hbm) = refs[:8], refs[8:11]
-    outs, margin_ref = refs[11:19], refs[19]
-    hid, fro, hea, wt, up, gains, gain, pol, block, sems = refs[20:]
+    parts, (hid, fro, hea) = refs[:8], refs[8:11]
+    outs, margin_ref = refs[11:13], refs[13]
+    wt, up, gains, gain, pol, block, sems = refs[14:]
     width = fro.shape[1]
 
     loads = [
         pltpu.make_async_copy(parts[i], block.at[pl.ds(32 * i, 32)], sems.at[i]) for i in range(8)
     ]
-    loads.append(pltpu.make_async_copy(hidden_hbm, hid, sems.at[8]))
-    loads.append(pltpu.make_async_copy(frozen_hbm, fro, sems.at[9]))
-    loads.append(pltpu.make_async_copy(head_hbm, hea, sems.at[10]))
     for copy in loads:
         copy.start()
-    for copy in loads[:8]:
+    for copy in loads:
         copy.wait()
 
     pz, py, px, pc = (place_ref[i] for i in range(4))
     sums = jnp.zeros((1, 128), F32)
-    for c in range(2):
+    for other in range(2):
         for yl in range(2):
             y = (py & 2) + yl
-            inside = pz * 4 + px + ((py - y) & 3) * 32 if c else pz * 4 + y
-            held = block[((pc + c) & 1) * 128 + inside]
+            inside = jnp.where(pc == other, pz * 4 + y, pz * 4 + px + ((py - y) & 3) * 32)
+            held = block[other * 128 + inside]
             sums += held[0:1, LANES - 128 :].astype(F32)
     lane = SUMS_AT - (LANES - 128)
     sides = [sum(sums[:, lane + 3 * s + j : lane + 3 * s + j + 1] for j in range(3)) for s in (0, 1)]
@@ -86,33 +81,34 @@
     source = slots(place_ref, 1)
     for chunk in range(CHUNKS):
         for q in range(4):
-            held = block[source(chunk, q)]
+            held = block[(q // 2) * 128 + source(chunk, q // 2, q % 2)]
             rows = slice(16 * q, 16 * q + 16)
             up[rows, chunk * UP : (chunk + 1) * UP] = held[:, :UP]
             wt[rows, chunk * DOWN : (chunk + 1) * DOWN] = held[:, UP : UP + DOWN]
             gains[q, chunk : chunk + 1, :] = held[0:1, LANES - 128 :].astype(F32)
     lane = GAIN_AT - (LANES - 128)
-    gain[...] = jnp.concatenate([gains[q][:, lane : lane + 32] for q in range(4)], axis=1)
-
-    loads[8].wait()
-    tile = 2688
-
-    def low_step(i, total):
-        at = pl.ds(pl.multiple_of(i * tile, 128), tile)
-        return total + dot(hid[:, at], wt[:, at], NT)
-
-    low = lax.fori_loop(0, wt.shape[1] // tile, low_step, jnp.zeros((128, ORDER), F32)).astype(BF)
+    parts_of_gain = [gains[q][:, lane : lane + 32] for q in range(4)]
+    ordered = jnp.concatenate(parts_of_gain, axis=1)
+    swapped = jnp.concatenate(parts_of_gain[2:] + parts_of_gain[:2], axis=1)
+    gain[...] = jnp.where(pc == 0, ordered, swapped)
+
+    tile = 5888
+    main = wt.shape[1] // tile
+    low = dot(hid[:, main * tile :], wt[:, main * tile :], NT)
+    for i in range(main):
+        at = slice(i * tile, i * tile + tile)
+        low += dot(hid[:, at], wt[:, at], NT)
+    low = low.astype(BF)
     low_t = low.astype(F32).T.astype(BF)
 
-    loads[9].wait()
-    loads[10].wait()
     step = 512
 
     def gained(i):
         pieces = []
         for j in range(step // 128):
-            at = pl.ds(pl.multiple_of(i * step + j * 128, 128), 128)
-            pieces.append(hea[:, at].astype(F32) * gain[pl.ds(i * (step // 128) + j, 1), :])
+            at = slice(i * step + j * 128, i * step + j * 128 + 128)
+            chunk = i * (step // 128) + j
+            pieces.append(hea[:, at].astype(F32) * gain[chunk : chunk + 1, :])
         return jnp.concatenate(pieces, axis=1)
 
     def fold(v):
@@ -120,13 +116,15 @@
 
     def state_step(i, carry):
         squares, inner = carry
-        at = pl.ds(pl.multiple_of(i * step, 128), step)
+        at = slice(i * step, i * step + step)
         state = fro[:, at].astype(F32) + SCALE * dot(low, up[:, at], NN)
         pol[:, at] = state
         return squares + fold(state * state), inner + fold(gained(i) * state)
 
     zero = jnp.zeros((128, 128), F32)
-    squares, inner = lax.fori_loop(0, width // step, state_step, (zero, zero))
+    squares, inner = zero, zero
+    for i in range(width // step):
+        squares, inner = state_step(i, (squares, inner))
     rms = jnp.sqrt(jnp.sum(squares, axis=1, keepdims=True) / width + EPS)
     inner = slope * jnp.sum(inner, axis=1, keepdims=True)
     first = slope / rms
@@ -143,29 +141,43 @@
         share = (SCALE * dot(low_t, high, NN)).astype(BF)
         for j in range(step // 128):
             for q in range(4):
-                block[target(i * (step // 128) + j, q), :, :UP] = share[
+                outs[q // 2][target(i * (step // 128) + j, q // 2, q % 2), :, :UP] = share[
                     16 * q : 16 * q + 16, 128 * j : 128 * j + 128
                 ]
     grad_low = (SCALE * total).T.astype(BF)
 
+    tile = 1024
+    for begin in range(0, wt.shape[1], tile):
+        at = slice(begin, min(begin + tile, wt.shape[1]))
+        wt[:, at] = dot(grad_low, hid[:, at], NN).astype(BF)
     for chunk in range(CHUNKS):
-        begin = chunk * DOWN // 128 * 128
-        shift = chunk * DOWN - begin
-        span = 512 if shift + DOWN <= 512 else 640
-        share = dot(grad_low, hid[:, begin : begin + span], NN)
-        if shift:
-            share = pltpu.roll(share, span - shift, 1)
-        share = share[:, :512].astype(BF)
         for q in range(4):
-            block[target(chunk, q), :, UP:] = share[16 * q : 16 * q + 16]
-
-    stores = [
-        pltpu.make_async_copy(block.at[pl.ds(32 * i, 32)], outs[i], sems.at[i]) for i in range(8)
-    ]
-    for copy in stores:
+            outs[q // 2][target(chunk, q // 2, q % 2), :, UP : UP + DOWN] = wt[
+                16 * q : 16 * q + 16, chunk * DOWN : (chunk + 1) * DOWN
+            ]
+
+
+def bring(after_ref, *refs):
+    sems = refs[6]
+    copies = [pltpu.make_async_copy(refs[i], refs[3 + i], sems.at[i]) for i in range(3)]
+    for copy in copies:
         copy.start()
-    for copy in stores:
+    for copy in copies:
         copy.wait()
+
+
+def brought(after, *arrays):
+    any_space = pl.BlockSpec(memory_space=pl.ANY)
+    size = sum(v.size * 2 for v in arrays)
+    return pl.pallas_call(
+        bring,
+        out_shape=[pltpu.VMEM(v.shape, v.dtype) for v in arrays],
+        in_specs=[any_space] * 4,
+        out_specs=[pl.BlockSpec(memory_space=pltpu.VMEM)] * 3,
+        scratch_shapes=[pltpu.SemaphoreType.DMA((3,))],
+        compiler_params=pltpu.CompilerParams(vmem_limit_bytes=1024 * 1024),
+        cost_estimate=pl.CostEstimate(flops=0, bytes_accessed=2 * size, transcendentals=0),
+    )(after, *[pltpu.with_memory_space_constraint(v, pltpu.HBM) for v in arrays])
 
 
 def shares(place, starts, parts, hidden, frozen, head):
@@ -173,32 +185,30 @@
     width = frozen.shape[1]
     any_space = pl.BlockSpec(memory_space=pl.ANY)
     smem = pl.BlockSpec(memory_space=pltpu.SMEM)
+    vmem = pl.BlockSpec(memory_space=pltpu.VMEM)
+    near = [pltpu.with_memory_space_constraint(v, pltpu.VMEM) for v in (hidden, frozen, head)]
     outs = pl.pallas_call(
         kernel,
-        out_shape=[jax.ShapeDtypeStruct((32, 16, LANES), BF)] * 8
-        + [jax.ShapeDtypeStruct((8, 128), F32)],
-        in_specs=[smem, smem] + [any_space] * 11,
-        out_specs=[any_space] * 8 + [pl.BlockSpec(memory_space=pltpu.VMEM)],
+        out_shape=[pltpu.VMEM((128, 16, LANES), BF)] * 2 + [jax.ShapeDtypeStruct((8, 128), F32)],
+        in_specs=[smem, smem] + [any_space] * 8 + [vmem] * 3,
+        out_specs=[vmem] * 3,
         scratch_shapes=[
-            pltpu.VMEM((rows, units), BF),
-            pltpu.VMEM((rows, width), BF),
-            pltpu.VMEM((rows, width), BF),
             pltpu.VMEM((ORDER, units), BF),
             pltpu.VMEM((ORDER, width), BF),
             pltpu.VMEM((4, CHUNKS, 128), F32),
             pltpu.VMEM((CHUNKS, 128), F32),
             pltpu.VMEM((rows, width), F32),
             pltpu.VMEM((256, 16, LANES), BF),
-            pltpu.SemaphoreType.DMA((11,)),
+            pltpu.SemaphoreType.DMA((8,)),
         ],
-        compiler_params=pltpu.CompilerParams(vmem_limit_bytes=40 * 1024 * 1024),
+        compiler_params=pltpu.CompilerParams(vmem_limit_bytes=24 * 1024 * 1024),
         cost_estimate=pl.CostEstimate(
             flops=2 * rows * ORDER * (2 * units + 4 * width),
             bytes_accessed=2 * rows * (units + 2 * width) + 4 * 256 * 16 * LANES,
             transcendentals=0,
         ),
-    )(place, starts, *parts, hidden, frozen, head)
-    return outs[:4], outs[4:8], outs[8][0, 0:1]
+    )(place, starts, *parts, *near)
+    return outs[0], outs[1], outs[2][0, 0:1]
 
 
 def device(z, y, x, c):
@@ -260,18 +270,23 @@
     )
     held = crosswise(jnp.broadcast_to(quarter[None], (32, 16, LANES)))
     own = [held] + [ring(held, step) for step in (1, 2, 3)]
-    other = [other_core(v) for v in own]
-
-    own, other, margin = shares(
-        place,
-        starts,
-        [*own, *other],
+    width = frozen.shape[3]
+    near = brought(
+        held,
         gated_hidden_input.reshape(-1, gated_hidden_input.shape[3]),
-        frozen.reshape(-1, frozen.shape[3]),
-        head_gradient_rows.reshape(-1, frozen.shape[3]),
-    )
-
-    chip = [total_of(a, other_core(b)).astype(BF) for a, b in zip(own, other)]
+        frozen.reshape(-1, width),
+        head_gradient_rows.reshape(-1, width),
+    )
+    held, *near = lax.optimization_barrier((held, *near))
+    other = [other_core(v) for v in (held, *own[1:])]
+
+    own, other, margin = shares(place, starts, [*own, *other], *near)
+
+    came = other_core(other)
+    chip = [
+        total_of(own[32 * i : 32 * i + 32], came[32 * i : 32 * i + 32]).astype(BF)
+        for i in range(4)
+    ]
     came = [ring(chip[step], step) for step in (1, 2, 3)]
     line = total_of(chip[0], *came).astype(BF)
     share = jnp.sum(crosswise(line).astype(F32), axis=0)

time: 139 us -> 139 us (level)
  local copies, waits for them, and re-layouts: 4.25 us -> 13.4 us
  waiting for transfers between devices: 29.9 us -> 25.3 us
  Pallas kernels: 19.5 us -> 17.1 us
    unnamed x6 -> x12, local copies, waits for them, and re-layouts: 0.02 us -> 9.13 us
    ppermute x6, waiting for transfers between devices: 24.2 us -> 16.2 us  [ring(): return lax.ppermute(values, FINE_AXES, pairs)]
    ppermute x8 -> x5, waiting for transfers between devices: 3.08 us -> 6.52 us  [other_core(): return lax.ppermute(values, 'c', [(0, 1), (1, 0)])]
    pallas_call x1 -> x2, Pallas kernels: 19.5 us -> 17.1 us  [the longest x1 12.7 us: shares(): pl.pallas_call(kernel, out_shape=[pltpu.VMEM((128, 16, LANES), BF)] * 2 +...]
    ppermute x8 -> x5, starting transfers between devices: 12.1 us -> 11.5 us  [other_core(): return lax.ppermute(values, 'c', [(0, 1), (1, 0)])]
  transfers between devices with their start and end apart: 15 -> 12, of which waited for: 8 -> 8; matrix products, arithmetic and copies ran while one was open for 1% -> 0% of each run, Pallas kernels for 0% -> 3%
where the time goes in v4:
time: 139 us; the launch traced here: 138 us
  blocking collectives  50.7 us (36%)
  starting transfers between devices  27.3 us (20%)
  waiting for transfers between devices  25.3 us (18%)
  Pallas kernels  17.1 us (12%)
  local copies, waits for them, and re-layouts  13.4 us (10%)
  between operations  2.61 us (2%)
  other arithmetic  2.13 us (2%)
    all_to_all x2, blocking collectives, crosswise(): lax.all_to_all(values, FINE_AXES, 0, 0, axis_index_groups=groups, tiled=T...  50.7 us
    ppermute x6, waiting for transfers between devices, ring(): return lax.ppermute(values, FINE_AXES, pairs)  16.2 us
    pallas_call x1, Pallas kernels, shares(): pl.pallas_call(kernel, out_shape=[pltpu.VMEM((128, 16, LANES), BF)] * 2 +...  12.7 us
    ppermute x5, starting transfers between devices, other_core(): return lax.ppermute(values, 'c', [(0, 1), (1, 0)])  11.5 us
    unnamed x12, local copies, waits for them, and re-layouts  9.13 us
    ppermute x6, starting transfers between devices, ring(): return lax.ppermute(values, FINE_AXES, pairs)  8.14 us
    all_to_all x1, starting transfers between devices, local(): whole = lax.all_to_all(copies, CTX, 0, 0, tiled=True)  7.66 us
    ppermute x5, waiting for transfers between devices, other_core(): return lax.ppermute(values, 'c', [(0, 1), (1, 0)])  6.52 us
  transfers between devices with their start and end apart: 12, of which 8 were waited for; matrix products, arithmetic and copies ran while one was open for 0% of the time, Pallas kernels for 3%

profile of v4, /device:TPU:1, one launch (start us, length us, event | category | flops | bytes accessed | tf_op | source)
XLA Modules:
  0.0 138.4 jit_solution(14223374332126367348)
XLA Ops:
  0.6 0.0 copy-start
  0.7 0.9 fusion
  1.6 0.1 copy.13
  1.7 0.1 convert_element_type.66
  1.8 0.7 constant_dynamic-slice_fusion
  2.5 0.7 dynamic-slice_bitcast_fusion.1
  3.2 0.1 fusion.2
  3.3 0.1 pad.2.clone
  3.4 0.1 broadcast_in_dim.31
  3.4 29.6 %all_to_all.15.after_ref.refs_0_ = bf16[32,16,640]{2,1,0:T(8,128)(2,1)S(1)} all-to-all(bf16[32,16,640]{2,1,0:T(8,128)(2,1)S(1)} %broadcast_in_dim.31), channel_id=1, replica_groups={{0,2,16,18,32,34,48,50,64,66,80,82,96,98,112,114,128,130,144,146,160,16..., dimensions={0} | all-to-all | bytes 1310720 | tf_op jit(solution)/shard_map/all_to_all | solution.py:229
  33.1 3.6 %collective-permute-start.2 = (bf16[32,16,640]{2,1,0:T(8,128)(2,1)S(1)}, bf16[32,16,640]{2,1,0:T(8,128)(2,1)S(1)}, u32[]{:S(2)}, u32[]{:S(2)}) collective-permute-start(bf16[32,16,640]{2,1,0:T(8,128)(2,1)S(1)} %all_to_all.15.after_ref.refs_0_), channel_id=1, source_target_pairs={{0,12},{1,19},{4,0},{5,23},{8,4},{9,27},{12,8},{13,31},{2,14},{3,1... | collective-permute-start | bytes 1966088 | tf_op jit(solution)/shard_map/ppermute | solution.py:223
  36.7 0.0 collective-permute-start.1
  36.7 0.7 collective-permute-start
  37.4 4.4 %shard_map.106 = (bf16[128,29568]{1,0:T(8,128)(2,1)S(1)}, bf16[128,8192]{1,0:T(8,128)(2,1)S(1)}, bf16[128,8192]{1,0:T(8,128)(2,1)S(1)}) custom-call(bf16[32,16,640]{2,1,0:T(8,128)(2,1)S(1)} %all_to_all.15.after_ref.refs_0_, bf16[128,29568]{1,0:T(8,128)(2,1)} %bitcast.33, bf16[128,8192]{1,0:T(8,128)(2,1)} %bitcast.34, bf16[128,8192]{1,0:T(8,128)(2,1)} %bitcast.35), custom_call_target="tpu_custom_call" | custom-call | bytes 23527424 | tf_op jit(solution)/shard_map/pallas_call | solution.py:172
  41.8 3.0 %copy-done.1 = bf16[128,29568]{1,0:T(8,128)(2,1)} copy-done((bf16[128,29568]{1,0:T(8,128)(2,1)}, bf16[128,29568]{1,0:T(8,128)(2,1)S(1)}, u32[]{:S(2)}) %copy-start.1) | copy-done | bytes 7569432
  44.8 1.4 %copy-done.3 = bf16[128,8192]{1,0:T(8,128)(2,1)} copy-done((bf16[128,8192]{1,0:T(8,128)(2,1)}, bf16[128,8192]{1,0:T(8,128)(2,1)S(1)}, u32[]{:S(2)}) %copy-start.3) | copy-done | bytes 2097176
  46.2 4.0 %collective-permute-start.3 = (bf16[32,16,640]{2,1,0:T(8,128)(2,1)S(1)}, bf16[32,16,640]{2,1,0:T(8,128)(2,1)}, u32[]{:S(2)}, u32[]{:S(2)}) collective-permute-start(bf16[32,16,640]{2,1,0:T(8,128)(2,1)S(1)} %all_to_all.15.after_ref.refs_0_), channel_id=1, source_target_pairs={{0,1},{1,0},{2,3},{3,2},{4,5},{5,4},{6,7},{7,6},{8,9},{9,8},{10,11... | collective-permute-start | bytes 1966088 | tf_op jit(solution)/shard_map/ppermute | solution.py:233
  50.2 1.1 collective-permute-done.2.refs_3_
  51.2 3.2 %collective-permute-start.6 = (bf16[32,16,640]{2,1,0:T(8,128)(2,1)S(1)}, bf16[32,16,640]{2,1,0:T(8,128)(2,1)}, u32[]{:S(2)}, u32[]{:S(2)}) collective-permute-start(bf16[32,16,640]{2,1,0:T(8,128)(2,1)S(1)} %collective-permute-done.2.refs_3_), channel_id=1, source_target_pairs={{0,1},{1,0},{2,3},{3,2},{4,5},{5,4},{6,7},{7,6},{8,9},{9,8},{10,11... | collective-permute-start | bytes 1966088 | tf_op jit(solution)/shard_map/ppermute | solution.py:233
  54.5 0.0 collective-permute-done.1.refs_2_
  54.5 0.0 collective-permute-start.5
  54.5 0.3 collective-permute-done.refs_1_
  54.8 3.8 %collective-permute-start.4 = (bf16[32,16,640]{2,1,0:T(8,128)(2,1)}, bf16[32,16,640]{2,1,0:T(8,128)(2,1)}, u32[]{:S(2)}, u32[]{:S(2)}) collective-permute-start(bf16[32,16,640]{2,1,0:T(8,128)(2,1)} %collective-permute-done.refs_1_), channel_id=1, source_target_pairs={{0,1},{1,0},{2,3},{3,2},{4,5},{5,4},{6,7},{7,6},{8,9},{9,8},{10,11... | collective-permute-start | bytes 1966088 | tf_op jit(solution)/shard_map/ppermute | solution.py:233
  58.5 0.1 pad_add_fusion.place_ref
  58.6 0.0 collective-permute-done.3.refs_4_
  58.6 0.0 collective-permute-done.6.refs_7_
  58.6 2.0 %collective-permute-done.4.refs_5_ = bf16[32,16,640]{2,1,0:T(8,128)(2,1)} collective-permute-done((bf16[32,16,640]{2,1,0:T(8,128)(2,1)}, bf16[32,16,640]{2,1,0:T(8,128)(2,1)}, u32[]{:S(2)}, u32[]{:S(2)}) %collective-permute-start.4) | collective-permute-done | bytes 655392 | tf_op jit(solution)/shard_map/ppermute | solution.py:233
  60.6 3.1 %copy-done.2 = bf16[128,29568]{1,0:T(8,128)(2,1)S(1)} copy-done((bf16[128,29568]{1,0:T(8,128)(2,1)S(1)}, bf16[128,29568]{1,0:T(8,128)(2,1)}, u32[]{:S(2)}) %copy-start.2) | copy-done | bytes 7569432
  63.8 1.6 %copy-done.4 = bf16[128,8192]{1,0:T(8,128)(2,1)S(1)} copy-done((bf16[128,8192]{1,0:T(8,128)(2,1)S(1)}, bf16[128,8192]{1,0:T(8,128)(2,1)}, u32[]{:S(2)}) %copy-start.4) | copy-done | bytes 2097176
  65.3 12.7 %shard_map.107 = (bf16[128,16,640]{2,1,0:T(8,128)(2,1)S(1)}, bf16[128,16,640]{2,1,0:T(8,128)(2,1)S(1)}, f32[8,128]{1,0:T(8,128)S(1)}) custom-call(s32[4]{0:T(128)S(1)} %pad_add_fusion.place_ref, s32[1,2]{1,0:T(1,128)S(1)} %copy-done.5, bf16[32,16,640]{2,1,0:T(8,128)(2,1)S(1)} %all_to_all.15.after_ref.refs_0_, ...), custom_call_target="tpu_custom_call" | custom-call | flops 1505755136 | bytes 22249472 | tf_op jit(solution)/shard_map/pallas_call | solution.py:190
  78.0 0.5 collective-permute-start.7
  78.5 4.5 %collective-permute-done.7 = bf16[128,16,640]{2,1,0:T(8,128)(2,1)S(1)} collective-permute-done((bf16[128,16,640]{2,1,0:T(8,128)(2,1)S(1)}, bf16[128,16,640]{2,1,0:T(8,128)(2,1)S(1)}, u32[]{:S(2)}, u32[]{:S(2)}) %collective-permute-start.7) | collective-permute-done | bytes 2621472 | tf_op jit(solution)/shard_map/ppermute | solution.py:233
  83.0 0.5 add_convert_fusion.3
  83.6 0.7 collective-permute-start.8
  84.3 2.0 %collective-permute-start.10 = (bf16[32,16,640]{2,1,0:T(8,128)(2,1)S(1)}, bf16[32,16,640]{2,1,0:T(8,128)(2,1)S(1)}, u32[]{:S(2)}, u32[]{:S(2)}) collective-permute-start(bf16[32,16,640]{2,1,0:T(8,128)(2,1)S(1)} %get-tuple-element.24), channel_id=1, source_target_pairs={{0,12},{1,19},{4,0},{5,23},{8,4},{9,27},{12,8},{13,31},{2,14},{3,1... | collective-permute-start | bytes 1966088 | tf_op jit(solution)/shard_map/ppermute | solution.py:223
  86.3 1.1 collective-permute-start.9
  87.4 7.2 %collective-permute-done.8 = bf16[32,16,640]{2,1,0:T(8,128)(2,1)S(1)} collective-permute-done((bf16[32,16,640]{2,1,0:T(8,128)(2,1)S(1)}, bf16[32,16,640]{2,1,0:T(8,128)(2,1)S(1)}, u32[]{:S(2)}, u32[]{:S(2)}) %collective-permute-start.8) | collective-permute-done | bytes 655392 | tf_op jit(solution)/shard_map/ppermute | solution.py:223
  94.6 6.3 %collective-permute-done.10 = bf16[32,16,640]{2,1,0:T(8,128)(2,1)S(1)} collective-permute-done((bf16[32,16,640]{2,1,0:T(8,128)(2,1)S(1)}, bf16[32,16,640]{2,1,0:T(8,128)(2,1)S(1)}, u32[]{:S(2)}, u32[]{:S(2)}) %collective-permute-start.10) | collective-permute-done | bytes 655392 | tf_op jit(solution)/shard_map/ppermute | solution.py:223
  100.9 1.3 collective-permute-done.9
  102.2 0.4 add_convert_fusion
  102.6 21.1 %all_to_all.16 = bf16[32,16,640]{2,1,0:T(8,128)(2,1)S(1)} all-to-all(bf16[32,16,640]{2,1,0:T(8,128)(2,1)S(1)} %add_convert_fusion), channel_id=1, replica_groups={{0,2,16,18,32,34,48,50,64,66,80,82,96,98,112,114,128,130,144,146,160,16..., dimensions={0} | all-to-all | bytes 1310720 | tf_op jit(solution)/shard_map/all_to_all | solution.py:229
  123.7 0.1 convert_reduce_fusion
  123.8 0.7 broadcast_in_dim.32
  124.5 7.7 %all-to-all-start.2 = ((f32[4,16,640]{2,1,0:T(8,128)}), f32[4,16,640]{2,1,0:T(8,128)S(1)}, u32[]{:S(2)}, u32[]{:S(2)}) async-start(f32[4,16,640]{2,1,0:T(8,128)} %broadcast_in_dim.32), calls=%async_computation.2 | async-start | bytes 327680 | tf_op jit(solution)/shard_map/all_to_all | solution.py:294
  132.1 0.5 slice.33
  133.4 2.6 %all-to-all-done.2 = f32[4,16,640]{2,1,0:T(8,128)S(1)} async-done(((f32[4,16,640]{2,1,0:T(8,128)}), f32[4,16,640]{2,1,0:T(8,128)S(1)}, u32[]{:S(2)}, u32[]{:S(2)}) %all-to-all-start.2) | async-done | bytes 163872 | tf_op jit(solution)/shard_map/all_to_all | solution.py:294
  136.0 0.6 slice.49
  136.6 0.7 slice_bitcast_fusion
  (15 shorter events, 0.1 us)
Async XLA Ops:
  0.6 1.8 %copy-start = (bf16[462,64]{0,1:T(8,128)(2,1)S(1)}, bf16[462,64]{0,1:T(8,128)(2,1)}, u32[]{:S(2)}) copy-start(bf16[462,64]{0,1:T(8,128)(2,1)} %param.11) | copy-start | bytes 177412
  33.1 18.2 %collective-permute-start.2 = (bf16[32,16,640]{2,1,0:T(8,128)(2,1)S(1)}, bf16[32,16,640]{2,1,0:T(8,128)(2,1)S(1)}, u32[]{:S(2)}, u32[]{:S(2)}) collective-permute-start(bf16[32,16,640]{2,1,0:T(8,128)(2,1)S(1)} %all_to_all.15.after_ref.refs_0_), channel_id=1, source_target_pairs={{0,12},{1,19},{4,0},{5,23},{8,4},{9,27},{12,8},{13,31},{2,14},{3,1... | collective-permute-start | bytes 1966088 | tf_op jit(solution)/shard_map/ppermute | solution.py:223
  36.7 17.8 %collective-permute-start.1 = (bf16[32,16,640]{2,1,0:T(8,128)(2,1)S(1)}, bf16[32,16,640]{2,1,0:T(8,128)(2,1)}, u32[]{:S(2)}, u32[]{:S(2)}) collective-permute-start(bf16[32,16,640]{2,1,0:T(8,128)(2,1)S(1)} %all_to_all.15.after_ref.refs_0_), channel_id=1, source_target_pairs={{0,8},{1,17},{4,12},{5,21},{8,0},{9,25},{12,4},{13,29},{2,10},{3,1... | collective-permute-start | bytes 1966088 | tf_op jit(solution)/shard_map/ppermute | solution.py:223
  36.7 18.1 %collective-permute-start = (bf16[32,16,640]{2,1,0:T(8,128)(2,1)S(1)}, bf16[32,16,640]{2,1,0:T(8,128)(2,1)}, u32[]{:S(2)}, u32[]{:S(2)}) collective-permute-start(bf16[32,16,640]{2,1,0:T(8,128)(2,1)S(1)} %all_to_all.15.after_ref.refs_0_), channel_id=1, source_target_pairs={{0,4},{1,3},{4,8},{5,7},{8,12},{9,11},{12,0},{13,15},{2,6},{3,17},... | collective-permute-start | bytes 1966088 | tf_op jit(solution)/shard_map/ppermute | solution.py:223
  37.4 23.2 %copy-start.5 = (s32[1,2]{1,0:T(1,128)S(1)}, s32[1,2]{1,0:T(1,128)}, u32[]{:S(2)}) copy-start(s32[1,2]{1,0:T(1,128)} %starts_ref.1) | copy-start | bytes 28
  41.8 3.0 %copy-start.1 = (bf16[128,29568]{1,0:T(8,128)(2,1)}, bf16[128,29568]{1,0:T(8,128)(2,1)S(1)}, u32[]{:S(2)}) copy-start(bf16[128,29568]{1,0:T(8,128)(2,1)S(1)} %get-tuple-element.17.refs_8_) | copy-start | bytes 22708228
  44.8 1.4 %copy-start.3 = (bf16[128,8192]{1,0:T(8,128)(2,1)}, bf16[128,8192]{1,0:T(8,128)(2,1)S(1)}, u32[]{:S(2)}) copy-start(bf16[128,8192]{1,0:T(8,128)(2,1)S(1)} %get-tuple-element.19.refs_10_) | copy-start | bytes 6291460
  46.2 12.5 %collective-permute-start.3 = (bf16[32,16,640]{2,1,0:T(8,128)(2,1)S(1)}, bf16[32,16,640]{2,1,0:T(8,128)(2,1)}, u32[]{:S(2)}, u32[]{:S(2)}) collective-permute-start(bf16[32,16,640]{2,1,0:T(8,128)(2,1)S(1)} %all_to_all.15.after_ref.refs_0_), channel_id=1, source_target_pairs={{0,1},{1,0},{2,3},{3,2},{4,5},{5,4},{6,7},{7,6},{8,9},{9,8},{10,11... | collective-permute-start | bytes 1966088 | tf_op jit(solution)/shard_map/ppermute | solution.py:233
  51.2 7.4 %collective-permute-start.6 = (bf16[32,16,640]{2,1,0:T(8,128)(2,1)S(1)}, bf16[32,16,640]{2,1,0:T(8,128)(2,1)}, u32[]{:S(2)}, u32[]{:S(2)}) collective-permute-start(bf16[32,16,640]{2,1,0:T(8,128)(2,1)S(1)} %collective-permute-done.2.refs_3_), channel_id=1, source_target_pairs={{0,1},{1,0},{2,3},{3,2},{4,5},{5,4},{6,7},{7,6},{8,9},{9,8},{10,11... | collective-permute-start | bytes 1966088 | tf_op jit(solution)/shard_map/ppermute | solution.py:233
  54.5 4.1 %collective-permute-start.5 = (bf16[32,16,640]{2,1,0:T(8,128)(2,1)}, bf16[32,16,640]{2,1,0:T(8,128)(2,1)}, u32[]{:S(2)}, u32[]{:S(2)}) collective-permute-start(bf16[32,16,640]{2,1,0:T(8,128)(2,1)} %collective-permute-done.1.refs_2_), channel_id=1, source_target_pairs={{0,1},{1,0},{2,3},{3,2},{4,5},{5,4},{6,7},{7,6},{8,9},{9,8},{10,11... | collective-permute-start | bytes 1966088 | tf_op jit(solution)/shard_map/ppermute | solution.py:233
  54.8 5.8 %collective-permute-start.4 = (bf16[32,16,640]{2,1,0:T(8,128)(2,1)}, bf16[32,16,640]{2,1,0:T(8,128)(2,1)}, u32[]{:S(2)}, u32[]{:S(2)}) collective-permute-start(bf16[32,16,640]{2,1,0:T(8,128)(2,1)} %collective-permute-done.refs_1_), channel_id=1, source_target_pairs={{0,1},{1,0},{2,3},{3,2},{4,5},{5,4},{6,7},{7,6},{8,9},{9,8},{10,11... | collective-permute-start | bytes 1966088 | tf_op jit(solution)/shard_map/ppermute | solution.py:233
  60.6 3.1 %copy-start.2 = (bf16[128,29568]{1,0:T(8,128)(2,1)S(1)}, bf16[128,29568]{1,0:T(8,128)(2,1)}, u32[]{:S(2)}) copy-start(bf16[128,29568]{1,0:T(8,128)(2,1)} %copy-done.1) | copy-start | bytes 22708228
  63.8 1.6 %copy-start.4 = (bf16[128,8192]{1,0:T(8,128)(2,1)S(1)}, bf16[128,8192]{1,0:T(8,128)(2,1)}, u32[]{:S(2)}) copy-start(bf16[128,8192]{1,0:T(8,128)(2,1)} %copy-done.3) | copy-start | bytes 6291460
  78.0 5.0 %collective-permute-start.7 = (bf16[128,16,640]{2,1,0:T(8,128)(2,1)S(1)}, bf16[128,16,640]{2,1,0:T(8,128)(2,1)S(1)}, u32[]{:S(2)}, u32[]{:S(2)}) collective-permute-start(bf16[128,16,640]{2,1,0:T(8,128)(2,1)S(1)} %get-tuple-element.22), channel_id=1, source_target_pairs={{0,1},{1,0},{2,3},{3,2},{4,5},{5,4},{6,7},{7,6},{8,9},{9,8},{10,11... | collective-permute-start | bytes 7864328 | tf_op jit(solution)/shard_map/ppermute | solution.py:233
  83.6 11.0 %collective-permute-start.8 = (bf16[32,16,640]{2,1,0:T(8,128)(2,1)S(1)}, bf16[32,16,640]{2,1,0:T(8,128)(2,1)S(1)}, u32[]{:S(2)}, u32[]{:S(2)}) collective-permute-start(bf16[32,16,640]{2,1,0:T(8,128)(2,1)S(1)} %get-tuple-element.23), channel_id=1, source_target_pairs={{0,4},{1,3},{4,8},{5,7},{8,12},{9,11},{12,0},{13,15},{2,6},{3,17},... | collective-permute-start | bytes 1966088 | tf_op jit(solution)/shard_map/ppermute | solution.py:223
  84.3 16.6 %collective-permute-start.10 = (bf16[32,16,640]{2,1,0:T(8,128)(2,1)S(1)}, bf16[32,16,640]{2,1,0:T(8,128)(2,1)S(1)}, u32[]{:S(2)}, u32[]{:S(2)}) collective-permute-start(bf16[32,16,640]{2,1,0:T(8,128)(2,1)S(1)} %get-tuple-element.24), channel_id=1, source_target_pairs={{0,12},{1,19},{4,0},{5,23},{8,4},{9,27},{12,8},{13,31},{2,14},{3,1... | collective-permute-start | bytes 1966088 | tf_op jit(solution)/shard_map/ppermute | solution.py:223
  86.3 15.9 %collective-permute-start.9 = (bf16[32,16,640]{2,1,0:T(8,128)(2,1)S(1)}, bf16[32,16,640]{2,1,0:T(8,128)(2,1)S(1)}, u32[]{:S(2)}, u32[]{:S(2)}) collective-permute-start(bf16[32,16,640]{2,1,0:T(8,128)(2,1)S(1)} %get-tuple-element.25), channel_id=1, source_target_pairs={{0,8},{1,17},{4,12},{5,21},{8,0},{9,25},{12,4},{13,29},{2,10},{3,1... | collective-permute-start | bytes 1966088 | tf_op jit(solution)/shard_map/ppermute | solution.py:223
  124.5 11.5 %all-to-all-start.2 = ((f32[4,16,640]{2,1,0:T(8,128)}), f32[4,16,640]{2,1,0:T(8,128)S(1)}, u32[]{:S(2)}, u32[]{:S(2)}) async-start(f32[4,16,640]{2,1,0:T(8,128)} %broadcast_in_dim.32), calls=%async_computation.2 | async-start | bytes 327680 | tf_op jit(solution)/shard_map/all_to_all | solution.py:294

commit v5 on v4

--- a/solution.py
+++ b/solution.py
@@ -32,13 +32,13 @@
     return lax.dot_general(a, b, dims, preferred_element_type=F32)
 
 
-def slots(place, sign):
+def slots(place, sign, planes):
     py, px, pc = place[1], place[2], place[3]
-    dxs = [((sign * (px - x)) & 3) * 32 for x in range(4)]
-    dys = [((sign * (py - y)) & 3) * 32 for y in range(4)]
+    dxs = [((sign * (px - x)) & 3) * (planes * 4) for x in range(4)]
+    dys = [((sign * (py - y)) & 3) * (planes * 4) for y in range(4)]
 
     def flat(chunk, other, yl):
-        z, yh, x = chunk // 8, chunk // 4 % 2, chunk % 4
+        z, yh, x = chunk // 8 % planes, chunk // 4 % 2, chunk % 4
         y = yh * 2 + yl
         first = pc == other
         return jnp.where(first, dxs[x] + (z * 4 + y), dys[y] + (z * 4 + x))
@@ -46,10 +46,24 @@
     return flat
 
 
+def down_gradient(chunks, grad_low, hid, held, outs, target):
+    origin = chunks[0] * DOWN // 128 * 128
+    stop = -(-(chunks[-1] + 1) * DOWN // 128) * 128
+    for begin in range(origin, stop, 1024):
+        end = min(begin + 1024, stop)
+        held[:, begin - origin : end - origin] = dot(grad_low, hid[:, begin:end], NN).astype(BF)
+    for chunk in chunks:
+        begin = chunk * DOWN - origin
+        for q in range(4):
+            outs[q // 2][target(chunk, q // 2, q % 2), :, UP : UP + DOWN] = held[
+                16 * q : 16 * q + 16, begin : begin + DOWN
+            ]
+
+
 def kernel(place_ref, starts_ref, *refs):
     parts, (hid, fro, hea) = refs[:8], refs[8:11]
-    outs, margin_ref = refs[11:13], refs[13]
-    wt, up, gains, gain, pol, block, sems = refs[14:]
+    outs, up_rest, low_ref, margin_ref = refs[11:13], refs[13], refs[14], refs[15]
+    wt, up, gains, gain, pol, block, sems = refs[16:]
     width = fro.shape[1]
 
     loads = [
@@ -78,7 +92,7 @@
     weight = jnp.where(row < 64, -BETA, BETA)
     slope = jnp.where(position >= start, weight, 0.0) / (1.0 + jnp.exp(margin))
 
-    source = slots(place_ref, 1)
+    source = slots(place_ref, 1, 8)
     for chunk in range(CHUNKS):
         for q in range(4):
             held = block[(q // 2) * 128 + source(chunk, q // 2, q % 2)]
@@ -130,7 +144,7 @@
     first = slope / rms
     second = inner / (width * rms * rms * rms)
 
-    target = slots(place_ref, -1)
+    target = slots(place_ref, -1, 4)
     total = jnp.zeros((128, ORDER), F32)
     for i in range(width // step):
         at = slice(i * step, (i + 1) * step)
@@ -139,6 +153,9 @@
         rest = (grad - high.astype(F32)).astype(BF)
         total += dot(high, up[:, at], NT) + dot(rest, up[:, at], NT)
         share = (SCALE * dot(low_t, high, NN)).astype(BF)
+        if i * step >= width // 2:
+            up_rest[:, i * step - width // 2 : (i + 1) * step - width // 2] = share
+            continue
         for j in range(step // 128):
             for q in range(4):
                 outs[q // 2][target(i * (step // 128) + j, q // 2, q % 2), :, :UP] = share[
@@ -146,18 +163,23 @@
                 ]
     grad_low = (SCALE * total).T.astype(BF)
 
-    tile = 1024
-    for begin in range(0, wt.shape[1], tile):
-        at = slice(begin, min(begin + tile, wt.shape[1]))
-        wt[:, at] = dot(grad_low, hid[:, at], NN).astype(BF)
-    for chunk in range(CHUNKS):
+    low_ref[...] = grad_low
+    down_gradient(range(CHUNKS // 2), grad_low, hid, wt, outs, target)
+
+
+def second_kernel(place_ref, low_ref, up_rest, hid, *refs):
+    outs, held = refs[:2], refs[2]
+    target = slots(place_ref, -1, 4)
+    chunks = range(CHUNKS // 2, CHUNKS)
+    for i, chunk in enumerate(chunks):
         for q in range(4):
-            outs[q // 2][target(chunk, q // 2, q % 2), :, UP : UP + DOWN] = wt[
-                16 * q : 16 * q + 16, chunk * DOWN : (chunk + 1) * DOWN
+            outs[q // 2][target(chunk, q // 2, q % 2), :, :UP] = up_rest[
+                16 * q : 16 * q + 16, UP * i : UP * i + UP
             ]
-
-
-def bring(after_ref, *refs):
+    down_gradient(chunks, low_ref[...], hid, held, outs, target)
+
+
+def bring(after_ref, place_ref, *refs):
     sems = refs[6]
     copies = [pltpu.make_async_copy(refs[i], refs[3 + i], sems.at[i]) for i in range(3)]
     for copy in copies:
@@ -166,18 +188,22 @@
         copy.wait()
 
 
-def brought(after, *arrays):
+def brought(after, place, *arrays):
     any_space = pl.BlockSpec(memory_space=pl.ANY)
     size = sum(v.size * 2 for v in arrays)
     return pl.pallas_call(
         bring,
         out_shape=[pltpu.VMEM(v.shape, v.dtype) for v in arrays],
-        in_specs=[any_space] * 4,
+        in_specs=[any_space, pl.BlockSpec(memory_space=pltpu.SMEM)] + [any_space] * 3,
         out_specs=[pl.BlockSpec(memory_space=pltpu.VMEM)] * 3,
         scratch_shapes=[pltpu.SemaphoreType.DMA((3,))],
         compiler_params=pltpu.CompilerParams(vmem_limit_bytes=1024 * 1024),
         cost_estimate=pl.CostEstimate(flops=0, bytes_accessed=2 * size, transcendentals=0),
-    )(after, *[pltpu.with_memory_space_constraint(v, pltpu.HBM) for v in arrays])
+    )(after, place, *[pltpu.with_memory_space_constraint(v, pltpu.HBM) for v in arrays])
+
+
+def near_vmem(*arrays):
+    return [pltpu.with_memory_space_constraint(v, pltpu.VMEM) for v in arrays]
 
 
 def shares(place, starts, parts, hidden, frozen, head):
@@ -186,12 +212,16 @@
     any_space = pl.BlockSpec(memory_space=pl.ANY)
     smem = pl.BlockSpec(memory_space=pltpu.SMEM)
     vmem = pl.BlockSpec(memory_space=pltpu.VMEM)
-    near = [pltpu.with_memory_space_constraint(v, pltpu.VMEM) for v in (hidden, frozen, head)]
-    outs = pl.pallas_call(
+    *outs, up_rest, grad_low, margin = pl.pallas_call(
         kernel,
-        out_shape=[pltpu.VMEM((128, 16, LANES), BF)] * 2 + [jax.ShapeDtypeStruct((8, 128), F32)],
+        out_shape=[pltpu.VMEM((64, 16, LANES), BF)] * 2
+        + [
+            pltpu.VMEM((ORDER, width // 2), BF),
+            pltpu.VMEM((ORDER, rows), BF),
+            jax.ShapeDtypeStruct((8, 128), F32),
+        ],
         in_specs=[smem, smem] + [any_space] * 8 + [vmem] * 3,
-        out_specs=[vmem] * 3,
+        out_specs=[vmem] * 5,
         scratch_shapes=[
             pltpu.VMEM((ORDER, units), BF),
             pltpu.VMEM((ORDER, width), BF),
@@ -201,14 +231,27 @@
             pltpu.VMEM((256, 16, LANES), BF),
             pltpu.SemaphoreType.DMA((8,)),
         ],
-        compiler_params=pltpu.CompilerParams(vmem_limit_bytes=24 * 1024 * 1024),
+        compiler_params=pltpu.CompilerParams(vmem_limit_bytes=20 * 1024 * 1024),
         cost_estimate=pl.CostEstimate(
             flops=2 * rows * ORDER * (2 * units + 4 * width),
             bytes_accessed=2 * rows * (units + 2 * width) + 4 * 256 * 16 * LANES,
             transcendentals=0,
         ),
-    )(place, starts, *parts, *near)
-    return outs[0], outs[1], outs[2][0, 0:1]
+    )(place, starts, *parts, *near_vmem(hidden, frozen, head))
+    rest = pl.pallas_call(
+        second_kernel,
+        out_shape=[pltpu.VMEM((64, 16, LANES), BF)] * 2,
+        in_specs=[smem] + [vmem] * 3,
+        out_specs=[vmem] * 2,
+        scratch_shapes=[pltpu.VMEM((ORDER, (units // 256 + 1) * 128), BF)],
+        compiler_params=pltpu.CompilerParams(vmem_limit_bytes=4 * 1024 * 1024),
+        cost_estimate=pl.CostEstimate(
+            flops=rows * ORDER * units,
+            bytes_accessed=rows * units + 2 * 128 * 16 * LANES,
+            transcendentals=0,
+        ),
+    )(place, *near_vmem(grad_low, up_rest, hidden))
+    return outs, rest, margin[0, 0:1]
 
 
 def device(z, y, x, c):
@@ -273,6 +316,7 @@
     width = frozen.shape[3]
     near = brought(
         held,
+        place,
         gated_hidden_input.reshape(-1, gated_hidden_input.shape[3]),
         frozen.reshape(-1, width),
         head_gradient_rows.reshape(-1, width),
@@ -280,15 +324,18 @@
     held, *near = lax.optimization_barrier((held, *near))
     other = [other_core(v) for v in (held, *own[1:])]
 
-    own, other, margin = shares(place, starts, [*own, *other], *near)
-
-    came = other_core(other)
-    chip = [
-        total_of(own[32 * i : 32 * i + 32], came[32 * i : 32 * i + 32]).astype(BF)
-        for i in range(4)
-    ]
-    came = [ring(chip[step], step) for step in (1, 2, 3)]
-    line = total_of(chip[0], *came).astype(BF)
+    first, second, margin = shares(place, starts, [*own, *other], *near)
+
+    lines = []
+    for own, other in (first, second):
+        came = other_core(other)
+        chip = [
+            total_of(own[16 * i : 16 * i + 16], came[16 * i : 16 * i + 16]).astype(BF)
+            for i in range(4)
+        ]
+        came = [ring(chip[step], step) for step in (1, 2, 3)]
+        lines.append(total_of(chip[0], *came).astype(BF))
+    line = jnp.concatenate(lines)
     share = jnp.sum(crosswise(line).astype(F32), axis=0)
     copies = jnp.broadcast_to(share[None], (4, 16, LANES))
     whole = lax.all_to_all(copies, CTX, 0, 0, tiled=True)

time: 139 us -> 131 us (0.942)
  local copies, waits for them, and re-layouts: 13.4 us -> 4.24 us
  waiting for transfers between devices: 25.3 us -> 17 us
  starting transfers between devices: 27.3 us -> 33.4 us
  blocking collectives: 50.7 us -> 52.4 us
    unnamed x12 -> x4, local copies, waits for them, and re-layouts: 9.13 us -> 0.01 us
    ppermute x6 -> x9, starting transfers between devices: 8.14 us -> 15.7 us  [ring(): return lax.ppermute(values, FINE_AXES, pairs)]
    ppermute x6 -> x9, waiting for transfers between devices: 16.2 us -> 11.8 us  [ring(): return lax.ppermute(values, FINE_AXES, pairs)]
    ppermute x5 -> x6, waiting for transfers between devices: 6.52 us -> 2.61 us  [other_core(): return lax.ppermute(values, 'c', [(0, 1), (1, 0)])]
    all_to_all x2, blocking collectives: 50.7 us -> 52.4 us  [crosswise(): lax.all_to_all(values, FINE_AXES, 0, 0, axis_index_groups=groups, tiled=T...]
    all_to_all x1, starting transfers between devices: 7.66 us -> 5.97 us  [local(): whole = lax.all_to_all(copies, CTX, 0, 0, tiled=True)]
    pallas_call x1 -> x2, Pallas kernels: 12.7 us -> 13.5 us  [the longest x1 11.9 us: shares(): pl.pallas_call(kernel, out_shape=[pltpu.VMEM((64, 16, LANES), BF)] * 2 +...]
    ppermute x5 -> x6, starting transfers between devices: 11.5 us -> 11.8 us  [other_core(): return lax.ppermute(values, 'c', [(0, 1), (1, 0)])]
  transfers between devices with their start and end apart: 12 -> 16, of which waited for: 8 -> 9; matrix products, arithmetic and copies ran while one was open for 0% -> 1% of each run, Pallas kernels for 3% -> 5%
where the time goes in v5:
time: 131 us; the launch traced here: 130 us
  blocking collectives  52.4 us (40%)
  starting transfers between devices  33.4 us (25%)
  Pallas kernels  18.4 us (14%)
  waiting for transfers between devices  17 us (13%)
  local copies, waits for them, and re-layouts  4.24 us (3%)
  between operations  2.62 us (2%)
  other arithmetic  2.21 us (2%)
    all_to_all x2, blocking collectives, crosswise(): lax.all_to_all(values, FINE_AXES, 0, 0, axis_index_groups=groups, tiled=T...  52.4 us
    ppermute x9, starting transfers between devices, ring(): return lax.ppermute(values, FINE_AXES, pairs)  15.7 us
    pallas_call x1, Pallas kernels, shares(): pl.pallas_call(kernel, out_shape=[pltpu.VMEM((64, 16, LANES), BF)] * 2 +...  11.9 us
    ppermute x9, waiting for transfers between devices, ring(): return lax.ppermute(values, FINE_AXES, pairs)  11.8 us
    ppermute x6, starting transfers between devices, other_core(): return lax.ppermute(values, 'c', [(0, 1), (1, 0)])  11.8 us
    all_to_all x1, starting transfers between devices, local(): whole = lax.all_to_all(copies, CTX, 0, 0, tiled=True)  5.97 us
    pallas_call x1, Pallas kernels, brought(): pl.pallas_call(bring, out_shape=[pltpu.VMEM(v.shape, v.dtype) for v in ar...  4.91 us
  transfers between devices with their start and end apart: 16, of which 9 were waited for; matrix products, arithmetic and copies ran while one was open for 1% of the time, Pallas kernels for 5%

profile of v5, /device:TPU:1, one launch (start us, length us, event | category | flops | bytes accessed | tf_op | source)
XLA Modules:
  0.0 130.3 jit_solution(17375023607160894987)
XLA Ops:
  0.6 0.0 copy-start
  0.7 0.9 fusion
  1.6 0.1 copy.13
  1.7 0.1 convert_element_type.117
  1.8 0.7 constant_dynamic-slice_fusion
  2.5 0.7 dynamic-slice_bitcast_fusion.1
  3.2 0.1 fusion.2
  3.3 0.1 pad.4.clone
  3.4 0.1 broadcast_in_dim.31
  3.4 29.6 %all_to_all.15.after_ref.refs_0_ = bf16[32,16,640]{2,1,0:T(8,128)(2,1)S(1)} all-to-all(bf16[32,16,640]{2,1,0:T(8,128)(2,1)S(1)} %broadcast_in_dim.31), channel_id=1, replica_groups={{0,2,16,18,32,34,48,50,64,66,80,82,96,98,112,114,128,130,144,146,160,16..., dimensions={0} | all-to-all | bytes 1310720 | tf_op jit(solution)/shard_map/all_to_all | solution.py:272
  33.1 3.6 %collective-permute-start.2 = (bf16[32,16,640]{2,1,0:T(8,128)(2,1)S(1)}, bf16[32,16,640]{2,1,0:T(8,128)(2,1)S(1)}, u32[]{:S(2)}, u32[]{:S(2)}) collective-permute-start(bf16[32,16,640]{2,1,0:T(8,128)(2,1)S(1)} %all_to_all.15.after_ref.refs_0_), channel_id=1, source_target_pairs={{0,12},{1,19},{4,0},{5,23},{8,4},{9,27},{12,8},{13,31},{2,14},{3,1... | collective-permute-start | bytes 1966088 | tf_op jit(solution)/shard_map/ppermute | solution.py:266
  36.7 0.7 collective-permute-start
  37.4 0.1 pad_add_fusion.place_ref
  37.5 4.9 %shard_map.106 = (bf16[128,29568]{1,0:T(8,128)(2,1)S(1)}, bf16[128,8192]{1,0:T(8,128)(2,1)S(1)}, bf16[128,8192]{1,0:T(8,128)(2,1)S(1)}) custom-call(bf16[32,16,640]{2,1,0:T(8,128)(2,1)S(1)} %all_to_all.15.after_ref.refs_0_, s32[4]{0:T(128)S(1)} %pad_add_fusion.place_ref, bf16[128,29568]{1,0:T(8,128)(2,1)} %bitcast.33, bf16[128,8192]{1,0:T(8,128)(2,1)} %bitcast.34, ...), custom_call_target="tpu_custom_call" | custom-call | bytes 23527424 | tf_op jit(solution)/shard_map/pallas_call | solution.py:194
  42.4 4.1 %collective-permute-start.3 = (bf16[32,16,640]{2,1,0:T(8,128)(2,1)S(1)}, bf16[32,16,640]{2,1,0:T(8,128)(2,1)S(1)}, u32[]{:S(2)}, u32[]{:S(2)}) collective-permute-start(bf16[32,16,640]{2,1,0:T(8,128)(2,1)S(1)} %all_to_all.15.after_ref.refs_0_), channel_id=1, source_target_pairs={{0,1},{1,0},{2,3},{3,2},{4,5},{5,4},{6,7},{7,6},{8,9},{9,8},{10,11... | collective-permute-start | bytes 1966088 | tf_op jit(solution)/shard_map/ppermute | solution.py:276
  46.5 4.8 %collective-permute-done.2.refs_3_ = bf16[32,16,640]{2,1,0:T(8,128)(2,1)S(1)} collective-permute-done((bf16[32,16,640]{2,1,0:T(8,128)(2,1)S(1)}, bf16[32,16,640]{2,1,0:T(8,128)(2,1)S(1)}, u32[]{:S(2)}, u32[]{:S(2)}) %collective-permute-start.2) | collective-permute-done | bytes 655392 | tf_op jit(solution)/shard_map/ppermute | solution.py:266
  51.2 3.2 %collective-permute-start.6 = (bf16[32,16,640]{2,1,0:T(8,128)(2,1)S(1)}, bf16[32,16,640]{2,1,0:T(8,128)(2,1)S(1)}, u32[]{:S(2)}, u32[]{:S(2)}) collective-permute-start(bf16[32,16,640]{2,1,0:T(8,128)(2,1)S(1)} %collective-permute-done.2.refs_3_), channel_id=1, source_target_pairs={{0,1},{1,0},{2,3},{3,2},{4,5},{5,4},{6,7},{7,6},{8,9},{9,8},{10,11... | collective-permute-start | bytes 1966088 | tf_op jit(solution)/shard_map/ppermute | solution.py:276
  54.5 0.2 collective-permute-done.refs_1_
  54.7 3.8 %collective-permute-start.4 = (bf16[32,16,640]{2,1,0:T(8,128)(2,1)S(1)}, bf16[32,16,640]{2,1,0:T(8,128)(2,1)S(1)}, u32[]{:S(2)}, u32[]{:S(2)}) collective-permute-start(bf16[32,16,640]{2,1,0:T(8,128)(2,1)S(1)} %collective-permute-done.refs_1_), channel_id=1, source_target_pairs={{0,1},{1,0},{2,3},{3,2},{4,5},{5,4},{6,7},{7,6},{8,9},{9,8},{10,11... | collective-permute-start | bytes 1966088 | tf_op jit(solution)/shard_map/ppermute | solution.py:276
  58.4 1.7 %collective-permute-done.4.refs_5_ = bf16[32,16,640]{2,1,0:T(8,128)(2,1)S(1)} collective-permute-done((bf16[32,16,640]{2,1,0:T(8,128)(2,1)S(1)}, bf16[32,16,640]{2,1,0:T(8,128)(2,1)S(1)}, u32[]{:S(2)}, u32[]{:S(2)}) %collective-permute-start.4) | collective-permute-done | bytes 655392 | tf_op jit(solution)/shard_map/ppermute | solution.py:276
  60.2 11.9 %shard_map.107 = (bf16[64,16,640]{2,1,0:T(8,128)(2,1)S(1)}, bf16[64,16,640]{2,1,0:T(8,128)(2,1)S(1)}, bf16[64,4096]{1,0:T(8,128)(2,1)S(1)}, bf16[64,128]{1,0:T(8,128)(2,1)S(1)}, f32[8,128]{1,0:T(8,128)S(1)}) custom-call(s32[4]{0:T(128)S(1)} %pad_add_fusion.place_ref, s32[1,2]{1,0:T(1,128)S(1)} %copy-done.1, ...), custom_call_target="tpu_custom_call" | custom-call | flops 1505755136 | bytes 22249472 | tf_op jit(solution)/shard_map/pallas_call | solution.py:215
  72.1 0.5 collective-permute-start.7
  72.6 1.6 %shard_map.108 = (bf16[64,16,640]{2,1,0:T(8,128)(2,1)S(1)}, bf16[64,16,640]{2,1,0:T(8,128)(2,1)S(1)}) custom-call(s32[4]{0:T(128)S(1)} %pad_add_fusion.place_ref, bf16[64,128]{1,0:T(8,128)(2,1)S(1)} %get-tuple-element.27.low_ref, bf16[64,4096]{1,0:T(8,128)(2,1)S(1)} %get-tuple-element.28.up_rest, bf16[128,29568]{1,0:T(8,128)(2,1)S(1)} %get-tuple-element.21.refs_8_.hid), custom_call_target="tpu_custom_call" | custom-call | flops 242221056 | bytes 6406144 | tf_op jit(solution)/shard_map/pallas_call | solution.py:241
  74.1 0.2 collective-permute-start.11
  74.3 0.9 collective-permute-done.7
  75.2 0.3 add_convert_fusion.8
  75.5 0.7 collective-permute-start.8
  76.2 2.0 %collective-permute-start.10 = (bf16[16,16,640]{2,1,0:T(8,128)(2,1)S(1)}, bf16[16,16,640]{2,1,0:T(8,128)(2,1)S(1)}, u32[]{:S(2)}, u32[]{:S(2)}) collective-permute-start(bf16[16,16,640]{2,1,0:T(8,128)(2,1)S(1)} %get-tuple-element.32), channel_id=1, source_target_pairs={{0,12},{1,19},{4,0},{5,23},{8,4},{9,27},{12,8},{13,31},{2,14},{3,1... | collective-permute-start | bytes 983048 | tf_op jit(solution)/shard_map/ppermute | solution.py:266
  78.2 1.1 collective-permute-start.9
  79.3 0.2 add_convert_fusion.3
  79.6 0.7 collective-permute-start.12
  80.3 2.3 %collective-permute-start.14 = (bf16[16,16,640]{2,1,0:T(8,128)(2,1)S(1)}, bf16[16,16,640]{2,1,0:T(8,128)(2,1)S(1)}, u32[]{:S(2)}, u32[]{:S(2)}) collective-permute-start(bf16[16,16,640]{2,1,0:T(8,128)(2,1)S(1)} %get-tuple-element.35), channel_id=1, source_target_pairs={{0,12},{1,19},{4,0},{5,23},{8,4},{9,27},{12,8},{13,31},{2,14},{3,1... | collective-permute-start | bytes 983048 | tf_op jit(solution)/shard_map/ppermute | solution.py:266
  82.5 0.5 collective-permute-done.8
  83.0 4.6 %collective-permute-start.13 = (bf16[16,16,640]{2,1,0:T(8,128)(2,1)S(1)}, bf16[16,16,640]{2,1,0:T(8,128)(2,1)S(1)}, u32[]{:S(2)}, u32[]{:S(2)}) collective-permute-start(bf16[16,16,640]{2,1,0:T(8,128)(2,1)S(1)} %get-tuple-element.36), channel_id=1, source_target_pairs={{0,8},{1,17},{4,12},{5,21},{8,0},{9,25},{12,4},{13,29},{2,10},{3,1... | collective-permute-start | bytes 983048 | tf_op jit(solution)/shard_map/ppermute | solution.py:266
  87.6 0.2 add_convert_fusion.5
  87.8 2.8 %collective-permute-done.12 = bf16[16,16,640]{2,1,0:T(8,128)(2,1)S(1)} collective-permute-done((bf16[16,16,640]{2,1,0:T(8,128)(2,1)S(1)}, bf16[16,16,640]{2,1,0:T(8,128)(2,1)S(1)}, u32[]{:S(2)}, u32[]{:S(2)}) %collective-permute-start.12) | collective-permute-done | bytes 327712 | tf_op jit(solution)/shard_map/ppermute | solution.py:266
  90.6 2.2 %collective-permute-done.14 = bf16[16,16,640]{2,1,0:T(8,128)(2,1)S(1)} collective-permute-done((bf16[16,16,640]{2,1,0:T(8,128)(2,1)S(1)}, bf16[16,16,640]{2,1,0:T(8,128)(2,1)S(1)}, u32[]{:S(2)}, u32[]{:S(2)}) %collective-permute-start.14) | collective-permute-done | bytes 327712 | tf_op jit(solution)/shard_map/ppermute | solution.py:266
  92.8 1.4 %collective-permute-done.13 = bf16[16,16,640]{2,1,0:T(8,128)(2,1)S(1)} collective-permute-done((bf16[16,16,640]{2,1,0:T(8,128)(2,1)S(1)}, bf16[16,16,640]{2,1,0:T(8,128)(2,1)S(1)}, u32[]{:S(2)}, u32[]{:S(2)}) %collective-permute-start.13) | collective-permute-done | bytes 327712 | tf_op jit(solution)/shard_map/ppermute | solution.py:266
  94.2 0.2 add_convert_fusion
  94.4 0.1 pad_maximum_fusion
  94.5 22.8 %all_to_all.16 = bf16[32,16,640]{2,1,0:T(8,128)(2,1)S(1)} all-to-all(bf16[32,16,640]{2,1,0:T(8,128)(2,1)S(1)} %pad_maximum_fusion), channel_id=1, replica_groups={{0,2,16,18,32,34,48,50,64,66,80,82,96,98,112,114,128,130,144,146,160,16..., dimensions={0} | all-to-all | bytes 1310720 | tf_op jit(solution)/shard_map/all_to_all | solution.py:272
  117.2 0.1 convert_reduce_fusion
  117.4 0.7 broadcast_in_dim.32
  118.0 6.0 %all-to-all-start.2 = ((f32[4,16,640]{2,1,0:T(8,128)}), f32[4,16,640]{2,1,0:T(8,128)S(1)}, u32[]{:S(2)}, u32[]{:S(2)}) async-start(f32[4,16,640]{2,1,0:T(8,128)} %broadcast_in_dim.32), calls=%async_computation.2 | async-start | bytes 327680 | tf_op jit(solution)/shard_map/all_to_all | solution.py:341
  124.0 0.5 slice.57
  125.2 2.6 %all-to-all-done.2 = f32[4,16,640]{2,1,0:T(8,128)S(1)} async-done(((f32[4,16,640]{2,1,0:T(8,128)}), f32[4,16,640]{2,1,0:T(8,128)S(1)}, u32[]{:S(2)}, u32[]{:S(2)}) %all-to-all-start.2) | async-done | bytes 163872 | tf_op jit(solution)/shard_map/all_to_all | solution.py:341
  127.9 0.6 slice.85
  128.5 0.7 slice_bitcast_fusion
  (19 shorter events, 0.1 us)
Async XLA Ops:
  0.6 1.8 %copy-start = (bf16[462,64]{0,1:T(8,128)(2,1)S(1)}, bf16[462,64]{0,1:T(8,128)(2,1)}, u32[]{:S(2)}) copy-start(bf16[462,64]{0,1:T(8,128)(2,1)} %param.11) | copy-start | bytes 177412
  33.1 18.2 %collective-permute-start.2 = (bf16[32,16,640]{2,1,0:T(8,128)(2,1)S(1)}, bf16[32,16,640]{2,1,0:T(8,128)(2,1)S(1)}, u32[]{:S(2)}, u32[]{:S(2)}) collective-permute-start(bf16[32,16,640]{2,1,0:T(8,128)(2,1)S(1)} %all_to_all.15.after_ref.refs_0_), channel_id=1, source_target_pairs={{0,12},{1,19},{4,0},{5,23},{8,4},{9,27},{12,8},{13,31},{2,14},{3,1... | collective-permute-start | bytes 1966088 | tf_op jit(solution)/shard_map/ppermute | solution.py:266
  36.7 17.8 %collective-permute-start.1 = (bf16[32,16,640]{2,1,0:T(8,128)(2,1)S(1)}, bf16[32,16,640]{2,1,0:T(8,128)(2,1)S(1)}, u32[]{:S(2)}, u32[]{:S(2)}) collective-permute-start(bf16[32,16,640]{2,1,0:T(8,128)(2,1)S(1)} %all_to_all.15.after_ref.refs_0_), channel_id=1, source_target_pairs={{0,8},{1,17},{4,12},{5,21},{8,0},{9,25},{12,4},{13,29},{2,10},{3,1... | collective-permute-start | bytes 1966088 | tf_op jit(solution)/shard_map/ppermute | solution.py:266
  36.7 18.0 %collective-permute-start = (bf16[32,16,640]{2,1,0:T(8,128)(2,1)S(1)}, bf16[32,16,640]{2,1,0:T(8,128)(2,1)S(1)}, u32[]{:S(2)}, u32[]{:S(2)}) collective-permute-start(bf16[32,16,640]{2,1,0:T(8,128)(2,1)S(1)} %all_to_all.15.after_ref.refs_0_), channel_id=1, source_target_pairs={{0,4},{1,3},{4,8},{5,7},{8,12},{9,11},{12,0},{13,15},{2,6},{3,17},... | collective-permute-start | bytes 1966088 | tf_op jit(solution)/shard_map/ppermute | solution.py:266
  37.5 22.7 %copy-start.1 = (s32[1,2]{1,0:T(1,128)S(1)}, s32[1,2]{1,0:T(1,128)}, u32[]{:S(2)}) copy-start(s32[1,2]{1,0:T(1,128)} %starts_ref.1) | copy-start | bytes 28
  42.4 16.1 %collective-permute-start.3 = (bf16[32,16,640]{2,1,0:T(8,128)(2,1)S(1)}, bf16[32,16,640]{2,1,0:T(8,128)(2,1)S(1)}, u32[]{:S(2)}, u32[]{:S(2)}) collective-permute-start(bf16[32,16,640]{2,1,0:T(8,128)(2,1)S(1)} %all_to_all.15.after_ref.refs_0_), channel_id=1, source_target_pairs={{0,1},{1,0},{2,3},{3,2},{4,5},{5,4},{6,7},{7,6},{8,9},{9,8},{10,11... | collective-permute-start | bytes 1966088 | tf_op jit(solution)/shard_map/ppermute | solution.py:276
  51.2 7.2 %collective-permute-start.6 = (bf16[32,16,640]{2,1,0:T(8,128)(2,1)S(1)}, bf16[32,16,640]{2,1,0:T(8,128)(2,1)S(1)}, u32[]{:S(2)}, u32[]{:S(2)}) collective-permute-start(bf16[32,16,640]{2,1,0:T(8,128)(2,1)S(1)} %collective-permute-done.2.refs_3_), channel_id=1, source_target_pairs={{0,1},{1,0},{2,3},{3,2},{4,5},{5,4},{6,7},{7,6},{8,9},{9,8},{10,11... | collective-permute-start | bytes 1966088 | tf_op jit(solution)/shard_map/ppermute | solution.py:276
  54.5 4.0 %collective-permute-start.5 = (bf16[32,16,640]{2,1,0:T(8,128)(2,1)S(1)}, bf16[32,16,640]{2,1,0:T(8,128)(2,1)S(1)}, u32[]{:S(2)}, u32[]{:S(2)}) collective-permute-start(bf16[32,16,640]{2,1,0:T(8,128)(2,1)S(1)} %collective-permute-done.1.refs_2_), channel_id=1, source_target_pairs={{0,1},{1,0},{2,3},{3,2},{4,5},{5,4},{6,7},{7,6},{8,9},{9,8},{10,11... | collective-permute-start | bytes 1966088 | tf_op jit(solution)/shard_map/ppermute | solution.py:276
  54.7 5.5 %collective-permute-start.4 = (bf16[32,16,640]{2,1,0:T(8,128)(2,1)S(1)}, bf16[32,16,640]{2,1,0:T(8,128)(2,1)S(1)}, u32[]{:S(2)}, u32[]{:S(2)}) collective-permute-start(bf16[32,16,640]{2,1,0:T(8,128)(2,1)S(1)} %collective-permute-done.refs_1_), channel_id=1, source_target_pairs={{0,1},{1,0},{2,3},{3,2},{4,5},{5,4},{6,7},{7,6},{8,9},{9,8},{10,11... | collective-permute-start | bytes 1966088 | tf_op jit(solution)/shard_map/ppermute | solution.py:276
  72.1 3.1 %collective-permute-start.7 = (bf16[64,16,640]{2,1,0:T(8,128)(2,1)S(1)}, bf16[64,16,640]{2,1,0:T(8,128)(2,1)S(1)}, u32[]{:S(2)}, u32[]{:S(2)}) collective-permute-start(bf16[64,16,640]{2,1,0:T(8,128)(2,1)S(1)} %get-tuple-element.26), channel_id=1, source_target_pairs={{0,1},{1,0},{2,3},{3,2},{4,5},{5,4},{6,7},{7,6},{8,9},{9,8},{10,11... | collective-permute-start | bytes 3932168 | tf_op jit(solution)/shard_map/ppermute | solution.py:276
  74.1 5.2 %collective-permute-start.11 = (bf16[64,16,640]{2,1,0:T(8,128)(2,1)S(1)}, bf16[64,16,640]{2,1,0:T(8,128)(2,1)S(1)}, u32[]{:S(2)}, u32[]{:S(2)}) collective-permute-start(bf16[64,16,640]{2,1,0:T(8,128)(2,1)S(1)} %get-tuple-element.30), channel_id=1, source_target_pairs={{0,1},{1,0},{2,3},{3,2},{4,5},{5,4},{6,7},{7,6},{8,9},{9,8},{10,11... | collective-permute-start | bytes 3932168 | tf_op jit(solution)/shard_map/ppermute | solution.py:276
  75.5 7.5 %collective-permute-start.8 = (bf16[16,16,640]{2,1,0:T(8,128)(2,1)S(1)}, bf16[16,16,640]{2,1,0:T(8,128)(2,1)S(1)}, u32[]{:S(2)}, u32[]{:S(2)}) collective-permute-start(bf16[16,16,640]{2,1,0:T(8,128)(2,1)S(1)} %get-tuple-element.31), channel_id=1, source_target_pairs={{0,4},{1,3},{4,8},{5,7},{8,12},{9,11},{12,0},{13,15},{2,6},{3,17},... | collective-permute-start | bytes 983048 | tf_op jit(solution)/shard_map/ppermute | solution.py:266
  76.2 11.4 %collective-permute-start.10 = (bf16[16,16,640]{2,1,0:T(8,128)(2,1)S(1)}, bf16[16,16,640]{2,1,0:T(8,128)(2,1)S(1)}, u32[]{:S(2)}, u32[]{:S(2)}) collective-permute-start(bf16[16,16,640]{2,1,0:T(8,128)(2,1)S(1)} %get-tuple-element.32), channel_id=1, source_target_pairs={{0,12},{1,19},{4,0},{5,23},{8,4},{9,27},{12,8},{13,31},{2,14},{3,1... | collective-permute-start | bytes 983048 | tf_op jit(solution)/shard_map/ppermute | solution.py:266
  78.2 9.3 %collective-permute-start.9 = (bf16[16,16,640]{2,1,0:T(8,128)(2,1)S(1)}, bf16[16,16,640]{2,1,0:T(8,128)(2,1)S(1)}, u32[]{:S(2)}, u32[]{:S(2)}) collective-permute-start(bf16[16,16,640]{2,1,0:T(8,128)(2,1)S(1)} %get-tuple-element.33), channel_id=1, source_target_pairs={{0,8},{1,17},{4,12},{5,21},{8,0},{9,25},{12,4},{13,29},{2,10},{3,1... | collective-permute-start | bytes 983048 | tf_op jit(solution)/shard_map/ppermute | solution.py:266
  79.6 11.1 %collective-permute-start.12 = (bf16[16,16,640]{2,1,0:T(8,128)(2,1)S(1)}, bf16[16,16,640]{2,1,0:T(8,128)(2,1)S(1)}, u32[]{:S(2)}, u32[]{:S(2)}) collective-permute-start(bf16[16,16,640]{2,1,0:T(8,128)(2,1)S(1)} %get-tuple-element.34), channel_id=1, source_target_pairs={{0,4},{1,3},{4,8},{5,7},{8,12},{9,11},{12,0},{13,15},{2,6},{3,17},... | collective-permute-start | bytes 983048 | tf_op jit(solution)/shard_map/ppermute | solution.py:266
  80.3 12.5 %collective-permute-start.14 = (bf16[16,16,640]{2,1,0:T(8,128)(2,1)S(1)}, bf16[16,16,640]{2,1,0:T(8,128)(2,1)S(1)}, u32[]{:S(2)}, u32[]{:S(2)}) collective-permute-start(bf16[16,16,640]{2,1,0:T(8,128)(2,1)S(1)} %get-tuple-element.35), channel_id=1, source_target_pairs={{0,12},{1,19},{4,0},{5,23},{8,4},{9,27},{12,8},{13,31},{2,14},{3,1... | collective-permute-start | bytes 983048 | tf_op jit(solution)/shard_map/ppermute | solution.py:266
  83.0 11.2 %collective-permute-start.13 = (bf16[16,16,640]{2,1,0:T(8,128)(2,1)S(1)}, bf16[16,16,640]{2,1,0:T(8,128)(2,1)S(1)}, u32[]{:S(2)}, u32[]{:S(2)}) collective-permute-start(bf16[16,16,640]{2,1,0:T(8,128)(2,1)S(1)} %get-tuple-element.36), channel_id=1, source_target_pairs={{0,8},{1,17},{4,12},{5,21},{8,0},{9,25},{12,4},{13,29},{2,10},{3,1... | collective-permute-start | bytes 983048 | tf_op jit(solution)/shard_map/ppermute | solution.py:266
  118.0 9.8 %all-to-all-start.2 = ((f32[4,16,640]{2,1,0:T(8,128)}), f32[4,16,640]{2,1,0:T(8,128)S(1)}, u32[]{:S(2)}, u32[]{:S(2)}) async-start(f32[4,16,640]{2,1,0:T(8,128)} %broadcast_in_dim.32), calls=%async_computation.2 | async-start | bytes 327680 | tf_op jit(solution)/shard_map/all_to_all | solution.py:341

commit v6 on v5

--- a/solution.py
+++ b/solution.py
@@ -34,14 +34,13 @@
 
 def slots(place, sign, planes):
     py, px, pc = place[1], place[2], place[3]
-    dxs = [((sign * (px - x)) & 3) * (planes * 4) for x in range(4)]
-    dys = [((sign * (py - y)) & 3) * (planes * 4) for y in range(4)]
+    dxs = [((sign * (px - x)) & 3) * planes for x in range(4)]
+    dys = [((sign * (py - y)) & 3) * planes for y in range(4)]
 
     def flat(chunk, other, yl):
         z, yh, x = chunk // 8 % planes, chunk // 4 % 2, chunk % 4
-        y = yh * 2 + yl
-        first = pc == other
-        return jnp.where(first, dxs[x] + (z * 4 + y), dys[y] + (z * 4 + x))
+        dx, dy = dxs[x], dys[yh * 2 + yl]
+        return jnp.where(pc == other, dx * 4 + dy, dy * 4 + dx) + z
 
     return flat
 
@@ -61,13 +60,18 @@
 
 
 def kernel(place_ref, starts_ref, *refs):
-    parts, (hid, fro, hea) = refs[:8], refs[8:11]
-    outs, up_rest, low_ref, margin_ref = refs[11:13], refs[13], refs[14], refs[15]
-    wt, up, gains, gain, pol, block, sems = refs[16:]
+    parts, (hid, fro, hea) = refs[:16], refs[16:19]
+    outs, up_rest, low_ref, margin_ref = refs[19:21], refs[21], refs[22], refs[23]
+    wt, up, gains, gain, pol, block, sems = refs[24:]
     width = fro.shape[1]
 
     loads = [
-        pltpu.make_async_copy(parts[i], block.at[pl.ds(32 * i, 32)], sems.at[i]) for i in range(8)
+        pltpu.make_async_copy(
+            parts[i],
+            block.at[pl.ds(32 * (i // 2) + 8 * (i % 2), 8 + 16 * (i % 2))],
+            sems.at[i],
+        )
+        for i in range(16)
     ]
     for copy in loads:
         copy.start()
@@ -79,7 +83,8 @@
     for other in range(2):
         for yl in range(2):
             y = (py & 2) + yl
-            inside = jnp.where(pc == other, pz * 4 + y, pz * 4 + px + ((py - y) & 3) * 32)
+            dy = (py - y) & 3
+            inside = jnp.where(pc == other, dy * 8, dy * 32) + pz
             held = block[other * 128 + inside]
             sums += held[0:1, LANES - 128 :].astype(F32)
     lane = SUMS_AT - (LANES - 128)
@@ -179,6 +184,68 @@
     down_gradient(chunks, low_ref[...], hid, held, outs, target)
 
 
+def pack(place_ref, starts_ref, ratio_ref, down_ref, up_ref, gain_ref, out_ref):
+    yl, core = place_ref[1] & 1, place_ref[3]
+    begin = pl.multiple_of(core * 32 + yl * 16, 16)
+    position = lax.broadcasted_iota(jnp.int32, (2, 64), 1) + (yl * 2 + core) * 64
+    side = lax.broadcasted_iota(jnp.int32, (2, 64), 0)
+    start = jnp.where(side == 0, starts_ref[0, 0], starts_ref[0, 1])
+    total = jnp.sum(jnp.where(position >= start, ratio_ref[...], 0.0), axis=1, keepdims=True)
+    high = total.astype(BF).astype(F32)
+    middle = (total - high).astype(BF).astype(F32)
+    low = total - high - middle
+
+    lane = lax.broadcasted_iota(jnp.int32, (8, 128), 1)
+    at = GAIN_AT - (LANES - 128)
+    gain = jnp.broadcast_to(gain_ref[...].astype(F32), (8, 128))
+    gain = pltpu.roll(gain, (at + 128 - (core * 2 + yl) * 32) & 127, 1)
+    tail = jnp.where((lane >= at) & (lane < at + 32), gain, 0.0)
+    for s in range(2):
+        for j, part in enumerate((high, middle, low)):
+            tail = jnp.where(lane == at + 32 + 3 * s + j, part[s : s + 1], tail)
+    tail = jnp.concatenate([tail, tail], axis=0).astype(BF)
+    rows = pl.ds(begin, 16)
+    for i in range(8):
+        out_ref[i, :, :UP] = up_ref[rows, :]
+        out_ref[i, :, LANES - 128 :] = tail
+        out_ref[i, :, UP:GAIN_AT] = down_ref[rows, :]
+
+
+def packed(place, starts, ratio, down, up, gain):
+    smem = pl.BlockSpec(memory_space=pltpu.SMEM)
+    vmem = pl.BlockSpec(memory_space=pltpu.VMEM)
+    return pl.pallas_call(
+        pack,
+        out_shape=jax.ShapeDtypeStruct((8, 16, LANES), BF),
+        in_specs=[smem, smem] + [vmem] * 4,
+        out_specs=vmem,
+        compiler_params=pltpu.CompilerParams(vmem_limit_bytes=4 * 1024 * 1024),
+    )(place, starts, ratio, down, up, gain)
+
+
+def finish(place_ref, *refs):
+    down_ref, up_ref = refs[4:]
+    for i in range(4):
+        core, yl = (place_ref[3] + i // 2) & 1, (place_ref[1] + i % 2) & 1
+        rows = pl.ds(pl.multiple_of(core * 32 + yl * 16, 16), 16)
+        up_ref[rows, :] = refs[i][:, :UP]
+        down_ref[rows, :] = refs[i][:, UP:GAIN_AT]
+
+
+def finished(place, *shares_):
+    vmem = pl.BlockSpec(memory_space=pltpu.VMEM)
+    return pl.pallas_call(
+        finish,
+        out_shape=[
+            jax.ShapeDtypeStruct((ORDER, DOWN), F32),
+            jax.ShapeDtypeStruct((ORDER, UP), F32),
+        ],
+        in_specs=[pl.BlockSpec(memory_space=pltpu.SMEM)] + [vmem] * 4,
+        out_specs=[vmem] * 2,
+        compiler_params=pltpu.CompilerParams(vmem_limit_bytes=4 * 1024 * 1024),
+    )(place, *shares_)
+
+
 def bring(after_ref, place_ref, *refs):
     sems = refs[6]
     copies = [pltpu.make_async_copy(refs[i], refs[3 + i], sems.at[i]) for i in range(3)]
@@ -220,7 +287,7 @@
             pltpu.VMEM((ORDER, rows), BF),
             jax.ShapeDtypeStruct((8, 128), F32),
         ],
-        in_specs=[smem, smem] + [any_space] * 8 + [vmem] * 3,
+        in_specs=[smem, smem] + [any_space] * 16 + [vmem] * 3,
         out_specs=[vmem] * 5,
         scratch_shapes=[
             pltpu.VMEM((ORDER, units), BF),
@@ -229,7 +296,7 @@
             pltpu.VMEM((CHUNKS, 128), F32),
             pltpu.VMEM((rows, width), F32),
             pltpu.VMEM((256, 16, LANES), BF),
-            pltpu.SemaphoreType.DMA((8,)),
+            pltpu.SemaphoreType.DMA((16,)),
         ],
         compiler_params=pltpu.CompilerParams(vmem_limit_bytes=20 * 1024 * 1024),
         cost_estimate=pl.CostEstimate(
@@ -258,18 +325,13 @@
     return (((z * 2 + y // 2) * 4 + x) * 2 + y % 2) * 2 + c
 
 
-def ring(values, step):
-    pairs = [
-        (device(z, y, x, c), device(z, (y + step * c) % 4, (x + step * (1 - c)) % 4, c))
-        for z, y, x, c in itertools.product(range(8), range(4), range(4), range(2))
-    ]
+def ring(values, step, turn=0):
+    pairs = []
+    for z, y, x, c in itertools.product(range(8), range(4), range(4), range(2)):
+        along_y = c ^ turn
+        to = device(z, (y + step * along_y) % 4, (x + step * (1 - along_y)) % 4, c)
+        pairs.append((device(z, y, x, c), to))
     return lax.ppermute(values, FINE_AXES, pairs)
-
-
-def crosswise(values):
-    groups = [[device(z, y, x, 0) for z in range(8) for y in range(4)] for x in range(4)]
-    groups += [[device(z, y, x, 1) for z in range(8) for x in range(4)] for y in range(4)]
-    return lax.all_to_all(values, FINE_AXES, 0, 0, axis_index_groups=groups, tiled=True)
 
 
 def other_core(values):
@@ -290,39 +352,42 @@
     logratio,
     starts,
 ):
-    row_block = frozen.shape[2]
-    yh, yl, core = lax.axis_index("yh"), lax.axis_index("yl"), lax.axis_index("c")
-    place = jnp.stack([lax.axis_index("z"), yh * 2 + yl, lax.axis_index("x"), core])
-
-    positions = (yl * 2 + core) * row_block + lax.broadcasted_iota(
-        jnp.int32, (1, 1, row_block), 2
+    yl, core = lax.axis_index("yl"), lax.axis_index("c")
+    place = jnp.stack([lax.axis_index("z"), lax.axis_index("yh") * 2 + yl, lax.axis_index("x"), core])
+
+    quarter = packed(
+        place,
+        starts,
+        logratio[0],
+        down_factor_weight.T,
+        up_factor_weight,
+        final_norm_gain[None],
     )
-    partial = jnp.sum(jnp.where(positions >= starts[:, :, None], logratio, 0.0), axis=2)[0]
-    high = lax.reduce_precision(partial, 8, 7)
-    middle = lax.reduce_precision(partial - high, 8, 7)
-    low = partial - high - middle
-    sums = jnp.stack([high, middle, low], axis=1).reshape(1, 6).astype(BF)
-
-    begin = core * 32 + yl * 16
-    rows_of_down = lax.dynamic_slice_in_dim(down_factor_weight.T, begin, 16, axis=0)
-    rows_of_up = lax.dynamic_slice_in_dim(up_factor_weight, begin, 16, axis=0)
-    gain_part = lax.dynamic_slice_in_dim(final_norm_gain, (core * 2 + yl) * 32, 32)
-    tail = jnp.concatenate([gain_part[None], sums, jnp.zeros((1, LANES - SUMS_AT - 6), BF)], axis=1)
-    quarter = jnp.concatenate(
-        [rows_of_up, rows_of_down, jnp.broadcast_to(tail, (16, tail.shape[1]))], axis=1
+    held = lax.all_to_all(quarter, "z", 0, 0, tiled=True)
+    early = lax.optimization_barrier(
+        (
+            ring(held, 2),
+            *[ring(held, step, 1) for step in (1, 2, 3)],
+            ring(held, 1),
+            ring(held, 3),
+        )
     )
-    held = crosswise(jnp.broadcast_to(quarter[None], (32, 16, LANES)))
-    own = [held] + [ring(held, step) for step in (1, 2, 3)]
+    side = jnp.concatenate(early[1:4])
+    own = [held, side, early[4], ring(side, 1)]
+    own += [early[0], ring(side, 2), early[5], ring(side, 3)]
     width = frozen.shape[3]
     near = brought(
-        held,
+        side,
         place,
         gated_hidden_input.reshape(-1, gated_hidden_input.shape[3]),
         frozen.reshape(-1, width),
         head_gradient_rows.reshape(-1, width),
     )
-    held, *near = lax.optimization_barrier((held, *near))
-    other = [other_core(v) for v in (held, *own[1:])]
+    small = [other_core(v) for v in own[::2]]
+    side, *rest = lax.optimization_barrier((side, *near, *small))
+    near, small = rest[:3], rest[3:]
+    large = [other_core(v) for v in (side, *own[3::2])]
+    other = [v for pair in zip(small, large) for v in pair]
 
     first, second, margin = shares(place, starts, [*own, *other], *near)
 
@@ -334,18 +399,16 @@
             for i in range(4)
         ]
         came = [ring(chip[step], step) for step in (1, 2, 3)]
-        lines.append(total_of(chip[0], *came).astype(BF))
-    line = jnp.concatenate(lines)
-    share = jnp.sum(crosswise(line).astype(F32), axis=0)
-    copies = jnp.broadcast_to(share[None], (4, 16, LANES))
-    whole = lax.all_to_all(copies, CTX, 0, 0, tiled=True)
-    whole = whole.reshape(2, 2, 16, LANES).transpose(1, 0, 2, 3)
-    whole = whole.reshape(ORDER, LANES)
-    return (
-        jnp.logaddexp(0.0, -margin),
-        whole[:, UP : UP + DOWN].T,
-        whole[:, :UP],
-    )
+        lines.append(total_of(chip[0], *came).astype(BF).reshape(4, 4, 16, LANES))
+    line = jnp.concatenate(lines, axis=1)
+    came = [ring(line[step], step, 1) for step in (1, 2, 3)]
+    plane = total_of(line[0], *came).astype(BF)
+    share = jnp.sum(lax.all_to_all(plane, "z", 0, 0, tiled=True).astype(F32), axis=0)
+    spread = [
+        lax.ppermute(share, CTX, [(i, i ^ step) for i in range(4)]) for step in (2, 1, 3)
+    ]
+    down_gradient_t, up_gradient = finished(place, share, *spread)
+    return jnp.logaddexp(0.0, -margin), down_gradient_t.T, up_gradient
 
 
 def solution(mesh):

time: 131 us -> 127 us (0.969)
  blocking collectives: 52.4 us -> 27.7 us
  waiting for transfers between devices: 17 us -> 28 us
  starting transfers between devices: 33.4 us -> 39.4 us
  Pallas kernels: 18.4 us -> 23.2 us
    all_to_all x2, blocking collectives: 52.4 us -> 27.7 us  [the longest x1 17 us: local(): held = lax.all_to_all(quarter, 'z', 0, 0, tiled=True)]
    ppermute x9 -> x18, waiting for transfers between devices: 11.8 us -> 24.1 us  [ring(): return lax.ppermute(values, FINE_AXES, pairs)]
    all_to_all x1 -> x0, starting transfers between devices: 5.97 us -> none  [local(): whole = lax.all_to_all(copies, CTX, 0, 0, tiled=True)]
    ppermute x9 -> x18, starting transfers between devices: 15.7 us -> 21.3 us  [ring(): return lax.ppermute(values, FINE_AXES, pairs)]
    ppermute x0 -> x3, starting transfers between devices: none -> 4.33 us  [local(): lax.ppermute(share, CTX, [(i, i ^ step) for i in range(4)])]
    unnamed x4 -> x14, local copies, waits for them, and re-layouts: 0.01 us -> 3.59 us
    pallas_call x1, Pallas kernels: 11.9 us -> 14.8 us  [shares(): pl.pallas_call(kernel, out_shape=[pltpu.VMEM((64, 16, LANES), BF)] * 2 +...]
    all_to_all x1 -> x0, waiting for transfers between devices: 2.61 us -> none  [local(): whole = lax.all_to_all(copies, CTX, 0, 0, tiled=True)]
  transfers between devices with their start and end apart: 16 -> 31, of which waited for: 9 -> 17; matrix products, arithmetic and copies ran while one was open for 1% -> 1% of each run, Pallas kernels for 5% -> 5%
where the time goes in v6:
time: 127 us; the launch traced here: 126 us
  starting transfers between devices  39.4 us (31%)
  waiting for transfers between devices  28 us (22%)
  blocking collectives  27.7 us (22%)
  Pallas kernels  23.2 us (18%)
  local copies, waits for them, and re-layouts  4.12 us (3%)
  between operations  2.67 us (2%)
    ppermute x18, waiting for transfers between devices, ring(): return lax.ppermute(values, FINE_AXES, pairs)  24.1 us
    ppermute x18, starting transfers between devices, ring(): return lax.ppermute(values, FINE_AXES, pairs)  21.3 us
    all_to_all x1, blocking collectives, local(): held = lax.all_to_all(quarter, 'z', 0, 0, tiled=True)  17 us
    pallas_call x1, Pallas kernels, shares(): pl.pallas_call(kernel, out_shape=[pltpu.VMEM((64, 16, LANES), BF)] * 2 +...  14.8 us
    ppermute x10, starting transfers between devices, other_core(): return lax.ppermute(values, 'c', [(0, 1), (1, 0)])  13.8 us
    all_to_all x1, blocking collectives, local(): lax.all_to_all(plane, 'z', 0, 0, tiled=True).astype(F32)  10.7 us
    pallas_call x1, Pallas kernels, brought(): pl.pallas_call(bring, out_shape=[pltpu.VMEM(v.shape, v.dtype) for v in ar...  4.91 us
    ppermute x3, starting transfers between devices, local(): lax.ppermute(share, CTX, [(i, i ^ step) for i in range(4)])  4.33 us
  transfers between devices with their start and end apart: 31, of which 17 were waited for; matrix products, arithmetic and copies ran while one was open for 1% of the time, Pallas kernels for 5%

profile of v6, /device:TPU:1, one launch (start us, length us, event | category | flops | bytes accessed | tf_op | source)
XLA Modules:
  0.0 126.4 jit_solution(1249235259401976898)
XLA Ops:
  0.7 0.8 copy-done
  1.6 0.7 copy-done.1
  2.3 0.7 copy-done.2
  2.9 0.7 copy-done.4
  3.6 0.7 copy-done.5
  4.3 0.6 shard_map.103
  4.9 17.0 %all_to_all.10.refs_0_ = bf16[8,16,640]{2,1,0:T(8,128)(2,1)S(1)} all-to-all(bf16[8,16,640]{2,1,0:T(8,128)(2,1)S(1)} %shard_map.103), channel_id=1, replica_groups=mesh['z'=8,'yh'=2,'x'=4,'yl'=2,'c'=2] {'z'}, dimensions={0} | all-to-all | bytes 327680 | tf_op jit(solution)/shard_map/all_to_all | solution.py:366
  21.9 2.7 %collective-permute-start.5 = (bf16[8,16,640]{2,1,0:T(8,128)(2,1)S(1)}, bf16[8,16,640]{2,1,0:T(8,128)(2,1)S(1)}, u32[]{:S(2)}, u32[]{:S(2)}) collective-permute-start(bf16[8,16,640]{2,1,0:T(8,128)(2,1)S(1)} %all_to_all.10.refs_0_), channel_id=1, source_target_pairs={{0,12},{1,19},{4,0},{5,23},{8,4},{9,27},{12,8},{13,31},{2,14},{3,1... | collective-permute-start | bytes 491528 | tf_op jit(solution)/shard_map/ppermute | solution.py:334
  24.6 2.5 %collective-permute-start.3 = (bf16[8,16,640]{2,1,0:T(8,128)(2,1)S(1)}, bf16[8,16,640]{2,1,0:T(8,128)(2,1)S(1)}, u32[]{:S(2)}, u32[]{:S(2)}) collective-permute-start(bf16[8,16,640]{2,1,0:T(8,128)(2,1)S(1)} %all_to_all.10.refs_0_), channel_id=1, source_target_pairs={{0,18},{1,13},{4,22},{5,1},{8,26},{9,5},{12,30},{13,9},{2,0},{3,15... | collective-permute-start | bytes 491528 | tf_op jit(solution)/shard_map/ppermute | solution.py:334
  27.1 0.5 collective-permute-start.2
  27.6 0.6 collective-permute-start.1
  28.2 1.6 %collective-permute-start = (bf16[8,16,640]{2,1,0:T(8,128)(2,1)S(1)}, bf16[8,16,640]{2,1,0:T(8,128)(2,1)S(1)}, u32[]{:S(2)}, u32[]{:S(2)}) collective-permute-start(bf16[8,16,640]{2,1,0:T(8,128)(2,1)S(1)} %all_to_all.10.refs_0_), channel_id=1, source_target_pairs={{0,8},{1,17},{4,12},{5,21},{8,0},{9,25},{12,4},{13,29},{2,10},{3,1... | collective-permute-start | bytes 491528 | tf_op jit(solution)/shard_map/ppermute | solution.py:334
  30.0 2.4 %collective-permute-done.3 = bf16[8,16,640]{2,1,0:T(8,128)(2,1)S(1)} collective-permute-done((bf16[8,16,640]{2,1,0:T(8,128)(2,1)S(1)}, bf16[8,16,640]{2,1,0:T(8,128)(2,1)S(1)}, u32[]{:S(2)}, u32[]{:S(2)}) %collective-permute-start.3) | collective-permute-done | bytes 163872 | tf_op jit(solution)/shard_map/ppermute | solution.py:334
  32.4 1.5 %collective-permute-done.2 = bf16[8,16,640]{2,1,0:T(8,128)(2,1)S(1)} collective-permute-done((bf16[8,16,640]{2,1,0:T(8,128)(2,1)S(1)}, bf16[8,16,640]{2,1,0:T(8,128)(2,1)S(1)}, u32[]{:S(2)}, u32[]{:S(2)}) %collective-permute-start.2) | collective-permute-done | bytes 163872 | tf_op jit(solution)/shard_map/ppermute | solution.py:334
  34.0 2.7 %collective-permute-done.1 = bf16[8,16,640]{2,1,0:T(8,128)(2,1)S(1)} collective-permute-done((bf16[8,16,640]{2,1,0:T(8,128)(2,1)S(1)}, bf16[8,16,640]{2,1,0:T(8,128)(2,1)S(1)}, u32[]{:S(2)}, u32[]{:S(2)}) %collective-permute-start.1) | collective-permute-done | bytes 163872 | tf_op jit(solution)/shard_map/ppermute | solution.py:334
  36.7 2.7 %collective-permute-start.8 = (bf16[24,16,640]{2,1,0:T(8,128)(2,1)S(1)}, bf16[24,16,640]{2,1,0:T(8,128)(2,1)S(1)}, u32[]{:S(2)}, u32[]{:S(2)}) collective-permute-start(bf16[24,16,640]{2,1,0:T(8,128)(2,1)S(1)} %constant_dynamic-update-slice_fusion.after_ref.refs_1_), channel_id=1, source_target_pairs={{0,12},{1,19},{4,0},{5,23},{8,4},{9,27},{12,8},{13,31},{2,14},{3,1... | collective-permute-start | bytes 1474568 | tf_op jit(solution)/shard_map/ppermute | solution.py:334
  39.4 0.7 collective-permute-start.6
  40.1 4.8 %collective-permute-start.9 = (bf16[8,16,640]{2,1,0:T(8,128)(2,1)S(1)}, bf16[8,16,640]{2,1,0:T(8,128)(2,1)S(1)}, u32[]{:S(2)}, u32[]{:S(2)}) collective-permute-start(bf16[8,16,640]{2,1,0:T(8,128)(2,1)S(1)} %all_to_all.10.refs_0_), channel_id=1, source_target_pairs={{0,1},{1,0},{2,3},{3,2},{4,5},{5,4},{6,7},{7,6},{8,9},{9,8},{10,11... | collective-permute-start | bytes 491528 | tf_op jit(solution)/shard_map/ppermute | solution.py:338
  44.9 1.0 collective-permute-done.9.refs_8_
  46.5 4.9 %shard_map.104 = (bf16[128,29568]{1,0:T(8,128)(2,1)S(1)}, bf16[128,8192]{1,0:T(8,128)(2,1)S(1)}, bf16[128,8192]{1,0:T(8,128)(2,1)S(1)}) custom-call(bf16[24,16,640]{2,1,0:T(8,128)(2,1)S(1)} %constant_dynamic-update-slice_fusion.after_ref.refs_1_, s32[4]{0:T(128)S(1)} %pad_add_fusion.place_ref, bf16[128,29568]{1,0:T(8,128)(2,1)} %bitcast.28, ...), custom_call_target="tpu_custom_call" | custom-call | bytes 23527424 | tf_op jit(solution)/shard_map/pallas_call | solution.py:261
  51.8 3.7 %collective-permute-start.16 = (bf16[24,16,640]{2,1,0:T(8,128)(2,1)S(1)}, bf16[24,16,640]{2,1,0:T(8,128)(2,1)S(1)}, u32[]{:S(2)}, u32[]{:S(2)}) collective-permute-start(bf16[24,16,640]{2,1,0:T(8,128)(2,1)S(1)} %collective-permute-done.8.refs_7_), channel_id=1, source_target_pairs={{0,1},{1,0},{2,3},{3,2},{4,5},{5,4},{6,7},{7,6},{8,9},{9,8},{10,11... | collective-permute-start | bytes 1474568 | tf_op jit(solution)/shard_map/ppermute | solution.py:338
  55.6 3.7 %collective-permute-start.14 = (bf16[24,16,640]{2,1,0:T(8,128)(2,1)S(1)}, bf16[24,16,640]{2,1,0:T(8,128)(2,1)S(1)}, u32[]{:S(2)}, u32[]{:S(2)}) collective-permute-start(bf16[24,16,640]{2,1,0:T(8,128)(2,1)S(1)} %collective-permute-done.6.refs_3_), channel_id=1, source_target_pairs={{0,1},{1,0},{2,3},{3,2},{4,5},{5,4},{6,7},{7,6},{8,9},{9,8},{10,11... | collective-permute-start | bytes 1474568 | tf_op jit(solution)/shard_map/ppermute | solution.py:338
  59.3 1.5 %collective-permute-done.14.refs_11_ = bf16[24,16,640]{2,1,0:T(8,128)(2,1)S(1)} collective-permute-done((bf16[24,16,640]{2,1,0:T(8,128)(2,1)S(1)}, bf16[24,16,640]{2,1,0:T(8,128)(2,1)S(1)}, u32[]{:S(2)}, u32[]{:S(2)}) %collective-permute-start.14) | collective-permute-done | bytes 491552 | tf_op jit(solution)/shard_map/ppermute | solution.py:338
  60.7 14.8 %shard_map.105 = (bf16[64,16,640]{2,1,0:T(8,128)(2,1)S(1)}, bf16[64,16,640]{2,1,0:T(8,128)(2,1)S(1)}, bf16[64,4096]{1,0:T(8,128)(2,1)S(1)}, bf16[64,128]{1,0:T(8,128)(2,1)S(1)}, f32[8,128]{1,0:T(8,128)S(1)}) custom-call(s32[4]{0:T(128)S(1)} %pad_add_fusion.place_ref, s32[1,2]{1,0:T(1,128)S(1)} %copy-done.3, bf16[8,16,640]{2,1,0:T(8,128)(2,1)S(1)} %all_to_all.10.refs_0_, ...), custom_call_target="tpu_custom_call" | custom-call | flops 1505755136 | bytes 22249472 | tf_op jit(solution)/shard_map/pallas_call | solution.py:282
  75.6 0.5 collective-permute-start.17
  76.0 1.6 %shard_map.106 = (bf16[64,16,640]{2,1,0:T(8,128)(2,1)S(1)}, bf16[64,16,640]{2,1,0:T(8,128)(2,1)S(1)}) custom-call(s32[4]{0:T(128)S(1)} %pad_add_fusion.place_ref, bf16[64,128]{1,0:T(8,128)(2,1)S(1)} %get-tuple-element.49.low_ref, bf16[64,4096]{1,0:T(8,128)(2,1)S(1)} %get-tuple-element.50.up_rest, bf16[128,29568]{1,0:T(8,128)(2,1)S(1)} %get-tuple-element.43.refs_16_.hid), custom_call_target="tpu_custom_call" | custom-call | flops 242221056 | bytes 6406144 | tf_op jit(solution)/shard_map/pallas_call | solution.py:308
  77.9 0.8 collective-permute-done.17
  79.1 2.7 %collective-permute-start.20 = (bf16[16,16,640]{2,1,0:T(8,128)(2,1)S(1)}, bf16[16,16,640]{2,1,0:T(8,128)(2,1)S(1)}, u32[]{:S(2)}, u32[]{:S(2)}) collective-permute-start(bf16[16,16,640]{2,1,0:T(8,128)(2,1)S(1)} %get-tuple-element.56), channel_id=1, source_target_pairs={{0,12},{1,19},{4,0},{5,23},{8,4},{9,27},{12,8},{13,31},{2,14},{3,1... | collective-permute-start | bytes 983048 | tf_op jit(solution)/shard_map/ppermute | solution.py:334
  81.8 1.1 collective-permute-start.19
  83.2 0.9 collective-permute-start.22
  84.1 1.8 %collective-permute-start.24 = (bf16[16,16,640]{2,1,0:T(8,128)(2,1)S(1)}, bf16[16,16,640]{2,1,0:T(8,128)(2,1)S(1)}, u32[]{:S(2)}, u32[]{:S(2)}) collective-permute-start(bf16[16,16,640]{2,1,0:T(8,128)(2,1)S(1)} %get-tuple-element.59), channel_id=1, source_target_pairs={{0,12},{1,19},{4,0},{5,23},{8,4},{9,27},{12,8},{13,31},{2,14},{3,1... | collective-permute-start | bytes 983048 | tf_op jit(solution)/shard_map/ppermute | solution.py:334
  85.9 0.5 collective-permute-done.18
  86.5 0.4 collective-permute-start.23
  86.9 2.4 %collective-permute-done.20 = bf16[16,16,640]{2,1,0:T(8,128)(2,1)S(1)} collective-permute-done((bf16[16,16,640]{2,1,0:T(8,128)(2,1)S(1)}, bf16[16,16,640]{2,1,0:T(8,128)(2,1)S(1)}, u32[]{:S(2)}, u32[]{:S(2)}) %collective-permute-start.20) | collective-permute-done | bytes 327712 | tf_op jit(solution)/shard_map/ppermute | solution.py:334
  89.3 1.6 %collective-permute-done.19 = bf16[16,16,640]{2,1,0:T(8,128)(2,1)S(1)} collective-permute-done((bf16[16,16,640]{2,1,0:T(8,128)(2,1)S(1)}, bf16[16,16,640]{2,1,0:T(8,128)(2,1)S(1)}, u32[]{:S(2)}, u32[]{:S(2)}) %collective-permute-start.19) | collective-permute-done | bytes 327712 | tf_op jit(solution)/shard_map/ppermute | solution.py:334
  91.2 3.0 %collective-permute-done.22 = bf16[16,16,640]{2,1,0:T(8,128)(2,1)S(1)} collective-permute-done((bf16[16,16,640]{2,1,0:T(8,128)(2,1)S(1)}, bf16[16,16,640]{2,1,0:T(8,128)(2,1)S(1)}, u32[]{:S(2)}, u32[]{:S(2)}) %collective-permute-start.22) | collective-permute-done | bytes 327712 | tf_op jit(solution)/shard_map/ppermute | solution.py:334
  94.2 2.2 %collective-permute-done.24 = bf16[16,16,640]{2,1,0:T(8,128)(2,1)S(1)} collective-permute-done((bf16[16,16,640]{2,1,0:T(8,128)(2,1)S(1)}, bf16[16,16,640]{2,1,0:T(8,128)(2,1)S(1)}, u32[]{:S(2)}, u32[]{:S(2)}) %collective-permute-start.24) | collective-permute-done | bytes 327712 | tf_op jit(solution)/shard_map/ppermute | solution.py:334
  96.4 1.6 %collective-permute-done.23 = bf16[16,16,640]{2,1,0:T(8,128)(2,1)S(1)} collective-permute-done((bf16[16,16,640]{2,1,0:T(8,128)(2,1)S(1)}, bf16[16,16,640]{2,1,0:T(8,128)(2,1)S(1)}, u32[]{:S(2)}, u32[]{:S(2)}) %collective-permute-start.23) | collective-permute-done | bytes 327712 | tf_op jit(solution)/shard_map/ppermute | solution.py:334
  98.3 2.7 %collective-permute-start.27 = (bf16[8,16,640]{2,1,0:T(8,128)(2,1)S(1)}, bf16[8,16,640]{2,1,0:T(8,128)(2,1)S(1)}, u32[]{:S(2)}, u32[]{:S(2)}) collective-permute-start(bf16[8,16,640]{2,1,0:T(8,128)(2,1)S(1)} %get-tuple-element.62), channel_id=1, source_target_pairs={{0,18},{1,13},{4,22},{5,1},{8,26},{9,5},{12,30},{13,9},{2,0},{3,15... | collective-permute-start | bytes 491528 | tf_op jit(solution)/shard_map/ppermute | solution.py:334
  101.0 3.0 %collective-permute-done.25 = bf16[8,16,640]{2,1,0:T(8,128)(2,1)S(1)} collective-permute-done((bf16[8,16,640]{2,1,0:T(8,128)(2,1)S(1)}, bf16[8,16,640]{2,1,0:T(8,128)(2,1)S(1)}, u32[]{:S(2)}, u32[]{:S(2)}) %collective-permute-start.25) | collective-permute-done | bytes 163872 | tf_op jit(solution)/shard_map/ppermute | solution.py:334
  104.0 1.0 collective-permute-done.27
  105.0 1.9 %collective-permute-done.26 = bf16[8,16,640]{2,1,0:T(8,128)(2,1)S(1)} collective-permute-done((bf16[8,16,640]{2,1,0:T(8,128)(2,1)S(1)}, bf16[8,16,640]{2,1,0:T(8,128)(2,1)S(1)}, u32[]{:S(2)}, u32[]{:S(2)}) %collective-permute-start.26) | collective-permute-done | bytes 163872 | tf_op jit(solution)/shard_map/ppermute | solution.py:334
  107.0 10.7 %all_to_all.11 = bf16[8,16,640]{2,1,0:T(8,128)(2,1)S(1)} all-to-all(bf16[8,16,640]{2,1,0:T(8,128)(2,1)S(1)} %fusion.2), channel_id=1, replica_groups=mesh['z'=8,'yh'=2,'x'=4,'yl'=2,'c'=2] {'z'}, dimensions={0} | all-to-all | bytes 327680 | tf_op jit(solution)/shard_map/all_to_all | solution.py:406
  117.8 3.4 %collective-permute-start.30 = (f32[16,640]{1,0:T(8,128)S(1)}, f32[16,640]{1,0:T(8,128)S(1)}, u32[]{:S(2)}, u32[]{:S(2)}) collective-permute-start(f32[16,640]{1,0:T(8,128)S(1)} %convert_reduce_fusion.refs_0_), channel_id=1, source_target_pairs={{0,3},{1,2},{2,1},{3,0},{4,7},{5,6},{6,5},{7,4},{8,11},{9,10},{10,... | collective-permute-start | bytes 122888 | tf_op jit(solution)/shard_map/ppermute | solution.py:408
  121.2 0.9 collective-permute-start.28
  122.1 0.5 slice.63
  123.4 0.7 collective-permute-done.28.refs_1_
  124.0 1.2 shard_map.107
  (45 shorter events, 2.8 us)
Async XLA Ops:
  0.7 0.8 copy-start
  1.6 0.7 copy-start.1
  2.3 0.7 copy-start.2
  2.9 0.7 copy-start.4
  3.6 0.7 copy-start.5
  21.9 6.3 %collective-permute-start.5 = (bf16[8,16,640]{2,1,0:T(8,128)(2,1)S(1)}, bf16[8,16,640]{2,1,0:T(8,128)(2,1)S(1)}, u32[]{:S(2)}, u32[]{:S(2)}) collective-permute-start(bf16[8,16,640]{2,1,0:T(8,128)(2,1)S(1)} %all_to_all.10.refs_0_), channel_id=1, source_target_pairs={{0,12},{1,19},{4,0},{5,23},{8,4},{9,27},{12,8},{13,31},{2,14},{3,1... | collective-permute-start | bytes 491528 | tf_op jit(solution)/shard_map/ppermute | solution.py:334
  24.6 5.4 %collective-permute-start.4 = (bf16[8,16,640]{2,1,0:T(8,128)(2,1)S(1)}, bf16[8,16,640]{2,1,0:T(8,128)(2,1)S(1)}, u32[]{:S(2)}, u32[]{:S(2)}) collective-permute-start(bf16[8,16,640]{2,1,0:T(8,128)(2,1)S(1)} %all_to_all.10.refs_0_), channel_id=1, source_target_pairs={{0,4},{1,3},{4,8},{5,7},{8,12},{9,11},{12,0},{13,15},{2,6},{3,17},... | collective-permute-start | bytes 491528 | tf_op jit(solution)/shard_map/ppermute | solution.py:334
  24.6 7.8 %collective-permute-start.3 = (bf16[8,16,640]{2,1,0:T(8,128)(2,1)S(1)}, bf16[8,16,640]{2,1,0:T(8,128)(2,1)S(1)}, u32[]{:S(2)}, u32[]{:S(2)}) collective-permute-start(bf16[8,16,640]{2,1,0:T(8,128)(2,1)S(1)} %all_to_all.10.refs_0_), channel_id=1, source_target_pairs={{0,18},{1,13},{4,22},{5,1},{8,26},{9,5},{12,30},{13,9},{2,0},{3,15... | collective-permute-start | bytes 491528 | tf_op jit(solution)/shard_map/ppermute | solution.py:334
  27.1 6.9 %collective-permute-start.2 = (bf16[8,16,640]{2,1,0:T(8,128)(2,1)S(1)}, bf16[8,16,640]{2,1,0:T(8,128)(2,1)S(1)}, u32[]{:S(2)}, u32[]{:S(2)}) collective-permute-start(bf16[8,16,640]{2,1,0:T(8,128)(2,1)S(1)} %all_to_all.10.refs_0_), channel_id=1, source_target_pairs={{0,16},{1,9},{4,20},{5,13},{8,24},{9,1},{12,28},{13,5},{2,18},{3,1... | collective-permute-start | bytes 491528 | tf_op jit(solution)/shard_map/ppermute | solution.py:334
  27.6 9.0 %collective-permute-start.1 = (bf16[8,16,640]{2,1,0:T(8,128)(2,1)S(1)}, bf16[8,16,640]{2,1,0:T(8,128)(2,1)S(1)}, u32[]{:S(2)}, u32[]{:S(2)}) collective-permute-start(bf16[8,16,640]{2,1,0:T(8,128)(2,1)S(1)} %all_to_all.10.refs_0_), channel_id=1, source_target_pairs={{0,2},{1,5},{4,6},{5,9},{8,10},{9,13},{12,14},{13,1},{2,16},{3,7},... | collective-permute-start | bytes 491528 | tf_op jit(solution)/shard_map/ppermute | solution.py:334
  28.2 8.4 %collective-permute-start = (bf16[8,16,640]{2,1,0:T(8,128)(2,1)S(1)}, bf16[8,16,640]{2,1,0:T(8,128)(2,1)S(1)}, u32[]{:S(2)}, u32[]{:S(2)}) collective-permute-start(bf16[8,16,640]{2,1,0:T(8,128)(2,1)S(1)} %all_to_all.10.refs_0_), channel_id=1, source_target_pairs={{0,8},{1,17},{4,12},{5,21},{8,0},{9,25},{12,4},{13,29},{2,10},{3,1... | collective-permute-start | bytes 491528 | tf_op jit(solution)/shard_map/ppermute | solution.py:334
  36.7 15.1 %collective-permute-start.8 = (bf16[24,16,640]{2,1,0:T(8,128)(2,1)S(1)}, bf16[24,16,640]{2,1,0:T(8,128)(2,1)S(1)}, u32[]{:S(2)}, u32[]{:S(2)}) collective-permute-start(bf16[24,16,640]{2,1,0:T(8,128)(2,1)S(1)} %constant_dynamic-update-slice_fusion.after_ref.refs_1_), channel_id=1, source_target_pairs={{0,12},{1,19},{4,0},{5,23},{8,4},{9,27},{12,8},{13,31},{2,14},{3,1... | collective-permute-start | bytes 1474568 | tf_op jit(solution)/shard_map/ppermute | solution.py:334
  39.4 16.1 %collective-permute-start.7 = (bf16[24,16,640]{2,1,0:T(8,128)(2,1)S(1)}, bf16[24,16,640]{2,1,0:T(8,128)(2,1)S(1)}, u32[]{:S(2)}, u32[]{:S(2)}) collective-permute-start(bf16[24,16,640]{2,1,0:T(8,128)(2,1)S(1)} %constant_dynamic-update-slice_fusion.after_ref.refs_1_), channel_id=1, source_target_pairs={{0,8},{1,17},{4,12},{5,21},{8,0},{9,25},{12,4},{13,29},{2,10},{3,1... | collective-permute-start | bytes 1474568 | tf_op jit(solution)/shard_map/ppermute | solution.py:334
  39.4 16.1 %collective-permute-start.6 = (bf16[24,16,640]{2,1,0:T(8,128)(2,1)S(1)}, bf16[24,16,640]{2,1,0:T(8,128)(2,1)S(1)}, u32[]{:S(2)}, u32[]{:S(2)}) collective-permute-start(bf16[24,16,640]{2,1,0:T(8,128)(2,1)S(1)} %constant_dynamic-update-slice_fusion.after_ref.refs_1_), channel_id=1, source_target_pairs={{0,4},{1,3},{4,8},{5,7},{8,12},{9,11},{12,0},{13,15},{2,6},{3,17},... | collective-permute-start | bytes 1474568 | tf_op jit(solution)/shard_map/ppermute | solution.py:334
  40.1 5.8 %collective-permute-start.9 = (bf16[8,16,640]{2,1,0:T(8,128)(2,1)S(1)}, bf16[8,16,640]{2,1,0:T(8,128)(2,1)S(1)}, u32[]{:S(2)}, u32[]{:S(2)}) collective-permute-start(bf16[8,16,640]{2,1,0:T(8,128)(2,1)S(1)} %all_to_all.10.refs_0_), channel_id=1, source_target_pairs={{0,1},{1,0},{2,3},{3,2},{4,5},{5,4},{6,7},{7,6},{8,9},{9,8},{10,11... | collective-permute-start | bytes 491528 | tf_op jit(solution)/shard_map/ppermute | solution.py:338
  44.9 1.4 %collective-permute-start.10 = (bf16[8,16,640]{2,1,0:T(8,128)(2,1)S(1)}, bf16[8,16,640]{2,1,0:T(8,128)(2,1)S(1)}, u32[]{:S(2)}, u32[]{:S(2)}) collective-permute-start(bf16[8,16,640]{2,1,0:T(8,128)(2,1)S(1)} %collective-permute-done.4.refs_2_), channel_id=1, source_target_pairs={{0,1},{1,0},{2,3},{3,2},{4,5},{5,4},{6,7},{7,6},{8,9},{9,8},{10,11... | collective-permute-start | bytes 491528 | tf_op jit(solution)/shard_map/ppermute | solution.py:338
  45.9 5.5 %collective-permute-start.11 = (bf16[8,16,640]{2,1,0:T(8,128)(2,1)S(1)}, bf16[8,16,640]{2,1,0:T(8,128)(2,1)S(1)}, u32[]{:S(2)}, u32[]{:S(2)}) collective-permute-start(bf16[8,16,640]{2,1,0:T(8,128)(2,1)S(1)} %collective-permute-done.refs_4_), channel_id=1, source_target_pairs={{0,1},{1,0},{2,3},{3,2},{4,5},{5,4},{6,7},{7,6},{8,9},{9,8},{10,11... | collective-permute-start | bytes 491528 | tf_op jit(solution)/shard_map/ppermute | solution.py:338
  46.3 5.2 %collective-permute-start.12 = (bf16[8,16,640]{2,1,0:T(8,128)(2,1)S(1)}, bf16[8,16,640]{2,1,0:T(8,128)(2,1)S(1)}, u32[]{:S(2)}, u32[]{:S(2)}) collective-permute-start(bf16[8,16,640]{2,1,0:T(8,128)(2,1)S(1)} %collective-permute-done.5.refs_6_), channel_id=1, source_target_pairs={{0,1},{1,0},{2,3},{3,2},{4,5},{5,4},{6,7},{7,6},{8,9},{9,8},{10,11... | collective-permute-start | bytes 491528 | tf_op jit(solution)/shard_map/ppermute | solution.py:338
  46.5 14.2 %copy-start.3 = (s32[1,2]{1,0:T(1,128)S(1)}, s32[1,2]{1,0:T(1,128)}, u32[]{:S(2)}) copy-start(s32[1,2]{1,0:T(1,128)} %starts_ref.3) | copy-start | bytes 28
  51.5 7.8 %collective-permute-start.13 = (bf16[24,16,640]{2,1,0:T(8,128)(2,1)S(1)}, bf16[24,16,640]{2,1,0:T(8,128)(2,1)S(1)}, u32[]{:S(2)}, u32[]{:S(2)}) collective-permute-start(bf16[24,16,640]{2,1,0:T(8,128)(2,1)S(1)} %constant_dynamic-update-slice_fusion.after_ref.refs_1_), channel_id=1, source_target_pairs={{0,1},{1,0},{2,3},{3,2},{4,5},{5,4},{6,7},{7,6},{8,9},{9,8},{10,11... | collective-permute-start | bytes 1474568 | tf_op jit(solution)/shard_map/ppermute | solution.py:338
  51.8 7.4 %collective-permute-start.16 = (bf16[24,16,640]{2,1,0:T(8,128)(2,1)S(1)}, bf16[24,16,640]{2,1,0:T(8,128)(2,1)S(1)}, u32[]{:S(2)}, u32[]{:S(2)}) collective-permute-start(bf16[24,16,640]{2,1,0:T(8,128)(2,1)S(1)} %collective-permute-done.8.refs_7_), channel_id=1, source_target_pairs={{0,1},{1,0},{2,3},{3,2},{4,5},{5,4},{6,7},{7,6},{8,9},{9,8},{10,11... | collective-permute-start | bytes 1474568 | tf_op jit(solution)/shard_map/ppermute | solution.py:338
  55.6 3.7 %collective-permute-start.15 = (bf16[24,16,640]{2,1,0:T(8,128)(2,1)S(1)}, bf16[24,16,640]{2,1,0:T(8,128)(2,1)S(1)}, u32[]{:S(2)}, u32[]{:S(2)}) collective-permute-start(bf16[24,16,640]{2,1,0:T(8,128)(2,1)S(1)} %collective-permute-done.7.refs_5_), channel_id=1, source_target_pairs={{0,1},{1,0},{2,3},{3,2},{4,5},{5,4},{6,7},{7,6},{8,9},{9,8},{10,11... | collective-permute-start | bytes 1474568 | tf_op jit(solution)/shard_map/ppermute | solution.py:338
  55.6 5.2 %collective-permute-start.14 = (bf16[24,16,640]{2,1,0:T(8,128)(2,1)S(1)}, bf16[24,16,640]{2,1,0:T(8,128)(2,1)S(1)}, u32[]{:S(2)}, u32[]{:S(2)}) collective-permute-start(bf16[24,16,640]{2,1,0:T(8,128)(2,1)S(1)} %collective-permute-done.6.refs_3_), channel_id=1, source_target_pairs={{0,1},{1,0},{2,3},{3,2},{4,5},{5,4},{6,7},{7,6},{8,9},{9,8},{10,11... | collective-permute-start | bytes 1474568 | tf_op jit(solution)/shard_map/ppermute | solution.py:338
  75.6 3.1 %collective-permute-start.17 = (bf16[64,16,640]{2,1,0:T(8,128)(2,1)S(1)}, bf16[64,16,640]{2,1,0:T(8,128)(2,1)S(1)}, u32[]{:S(2)}, u32[]{:S(2)}) collective-permute-start(bf16[64,16,640]{2,1,0:T(8,128)(2,1)S(1)} %get-tuple-element.48), channel_id=1, source_target_pairs={{0,1},{1,0},{2,3},{3,2},{4,5},{5,4},{6,7},{7,6},{8,9},{9,8},{10,11... | collective-permute-start | bytes 3932168 | tf_op jit(solution)/shard_map/ppermute | solution.py:338
  77.7 5.2 %collective-permute-start.21 = (bf16[64,16,640]{2,1,0:T(8,128)(2,1)S(1)}, bf16[64,16,640]{2,1,0:T(8,128)(2,1)S(1)}, u32[]{:S(2)}, u32[]{:S(2)}) collective-permute-start(bf16[64,16,640]{2,1,0:T(8,128)(2,1)S(1)} %get-tuple-element.52), channel_id=1, source_target_pairs={{0,1},{1,0},{2,3},{3,2},{4,5},{5,4},{6,7},{7,6},{8,9},{9,8},{10,11... | collective-permute-start | bytes 3932168 | tf_op jit(solution)/shard_map/ppermute | solution.py:338
  79.0 7.5 %collective-permute-start.18 = (bf16[16,16,640]{2,1,0:T(8,128)(2,1)S(1)}, bf16[16,16,640]{2,1,0:T(8,128)(2,1)S(1)}, u32[]{:S(2)}, u32[]{:S(2)}) collective-permute-start(bf16[16,16,640]{2,1,0:T(8,128)(2,1)S(1)} %get-tuple-element.55), channel_id=1, source_target_pairs={{0,4},{1,3},{4,8},{5,7},{8,12},{9,11},{12,0},{13,15},{2,6},{3,17},... | collective-permute-start | bytes 983048 | tf_op jit(solution)/shard_map/ppermute | solution.py:334
  79.1 10.3 %collective-permute-start.20 = (bf16[16,16,640]{2,1,0:T(8,128)(2,1)S(1)}, bf16[16,16,640]{2,1,0:T(8,128)(2,1)S(1)}, u32[]{:S(2)}, u32[]{:S(2)}) collective-permute-start(bf16[16,16,640]{2,1,0:T(8,128)(2,1)S(1)} %get-tuple-element.56), channel_id=1, source_target_pairs={{0,12},{1,19},{4,0},{5,23},{8,4},{9,27},{12,8},{13,31},{2,14},{3,1... | collective-permute-start | bytes 983048 | tf_op jit(solution)/shard_map/ppermute | solution.py:334
  81.8 9.2 %collective-permute-start.19 = (bf16[16,16,640]{2,1,0:T(8,128)(2,1)S(1)}, bf16[16,16,640]{2,1,0:T(8,128)(2,1)S(1)}, u32[]{:S(2)}, u32[]{:S(2)}) collective-permute-start(bf16[16,16,640]{2,1,0:T(8,128)(2,1)S(1)} %get-tuple-element.57), channel_id=1, source_target_pairs={{0,8},{1,17},{4,12},{5,21},{8,0},{9,25},{12,4},{13,29},{2,10},{3,1... | collective-permute-start | bytes 983048 | tf_op jit(solution)/shard_map/ppermute | solution.py:334
  83.2 11.0 %collective-permute-start.22 = (bf16[16,16,640]{2,1,0:T(8,128)(2,1)S(1)}, bf16[16,16,640]{2,1,0:T(8,128)(2,1)S(1)}, u32[]{:S(2)}, u32[]{:S(2)}) collective-permute-start(bf16[16,16,640]{2,1,0:T(8,128)(2,1)S(1)} %get-tuple-element.58), channel_id=1, source_target_pairs={{0,4},{1,3},{4,8},{5,7},{8,12},{9,11},{12,0},{13,15},{2,6},{3,17},... | collective-permute-start | bytes 983048 | tf_op jit(solution)/shard_map/ppermute | solution.py:334
  84.1 12.2 %collective-permute-start.24 = (bf16[16,16,640]{2,1,0:T(8,128)(2,1)S(1)}, bf16[16,16,640]{2,1,0:T(8,128)(2,1)S(1)}, u32[]{:S(2)}, u32[]{:S(2)}) collective-permute-start(bf16[16,16,640]{2,1,0:T(8,128)(2,1)S(1)} %get-tuple-element.59), channel_id=1, source_target_pairs={{0,12},{1,19},{4,0},{5,23},{8,4},{9,27},{12,8},{13,31},{2,14},{3,1... | collective-permute-start | bytes 983048 | tf_op jit(solution)/shard_map/ppermute | solution.py:334
  86.5 11.5 %collective-permute-start.23 = (bf16[16,16,640]{2,1,0:T(8,128)(2,1)S(1)}, bf16[16,16,640]{2,1,0:T(8,128)(2,1)S(1)}, u32[]{:S(2)}, u32[]{:S(2)}) collective-permute-start(bf16[16,16,640]{2,1,0:T(8,128)(2,1)S(1)} %get-tuple-element.60), channel_id=1, source_target_pairs={{0,8},{1,17},{4,12},{5,21},{8,0},{9,25},{12,4},{13,29},{2,10},{3,1... | collective-permute-start | bytes 983048 | tf_op jit(solution)/shard_map/ppermute | solution.py:334
  98.2 5.8 %collective-permute-start.25 = (bf16[8,16,640]{2,1,0:T(8,128)(2,1)S(1)}, bf16[8,16,640]{2,1,0:T(8,128)(2,1)S(1)}, u32[]{:S(2)}, u32[]{:S(2)}) collective-permute-start(bf16[8,16,640]{2,1,0:T(8,128)(2,1)S(1)} %get-tuple-element.61), channel_id=1, source_target_pairs={{0,2},{1,5},{4,6},{5,9},{8,10},{9,13},{12,14},{13,1},{2,16},{3,7},... | collective-permute-start | bytes 491528 | tf_op jit(solution)/shard_map/ppermute | solution.py:334
  98.3 6.7 %collective-permute-start.27 = (bf16[8,16,640]{2,1,0:T(8,128)(2,1)S(1)}, bf16[8,16,640]{2,1,0:T(8,128)(2,1)S(1)}, u32[]{:S(2)}, u32[]{:S(2)}) collective-permute-start(bf16[8,16,640]{2,1,0:T(8,128)(2,1)S(1)} %get-tuple-element.62), channel_id=1, source_target_pairs={{0,18},{1,13},{4,22},{5,1},{8,26},{9,5},{12,30},{13,9},{2,0},{3,15... | collective-permute-start | bytes 491528 | tf_op jit(solution)/shard_map/ppermute | solution.py:334
  101.0 6.0 %collective-permute-start.26 = (bf16[8,16,640]{2,1,0:T(8,128)(2,1)S(1)}, bf16[8,16,640]{2,1,0:T(8,128)(2,1)S(1)}, u32[]{:S(2)}, u32[]{:S(2)}) collective-permute-start(bf16[8,16,640]{2,1,0:T(8,128)(2,1)S(1)} %get-tuple-element.63), channel_id=1, source_target_pairs={{0,16},{1,9},{4,20},{5,13},{8,24},{9,1},{12,28},{13,5},{2,18},{3,1... | collective-permute-start | bytes 491528 | tf_op jit(solution)/shard_map/ppermute | solution.py:334
  117.8 5.6 %collective-permute-start.30 = (f32[16,640]{1,0:T(8,128)S(1)}, f32[16,640]{1,0:T(8,128)S(1)}, u32[]{:S(2)}, u32[]{:S(2)}) collective-permute-start(f32[16,640]{1,0:T(8,128)S(1)} %convert_reduce_fusion.refs_0_), channel_id=1, source_target_pairs={{0,3},{1,2},{2,1},{3,0},{4,7},{5,6},{6,5},{7,4},{8,11},{9,10},{10,... | collective-permute-start | bytes 122888 | tf_op jit(solution)/shard_map/ppermute | solution.py:408
  121.2 2.2 %collective-permute-start.29 = (f32[16,640]{1,0:T(8,128)S(1)}, f32[16,640]{1,0:T(8,128)S(1)}, u32[]{:S(2)}, u32[]{:S(2)}) collective-permute-start(f32[16,640]{1,0:T(8,128)S(1)} %convert_reduce_fusion.refs_0_), channel_id=1, source_target_pairs={{0,1},{1,0},{2,3},{3,2},{4,5},{5,4},{6,7},{7,6},{8,9},{9,8},{10,11... | collective-permute-start | bytes 122888 | tf_op jit(solution)/shard_map/ppermute | solution.py:408
  121.2 2.9 %collective-permute-start.28 = (f32[16,640]{1,0:T(8,128)S(1)}, f32[16,640]{1,0:T(8,128)S(1)}, u32[]{:S(2)}, u32[]{:S(2)}) collective-permute-start(f32[16,640]{1,0:T(8,128)S(1)} %convert_reduce_fusion.refs_0_), channel_id=1, source_target_pairs={{0,2},{1,3},{2,0},{3,1},{4,6},{5,7},{6,4},{7,5},{8,10},{9,11},{10,... | collective-permute-start | bytes 122888 | tf_op jit(solution)/shard_map/ppermute | solution.py:408

commit v7 on v6

--- a/solution.py
+++ b/solution.py
@@ -36,42 +36,34 @@
     py, px, pc = place[1], place[2], place[3]
     dxs = [((sign * (px - x)) & 3) * planes for x in range(4)]
     dys = [((sign * (py - y)) & 3) * planes for y in range(4)]
-
-    def flat(chunk, other, yl):
-        z, yh, x = chunk // 8 % planes, chunk // 4 % 2, chunk % 4
+    for x, yh, other, yl in itertools.product(range(4), range(2), range(2), range(2)):
         dx, dy = dxs[x], dys[yh * 2 + yl]
-        return jnp.where(pc == other, dx * 4 + dy, dy * 4 + dx) + z
-
-    return flat
-
-
-def down_gradient(chunks, grad_low, hid, held, outs, target):
-    origin = chunks[0] * DOWN // 128 * 128
-    stop = -(-(chunks[-1] + 1) * DOWN // 128) * 128
+        yield x, yh, other, yl, jnp.where(pc == other, dx * 4 + dy, dy * 4 + dx)
+
+
+def to_blocks(place, outs, first, up_share, grad_low, hid, held):
+    origin = first * DOWN // 128 * 128
+    stop = -(-(first + 32) * DOWN // 128) * 128
     for begin in range(origin, stop, 1024):
         end = min(begin + 1024, stop)
         held[:, begin - origin : end - origin] = dot(grad_low, hid[:, begin:end], NN).astype(BF)
-    for chunk in chunks:
-        begin = chunk * DOWN - origin
-        for q in range(4):
-            outs[q // 2][target(chunk, q // 2, q % 2), :, UP : UP + DOWN] = held[
-                16 * q : 16 * q + 16, begin : begin + DOWN
-            ]
+    for x, yh, other, yl, base in slots(place, -1, 4):
+        rows = slice(32 * other + 16 * yl, 32 * other + 16 * yl + 16)
+        for z in range(4):
+            chunk = z * 8 + yh * 4 + x
+            begin = (first + chunk) * DOWN - origin
+            outs[other][base + z, :, :UP] = up_share[rows, chunk * UP : chunk * UP + UP]
+            outs[other][base + z, :, UP:GAIN_AT] = held[rows, begin : begin + DOWN]
 
 
 def kernel(place_ref, starts_ref, *refs):
-    parts, (hid, fro, hea) = refs[:16], refs[16:19]
-    outs, up_rest, low_ref, margin_ref = refs[19:21], refs[21], refs[22], refs[23]
-    wt, up, gains, gain, pol, block, sems = refs[24:]
+    parts, (hid, fro, hea) = refs[:8], refs[8:11]
+    outs, up_rest, low_ref, margin_ref = refs[11:13], refs[13], refs[14], refs[15]
+    wt, up, gains, gain, pol, block, sems = refs[16:]
     width = fro.shape[1]
 
     loads = [
-        pltpu.make_async_copy(
-            parts[i],
-            block.at[pl.ds(32 * (i // 2) + 8 * (i % 2), 8 + 16 * (i % 2))],
-            sems.at[i],
-        )
-        for i in range(16)
+        pltpu.make_async_copy(parts[i], block.at[pl.ds(32 * i, 32)], sems.at[i]) for i in range(8)
     ]
     for copy in loads:
         copy.start()
@@ -97,13 +89,14 @@
     weight = jnp.where(row < 64, -BETA, BETA)
     slope = jnp.where(position >= start, weight, 0.0) / (1.0 + jnp.exp(margin))
 
-    source = slots(place_ref, 1, 8)
-    for chunk in range(CHUNKS):
-        for q in range(4):
-            held = block[(q // 2) * 128 + source(chunk, q // 2, q % 2)]
-            rows = slice(16 * q, 16 * q + 16)
+    for x, yh, other, yl, base in slots(place_ref, 1, 8):
+        q = other * 2 + yl
+        rows = slice(16 * q, 16 * q + 16)
+        for z in range(8):
+            chunk = z * 8 + yh * 4 + x
+            held = block[other * 128 + base + z]
             up[rows, chunk * UP : (chunk + 1) * UP] = held[:, :UP]
-            wt[rows, chunk * DOWN : (chunk + 1) * DOWN] = held[:, UP : UP + DOWN]
+            wt[rows, chunk * DOWN : (chunk + 1) * DOWN] = held[:, UP:GAIN_AT]
             gains[q, chunk : chunk + 1, :] = held[0:1, LANES - 128 :].astype(F32)
     lane = GAIN_AT - (LANES - 128)
     parts_of_gain = [gains[q][:, lane : lane + 32] for q in range(4)]
@@ -149,7 +142,6 @@
     first = slope / rms
     second = inner / (width * rms * rms * rms)
 
-    target = slots(place_ref, -1, 4)
     total = jnp.zeros((128, ORDER), F32)
     for i in range(width // step):
         at = slice(i * step, (i + 1) * step)
@@ -158,33 +150,28 @@
         rest = (grad - high.astype(F32)).astype(BF)
         total += dot(high, up[:, at], NT) + dot(rest, up[:, at], NT)
         share = (SCALE * dot(low_t, high, NN)).astype(BF)
-        if i * step >= width // 2:
+        if i * step < width // 2:
+            up[:, at] = share
+        else:
             up_rest[:, i * step - width // 2 : (i + 1) * step - width // 2] = share
-            continue
-        for j in range(step // 128):
-            for q in range(4):
-                outs[q // 2][target(i * (step // 128) + j, q // 2, q % 2), :, :UP] = share[
-                    16 * q : 16 * q + 16, 128 * j : 128 * j + 128
-                ]
     grad_low = (SCALE * total).T.astype(BF)
 
     low_ref[...] = grad_low
-    down_gradient(range(CHUNKS // 2), grad_low, hid, wt, outs, target)
+    to_blocks(place_ref, outs, 0, up, grad_low, hid, wt)
 
 
 def second_kernel(place_ref, low_ref, up_rest, hid, *refs):
-    outs, held = refs[:2], refs[2]
-    target = slots(place_ref, -1, 4)
-    chunks = range(CHUNKS // 2, CHUNKS)
-    for i, chunk in enumerate(chunks):
-        for q in range(4):
-            outs[q // 2][target(chunk, q // 2, q % 2), :, :UP] = up_rest[
-                16 * q : 16 * q + 16, UP * i : UP * i + UP
-            ]
-    down_gradient(chunks, low_ref[...], hid, held, outs, target)
-
-
-def pack(place_ref, starts_ref, ratio_ref, down_ref, up_ref, gain_ref, out_ref):
+    to_blocks(place_ref, refs[:2], CHUNKS // 2, up_rest, low_ref[...], hid, refs[2])
+
+
+def pack(place_ref, *refs):
+    out_ref, sems = refs[5], refs[11]
+    copies = [pltpu.make_async_copy(refs[i], refs[6 + i], sems.at[i]) for i in range(5)]
+    for copy in copies:
+        copy.start()
+    for copy in copies:
+        copy.wait()
+    starts_ref, ratio_ref, down_ref, up_ref, gain_ref = refs[6:11]
     yl, core = place_ref[1] & 1, place_ref[3]
     begin = pl.multiple_of(core * 32 + yl * 16, 16)
     position = lax.broadcasted_iota(jnp.int32, (2, 64), 1) + (yl * 2 + core) * 64
@@ -211,16 +198,19 @@
         out_ref[i, :, UP:GAIN_AT] = down_ref[rows, :]
 
 
-def packed(place, starts, ratio, down, up, gain):
-    smem = pl.BlockSpec(memory_space=pltpu.SMEM)
-    vmem = pl.BlockSpec(memory_space=pltpu.VMEM)
+def packed(place, starts, *arrays):
+    arrays = [starts, *arrays]
     return pl.pallas_call(
         pack,
         out_shape=jax.ShapeDtypeStruct((8, 16, LANES), BF),
-        in_specs=[smem, smem] + [vmem] * 4,
-        out_specs=vmem,
+        in_specs=[pl.BlockSpec(memory_space=pltpu.SMEM)]
+        + [pl.BlockSpec(memory_space=pl.ANY)] * 5,
+        out_specs=pl.BlockSpec(memory_space=pltpu.VMEM),
+        scratch_shapes=[pltpu.SMEM(starts.shape, starts.dtype)]
+        + [pltpu.VMEM(v.shape, v.dtype) for v in arrays[1:]]
+        + [pltpu.SemaphoreType.DMA((5,))],
         compiler_params=pltpu.CompilerParams(vmem_limit_bytes=4 * 1024 * 1024),
-    )(place, starts, ratio, down, up, gain)
+    )(place, *[pltpu.with_memory_space_constraint(v, pltpu.HBM) for v in arrays])
 
 
 def finish(place_ref, *refs):
@@ -287,7 +277,7 @@
             pltpu.VMEM((ORDER, rows), BF),
             jax.ShapeDtypeStruct((8, 128), F32),
         ],
-        in_specs=[smem, smem] + [any_space] * 16 + [vmem] * 3,
+        in_specs=[smem, smem] + [any_space] * 8 + [vmem] * 3,
         out_specs=[vmem] * 5,
         scratch_shapes=[
             pltpu.VMEM((ORDER, units), BF),
@@ -296,7 +286,7 @@
             pltpu.VMEM((CHUNKS, 128), F32),
             pltpu.VMEM((rows, width), F32),
             pltpu.VMEM((256, 16, LANES), BF),
-            pltpu.SemaphoreType.DMA((16,)),
+            pltpu.SemaphoreType.DMA((8,)),
         ],
         compiler_params=pltpu.CompilerParams(vmem_limit_bytes=20 * 1024 * 1024),
         cost_estimate=pl.CostEstimate(
@@ -364,30 +354,18 @@
         final_norm_gain[None],
     )
     held = lax.all_to_all(quarter, "z", 0, 0, tiled=True)
-    early = lax.optimization_barrier(
-        (
-            ring(held, 2),
-            *[ring(held, step, 1) for step in (1, 2, 3)],
-            ring(held, 1),
-            ring(held, 3),
-        )
-    )
-    side = jnp.concatenate(early[1:4])
-    own = [held, side, early[4], ring(side, 1)]
-    own += [early[0], ring(side, 2), early[5], ring(side, 3)]
+    line = jnp.concatenate([held] + [ring(held, step, 1) for step in (1, 2, 3)])
+    own = [line] + [ring(line, step) for step in (1, 2, 3)]
     width = frozen.shape[3]
     near = brought(
-        side,
+        line,
         place,
         gated_hidden_input.reshape(-1, gated_hidden_input.shape[3]),
         frozen.reshape(-1, width),
         head_gradient_rows.reshape(-1, width),
     )
-    small = [other_core(v) for v in own[::2]]
-    side, *rest = lax.optimization_barrier((side, *near, *small))
-    near, small = rest[:3], rest[3:]
-    large = [other_core(v) for v in (side, *own[3::2])]
-    other = [v for pair in zip(small, large) for v in pair]
+    line, *near = lax.optimization_barrier((line, *near))
+    other = [other_core(v) for v in (line, *own[1:])]
 
     first, second, margin = shares(place, starts, [*own, *other], *near)
 

time: 127 us -> 119 us (0.937)
  local copies, waits for them, and re-layouts: 4.12 us -> 0.6 us
  starting transfers between devices: 39.4 us -> 36.7 us
  Pallas kernels: 23.2 us -> 21.4 us
    unnamed x14 -> x5, local copies, waits for them, and re-layouts: 3.59 us -> 0.06 us
    ppermute x18 -> x15, starting transfers between devices: 21.3 us -> 17.8 us  [ring(): return lax.ppermute(values, FINE_AXES, pairs)]
    pallas_call x1, Pallas kernels: 14.8 us -> 12 us  [shares(): pl.pallas_call(kernel, out_shape=[pltpu.VMEM((64, 16, LANES), BF)] * 2 +...]
    ppermute x18 -> x15, waiting for transfers between devices: 24.1 us -> 25.1 us  [ring(): return lax.ppermute(values, FINE_AXES, pairs)]
    ppermute x10 -> x6, waiting for transfers between devices: 3.31 us -> 2.46 us  [other_core(): return lax.ppermute(values, 'c', [(0, 1), (1, 0)])]
    ppermute x10 -> x6, starting transfers between devices: 13.8 us -> 14.6 us  [other_core(): return lax.ppermute(values, 'c', [(0, 1), (1, 0)])]
  transfers between devices with their start and end apart: 31 -> 24, of which waited for: 17 -> 15; matrix products, arithmetic and copies ran while one was open for 1% -> 1% of each run, Pallas kernels for 5% -> 6%
where the time goes in v7:
time: 119 us; the launch traced here: 118 us
  starting transfers between devices  36.7 us (31%)
  waiting for transfers between devices  28.1 us (24%)
  blocking collectives  27.7 us (23%)
  Pallas kernels  21.4 us (18%)
  between operations  2.65 us (2%)
  other arithmetic  1.23 us (1%)
    ppermute x15, waiting for transfers between devices, ring(): return lax.ppermute(values, FINE_AXES, pairs)  25.1 us
    ppermute x15, starting transfers between devices, ring(): return lax.ppermute(values, FINE_AXES, pairs)  17.8 us
    all_to_all x1, blocking collectives, local(): held = lax.all_to_all(quarter, 'z', 0, 0, tiled=True)  17 us
    ppermute x6, starting transfers between devices, other_core(): return lax.ppermute(values, 'c', [(0, 1), (1, 0)])  14.6 us
    pallas_call x1, Pallas kernels, shares(): pl.pallas_call(kernel, out_shape=[pltpu.VMEM((64, 16, LANES), BF)] * 2 +...  12 us
    all_to_all x1, blocking collectives, local(): lax.all_to_all(plane, 'z', 0, 0, tiled=True).astype(F32)  10.7 us
    pallas_call x1, Pallas kernels, brought(): pl.pallas_call(bring, out_shape=[pltpu.VMEM(v.shape, v.dtype) for v in ar...  4.91 us
    ppermute x3, starting transfers between devices, local(): lax.ppermute(share, CTX, [(i, i ^ step) for i in range(4)])  4.36 us
  transfers between devices with their start and end apart: 24, of which 15 were waited for; matrix products, arithmetic and copies ran while one was open for 1% of the time, Pallas kernels for 6%

profile of v7, /device:TPU:1, one launch (start us, length us, event | category | flops | bytes accessed | tf_op | source)
XLA Modules:
  0.0 118.4 jit_solution(10316737693297562596)
XLA Ops:
  0.7 1.5 %shard_map.103 = bf16[8,16,640]{2,1,0:T(8,128)(2,1)S(1)} custom-call(s32[4]{0:T(128)S(1)} %pad_add_fusion.place_ref, s32[1,2]{1,0:T(1,128)} %starts_ref.1, f32[2,64]{1,0:T(2,128)} %bitcast.33, bf16[64,462]{1,0:T(8,128)(2,1)} %bitcast.32, bf16[64,128]{1,0:T(8,128)(2,1)} %refs_3_.1, bf16[1,128]{1,0:T(2,128)(2,1)} %bitcast.34), custom_call_target="tpu_custom_call" | custom-call | tf_op jit(solution)/shard_map/pallas_call | solution.py:203
  2.3 17.0 %all_to_all.10 = bf16[8,16,640]{2,1,0:T(8,128)(2,1)S(1)} all-to-all(bf16[8,16,640]{2,1,0:T(8,128)(2,1)S(1)} %shard_map.103), channel_id=1, replica_groups=mesh['z'=8,'yh'=2,'x'=4,'yl'=2,'c'=2] {'z'}, dimensions={0} | all-to-all | bytes 327680 | tf_op jit(solution)/shard_map/all_to_all | solution.py:356
  19.2 1.2 %collective-permute-start = (bf16[8,16,640]{2,1,0:T(8,128)(2,1)S(1)}, bf16[8,16,640]{2,1,0:T(8,128)(2,1)S(1)}, u32[]{:S(2)}, u32[]{:S(2)}) collective-permute-start(bf16[8,16,640]{2,1,0:T(8,128)(2,1)S(1)} %all_to_all.10), channel_id=1, source_target_pairs={{0,2},{1,5},{4,6},{5,9},{8,10},{9,13},{12,14},{13,1},{2,16},{3,7},... | collective-permute-start | bytes 491528 | tf_op jit(solution)/shard_map/ppermute | solution.py:324
  20.4 1.5 %collective-permute-start.2 = (bf16[8,16,640]{2,1,0:T(8,128)(2,1)S(1)}, bf16[8,16,640]{2,1,0:T(8,128)(2,1)S(1)}, u32[]{:S(2)}, u32[]{:S(2)}) collective-permute-start(bf16[8,16,640]{2,1,0:T(8,128)(2,1)S(1)} %all_to_all.10), channel_id=1, source_target_pairs={{0,18},{1,13},{4,22},{5,1},{8,26},{9,5},{12,30},{13,9},{2,0},{3,15... | collective-permute-start | bytes 491528 | tf_op jit(solution)/shard_map/ppermute | solution.py:324
  21.9 1.5 %collective-permute-start.1 = (bf16[8,16,640]{2,1,0:T(8,128)(2,1)S(1)}, bf16[8,16,640]{2,1,0:T(8,128)(2,1)S(1)}, u32[]{:S(2)}, u32[]{:S(2)}) collective-permute-start(bf16[8,16,640]{2,1,0:T(8,128)(2,1)S(1)} %all_to_all.10), channel_id=1, source_target_pairs={{0,16},{1,9},{4,20},{5,13},{8,24},{9,1},{12,28},{13,5},{2,18},{3,1... | collective-permute-start | bytes 491528 | tf_op jit(solution)/shard_map/ppermute | solution.py:324
  23.5 1.2 collective-permute-done
  24.6 2.9 %collective-permute-done.1 = bf16[8,16,640]{2,1,0:T(8,128)(2,1)S(1)} collective-permute-done((bf16[8,16,640]{2,1,0:T(8,128)(2,1)S(1)}, bf16[8,16,640]{2,1,0:T(8,128)(2,1)S(1)}, u32[]{:S(2)}, u32[]{:S(2)}) %collective-permute-start.1) | collective-permute-done | bytes 163872 | tf_op jit(solution)/shard_map/ppermute | solution.py:324
  27.7 2.8 %collective-permute-start.5 = (bf16[32,16,640]{2,1,0:T(8,128)(2,1)S(1)}, bf16[32,16,640]{2,1,0:T(8,128)(2,1)S(1)}, u32[]{:S(2)}, u32[]{:S(2)}) collective-permute-start(bf16[32,16,640]{2,1,0:T(8,128)(2,1)S(1)} %constant_dynamic-update-slice_fusion.after_ref.refs_0_), channel_id=1, source_target_pairs={{0,12},{1,19},{4,0},{5,23},{8,4},{9,27},{12,8},{13,31},{2,14},{3,1... | collective-permute-start | bytes 1966088 | tf_op jit(solution)/shard_map/ppermute | solution.py:324
  30.5 0.3 collective-permute-start.4
  30.8 0.7 collective-permute-start.3
  31.5 4.9 %shard_map.104 = (bf16[128,29568]{1,0:T(8,128)(2,1)S(1)}, bf16[128,8192]{1,0:T(8,128)(2,1)S(1)}, bf16[128,8192]{1,0:T(8,128)(2,1)S(1)}) custom-call(bf16[32,16,640]{2,1,0:T(8,128)(2,1)S(1)} %constant_dynamic-update-slice_fusion.after_ref.refs_0_, s32[4]{0:T(128)S(1)} %pad_add_fusion.place_ref, bf16[128,29568]{1,0:T(8,128)(2,1)} %bitcast.25, ...), custom_call_target="tpu_custom_call" | custom-call | bytes 23527424 | tf_op jit(solution)/shard_map/pallas_call | solution.py:251
  36.4 5.0 %collective-permute-start.6 = (bf16[32,16,640]{2,1,0:T(8,128)(2,1)S(1)}, bf16[32,16,640]{2,1,0:T(8,128)(2,1)S(1)}, u32[]{:S(2)}, u32[]{:S(2)}) collective-permute-start(bf16[32,16,640]{2,1,0:T(8,128)(2,1)S(1)} %constant_dynamic-update-slice_fusion.after_ref.refs_0_), channel_id=1, source_target_pairs={{0,1},{1,0},{2,3},{3,2},{4,5},{5,4},{6,7},{7,6},{8,9},{9,8},{10,11... | collective-permute-start | bytes 1966088 | tf_op jit(solution)/shard_map/ppermute | solution.py:328
  41.5 3.6 %collective-permute-done.5.refs_3_ = bf16[32,16,640]{2,1,0:T(8,128)(2,1)S(1)} collective-permute-done((bf16[32,16,640]{2,1,0:T(8,128)(2,1)S(1)}, bf16[32,16,640]{2,1,0:T(8,128)(2,1)S(1)}, u32[]{:S(2)}, u32[]{:S(2)}) %collective-permute-start.5) | collective-permute-done | bytes 655392 | tf_op jit(solution)/shard_map/ppermute | solution.py:324
  45.0 4.9 %collective-permute-start.9 = (bf16[32,16,640]{2,1,0:T(8,128)(2,1)S(1)}, bf16[32,16,640]{2,1,0:T(8,128)(2,1)S(1)}, u32[]{:S(2)}, u32[]{:S(2)}) collective-permute-start(bf16[32,16,640]{2,1,0:T(8,128)(2,1)S(1)} %collective-permute-done.5.refs_3_), channel_id=1, source_target_pairs={{0,1},{1,0},{2,3},{3,2},{4,5},{5,4},{6,7},{7,6},{8,9},{9,8},{10,11... | collective-permute-start | bytes 1966088 | tf_op jit(solution)/shard_map/ppermute | solution.py:328
  49.9 3.9 %collective-permute-start.7 = (bf16[32,16,640]{2,1,0:T(8,128)(2,1)S(1)}, bf16[32,16,640]{2,1,0:T(8,128)(2,1)S(1)}, u32[]{:S(2)}, u32[]{:S(2)}) collective-permute-start(bf16[32,16,640]{2,1,0:T(8,128)(2,1)S(1)} %collective-permute-done.3.refs_1_), channel_id=1, source_target_pairs={{0,1},{1,0},{2,3},{3,2},{4,5},{5,4},{6,7},{7,6},{8,9},{9,8},{10,11... | collective-permute-start | bytes 1966088 | tf_op jit(solution)/shard_map/ppermute | solution.py:328
  53.9 1.7 %collective-permute-done.7.refs_5_ = bf16[32,16,640]{2,1,0:T(8,128)(2,1)S(1)} collective-permute-done((bf16[32,16,640]{2,1,0:T(8,128)(2,1)S(1)}, bf16[32,16,640]{2,1,0:T(8,128)(2,1)S(1)}, u32[]{:S(2)}, u32[]{:S(2)}) %collective-permute-start.7) | collective-permute-done | bytes 655392 | tf_op jit(solution)/shard_map/ppermute | solution.py:328
  55.6 12.0 %shard_map.105 = (bf16[64,16,640]{2,1,0:T(8,128)(2,1)S(1)}, bf16[64,16,640]{2,1,0:T(8,128)(2,1)S(1)}, bf16[64,4096]{1,0:T(8,128)(2,1)S(1)}, bf16[64,128]{1,0:T(8,128)(2,1)S(1)}, f32[8,128]{1,0:T(8,128)S(1)}) custom-call(s32[4]{0:T(128)S(1)} %pad_add_fusion.place_ref, s32[1,2]{1,0:T(1,128)S(1)} %copy-done, ...), custom_call_target="tpu_custom_call" | custom-call | flops 1505755136 | bytes 22249472 | tf_op jit(solution)/shard_map/pallas_call | solution.py:272
  67.6 0.5 collective-permute-start.10
  68.1 1.7 %shard_map.106 = (bf16[64,16,640]{2,1,0:T(8,128)(2,1)S(1)}, bf16[64,16,640]{2,1,0:T(8,128)(2,1)S(1)}) custom-call(s32[4]{0:T(128)S(1)} %pad_add_fusion.place_ref, bf16[64,128]{1,0:T(8,128)(2,1)S(1)} %get-tuple-element.29.low_ref, bf16[64,4096]{1,0:T(8,128)(2,1)S(1)} %get-tuple-element.30.up_rest, bf16[128,29568]{1,0:T(8,128)(2,1)S(1)} %get-tuple-element.23.refs_8_.hid), custom_call_target="tpu_custom_call" | custom-call | flops 242221056 | bytes 6406144 | tf_op jit(solution)/shard_map/pallas_call | solution.py:298
  69.8 0.2 collective-permute-start.14
  70.0 0.7 collective-permute-done.10
  70.8 0.3 add_convert_fusion.8
  71.0 1.0 collective-permute-start.11
  72.0 1.8 %collective-permute-start.13 = (bf16[16,16,640]{2,1,0:T(8,128)(2,1)S(1)}, bf16[16,16,640]{2,1,0:T(8,128)(2,1)S(1)}, u32[]{:S(2)}, u32[]{:S(2)}) collective-permute-start(bf16[16,16,640]{2,1,0:T(8,128)(2,1)S(1)} %get-tuple-element.36), channel_id=1, source_target_pairs={{0,12},{1,19},{4,0},{5,23},{8,4},{9,27},{12,8},{13,31},{2,14},{3,1... | collective-permute-start | bytes 983048 | tf_op jit(solution)/shard_map/ppermute | solution.py:324
  73.8 1.0 collective-permute-start.12
  74.8 0.2 add_convert_fusion.3
  75.0 0.9 collective-permute-start.15
  76.0 1.8 %collective-permute-start.17 = (bf16[16,16,640]{2,1,0:T(8,128)(2,1)S(1)}, bf16[16,16,640]{2,1,0:T(8,128)(2,1)S(1)}, u32[]{:S(2)}, u32[]{:S(2)}) collective-permute-start(bf16[16,16,640]{2,1,0:T(8,128)(2,1)S(1)} %get-tuple-element.39), channel_id=1, source_target_pairs={{0,12},{1,19},{4,0},{5,23},{8,4},{9,27},{12,8},{13,31},{2,14},{3,1... | collective-permute-start | bytes 983048 | tf_op jit(solution)/shard_map/ppermute | solution.py:324
  77.8 0.8 collective-permute-done.11
  78.6 0.5 collective-permute-start.16
  79.0 2.3 %collective-permute-done.13 = bf16[16,16,640]{2,1,0:T(8,128)(2,1)S(1)} collective-permute-done((bf16[16,16,640]{2,1,0:T(8,128)(2,1)S(1)}, bf16[16,16,640]{2,1,0:T(8,128)(2,1)S(1)}, u32[]{:S(2)}, u32[]{:S(2)}) %collective-permute-start.13) | collective-permute-done | bytes 327712 | tf_op jit(solution)/shard_map/ppermute | solution.py:324
  81.3 1.6 %collective-permute-done.12 = bf16[16,16,640]{2,1,0:T(8,128)(2,1)S(1)} collective-permute-done((bf16[16,16,640]{2,1,0:T(8,128)(2,1)S(1)}, bf16[16,16,640]{2,1,0:T(8,128)(2,1)S(1)}, u32[]{:S(2)}, u32[]{:S(2)}) %collective-permute-start.12) | collective-permute-done | bytes 327712 | tf_op jit(solution)/shard_map/ppermute | solution.py:324
  83.0 0.2 add_convert_fusion.5
  83.2 2.9 %collective-permute-done.15 = bf16[16,16,640]{2,1,0:T(8,128)(2,1)S(1)} collective-permute-done((bf16[16,16,640]{2,1,0:T(8,128)(2,1)S(1)}, bf16[16,16,640]{2,1,0:T(8,128)(2,1)S(1)}, u32[]{:S(2)}, u32[]{:S(2)}) %collective-permute-start.15) | collective-permute-done | bytes 327712 | tf_op jit(solution)/shard_map/ppermute | solution.py:324
  86.1 2.3 %collective-permute-done.17 = bf16[16,16,640]{2,1,0:T(8,128)(2,1)S(1)} collective-permute-done((bf16[16,16,640]{2,1,0:T(8,128)(2,1)S(1)}, bf16[16,16,640]{2,1,0:T(8,128)(2,1)S(1)}, u32[]{:S(2)}, u32[]{:S(2)}) %collective-permute-start.17) | collective-permute-done | bytes 327712 | tf_op jit(solution)/shard_map/ppermute | solution.py:324
  88.3 1.6 %collective-permute-done.16 = bf16[16,16,640]{2,1,0:T(8,128)(2,1)S(1)} collective-permute-done((bf16[16,16,640]{2,1,0:T(8,128)(2,1)S(1)}, bf16[16,16,640]{2,1,0:T(8,128)(2,1)S(1)}, u32[]{:S(2)}, u32[]{:S(2)}) %collective-permute-start.16) | collective-permute-done | bytes 327712 | tf_op jit(solution)/shard_map/ppermute | solution.py:324
  90.0 0.2 add_convert_fusion
  90.4 2.7 %collective-permute-start.20 = (bf16[8,16,640]{2,1,0:T(8,128)(2,1)S(1)}, bf16[8,16,640]{2,1,0:T(8,128)(2,1)S(1)}, u32[]{:S(2)}, u32[]{:S(2)}) collective-permute-start(bf16[8,16,640]{2,1,0:T(8,128)(2,1)S(1)} %get-tuple-element.42), channel_id=1, source_target_pairs={{0,18},{1,13},{4,22},{5,1},{8,26},{9,5},{12,30},{13,9},{2,0},{3,15... | collective-permute-start | bytes 491528 | tf_op jit(solution)/shard_map/ppermute | solution.py:324
  93.0 3.0 %collective-permute-done.18 = bf16[8,16,640]{2,1,0:T(8,128)(2,1)S(1)} collective-permute-done((bf16[8,16,640]{2,1,0:T(8,128)(2,1)S(1)}, bf16[8,16,640]{2,1,0:T(8,128)(2,1)S(1)}, u32[]{:S(2)}, u32[]{:S(2)}) %collective-permute-start.18) | collective-permute-done | bytes 163872 | tf_op jit(solution)/shard_map/ppermute | solution.py:324
  96.0 1.0 collective-permute-done.20
  97.1 1.9 %collective-permute-done.19 = bf16[8,16,640]{2,1,0:T(8,128)(2,1)S(1)} collective-permute-done((bf16[8,16,640]{2,1,0:T(8,128)(2,1)S(1)}, bf16[8,16,640]{2,1,0:T(8,128)(2,1)S(1)}, u32[]{:S(2)}, u32[]{:S(2)}) %collective-permute-start.19) | collective-permute-done | bytes 163872 | tf_op jit(solution)/shard_map/ppermute | solution.py:324
  99.0 0.1 fusion.2
  99.1 10.7 %all_to_all.11 = bf16[8,16,640]{2,1,0:T(8,128)(2,1)S(1)} all-to-all(bf16[8,16,640]{2,1,0:T(8,128)(2,1)S(1)} %fusion.2), channel_id=1, replica_groups=mesh['z'=8,'yh'=2,'x'=4,'yl'=2,'c'=2] {'z'}, dimensions={0} | all-to-all | bytes 327680 | tf_op jit(solution)/shard_map/all_to_all | solution.py:384
  109.8 3.3 %collective-permute-start.23 = (f32[16,640]{1,0:T(8,128)S(1)}, f32[16,640]{1,0:T(8,128)S(1)}, u32[]{:S(2)}, u32[]{:S(2)}) collective-permute-start(f32[16,640]{1,0:T(8,128)S(1)} %convert_reduce_fusion.refs_0_), channel_id=1, source_target_pairs={{0,3},{1,2},{2,1},{3,0},{4,7},{5,6},{6,5},{7,4},{8,11},{9,10},{10,... | collective-permute-start | bytes 122888 | tf_op jit(solution)/shard_map/ppermute | solution.py:386
  113.1 1.1 collective-permute-start.21
  114.2 0.5 slice.63
  115.5 0.5 collective-permute-done.21.refs_1_
  116.0 1.2 %shard_map.107 = (f32[64,462]{1,0:T(8,128)}, f32[64,128]{1,0:T(8,128)}) custom-call(s32[4]{0:T(128)S(1)} %pad_add_fusion.place_ref, f32[16,640]{1,0:T(8,128)S(1)} %convert_reduce_fusion.refs_0_, f32[16,640]{1,0:T(8,128)S(1)} %collective-permute-done.21.refs_1_, f32[16,640]{1,0:T(8,128)S(1)} %collective-permute-done.22.refs_2_, ...), custom_call_target="tpu_custom_call" | custom-call | tf_op jit(solution)/shard_map/pallas_call | solution.py:227
  (22 shorter events, 0.4 us)
Async XLA Ops:
  19.2 5.4 %collective-permute-start = (bf16[8,16,640]{2,1,0:T(8,128)(2,1)S(1)}, bf16[8,16,640]{2,1,0:T(8,128)(2,1)S(1)}, u32[]{:S(2)}, u32[]{:S(2)}) collective-permute-start(bf16[8,16,640]{2,1,0:T(8,128)(2,1)S(1)} %all_to_all.10), channel_id=1, source_target_pairs={{0,2},{1,5},{4,6},{5,9},{8,10},{9,13},{12,14},{13,1},{2,16},{3,7},... | collective-permute-start | bytes 491528 | tf_op jit(solution)/shard_map/ppermute | solution.py:324
  20.4 7.2 %collective-permute-start.2 = (bf16[8,16,640]{2,1,0:T(8,128)(2,1)S(1)}, bf16[8,16,640]{2,1,0:T(8,128)(2,1)S(1)}, u32[]{:S(2)}, u32[]{:S(2)}) collective-permute-start(bf16[8,16,640]{2,1,0:T(8,128)(2,1)S(1)} %all_to_all.10), channel_id=1, source_target_pairs={{0,18},{1,13},{4,22},{5,1},{8,26},{9,5},{12,30},{13,9},{2,0},{3,15... | collective-permute-start | bytes 491528 | tf_op jit(solution)/shard_map/ppermute | solution.py:324
  21.9 5.7 %collective-permute-start.1 = (bf16[8,16,640]{2,1,0:T(8,128)(2,1)S(1)}, bf16[8,16,640]{2,1,0:T(8,128)(2,1)S(1)}, u32[]{:S(2)}, u32[]{:S(2)}) collective-permute-start(bf16[8,16,640]{2,1,0:T(8,128)(2,1)S(1)} %all_to_all.10), channel_id=1, source_target_pairs={{0,16},{1,9},{4,20},{5,13},{8,24},{9,1},{12,28},{13,5},{2,18},{3,1... | collective-permute-start | bytes 491528 | tf_op jit(solution)/shard_map/ppermute | solution.py:324
  27.7 17.4 %collective-permute-start.5 = (bf16[32,16,640]{2,1,0:T(8,128)(2,1)S(1)}, bf16[32,16,640]{2,1,0:T(8,128)(2,1)S(1)}, u32[]{:S(2)}, u32[]{:S(2)}) collective-permute-start(bf16[32,16,640]{2,1,0:T(8,128)(2,1)S(1)} %constant_dynamic-update-slice_fusion.after_ref.refs_0_), channel_id=1, source_target_pairs={{0,12},{1,19},{4,0},{5,23},{8,4},{9,27},{12,8},{13,31},{2,14},{3,1... | collective-permute-start | bytes 1966088 | tf_op jit(solution)/shard_map/ppermute | solution.py:324
  30.5 19.5 %collective-permute-start.4 = (bf16[32,16,640]{2,1,0:T(8,128)(2,1)S(1)}, bf16[32,16,640]{2,1,0:T(8,128)(2,1)S(1)}, u32[]{:S(2)}, u32[]{:S(2)}) collective-permute-start(bf16[32,16,640]{2,1,0:T(8,128)(2,1)S(1)} %constant_dynamic-update-slice_fusion.after_ref.refs_0_), channel_id=1, source_target_pairs={{0,8},{1,17},{4,12},{5,21},{8,0},{9,25},{12,4},{13,29},{2,10},{3,1... | collective-permute-start | bytes 1966088 | tf_op jit(solution)/shard_map/ppermute | solution.py:324
  30.8 19.1 %collective-permute-start.3 = (bf16[32,16,640]{2,1,0:T(8,128)(2,1)S(1)}, bf16[32,16,640]{2,1,0:T(8,128)(2,1)S(1)}, u32[]{:S(2)}, u32[]{:S(2)}) collective-permute-start(bf16[32,16,640]{2,1,0:T(8,128)(2,1)S(1)} %constant_dynamic-update-slice_fusion.after_ref.refs_0_), channel_id=1, source_target_pairs={{0,4},{1,3},{4,8},{5,7},{8,12},{9,11},{12,0},{13,15},{2,6},{3,17},... | collective-permute-start | bytes 1966088 | tf_op jit(solution)/shard_map/ppermute | solution.py:324
  31.5 24.1 %copy-start = (s32[1,2]{1,0:T(1,128)S(1)}, s32[1,2]{1,0:T(1,128)}, u32[]{:S(2)}) copy-start(s32[1,2]{1,0:T(1,128)} %starts_ref.1) | copy-start | bytes 28
  36.4 17.5 %collective-permute-start.6 = (bf16[32,16,640]{2,1,0:T(8,128)(2,1)S(1)}, bf16[32,16,640]{2,1,0:T(8,128)(2,1)S(1)}, u32[]{:S(2)}, u32[]{:S(2)}) collective-permute-start(bf16[32,16,640]{2,1,0:T(8,128)(2,1)S(1)} %constant_dynamic-update-slice_fusion.after_ref.refs_0_), channel_id=1, source_target_pairs={{0,1},{1,0},{2,3},{3,2},{4,5},{5,4},{6,7},{7,6},{8,9},{9,8},{10,11... | collective-permute-start | bytes 1966088 | tf_op jit(solution)/shard_map/ppermute | solution.py:328
  45.0 8.9 %collective-permute-start.9 = (bf16[32,16,640]{2,1,0:T(8,128)(2,1)S(1)}, bf16[32,16,640]{2,1,0:T(8,128)(2,1)S(1)}, u32[]{:S(2)}, u32[]{:S(2)}) collective-permute-start(bf16[32,16,640]{2,1,0:T(8,128)(2,1)S(1)} %collective-permute-done.5.refs_3_), channel_id=1, source_target_pairs={{0,1},{1,0},{2,3},{3,2},{4,5},{5,4},{6,7},{7,6},{8,9},{9,8},{10,11... | collective-permute-start | bytes 1966088 | tf_op jit(solution)/shard_map/ppermute | solution.py:328
  49.9 4.0 %collective-permute-start.8 = (bf16[32,16,640]{2,1,0:T(8,128)(2,1)S(1)}, bf16[32,16,640]{2,1,0:T(8,128)(2,1)S(1)}, u32[]{:S(2)}, u32[]{:S(2)}) collective-permute-start(bf16[32,16,640]{2,1,0:T(8,128)(2,1)S(1)} %collective-permute-done.4.refs_2_), channel_id=1, source_target_pairs={{0,1},{1,0},{2,3},{3,2},{4,5},{5,4},{6,7},{7,6},{8,9},{9,8},{10,11... | collective-permute-start | bytes 1966088 | tf_op jit(solution)/shard_map/ppermute | solution.py:328
  49.9 5.7 %collective-permute-start.7 = (bf16[32,16,640]{2,1,0:T(8,128)(2,1)S(1)}, bf16[32,16,640]{2,1,0:T(8,128)(2,1)S(1)}, u32[]{:S(2)}, u32[]{:S(2)}) collective-permute-start(bf16[32,16,640]{2,1,0:T(8,128)(2,1)S(1)} %collective-permute-done.3.refs_1_), channel_id=1, source_target_pairs={{0,1},{1,0},{2,3},{3,2},{4,5},{5,4},{6,7},{7,6},{8,9},{9,8},{10,11... | collective-permute-start | bytes 1966088 | tf_op jit(solution)/shard_map/ppermute | solution.py:328
  67.6 3.1 %collective-permute-start.10 = (bf16[64,16,640]{2,1,0:T(8,128)(2,1)S(1)}, bf16[64,16,640]{2,1,0:T(8,128)(2,1)S(1)}, u32[]{:S(2)}, u32[]{:S(2)}) collective-permute-start(bf16[64,16,640]{2,1,0:T(8,128)(2,1)S(1)} %get-tuple-element.28), channel_id=1, source_target_pairs={{0,1},{1,0},{2,3},{3,2},{4,5},{5,4},{6,7},{7,6},{8,9},{9,8},{10,11... | collective-permute-start | bytes 3932168 | tf_op jit(solution)/shard_map/ppermute | solution.py:328
  69.8 5.0 %collective-permute-start.14 = (bf16[64,16,640]{2,1,0:T(8,128)(2,1)S(1)}, bf16[64,16,640]{2,1,0:T(8,128)(2,1)S(1)}, u32[]{:S(2)}, u32[]{:S(2)}) collective-permute-start(bf16[64,16,640]{2,1,0:T(8,128)(2,1)S(1)} %get-tuple-element.32), channel_id=1, source_target_pairs={{0,1},{1,0},{2,3},{3,2},{4,5},{5,4},{6,7},{7,6},{8,9},{9,8},{10,11... | collective-permute-start | bytes 3932168 | tf_op jit(solution)/shard_map/ppermute | solution.py:328
  71.0 7.5 %collective-permute-start.11 = (bf16[16,16,640]{2,1,0:T(8,128)(2,1)S(1)}, bf16[16,16,640]{2,1,0:T(8,128)(2,1)S(1)}, u32[]{:S(2)}, u32[]{:S(2)}) collective-permute-start(bf16[16,16,640]{2,1,0:T(8,128)(2,1)S(1)} %get-tuple-element.35), channel_id=1, source_target_pairs={{0,4},{1,3},{4,8},{5,7},{8,12},{9,11},{12,0},{13,15},{2,6},{3,17},... | collective-permute-start | bytes 983048 | tf_op jit(solution)/shard_map/ppermute | solution.py:324
  72.0 9.3 %collective-permute-start.13 = (bf16[16,16,640]{2,1,0:T(8,128)(2,1)S(1)}, bf16[16,16,640]{2,1,0:T(8,128)(2,1)S(1)}, u32[]{:S(2)}, u32[]{:S(2)}) collective-permute-start(bf16[16,16,640]{2,1,0:T(8,128)(2,1)S(1)} %get-tuple-element.36), channel_id=1, source_target_pairs={{0,12},{1,19},{4,0},{5,23},{8,4},{9,27},{12,8},{13,31},{2,14},{3,1... | collective-permute-start | bytes 983048 | tf_op jit(solution)/shard_map/ppermute | solution.py:324
  73.8 9.2 %collective-permute-start.12 = (bf16[16,16,640]{2,1,0:T(8,128)(2,1)S(1)}, bf16[16,16,640]{2,1,0:T(8,128)(2,1)S(1)}, u32[]{:S(2)}, u32[]{:S(2)}) collective-permute-start(bf16[16,16,640]{2,1,0:T(8,128)(2,1)S(1)} %get-tuple-element.37), channel_id=1, source_target_pairs={{0,8},{1,17},{4,12},{5,21},{8,0},{9,25},{12,4},{13,29},{2,10},{3,1... | collective-permute-start | bytes 983048 | tf_op jit(solution)/shard_map/ppermute | solution.py:324
  75.0 11.0 %collective-permute-start.15 = (bf16[16,16,640]{2,1,0:T(8,128)(2,1)S(1)}, bf16[16,16,640]{2,1,0:T(8,128)(2,1)S(1)}, u32[]{:S(2)}, u32[]{:S(2)}) collective-permute-start(bf16[16,16,640]{2,1,0:T(8,128)(2,1)S(1)} %get-tuple-element.38), channel_id=1, source_target_pairs={{0,4},{1,3},{4,8},{5,7},{8,12},{9,11},{12,0},{13,15},{2,6},{3,17},... | collective-permute-start | bytes 983048 | tf_op jit(solution)/shard_map/ppermute | solution.py:324
  76.0 12.4 %collective-permute-start.17 = (bf16[16,16,640]{2,1,0:T(8,128)(2,1)S(1)}, bf16[16,16,640]{2,1,0:T(8,128)(2,1)S(1)}, u32[]{:S(2)}, u32[]{:S(2)}) collective-permute-start(bf16[16,16,640]{2,1,0:T(8,128)(2,1)S(1)} %get-tuple-element.39), channel_id=1, source_target_pairs={{0,12},{1,19},{4,0},{5,23},{8,4},{9,27},{12,8},{13,31},{2,14},{3,1... | collective-permute-start | bytes 983048 | tf_op jit(solution)/shard_map/ppermute | solution.py:324
  78.6 11.4 %collective-permute-start.16 = (bf16[16,16,640]{2,1,0:T(8,128)(2,1)S(1)}, bf16[16,16,640]{2,1,0:T(8,128)(2,1)S(1)}, u32[]{:S(2)}, u32[]{:S(2)}) collective-permute-start(bf16[16,16,640]{2,1,0:T(8,128)(2,1)S(1)} %get-tuple-element.40), channel_id=1, source_target_pairs={{0,8},{1,17},{4,12},{5,21},{8,0},{9,25},{12,4},{13,29},{2,10},{3,1... | collective-permute-start | bytes 983048 | tf_op jit(solution)/shard_map/ppermute | solution.py:324
  90.3 5.8 %collective-permute-start.18 = (bf16[8,16,640]{2,1,0:T(8,128)(2,1)S(1)}, bf16[8,16,640]{2,1,0:T(8,128)(2,1)S(1)}, u32[]{:S(2)}, u32[]{:S(2)}) collective-permute-start(bf16[8,16,640]{2,1,0:T(8,128)(2,1)S(1)} %get-tuple-element.41), channel_id=1, source_target_pairs={{0,2},{1,5},{4,6},{5,9},{8,10},{9,13},{12,14},{13,1},{2,16},{3,7},... | collective-permute-start | bytes 491528 | tf_op jit(solution)/shard_map/ppermute | solution.py:324
  90.4 6.7 %collective-permute-start.20 = (bf16[8,16,640]{2,1,0:T(8,128)(2,1)S(1)}, bf16[8,16,640]{2,1,0:T(8,128)(2,1)S(1)}, u32[]{:S(2)}, u32[]{:S(2)}) collective-permute-start(bf16[8,16,640]{2,1,0:T(8,128)(2,1)S(1)} %get-tuple-element.42), channel_id=1, source_target_pairs={{0,18},{1,13},{4,22},{5,1},{8,26},{9,5},{12,30},{13,9},{2,0},{3,15... | collective-permute-start | bytes 491528 | tf_op jit(solution)/shard_map/ppermute | solution.py:324
  93.0 6.0 %collective-permute-start.19 = (bf16[8,16,640]{2,1,0:T(8,128)(2,1)S(1)}, bf16[8,16,640]{2,1,0:T(8,128)(2,1)S(1)}, u32[]{:S(2)}, u32[]{:S(2)}) collective-permute-start(bf16[8,16,640]{2,1,0:T(8,128)(2,1)S(1)} %get-tuple-element.43), channel_id=1, source_target_pairs={{0,16},{1,9},{4,20},{5,13},{8,24},{9,1},{12,28},{13,5},{2,18},{3,1... | collective-permute-start | bytes 491528 | tf_op jit(solution)/shard_map/ppermute | solution.py:324
  109.8 5.6 %collective-permute-start.23 = (f32[16,640]{1,0:T(8,128)S(1)}, f32[16,640]{1,0:T(8,128)S(1)}, u32[]{:S(2)}, u32[]{:S(2)}) collective-permute-start(f32[16,640]{1,0:T(8,128)S(1)} %convert_reduce_fusion.refs_0_), channel_id=1, source_target_pairs={{0,3},{1,2},{2,1},{3,0},{4,7},{5,6},{6,5},{7,4},{8,11},{9,10},{10,... | collective-permute-start | bytes 122888 | tf_op jit(solution)/shard_map/ppermute | solution.py:386
  113.1 2.4 %collective-permute-start.22 = (f32[16,640]{1,0:T(8,128)S(1)}, f32[16,640]{1,0:T(8,128)S(1)}, u32[]{:S(2)}, u32[]{:S(2)}) collective-permute-start(f32[16,640]{1,0:T(8,128)S(1)} %convert_reduce_fusion.refs_0_), channel_id=1, source_target_pairs={{0,1},{1,0},{2,3},{3,2},{4,5},{5,4},{6,7},{7,6},{8,9},{9,8},{10,11... | collective-permute-start | bytes 122888 | tf_op jit(solution)/shard_map/ppermute | solution.py:386
  113.1 2.9 %collective-permute-start.21 = (f32[16,640]{1,0:T(8,128)S(1)}, f32[16,640]{1,0:T(8,128)S(1)}, u32[]{:S(2)}, u32[]{:S(2)}) collective-permute-start(f32[16,640]{1,0:T(8,128)S(1)} %convert_reduce_fusion.refs_0_), channel_id=1, source_target_pairs={{0,2},{1,3},{2,0},{3,1},{4,6},{5,7},{6,4},{7,5},{8,10},{9,11},{10,... | collective-permute-start | bytes 122888 | tf_op jit(solution)/shard_map/ppermute | solution.py:386

commit v8 on v7

--- a/solution.py
+++ b/solution.py
@@ -32,13 +32,13 @@
     return lax.dot_general(a, b, dims, preferred_element_type=F32)
 
 
-def slots(place, sign, planes):
+def slots(place, sign, planes, other):
     py, px, pc = place[1], place[2], place[3]
     dxs = [((sign * (px - x)) & 3) * planes for x in range(4)]
     dys = [((sign * (py - y)) & 3) * planes for y in range(4)]
-    for x, yh, other, yl in itertools.product(range(4), range(2), range(2), range(2)):
+    for x, yh, yl in itertools.product(range(4), range(2), range(2)):
         dx, dy = dxs[x], dys[yh * 2 + yl]
-        yield x, yh, other, yl, jnp.where(pc == other, dx * 4 + dy, dy * 4 + dx)
+        yield x, yh, yl, jnp.where(pc == other, dx * 4 + dy, dy * 4 + dx)
 
 
 def to_blocks(place, outs, first, up_share, grad_low, hid, held):
@@ -47,28 +47,40 @@
     for begin in range(origin, stop, 1024):
         end = min(begin + 1024, stop)
         held[:, begin - origin : end - origin] = dot(grad_low, hid[:, begin:end], NN).astype(BF)
-    for x, yh, other, yl, base in slots(place, -1, 4):
-        rows = slice(32 * other + 16 * yl, 32 * other + 16 * yl + 16)
-        for z in range(4):
-            chunk = z * 8 + yh * 4 + x
-            begin = (first + chunk) * DOWN - origin
-            outs[other][base + z, :, :UP] = up_share[rows, chunk * UP : chunk * UP + UP]
-            outs[other][base + z, :, UP:GAIN_AT] = held[rows, begin : begin + DOWN]
+    for other in range(2):
+        for x, yh, yl, base in slots(place, -1, 4, other):
+            rows = slice(32 * other + 16 * yl, 32 * other + 16 * yl + 16)
+            for z in range(4):
+                chunk = z * 8 + yh * 4 + x
+                begin = (first + chunk) * DOWN - origin
+                outs[other][base + z, :, :UP] = up_share[rows, chunk * UP : chunk * UP + UP]
+                outs[other][base + z, :, UP:GAIN_AT] = held[rows, begin : begin + DOWN]
 
 
 def kernel(place_ref, starts_ref, *refs):
-    parts, (hid, fro, hea) = refs[:8], refs[8:11]
-    outs, up_rest, low_ref, margin_ref = refs[11:13], refs[13], refs[14], refs[15]
-    wt, up, gains, gain, pol, block, sems = refs[16:]
+    parts, (hid, fro, hea) = refs[:16], refs[16:19]
+    outs, up_rest, low_ref, margin_ref = refs[19:21], refs[21], refs[22], refs[23]
+    wt, up, gains, gain, pol, block, sems = refs[24:]
     width = fro.shape[1]
 
     loads = [
-        pltpu.make_async_copy(parts[i], block.at[pl.ds(32 * i, 32)], sems.at[i]) for i in range(8)
+        pltpu.make_async_copy(parts[i], block.at[pl.ds(16 * i, 16)], sems.at[i]) for i in range(16)
     ]
     for copy in loads:
         copy.start()
-    for copy in loads:
-        copy.wait()
+
+    for other in range(2):
+        for copy in loads[8 * other : 8 * other + 8]:
+            copy.wait()
+        for x, yh, yl, base in slots(place_ref, 1, 8, other):
+            q = other * 2 + yl
+            rows = slice(16 * q, 16 * q + 16)
+            for z in range(8):
+                chunk = z * 8 + yh * 4 + x
+                held = block[other * 128 + base + z]
+                up[rows, chunk * UP : (chunk + 1) * UP] = held[:, :UP]
+                wt[rows, chunk * DOWN : (chunk + 1) * DOWN] = held[:, UP:GAIN_AT]
+                gains[q, chunk : chunk + 1, :] = held[0:1, LANES - 128 :].astype(F32)
 
     pz, py, px, pc = (place_ref[i] for i in range(4))
     sums = jnp.zeros((1, 128), F32)
@@ -89,15 +101,6 @@
     weight = jnp.where(row < 64, -BETA, BETA)
     slope = jnp.where(position >= start, weight, 0.0) / (1.0 + jnp.exp(margin))
 
-    for x, yh, other, yl, base in slots(place_ref, 1, 8):
-        q = other * 2 + yl
-        rows = slice(16 * q, 16 * q + 16)
-        for z in range(8):
-            chunk = z * 8 + yh * 4 + x
-            held = block[other * 128 + base + z]
-            up[rows, chunk * UP : (chunk + 1) * UP] = held[:, :UP]
-            wt[rows, chunk * DOWN : (chunk + 1) * DOWN] = held[:, UP:GAIN_AT]
-            gains[q, chunk : chunk + 1, :] = held[0:1, LANES - 128 :].astype(F32)
     lane = GAIN_AT - (LANES - 128)
     parts_of_gain = [gains[q][:, lane : lane + 32] for q in range(4)]
     ordered = jnp.concatenate(parts_of_gain, axis=1)
@@ -277,7 +280,7 @@
             pltpu.VMEM((ORDER, rows), BF),
             jax.ShapeDtypeStruct((8, 128), F32),
         ],
-        in_specs=[smem, smem] + [any_space] * 8 + [vmem] * 3,
+        in_specs=[smem, smem] + [any_space] * 16 + [vmem] * 3,
         out_specs=[vmem] * 5,
         scratch_shapes=[
             pltpu.VMEM((ORDER, units), BF),
@@ -286,7 +289,7 @@
             pltpu.VMEM((CHUNKS, 128), F32),
             pltpu.VMEM((rows, width), F32),
             pltpu.VMEM((256, 16, LANES), BF),
-            pltpu.SemaphoreType.DMA((8,)),
+            pltpu.SemaphoreType.DMA((16,)),
         ],
         compiler_params=pltpu.CompilerParams(vmem_limit_bytes=20 * 1024 * 1024),
         cost_estimate=pl.CostEstimate(
@@ -354,30 +357,37 @@
         final_norm_gain[None],
     )
     held = lax.all_to_all(quarter, "z", 0, 0, tiled=True)
-    line = jnp.concatenate([held] + [ring(held, step, 1) for step in (1, 2, 3)])
-    own = [line] + [ring(line, step) for step in (1, 2, 3)]
+    side = [ring(held, step, 1) for step in (1, 2, 3)]
+    line = [jnp.concatenate([held, side[0]]), jnp.concatenate(side[1:])]
+    behind = [ring(line[0], 1), ring(line[1], 1)]
+    ahead = [ring(line[0], 3), ring(line[1], 3)]
+    opposite = [ring(behind[0], 1), ring(ahead[1], 3)]
     width = frozen.shape[3]
     near = brought(
-        line,
+        line[1],
         place,
         gated_hidden_input.reshape(-1, gated_hidden_input.shape[3]),
         frozen.reshape(-1, width),
         head_gradient_rows.reshape(-1, width),
     )
-    line, *near = lax.optimization_barrier((line, *near))
-    other = [other_core(v) for v in (line, *own[1:])]
+    own = line + behind + opposite + ahead
+    *early, near_0, near_1, near_2 = lax.optimization_barrier((*line, *behind, *ahead, *near))
+    other = [other_core(v) for v in early[:4] + opposite + early[4:]]
+    near = (near_0, near_1, near_2)
 
     first, second, margin = shares(place, starts, [*own, *other], *near)
 
     lines = []
-    for own, other in (first, second):
+    for (own, other), way in ((first, 1), (second, 3)):
         came = other_core(other)
         chip = [
             total_of(own[16 * i : 16 * i + 16], came[16 * i : 16 * i + 16]).astype(BF)
             for i in range(4)
         ]
-        came = [ring(chip[step], step) for step in (1, 2, 3)]
-        lines.append(total_of(chip[0], *came).astype(BF).reshape(4, 4, 16, LANES))
+        passing = ring(chip[2], way)
+        direct = ring(chip[4 - way], 4 - way)
+        joined = ring(total_of(chip[way], passing).astype(BF), way)
+        lines.append(total_of(chip[0], direct, joined).astype(BF).reshape(4, 4, 16, LANES))
     line = jnp.concatenate(lines, axis=1)
     came = [ring(line[step], step, 1) for step in (1, 2, 3)]
     plane = total_of(line[0], *came).astype(BF)

time: 119 us -> 121 us (1.017)
  starting transfers between devices: 36.7 us -> 41.1 us
  waiting for transfers between devices: 28.1 us -> 24.8 us
    ppermute x15 -> x18, waiting for transfers between devices: 25.1 us -> 19.1 us  [ring(): return lax.ppermute(values, FINE_AXES, pairs)]
    ppermute x15 -> x18, starting transfers between devices: 17.8 us -> 20.8 us  [ring(): return lax.ppermute(values, FINE_AXES, pairs)]
    ppermute x6 -> x10, waiting for transfers between devices: 2.46 us -> 4.72 us  [other_core(): return lax.ppermute(values, 'c', [(0, 1), (1, 0)])]
    ppermute x3, starting transfers between devices: 4.36 us -> 6.36 us  [local(): lax.ppermute(share, CTX, [(i, i ^ step) for i in range(4)])]
    ppermute x6 -> x10, starting transfers between devices: 14.6 us -> 13.9 us  [other_core(): return lax.ppermute(values, 'c', [(0, 1), (1, 0)])]
  transfers between devices with their start and end apart: 24 -> 31, of which waited for: 15 -> 17; matrix products, arithmetic and copies ran while one was open for 1% -> 1% of each run, Pallas kernels for 6% -> 5%
where the time goes in v8:
time: 121 us
  starting transfers between devices  41.1 us (34%)
  blocking collectives  27.6 us (23%)
  waiting for transfers between devices  24.8 us (20%)
  Pallas kernels  22.5 us (19%)
  between operations  2.7 us (2%)
  other arithmetic  1.23 us (1%)
    ppermute x18, starting transfers between devices, ring(): return lax.ppermute(values, FINE_AXES, pairs)  20.8 us
    ppermute x18, waiting for transfers between devices, ring(): return lax.ppermute(values, FINE_AXES, pairs)  19.1 us
    all_to_all x1, blocking collectives, local(): held = lax.all_to_all(quarter, 'z', 0, 0, tiled=True)  17 us
    ppermute x10, starting transfers between devices, other_core(): return lax.ppermute(values, 'c', [(0, 1), (1, 0)])  13.9 us
    pallas_call x1, Pallas kernels, shares(): pl.pallas_call(kernel, out_shape=[pltpu.VMEM((64, 16, LANES), BF)] * 2 +...  13.1 us
    all_to_all x1, blocking collectives, local(): lax.all_to_all(plane, 'z', 0, 0, tiled=True).astype(F32)  10.7 us
    ppermute x3, starting transfers between devices, local(): lax.ppermute(share, CTX, [(i, i ^ step) for i in range(4)])  6.36 us
    pallas_call x1, Pallas kernels, brought(): pl.pallas_call(bring, out_shape=[pltpu.VMEM(v.shape, v.dtype) for v in ar...  4.91 us
  transfers between devices with their start and end apart: 31, of which 17 were waited for; matrix products, arithmetic and copies ran while one was open for 1% of the time, Pallas kernels for 5%

profile of v8, /device:TPU:1, one launch (start us, length us, event | category | flops | bytes accessed | tf_op | source)
XLA Modules:
  0.0 120.5 jit_solution(13641792156571785100)
XLA Ops:
  0.7 1.5 %shard_map.103 = bf16[8,16,640]{2,1,0:T(8,128)(2,1)S(1)} custom-call(s32[4]{0:T(128)S(1)} %pad_add_fusion.place_ref, s32[1,2]{1,0:T(1,128)} %starts_ref.1, f32[2,64]{1,0:T(2,128)} %bitcast.33, bf16[64,462]{1,0:T(8,128)(2,1)} %bitcast.32, bf16[64,128]{1,0:T(8,128)(2,1)} %refs_3_.1, bf16[1,128]{1,0:T(2,128)(2,1)} %bitcast.34), custom_call_target="tpu_custom_call" | custom-call | tf_op jit(solution)/shard_map/pallas_call | solution.py:206
  2.3 17.0 %all_to_all.10 = bf16[8,16,640]{2,1,0:T(8,128)(2,1)S(1)} all-to-all(bf16[8,16,640]{2,1,0:T(8,128)(2,1)S(1)} %shard_map.103), channel_id=1, replica_groups=mesh['z'=8,'yh'=2,'x'=4,'yl'=2,'c'=2] {'z'}, dimensions={0} | all-to-all | bytes 327680 | tf_op jit(solution)/shard_map/all_to_all | solution.py:359
  19.2 1.2 %collective-permute-start = (bf16[8,16,640]{2,1,0:T(8,128)(2,1)S(1)}, bf16[8,16,640]{2,1,0:T(8,128)(2,1)S(1)}, u32[]{:S(2)}, u32[]{:S(2)}) collective-permute-start(bf16[8,16,640]{2,1,0:T(8,128)(2,1)S(1)} %all_to_all.10), channel_id=1, source_target_pairs={{0,2},{1,5},{4,6},{5,9},{8,10},{9,13},{12,14},{13,1},{2,16},{3,7},... | collective-permute-start | bytes 491528 | tf_op jit(solution)/shard_map/ppermute | solution.py:327
  20.4 1.5 %collective-permute-start.2 = (bf16[8,16,640]{2,1,0:T(8,128)(2,1)S(1)}, bf16[8,16,640]{2,1,0:T(8,128)(2,1)S(1)}, u32[]{:S(2)}, u32[]{:S(2)}) collective-permute-start(bf16[8,16,640]{2,1,0:T(8,128)(2,1)S(1)} %all_to_all.10), channel_id=1, source_target_pairs={{0,18},{1,13},{4,22},{5,1},{8,26},{9,5},{12,30},{13,9},{2,0},{3,15... | collective-permute-start | bytes 491528 | tf_op jit(solution)/shard_map/ppermute | solution.py:327
  21.9 1.5 %collective-permute-start.1 = (bf16[8,16,640]{2,1,0:T(8,128)(2,1)S(1)}, bf16[8,16,640]{2,1,0:T(8,128)(2,1)S(1)}, u32[]{:S(2)}, u32[]{:S(2)}) collective-permute-start(bf16[8,16,640]{2,1,0:T(8,128)(2,1)S(1)} %all_to_all.10), channel_id=1, source_target_pairs={{0,16},{1,9},{4,20},{5,13},{8,24},{9,1},{12,28},{13,5},{2,18},{3,1... | collective-permute-start | bytes 491528 | tf_op jit(solution)/shard_map/ppermute | solution.py:327
  23.5 1.2 collective-permute-done
  24.6 1.4 %collective-permute-start.3 = (bf16[16,16,640]{2,1,0:T(8,128)(2,1)S(1)}, bf16[16,16,640]{2,1,0:T(8,128)(2,1)S(1)}, u32[]{:S(2)}, u32[]{:S(2)}) collective-permute-start(bf16[16,16,640]{2,1,0:T(8,128)(2,1)S(1)} %constant_dynamic-update-slice_fusion.refs_0_), channel_id=1, source_target_pairs={{0,4},{1,3},{4,8},{5,7},{8,12},{9,11},{12,0},{13,15},{2,6},{3,17},... | collective-permute-start | bytes 983048 | tf_op jit(solution)/shard_map/ppermute | solution.py:327
  26.0 1.6 %collective-permute-done.1 = bf16[8,16,640]{2,1,0:T(8,128)(2,1)S(1)} collective-permute-done((bf16[8,16,640]{2,1,0:T(8,128)(2,1)S(1)}, bf16[8,16,640]{2,1,0:T(8,128)(2,1)S(1)}, u32[]{:S(2)}, u32[]{:S(2)}) %collective-permute-start.1) | collective-permute-done | bytes 163872 | tf_op jit(solution)/shard_map/ppermute | solution.py:327
  27.6 2.8 %collective-permute-start.6 = (bf16[16,16,640]{2,1,0:T(8,128)(2,1)S(1)}, bf16[16,16,640]{2,1,0:T(8,128)(2,1)S(1)}, u32[]{:S(2)}, u32[]{:S(2)}) collective-permute-start(bf16[16,16,640]{2,1,0:T(8,128)(2,1)S(1)} %constant_dynamic-update-slice_fusion.2.after_ref.refs_1_), channel_id=1, source_target_pairs={{0,12},{1,19},{4,0},{5,23},{8,4},{9,27},{12,8},{13,31},{2,14},{3,1... | collective-permute-start | bytes 983048 | tf_op jit(solution)/shard_map/ppermute | solution.py:327
  30.5 0.5 collective-permute-start.8
  30.9 1.0 collective-permute-start.4
  31.9 4.9 %shard_map.104 = (bf16[128,29568]{1,0:T(8,128)(2,1)S(1)}, bf16[128,8192]{1,0:T(8,128)(2,1)S(1)}, bf16[128,8192]{1,0:T(8,128)(2,1)S(1)}) custom-call(bf16[16,16,640]{2,1,0:T(8,128)(2,1)S(1)} %constant_dynamic-update-slice_fusion.2.after_ref.refs_1_, s32[4]{0:T(128)S(1)} %pad_add_fusion.place_ref, bf16[128,29568]{1,0:T(8,128)(2,1)} %bitcast.25, ...), custom_call_target="tpu_custom_call" | custom-call | bytes 23527424 | tf_op jit(solution)/shard_map/pallas_call | solution.py:254
  36.9 2.7 %collective-permute-start.7 = (bf16[16,16,640]{2,1,0:T(8,128)(2,1)S(1)}, bf16[16,16,640]{2,1,0:T(8,128)(2,1)S(1)}, u32[]{:S(2)}, u32[]{:S(2)}) collective-permute-start(bf16[16,16,640]{2,1,0:T(8,128)(2,1)S(1)} %collective-permute-done.6.refs_7_), channel_id=1, source_target_pairs={{0,12},{1,19},{4,0},{5,23},{8,4},{9,27},{12,8},{13,31},{2,14},{3,1... | collective-permute-start | bytes 983048 | tf_op jit(solution)/shard_map/ppermute | solution.py:327
  39.6 7.2 %collective-permute-start.9 = (bf16[16,16,640]{2,1,0:T(8,128)(2,1)S(1)}, bf16[16,16,640]{2,1,0:T(8,128)(2,1)S(1)}, u32[]{:S(2)}, u32[]{:S(2)}) collective-permute-start(bf16[16,16,640]{2,1,0:T(8,128)(2,1)S(1)} %constant_dynamic-update-slice_fusion.refs_0_), channel_id=1, source_target_pairs={{0,1},{1,0},{2,3},{3,2},{4,5},{5,4},{6,7},{7,6},{8,9},{9,8},{10,11... | collective-permute-start | bytes 983048 | tf_op jit(solution)/shard_map/ppermute | solution.py:331
  46.9 0.4 collective-permute-start.11
  47.3 4.5 %collective-permute-start.12 = (bf16[16,16,640]{2,1,0:T(8,128)(2,1)S(1)}, bf16[16,16,640]{2,1,0:T(8,128)(2,1)S(1)}, u32[]{:S(2)}, u32[]{:S(2)}) collective-permute-start(bf16[16,16,640]{2,1,0:T(8,128)(2,1)S(1)} %collective-permute-done.4.refs_3_), channel_id=1, source_target_pairs={{0,1},{1,0},{2,3},{3,2},{4,5},{5,4},{6,7},{7,6},{8,9},{9,8},{10,11... | collective-permute-start | bytes 983048 | tf_op jit(solution)/shard_map/ppermute | solution.py:331
  51.9 0.5 collective-permute-start.16
  52.5 0.4 collective-permute-start.14
  52.9 0.2 collective-permute-done.12.refs_11_
  53.1 0.5 collective-permute-done.15.refs_14_
  53.6 0.5 collective-permute-done.16.refs_15_
  54.0 0.5 collective-permute-done.13.refs_12_
  54.5 0.5 collective-permute-done.14.refs_13_
  55.0 13.1 %shard_map.105 = (bf16[64,16,640]{2,1,0:T(8,128)(2,1)S(1)}, bf16[64,16,640]{2,1,0:T(8,128)(2,1)S(1)}, bf16[64,4096]{1,0:T(8,128)(2,1)S(1)}, bf16[64,128]{1,0:T(8,128)(2,1)S(1)}, f32[8,128]{1,0:T(8,128)S(1)}) custom-call(s32[4]{0:T(128)S(1)} %pad_add_fusion.place_ref, s32[1,2]{1,0:T(1,128)S(1)} %copy-done, ...), custom_call_target="tpu_custom_call" | custom-call | flops 1505755136 | bytes 22249472 | tf_op jit(solution)/shard_map/pallas_call | solution.py:275
  68.1 0.5 collective-permute-start.17
  68.6 1.7 %shard_map.106 = (bf16[64,16,640]{2,1,0:T(8,128)(2,1)S(1)}, bf16[64,16,640]{2,1,0:T(8,128)(2,1)S(1)}) custom-call(s32[4]{0:T(128)S(1)} %pad_add_fusion.place_ref, bf16[64,128]{1,0:T(8,128)(2,1)S(1)} %get-tuple-element.39.low_ref, bf16[64,4096]{1,0:T(8,128)(2,1)S(1)} %get-tuple-element.40.up_rest, bf16[128,29568]{1,0:T(8,128)(2,1)S(1)} %get-tuple-element.33.refs_16_.hid), custom_call_target="tpu_custom_call" | custom-call | flops 242221056 | bytes 6406144 | tf_op jit(solution)/shard_map/pallas_call | solution.py:301
  70.3 0.2 collective-permute-start.21
  70.5 0.7 collective-permute-done.17
  71.5 1.9 %collective-permute-done.21 = bf16[64,16,640]{2,1,0:T(8,128)(2,1)S(1)} collective-permute-done((bf16[64,16,640]{2,1,0:T(8,128)(2,1)S(1)}, bf16[64,16,640]{2,1,0:T(8,128)(2,1)S(1)}, u32[]{:S(2)}, u32[]{:S(2)}) %collective-permute-start.21) | collective-permute-done | bytes 1310752 | tf_op jit(solution)/shard_map/ppermute | solution.py:331
  73.5 1.1 collective-permute-start.23
  74.6 1.2 collective-permute-start.18
  75.8 3.1 %collective-permute-done.19 = bf16[16,16,640]{2,1,0:T(8,128)(2,1)S(1)} collective-permute-done((bf16[16,16,640]{2,1,0:T(8,128)(2,1)S(1)}, bf16[16,16,640]{2,1,0:T(8,128)(2,1)S(1)}, u32[]{:S(2)}, u32[]{:S(2)}) %collective-permute-start.19) | collective-permute-done | bytes 327712 | tf_op jit(solution)/shard_map/ppermute | solution.py:327
  79.3 0.8 collective-permute-done.23
  80.2 1.9 %collective-permute-start.24 = (bf16[16,16,640]{2,1,0:T(8,128)(2,1)S(1)}, bf16[16,16,640]{2,1,0:T(8,128)(2,1)S(1)}, u32[]{:S(2)}, u32[]{:S(2)}) collective-permute-start(bf16[16,16,640]{2,1,0:T(8,128)(2,1)S(1)} %add_convert_fusion.1), channel_id=1, source_target_pairs={{0,12},{1,19},{4,0},{5,23},{8,4},{9,27},{12,8},{13,31},{2,14},{3,1... | collective-permute-start | bytes 983048 | tf_op jit(solution)/shard_map/ppermute | solution.py:327
  82.1 1.5 %collective-permute-done.18 = bf16[16,16,640]{2,1,0:T(8,128)(2,1)S(1)} collective-permute-done((bf16[16,16,640]{2,1,0:T(8,128)(2,1)S(1)}, bf16[16,16,640]{2,1,0:T(8,128)(2,1)S(1)}, u32[]{:S(2)}, u32[]{:S(2)}) %collective-permute-start.18) | collective-permute-done | bytes 327712 | tf_op jit(solution)/shard_map/ppermute | solution.py:327
  83.6 3.0 %collective-permute-done.20 = bf16[16,16,640]{2,1,0:T(8,128)(2,1)S(1)} collective-permute-done((bf16[16,16,640]{2,1,0:T(8,128)(2,1)S(1)}, bf16[16,16,640]{2,1,0:T(8,128)(2,1)S(1)}, u32[]{:S(2)}, u32[]{:S(2)}) %collective-permute-start.20) | collective-permute-done | bytes 327712 | tf_op jit(solution)/shard_map/ppermute | solution.py:327
  86.7 3.3 %collective-permute-done.22 = bf16[16,16,640]{2,1,0:T(8,128)(2,1)S(1)} collective-permute-done((bf16[16,16,640]{2,1,0:T(8,128)(2,1)S(1)}, bf16[16,16,640]{2,1,0:T(8,128)(2,1)S(1)}, u32[]{:S(2)}, u32[]{:S(2)}) %collective-permute-start.22) | collective-permute-done | bytes 327712 | tf_op jit(solution)/shard_map/ppermute | solution.py:327
  90.4 2.7 %collective-permute-start.27 = (bf16[8,16,640]{2,1,0:T(8,128)(2,1)S(1)}, bf16[8,16,640]{2,1,0:T(8,128)(2,1)S(1)}, u32[]{:S(2)}, u32[]{:S(2)}) collective-permute-start(bf16[8,16,640]{2,1,0:T(8,128)(2,1)S(1)} %get-tuple-element.50), channel_id=1, source_target_pairs={{0,18},{1,13},{4,22},{5,1},{8,26},{9,5},{12,30},{13,9},{2,0},{3,15... | collective-permute-start | bytes 491528 | tf_op jit(solution)/shard_map/ppermute | solution.py:327
  93.1 1.0 collective-permute-start.26
  94.1 1.7 %collective-permute-done.25 = bf16[8,16,640]{2,1,0:T(8,128)(2,1)S(1)} collective-permute-done((bf16[8,16,640]{2,1,0:T(8,128)(2,1)S(1)}, bf16[8,16,640]{2,1,0:T(8,128)(2,1)S(1)}, u32[]{:S(2)}, u32[]{:S(2)}) %collective-permute-start.25) | collective-permute-done | bytes 163872 | tf_op jit(solution)/shard_map/ppermute | solution.py:327
  95.8 3.0 %collective-permute-done.26 = bf16[8,16,640]{2,1,0:T(8,128)(2,1)S(1)} collective-permute-done((bf16[8,16,640]{2,1,0:T(8,128)(2,1)S(1)}, bf16[8,16,640]{2,1,0:T(8,128)(2,1)S(1)}, u32[]{:S(2)}, u32[]{:S(2)}) %collective-permute-start.26) | collective-permute-done | bytes 163872 | tf_op jit(solution)/shard_map/ppermute | solution.py:327
  98.8 10.7 %all_to_all.11 = bf16[8,16,640]{2,1,0:T(8,128)(2,1)S(1)} all-to-all(bf16[8,16,640]{2,1,0:T(8,128)(2,1)S(1)} %fusion.2), channel_id=1, replica_groups=mesh['z'=8,'yh'=2,'x'=4,'yl'=2,'c'=2] {'z'}, dimensions={0} | all-to-all | bytes 327680 | tf_op jit(solution)/shard_map/all_to_all | solution.py:394
  109.5 3.7 %collective-permute-start.30 = (f32[16,640]{1,0:T(8,128)S(1)}, f32[16,640]{1,0:T(8,128)S(1)}, u32[]{:S(2)}, u32[]{:S(2)}) collective-permute-start(f32[16,640]{1,0:T(8,128)S(1)} %convert_reduce_fusion.refs_0_), channel_id=1, source_target_pairs={{0,3},{1,2},{2,1},{3,0},{4,7},{5,6},{6,5},{7,4},{8,11},{9,10},{10,... | collective-permute-start | bytes 122888 | tf_op jit(solution)/shard_map/ppermute | solution.py:396
  113.2 1.4 %collective-permute-start.29 = (f32[16,640]{1,0:T(8,128)S(1)}, f32[16,640]{1,0:T(8,128)S(1)}, u32[]{:S(2)}, u32[]{:S(2)}) collective-permute-start(f32[16,640]{1,0:T(8,128)S(1)} %convert_reduce_fusion.refs_0_), channel_id=1, source_target_pairs={{0,1},{1,0},{2,3},{3,2},{4,5},{5,4},{6,7},{7,6},{8,9},{9,8},{10,11... | collective-permute-start | bytes 122888 | tf_op jit(solution)/shard_map/ppermute | solution.py:396
  114.7 1.3 %collective-permute-start.28 = (f32[16,640]{1,0:T(8,128)S(1)}, f32[16,640]{1,0:T(8,128)S(1)}, u32[]{:S(2)}, u32[]{:S(2)}) collective-permute-start(f32[16,640]{1,0:T(8,128)S(1)} %convert_reduce_fusion.refs_0_), channel_id=1, source_target_pairs={{0,2},{1,3},{2,0},{3,1},{4,6},{5,7},{6,4},{7,5},{8,10},{9,11},{10,... | collective-permute-start | bytes 122888 | tf_op jit(solution)/shard_map/ppermute | solution.py:396
  115.9 0.5 slice.63
  117.2 1.0 collective-permute-done.28.refs_1_
  118.2 1.2 %shard_map.107 = (f32[64,462]{1,0:T(8,128)}, f32[64,128]{1,0:T(8,128)}) custom-call(s32[4]{0:T(128)S(1)} %pad_add_fusion.place_ref, f32[16,640]{1,0:T(8,128)S(1)} %convert_reduce_fusion.refs_0_, f32[16,640]{1,0:T(8,128)S(1)} %collective-permute-done.28.refs_1_, f32[16,640]{1,0:T(8,128)S(1)} %collective-permute-done.29.refs_2_, ...), custom_call_target="tpu_custom_call" | custom-call | tf_op jit(solution)/shard_map/pallas_call | solution.py:230
  (38 shorter events, 2.0 us)
Async XLA Ops:
  19.2 5.4 %collective-permute-start = (bf16[8,16,640]{2,1,0:T(8,128)(2,1)S(1)}, bf16[8,16,640]{2,1,0:T(8,128)(2,1)S(1)}, u32[]{:S(2)}, u32[]{:S(2)}) collective-permute-start(bf16[8,16,640]{2,1,0:T(8,128)(2,1)S(1)} %all_to_all.10), channel_id=1, source_target_pairs={{0,2},{1,5},{4,6},{5,9},{8,10},{9,13},{12,14},{13,1},{2,16},{3,7},... | collective-permute-start | bytes 491528 | tf_op jit(solution)/shard_map/ppermute | solution.py:327
  20.4 7.2 %collective-permute-start.2 = (bf16[8,16,640]{2,1,0:T(8,128)(2,1)S(1)}, bf16[8,16,640]{2,1,0:T(8,128)(2,1)S(1)}, u32[]{:S(2)}, u32[]{:S(2)}) collective-permute-start(bf16[8,16,640]{2,1,0:T(8,128)(2,1)S(1)} %all_to_all.10), channel_id=1, source_target_pairs={{0,18},{1,13},{4,22},{5,1},{8,26},{9,5},{12,30},{13,9},{2,0},{3,15... | collective-permute-start | bytes 491528 | tf_op jit(solution)/shard_map/ppermute | solution.py:327
  21.9 5.7 %collective-permute-start.1 = (bf16[8,16,640]{2,1,0:T(8,128)(2,1)S(1)}, bf16[8,16,640]{2,1,0:T(8,128)(2,1)S(1)}, u32[]{:S(2)}, u32[]{:S(2)}) collective-permute-start(bf16[8,16,640]{2,1,0:T(8,128)(2,1)S(1)} %all_to_all.10), channel_id=1, source_target_pairs={{0,16},{1,9},{4,20},{5,13},{8,24},{9,1},{12,28},{13,5},{2,18},{3,1... | collective-permute-start | bytes 491528 | tf_op jit(solution)/shard_map/ppermute | solution.py:327
  24.6 12.2 %collective-permute-start.3 = (bf16[16,16,640]{2,1,0:T(8,128)(2,1)S(1)}, bf16[16,16,640]{2,1,0:T(8,128)(2,1)S(1)}, u32[]{:S(2)}, u32[]{:S(2)}) collective-permute-start(bf16[16,16,640]{2,1,0:T(8,128)(2,1)S(1)} %constant_dynamic-update-slice_fusion.refs_0_), channel_id=1, source_target_pairs={{0,4},{1,3},{4,8},{5,7},{8,12},{9,11},{12,0},{13,15},{2,6},{3,17},... | collective-permute-start | bytes 983048 | tf_op jit(solution)/shard_map/ppermute | solution.py:327
  27.6 9.3 %collective-permute-start.6 = (bf16[16,16,640]{2,1,0:T(8,128)(2,1)S(1)}, bf16[16,16,640]{2,1,0:T(8,128)(2,1)S(1)}, u32[]{:S(2)}, u32[]{:S(2)}) collective-permute-start(bf16[16,16,640]{2,1,0:T(8,128)(2,1)S(1)} %constant_dynamic-update-slice_fusion.2.after_ref.refs_1_), channel_id=1, source_target_pairs={{0,12},{1,19},{4,0},{5,23},{8,4},{9,27},{12,8},{13,31},{2,14},{3,1... | collective-permute-start | bytes 983048 | tf_op jit(solution)/shard_map/ppermute | solution.py:327
  30.5 9.2 %collective-permute-start.8 = (bf16[16,16,640]{2,1,0:T(8,128)(2,1)S(1)}, bf16[16,16,640]{2,1,0:T(8,128)(2,1)S(1)}, u32[]{:S(2)}, u32[]{:S(2)}) collective-permute-start(bf16[16,16,640]{2,1,0:T(8,128)(2,1)S(1)} %constant_dynamic-update-slice_fusion.refs_0_), channel_id=1, source_target_pairs={{0,12},{1,19},{4,0},{5,23},{8,4},{9,27},{12,8},{13,31},{2,14},{3,1... | collective-permute-start | bytes 983048 | tf_op jit(solution)/shard_map/ppermute | solution.py:327
  30.9 8.7 %collective-permute-start.4 = (bf16[16,16,640]{2,1,0:T(8,128)(2,1)S(1)}, bf16[16,16,640]{2,1,0:T(8,128)(2,1)S(1)}, u32[]{:S(2)}, u32[]{:S(2)}) collective-permute-start(bf16[16,16,640]{2,1,0:T(8,128)(2,1)S(1)} %constant_dynamic-update-slice_fusion.2.after_ref.refs_1_), channel_id=1, source_target_pairs={{0,4},{1,3},{4,8},{5,7},{8,12},{9,11},{12,0},{13,15},{2,6},{3,17},... | collective-permute-start | bytes 983048 | tf_op jit(solution)/shard_map/ppermute | solution.py:327
  31.9 23.1 %copy-start = (s32[1,2]{1,0:T(1,128)S(1)}, s32[1,2]{1,0:T(1,128)}, u32[]{:S(2)}) copy-start(s32[1,2]{1,0:T(1,128)} %starts_ref.1) | copy-start | bytes 28
  36.8 10.5 %collective-permute-start.5 = (bf16[16,16,640]{2,1,0:T(8,128)(2,1)S(1)}, bf16[16,16,640]{2,1,0:T(8,128)(2,1)S(1)}, u32[]{:S(2)}, u32[]{:S(2)}) collective-permute-start(bf16[16,16,640]{2,1,0:T(8,128)(2,1)S(1)} %collective-permute-done.3.refs_2_), channel_id=1, source_target_pairs={{0,4},{1,3},{4,8},{5,7},{8,12},{9,11},{12,0},{13,15},{2,6},{3,17},... | collective-permute-start | bytes 983048 | tf_op jit(solution)/shard_map/ppermute | solution.py:327
  36.9 14.9 %collective-permute-start.7 = (bf16[16,16,640]{2,1,0:T(8,128)(2,1)S(1)}, bf16[16,16,640]{2,1,0:T(8,128)(2,1)S(1)}, u32[]{:S(2)}, u32[]{:S(2)}) collective-permute-start(bf16[16,16,640]{2,1,0:T(8,128)(2,1)S(1)} %collective-permute-done.6.refs_7_), channel_id=1, source_target_pairs={{0,12},{1,19},{4,0},{5,23},{8,4},{9,27},{12,8},{13,31},{2,14},{3,1... | collective-permute-start | bytes 983048 | tf_op jit(solution)/shard_map/ppermute | solution.py:327
  39.6 12.2 %collective-permute-start.9 = (bf16[16,16,640]{2,1,0:T(8,128)(2,1)S(1)}, bf16[16,16,640]{2,1,0:T(8,128)(2,1)S(1)}, u32[]{:S(2)}, u32[]{:S(2)}) collective-permute-start(bf16[16,16,640]{2,1,0:T(8,128)(2,1)S(1)} %constant_dynamic-update-slice_fusion.refs_0_), channel_id=1, source_target_pairs={{0,1},{1,0},{2,3},{3,2},{4,5},{5,4},{6,7},{7,6},{8,9},{9,8},{10,11... | collective-permute-start | bytes 983048 | tf_op jit(solution)/shard_map/ppermute | solution.py:331
  46.8 5.6 %collective-permute-start.10 = (bf16[16,16,640]{2,1,0:T(8,128)(2,1)S(1)}, bf16[16,16,640]{2,1,0:T(8,128)(2,1)S(1)}, u32[]{:S(2)}, u32[]{:S(2)}) collective-permute-start(bf16[16,16,640]{2,1,0:T(8,128)(2,1)S(1)} %constant_dynamic-update-slice_fusion.2.after_ref.refs_1_), channel_id=1, source_target_pairs={{0,1},{1,0},{2,3},{3,2},{4,5},{5,4},{6,7},{7,6},{8,9},{9,8},{10,11... | collective-permute-start | bytes 983048 | tf_op jit(solution)/shard_map/ppermute | solution.py:331
  46.9 5.6 %collective-permute-start.11 = (bf16[16,16,640]{2,1,0:T(8,128)(2,1)S(1)}, bf16[16,16,640]{2,1,0:T(8,128)(2,1)S(1)}, u32[]{:S(2)}, u32[]{:S(2)}) collective-permute-start(bf16[16,16,640]{2,1,0:T(8,128)(2,1)S(1)} %collective-permute-done.3.refs_2_), channel_id=1, source_target_pairs={{0,1},{1,0},{2,3},{3,2},{4,5},{5,4},{6,7},{7,6},{8,9},{9,8},{10,11... | collective-permute-start | bytes 983048 | tf_op jit(solution)/shard_map/ppermute | solution.py:331
  47.3 5.8 %collective-permute-start.12 = (bf16[16,16,640]{2,1,0:T(8,128)(2,1)S(1)}, bf16[16,16,640]{2,1,0:T(8,128)(2,1)S(1)}, u32[]{:S(2)}, u32[]{:S(2)}) collective-permute-start(bf16[16,16,640]{2,1,0:T(8,128)(2,1)S(1)} %collective-permute-done.4.refs_3_), channel_id=1, source_target_pairs={{0,1},{1,0},{2,3},{3,2},{4,5},{5,4},{6,7},{7,6},{8,9},{9,8},{10,11... | collective-permute-start | bytes 983048 | tf_op jit(solution)/shard_map/ppermute | solution.py:331
  51.8 1.7 %collective-permute-start.15 = (bf16[16,16,640]{2,1,0:T(8,128)(2,1)S(1)}, bf16[16,16,640]{2,1,0:T(8,128)(2,1)S(1)}, u32[]{:S(2)}, u32[]{:S(2)}) collective-permute-start(bf16[16,16,640]{2,1,0:T(8,128)(2,1)S(1)} %collective-permute-done.8.refs_6_), channel_id=1, source_target_pairs={{0,1},{1,0},{2,3},{3,2},{4,5},{5,4},{6,7},{7,6},{8,9},{9,8},{10,11... | collective-permute-start | bytes 983048 | tf_op jit(solution)/shard_map/ppermute | solution.py:331
  51.9 2.2 %collective-permute-start.16 = (bf16[16,16,640]{2,1,0:T(8,128)(2,1)S(1)}, bf16[16,16,640]{2,1,0:T(8,128)(2,1)S(1)}, u32[]{:S(2)}, u32[]{:S(2)}) collective-permute-start(bf16[16,16,640]{2,1,0:T(8,128)(2,1)S(1)} %collective-permute-done.6.refs_7_), channel_id=1, source_target_pairs={{0,1},{1,0},{2,3},{3,2},{4,5},{5,4},{6,7},{7,6},{8,9},{9,8},{10,11... | collective-permute-start | bytes 983048 | tf_op jit(solution)/shard_map/ppermute | solution.py:331
  52.4 2.1 %collective-permute-start.13 = (bf16[16,16,640]{2,1,0:T(8,128)(2,1)S(1)}, bf16[16,16,640]{2,1,0:T(8,128)(2,1)S(1)}, u32[]{:S(2)}, u32[]{:S(2)}) collective-permute-start(bf16[16,16,640]{2,1,0:T(8,128)(2,1)S(1)} %collective-permute-done.5.refs_4_), channel_id=1, source_target_pairs={{0,1},{1,0},{2,3},{3,2},{4,5},{5,4},{6,7},{7,6},{8,9},{9,8},{10,11... | collective-permute-start | bytes 983048 | tf_op jit(solution)/shard_map/ppermute | solution.py:331
  52.5 2.5 %collective-permute-start.14 = (bf16[16,16,640]{2,1,0:T(8,128)(2,1)S(1)}, bf16[16,16,640]{2,1,0:T(8,128)(2,1)S(1)}, u32[]{:S(2)}, u32[]{:S(2)}) collective-permute-start(bf16[16,16,640]{2,1,0:T(8,128)(2,1)S(1)} %collective-permute-done.7.refs_5_), channel_id=1, source_target_pairs={{0,1},{1,0},{2,3},{3,2},{4,5},{5,4},{6,7},{7,6},{8,9},{9,8},{10,11... | collective-permute-start | bytes 983048 | tf_op jit(solution)/shard_map/ppermute | solution.py:331
  68.1 3.1 %collective-permute-start.17 = (bf16[64,16,640]{2,1,0:T(8,128)(2,1)S(1)}, bf16[64,16,640]{2,1,0:T(8,128)(2,1)S(1)}, u32[]{:S(2)}, u32[]{:S(2)}) collective-permute-start(bf16[64,16,640]{2,1,0:T(8,128)(2,1)S(1)} %get-tuple-element.38), channel_id=1, source_target_pairs={{0,1},{1,0},{2,3},{3,2},{4,5},{5,4},{6,7},{7,6},{8,9},{9,8},{10,11... | collective-permute-start | bytes 3932168 | tf_op jit(solution)/shard_map/ppermute | solution.py:331
  70.3 3.1 %collective-permute-start.21 = (bf16[64,16,640]{2,1,0:T(8,128)(2,1)S(1)}, bf16[64,16,640]{2,1,0:T(8,128)(2,1)S(1)}, u32[]{:S(2)}, u32[]{:S(2)}) collective-permute-start(bf16[64,16,640]{2,1,0:T(8,128)(2,1)S(1)} %get-tuple-element.42), channel_id=1, source_target_pairs={{0,1},{1,0},{2,3},{3,2},{4,5},{5,4},{6,7},{7,6},{8,9},{9,8},{10,11... | collective-permute-start | bytes 3932168 | tf_op jit(solution)/shard_map/ppermute | solution.py:331
  71.4 7.5 %collective-permute-start.19 = (bf16[16,16,640]{2,1,0:T(8,128)(2,1)S(1)}, bf16[16,16,640]{2,1,0:T(8,128)(2,1)S(1)}, u32[]{:S(2)}, u32[]{:S(2)}) collective-permute-start(bf16[16,16,640]{2,1,0:T(8,128)(2,1)S(1)} %get-tuple-element.46), channel_id=1, source_target_pairs={{0,4},{1,3},{4,8},{5,7},{8,12},{9,11},{12,0},{13,15},{2,6},{3,17},... | collective-permute-start | bytes 983048 | tf_op jit(solution)/shard_map/ppermute | solution.py:327
  73.5 6.5 %collective-permute-start.23 = (bf16[16,16,640]{2,1,0:T(8,128)(2,1)S(1)}, bf16[16,16,640]{2,1,0:T(8,128)(2,1)S(1)}, u32[]{:S(2)}, u32[]{:S(2)}) collective-permute-start(bf16[16,16,640]{2,1,0:T(8,128)(2,1)S(1)} %get-tuple-element.48), channel_id=1, source_target_pairs={{0,12},{1,19},{4,0},{5,23},{8,4},{9,27},{12,8},{13,31},{2,14},{3,1... | collective-permute-start | bytes 983048 | tf_op jit(solution)/shard_map/ppermute | solution.py:327
  74.6 9.0 %collective-permute-start.18 = (bf16[16,16,640]{2,1,0:T(8,128)(2,1)S(1)}, bf16[16,16,640]{2,1,0:T(8,128)(2,1)S(1)}, u32[]{:S(2)}, u32[]{:S(2)}) collective-permute-start(bf16[16,16,640]{2,1,0:T(8,128)(2,1)S(1)} %get-tuple-element.45), channel_id=1, source_target_pairs={{0,12},{1,19},{4,0},{5,23},{8,4},{9,27},{12,8},{13,31},{2,14},{3,1... | collective-permute-start | bytes 983048 | tf_op jit(solution)/shard_map/ppermute | solution.py:327
  79.0 7.5 %collective-permute-start.20 = (bf16[16,16,640]{2,1,0:T(8,128)(2,1)S(1)}, bf16[16,16,640]{2,1,0:T(8,128)(2,1)S(1)}, u32[]{:S(2)}, u32[]{:S(2)}) collective-permute-start(bf16[16,16,640]{2,1,0:T(8,128)(2,1)S(1)} %add_convert_fusion.7), channel_id=1, source_target_pairs={{0,4},{1,3},{4,8},{5,7},{8,12},{9,11},{12,0},{13,15},{2,6},{3,17},... | collective-permute-start | bytes 983048 | tf_op jit(solution)/shard_map/ppermute | solution.py:327
  79.1 10.9 %collective-permute-start.22 = (bf16[16,16,640]{2,1,0:T(8,128)(2,1)S(1)}, bf16[16,16,640]{2,1,0:T(8,128)(2,1)S(1)}, u32[]{:S(2)}, u32[]{:S(2)}) collective-permute-start(bf16[16,16,640]{2,1,0:T(8,128)(2,1)S(1)} %get-tuple-element.47), channel_id=1, source_target_pairs={{0,4},{1,3},{4,8},{5,7},{8,12},{9,11},{12,0},{13,15},{2,6},{3,17},... | collective-permute-start | bytes 983048 | tf_op jit(solution)/shard_map/ppermute | solution.py:327
  80.2 9.9 %collective-permute-start.24 = (bf16[16,16,640]{2,1,0:T(8,128)(2,1)S(1)}, bf16[16,16,640]{2,1,0:T(8,128)(2,1)S(1)}, u32[]{:S(2)}, u32[]{:S(2)}) collective-permute-start(bf16[16,16,640]{2,1,0:T(8,128)(2,1)S(1)} %add_convert_fusion.1), channel_id=1, source_target_pairs={{0,12},{1,19},{4,0},{5,23},{8,4},{9,27},{12,8},{13,31},{2,14},{3,1... | collective-permute-start | bytes 983048 | tf_op jit(solution)/shard_map/ppermute | solution.py:327
  90.3 5.5 %collective-permute-start.25 = (bf16[8,16,640]{2,1,0:T(8,128)(2,1)S(1)}, bf16[8,16,640]{2,1,0:T(8,128)(2,1)S(1)}, u32[]{:S(2)}, u32[]{:S(2)}) collective-permute-start(bf16[8,16,640]{2,1,0:T(8,128)(2,1)S(1)} %get-tuple-element.49), channel_id=1, source_target_pairs={{0,2},{1,5},{4,6},{5,9},{8,10},{9,13},{12,14},{13,1},{2,16},{3,7},... | collective-permute-start | bytes 491528 | tf_op jit(solution)/shard_map/ppermute | solution.py:327
  90.4 5.4 %collective-permute-start.27 = (bf16[8,16,640]{2,1,0:T(8,128)(2,1)S(1)}, bf16[8,16,640]{2,1,0:T(8,128)(2,1)S(1)}, u32[]{:S(2)}, u32[]{:S(2)}) collective-permute-start(bf16[8,16,640]{2,1,0:T(8,128)(2,1)S(1)} %get-tuple-element.50), channel_id=1, source_target_pairs={{0,18},{1,13},{4,22},{5,1},{8,26},{9,5},{12,30},{13,9},{2,0},{3,15... | collective-permute-start | bytes 491528 | tf_op jit(solution)/shard_map/ppermute | solution.py:327
  93.1 5.7 %collective-permute-start.26 = (bf16[8,16,640]{2,1,0:T(8,128)(2,1)S(1)}, bf16[8,16,640]{2,1,0:T(8,128)(2,1)S(1)}, u32[]{:S(2)}, u32[]{:S(2)}) collective-permute-start(bf16[8,16,640]{2,1,0:T(8,128)(2,1)S(1)} %get-tuple-element.51), channel_id=1, source_target_pairs={{0,16},{1,9},{4,20},{5,13},{8,24},{9,1},{12,28},{13,5},{2,18},{3,1... | collective-permute-start | bytes 491528 | tf_op jit(solution)/shard_map/ppermute | solution.py:327
  109.5 7.6 %collective-permute-start.30 = (f32[16,640]{1,0:T(8,128)S(1)}, f32[16,640]{1,0:T(8,128)S(1)}, u32[]{:S(2)}, u32[]{:S(2)}) collective-permute-start(f32[16,640]{1,0:T(8,128)S(1)} %convert_reduce_fusion.refs_0_), channel_id=1, source_target_pairs={{0,3},{1,2},{2,1},{3,0},{4,7},{5,6},{6,5},{7,4},{8,11},{9,10},{10,... | collective-permute-start | bytes 122888 | tf_op jit(solution)/shard_map/ppermute | solution.py:396
  113.2 3.9 %collective-permute-start.29 = (f32[16,640]{1,0:T(8,128)S(1)}, f32[16,640]{1,0:T(8,128)S(1)}, u32[]{:S(2)}, u32[]{:S(2)}) collective-permute-start(f32[16,640]{1,0:T(8,128)S(1)} %convert_reduce_fusion.refs_0_), channel_id=1, source_target_pairs={{0,1},{1,0},{2,3},{3,2},{4,5},{5,4},{6,7},{7,6},{8,9},{9,8},{10,11... | collective-permute-start | bytes 122888 | tf_op jit(solution)/shard_map/ppermute | solution.py:396
  114.7 3.5 %collective-permute-start.28 = (f32[16,640]{1,0:T(8,128)S(1)}, f32[16,640]{1,0:T(8,128)S(1)}, u32[]{:S(2)}, u32[]{:S(2)}) collective-permute-start(f32[16,640]{1,0:T(8,128)S(1)} %convert_reduce_fusion.refs_0_), channel_id=1, source_target_pairs={{0,2},{1,3},{2,0},{3,1},{4,6},{5,7},{6,4},{7,5},{8,10},{9,11},{10,... | collective-permute-start | bytes 122888 | tf_op jit(solution)/shard_map/ppermute | solution.py:396

commit v9 on v8

--- a/solution.py
+++ b/solution.py
@@ -57,40 +57,64 @@
                 outs[other][base + z, :, UP:GAIN_AT] = held[rows, begin : begin + DOWN]
 
 
-def kernel(place_ref, starts_ref, *refs):
-    parts, (hid, fro, hea) = refs[:16], refs[16:19]
-    outs, up_rest, low_ref, margin_ref = refs[19:21], refs[21], refs[22], refs[23]
-    wt, up, gains, gain, pol, block, sems = refs[24:]
-    width = fro.shape[1]
-
+def assemble(place_ref, other, parts, block, sems, hid, wt, up, gains):
     loads = [
-        pltpu.make_async_copy(parts[i], block.at[pl.ds(16 * i, 16)], sems.at[i]) for i in range(16)
+        pltpu.make_async_copy(parts[i], block.at[pl.ds(16 * i, 16)], sems.at[i]) for i in range(8)
     ]
     for copy in loads:
         copy.start()
-
-    for other in range(2):
-        for copy in loads[8 * other : 8 * other + 8]:
-            copy.wait()
-        for x, yh, yl, base in slots(place_ref, 1, 8, other):
-            q = other * 2 + yl
-            rows = slice(16 * q, 16 * q + 16)
-            for z in range(8):
-                chunk = z * 8 + yh * 4 + x
-                held = block[other * 128 + base + z]
-                up[rows, chunk * UP : (chunk + 1) * UP] = held[:, :UP]
-                wt[rows, chunk * DOWN : (chunk + 1) * DOWN] = held[:, UP:GAIN_AT]
-                gains[q, chunk : chunk + 1, :] = held[0:1, LANES - 128 :].astype(F32)
+    for copy in loads:
+        copy.wait()
+    for x, yh, yl, base in slots(place_ref, 1, 8, other):
+        rows = slice(16 * yl, 16 * yl + 16)
+        for z in range(8):
+            chunk = z * 8 + yh * 4 + x
+            held = block[base + z]
+            up[rows, chunk * UP : (chunk + 1) * UP] = held[:, :UP]
+            wt[rows, chunk * DOWN : (chunk + 1) * DOWN] = held[:, UP:GAIN_AT]
+            gains[yl, chunk : chunk + 1, :] = held[0:1, LANES - 128 :].astype(F32)
 
     pz, py, px, pc = (place_ref[i] for i in range(4))
     sums = jnp.zeros((1, 128), F32)
-    for other in range(2):
-        for yl in range(2):
-            y = (py & 2) + yl
-            dy = (py - y) & 3
-            inside = jnp.where(pc == other, dy * 8, dy * 32) + pz
-            held = block[other * 128 + inside]
-            sums += held[0:1, LANES - 128 :].astype(F32)
+    for yl in range(2):
+        dy = (py - ((py & 2) + yl)) & 3
+        held = block[jnp.where(pc == other, dy * 8, dy * 32) + pz]
+        sums += held[0:1, LANES - 128 :].astype(F32)
+
+    tile = 5888
+    main = wt.shape[1] // tile
+    low = dot(hid[:, main * tile :], wt[:, main * tile :], NT)
+    for i in range(main):
+        at = slice(i * tile, i * tile + tile)
+        low += dot(hid[:, at], wt[:, at], NT)
+    return low, sums
+
+
+def own_kernel(place_ref, *refs):
+    parts, hid = refs[:8], refs[8]
+    up, low_ref, gains, sums_ref = refs[9:13]
+    block, wt, sems = refs[13:]
+    low, sums = assemble(place_ref, 0, parts, block, sems, hid, wt, up, gains)
+    low_ref[...] = low
+    sums_ref[...] = jnp.broadcast_to(sums, sums_ref.shape)
+
+
+def kernel(place_ref, starts_ref, *refs):
+    parts, (hid, fro, hea) = refs[:8], refs[8:11]
+    own_up, own_low, own_gains, own_sums = refs[11:15]
+    outs, up_rest, low_ref, margin_ref = refs[15:17], refs[17], refs[18], refs[19]
+    wt, up, gains, gain, pol, block, share_held, sems = refs[20:]
+    width = fro.shape[1]
+
+    up[:32, :] = own_up[...]
+    low, sums = assemble(
+        place_ref, 1, parts, block, sems, hid, wt, up.at[pl.ds(32, 32)], gains
+    )
+    low = jnp.concatenate([own_low[...], low], axis=1).astype(BF)
+    low_t = low.astype(F32).T.astype(BF)
+
+    py, pc = place_ref[1], place_ref[3]
+    sums += own_sums[0:1, :]
     lane = SUMS_AT - (LANES - 128)
     sides = [sum(sums[:, lane + 3 * s + j : lane + 3 * s + j + 1] for j in range(3)) for s in (0, 1)]
     margin = BETA * (sides[0] - sides[1])
@@ -102,19 +126,10 @@
     slope = jnp.where(position >= start, weight, 0.0) / (1.0 + jnp.exp(margin))
 
     lane = GAIN_AT - (LANES - 128)
-    parts_of_gain = [gains[q][:, lane : lane + 32] for q in range(4)]
+    parts_of_gain = [v[:, lane : lane + 32] for v in (own_gains[0], own_gains[1], gains[0], gains[1])]
     ordered = jnp.concatenate(parts_of_gain, axis=1)
     swapped = jnp.concatenate(parts_of_gain[2:] + parts_of_gain[:2], axis=1)
     gain[...] = jnp.where(pc == 0, ordered, swapped)
-
-    tile = 5888
-    main = wt.shape[1] // tile
-    low = dot(hid[:, main * tile :], wt[:, main * tile :], NT)
-    for i in range(main):
-        at = slice(i * tile, i * tile + tile)
-        low += dot(hid[:, at], wt[:, at], NT)
-    low = low.astype(BF)
-    low_t = low.astype(F32).T.astype(BF)
 
     step = 512
 
@@ -160,7 +175,7 @@
     grad_low = (SCALE * total).T.astype(BF)
 
     low_ref[...] = grad_low
-    to_blocks(place_ref, outs, 0, up, grad_low, hid, wt)
+    to_blocks(place_ref, outs, 0, up, grad_low, hid, share_held)
 
 
 def second_kernel(place_ref, low_ref, up_rest, hid, *refs):
@@ -266,12 +281,34 @@
     return [pltpu.with_memory_space_constraint(v, pltpu.VMEM) for v in arrays]
 
 
-def shares(place, starts, parts, hidden, frozen, head):
+def shares(place, starts, own, other, hidden, frozen, head):
     rows, units = hidden.shape
     width = frozen.shape[1]
     any_space = pl.BlockSpec(memory_space=pl.ANY)
     smem = pl.BlockSpec(memory_space=pltpu.SMEM)
     vmem = pl.BlockSpec(memory_space=pltpu.VMEM)
+    from_own = pl.pallas_call(
+        own_kernel,
+        out_shape=[
+            pltpu.VMEM((ORDER // 2, width), BF),
+            pltpu.VMEM((rows, ORDER // 2), F32),
+            pltpu.VMEM((2, CHUNKS, 128), F32),
+            pltpu.VMEM((8, 128), F32),
+        ],
+        in_specs=[smem] + [any_space] * 8 + [vmem],
+        out_specs=[vmem] * 4,
+        scratch_shapes=[
+            pltpu.VMEM((128, 16, LANES), BF),
+            pltpu.VMEM((ORDER // 2, units), BF),
+            pltpu.SemaphoreType.DMA((8,)),
+        ],
+        compiler_params=pltpu.CompilerParams(vmem_limit_bytes=8 * 1024 * 1024),
+        cost_estimate=pl.CostEstimate(
+            flops=rows * ORDER * units,
+            bytes_accessed=2 * rows * units + 4 * 128 * 16 * LANES,
+            transcendentals=0,
+        ),
+    )(place, *own, *near_vmem(hidden))
     *outs, up_rest, grad_low, margin = pl.pallas_call(
         kernel,
         out_shape=[pltpu.VMEM((64, 16, LANES), BF)] * 2
@@ -280,24 +317,25 @@
             pltpu.VMEM((ORDER, rows), BF),
             jax.ShapeDtypeStruct((8, 128), F32),
         ],
-        in_specs=[smem, smem] + [any_space] * 16 + [vmem] * 3,
+        in_specs=[smem, smem] + [any_space] * 8 + [vmem] * 7,
         out_specs=[vmem] * 5,
         scratch_shapes=[
-            pltpu.VMEM((ORDER, units), BF),
+            pltpu.VMEM((ORDER // 2, units), BF),
             pltpu.VMEM((ORDER, width), BF),
-            pltpu.VMEM((4, CHUNKS, 128), F32),
+            pltpu.VMEM((2, CHUNKS, 128), F32),
             pltpu.VMEM((CHUNKS, 128), F32),
             pltpu.VMEM((rows, width), F32),
-            pltpu.VMEM((256, 16, LANES), BF),
-            pltpu.SemaphoreType.DMA((16,)),
+            pltpu.VMEM((128, 16, LANES), BF),
+            pltpu.VMEM((ORDER, (units // 256 + 1) * 128), BF),
+            pltpu.SemaphoreType.DMA((8,)),
         ],
-        compiler_params=pltpu.CompilerParams(vmem_limit_bytes=20 * 1024 * 1024),
+        compiler_params=pltpu.CompilerParams(vmem_limit_bytes=18 * 1024 * 1024),
         cost_estimate=pl.CostEstimate(
             flops=2 * rows * ORDER * (2 * units + 4 * width),
             bytes_accessed=2 * rows * (units + 2 * width) + 4 * 256 * 16 * LANES,
             transcendentals=0,
         ),
-    )(place, starts, *parts, *near_vmem(hidden, frozen, head))
+    )(place, starts, *other, *near_vmem(hidden, frozen, head, *from_own))
     rest = pl.pallas_call(
         second_kernel,
         out_shape=[pltpu.VMEM((64, 16, LANES), BF)] * 2,
@@ -375,19 +413,17 @@
     other = [other_core(v) for v in early[:4] + opposite + early[4:]]
     near = (near_0, near_1, near_2)
 
-    first, second, margin = shares(place, starts, [*own, *other], *near)
+    first, second, margin = shares(place, starts, own, other, *near)
 
     lines = []
-    for (own, other), way in ((first, 1), (second, 3)):
+    for own, other in (first, second):
         came = other_core(other)
         chip = [
             total_of(own[16 * i : 16 * i + 16], came[16 * i : 16 * i + 16]).astype(BF)
             for i in range(4)
         ]
-        passing = ring(chip[2], way)
-        direct = ring(chip[4 - way], 4 - way)
-        joined = ring(total_of(chip[way], passing).astype(BF), way)
-        lines.append(total_of(chip[0], direct, joined).astype(BF).reshape(4, 4, 16, LANES))
+        came = [ring(chip[step], step) for step in (1, 2, 3)]
+        lines.append(total_of(chip[0], *came).astype(BF).reshape(4, 4, 16, LANES))
     line = jnp.concatenate(lines, axis=1)
     came = [ring(line[step], step, 1) for step in (1, 2, 3)]
     plane = total_of(line[0], *came).astype(BF)

time: 121 us -> 120 us (level)
  waiting for transfers between devices: 24.8 us -> 21.1 us
  Pallas kernels: 22.5 us -> 24.2 us
  starting transfers between devices: 41.1 us -> 42.7 us
    ppermute x10, waiting for transfers between devices: 4.72 us -> 0.8 us  [other_core(): return lax.ppermute(values, 'c', [(0, 1), (1, 0)])]
    pallas_call x0 -> x1, Pallas kernels: none -> 3.63 us  [shares(): pl.pallas_call(own_kernel, out_shape=[pltpu.VMEM((ORDER // 2, width), BF)...]
    ppermute x18, starting transfers between devices: 20.8 us -> 22.9 us  [ring(): return lax.ppermute(values, FINE_AXES, pairs)]
    pallas_call x1, Pallas kernels: 13.1 us -> 11.3 us  [shares(): pl.pallas_call(kernel, out_shape=[pltpu.VMEM((64, 16, LANES), BF)] * 2 +...]
  transfers between devices with their start and end apart: 31 -> 31, of which waited for: 17 -> 10; matrix products, arithmetic and copies ran while one was open for 1% -> 1% of each run, Pallas kernels for 5% -> 8%
where the time goes in v9:
time: 120 us
  starting transfers between devices  42.7 us (36%)
  blocking collectives  27.7 us (23%)
  Pallas kernels  24.2 us (20%)
  waiting for transfers between devices  21.1 us (18%)
  between operations  2.74 us (2%)
  other arithmetic  1.25 us (1%)
    ppermute x18, starting transfers between devices, ring(): return lax.ppermute(values, FINE_AXES, pairs)  22.9 us
    ppermute x18, waiting for transfers between devices, ring(): return lax.ppermute(values, FINE_AXES, pairs)  19.3 us
    all_to_all x1, blocking collectives, local(): held = lax.all_to_all(quarter, 'z', 0, 0, tiled=True)  17 us
    ppermute x10, starting transfers between devices, other_core(): return lax.ppermute(values, 'c', [(0, 1), (1, 0)])  13.9 us
    pallas_call x1, Pallas kernels, shares(): pl.pallas_call(kernel, out_shape=[pltpu.VMEM((64, 16, LANES), BF)] * 2 +...  11.3 us
    all_to_all x1, blocking collectives, local(): lax.all_to_all(plane, 'z', 0, 0, tiled=True).astype(F32)  10.8 us
    ppermute x3, starting transfers between devices, local(): lax.ppermute(share, CTX, [(i, i ^ step) for i in range(4)])  5.84 us
    pallas_call x1, Pallas kernels, brought(): pl.pallas_call(bring, out_shape=[pltpu.VMEM(v.shape, v.dtype) for v in ar...  4.91 us
  transfers between devices with their start and end apart: 31, of which 10 were waited for; matrix products, arithmetic and copies ran while one was open for 1% of the time, Pallas kernels for 8%

profile of v9, /device:TPU:1, one launch (start us, length us, event | category | flops | bytes accessed | tf_op | source)
XLA Modules:
  0.0 120.3 jit_solution(8727678438081461702)
XLA Ops:
  0.7 1.5 %shard_map.103 = bf16[8,16,640]{2,1,0:T(8,128)(2,1)S(1)} custom-call(s32[4]{0:T(128)S(1)} %pad_add_fusion.place_ref, s32[1,2]{1,0:T(1,128)} %starts_ref.1, f32[2,64]{1,0:T(2,128)} %bitcast.33, bf16[64,462]{1,0:T(8,128)(2,1)} %bitcast.32, bf16[64,128]{1,0:T(8,128)(2,1)} %refs_3_.1, bf16[1,128]{1,0:T(2,128)(2,1)} %bitcast.34), custom_call_target="tpu_custom_call" | custom-call | tf_op jit(solution)/shard_map/pallas_call | solution.py:221
  2.3 17.0 %all_to_all.10 = bf16[8,16,640]{2,1,0:T(8,128)(2,1)S(1)} all-to-all(bf16[8,16,640]{2,1,0:T(8,128)(2,1)S(1)} %shard_map.103), channel_id=1, replica_groups=mesh['z'=8,'yh'=2,'x'=4,'yl'=2,'c'=2] {'z'}, dimensions={0} | all-to-all | bytes 327680 | tf_op jit(solution)/shard_map/all_to_all | solution.py:397
  19.2 1.2 %collective-permute-start = (bf16[8,16,640]{2,1,0:T(8,128)(2,1)S(1)}, bf16[8,16,640]{2,1,0:T(8,128)(2,1)S(1)}, u32[]{:S(2)}, u32[]{:S(2)}) collective-permute-start(bf16[8,16,640]{2,1,0:T(8,128)(2,1)S(1)} %all_to_all.10), channel_id=1, source_target_pairs={{0,2},{1,5},{4,6},{5,9},{8,10},{9,13},{12,14},{13,1},{2,16},{3,7},... | collective-permute-start | bytes 491528 | tf_op jit(solution)/shard_map/ppermute | solution.py:365
  20.4 1.5 %collective-permute-start.2 = (bf16[8,16,640]{2,1,0:T(8,128)(2,1)S(1)}, bf16[8,16,640]{2,1,0:T(8,128)(2,1)S(1)}, u32[]{:S(2)}, u32[]{:S(2)}) collective-permute-start(bf16[8,16,640]{2,1,0:T(8,128)(2,1)S(1)} %all_to_all.10), channel_id=1, source_target_pairs={{0,18},{1,13},{4,22},{5,1},{8,26},{9,5},{12,30},{13,9},{2,0},{3,15... | collective-permute-start | bytes 491528 | tf_op jit(solution)/shard_map/ppermute | solution.py:365
  21.9 1.5 %collective-permute-start.1 = (bf16[8,16,640]{2,1,0:T(8,128)(2,1)S(1)}, bf16[8,16,640]{2,1,0:T(8,128)(2,1)S(1)}, u32[]{:S(2)}, u32[]{:S(2)}) collective-permute-start(bf16[8,16,640]{2,1,0:T(8,128)(2,1)S(1)} %all_to_all.10), channel_id=1, source_target_pairs={{0,16},{1,9},{4,20},{5,13},{8,24},{9,1},{12,28},{13,5},{2,18},{3,1... | collective-permute-start | bytes 491528 | tf_op jit(solution)/shard_map/ppermute | solution.py:365
  23.5 1.2 collective-permute-done
  24.6 1.4 %collective-permute-start.3 = (bf16[16,16,640]{2,1,0:T(8,128)(2,1)S(1)}, bf16[16,16,640]{2,1,0:T(8,128)(2,1)S(1)}, u32[]{:S(2)}, u32[]{:S(2)}) collective-permute-start(bf16[16,16,640]{2,1,0:T(8,128)(2,1)S(1)} %constant_dynamic-update-slice_fusion.refs_0_), channel_id=1, source_target_pairs={{0,4},{1,3},{4,8},{5,7},{8,12},{9,11},{12,0},{13,15},{2,6},{3,17},... | collective-permute-start | bytes 983048 | tf_op jit(solution)/shard_map/ppermute | solution.py:365
  26.0 1.6 %collective-permute-done.1 = bf16[8,16,640]{2,1,0:T(8,128)(2,1)S(1)} collective-permute-done((bf16[8,16,640]{2,1,0:T(8,128)(2,1)S(1)}, bf16[8,16,640]{2,1,0:T(8,128)(2,1)S(1)}, u32[]{:S(2)}, u32[]{:S(2)}) %collective-permute-start.1) | collective-permute-done | bytes 163872 | tf_op jit(solution)/shard_map/ppermute | solution.py:365
  27.6 2.8 %collective-permute-start.6 = (bf16[16,16,640]{2,1,0:T(8,128)(2,1)S(1)}, bf16[16,16,640]{2,1,0:T(8,128)(2,1)S(1)}, u32[]{:S(2)}, u32[]{:S(2)}) collective-permute-start(bf16[16,16,640]{2,1,0:T(8,128)(2,1)S(1)} %constant_dynamic-update-slice_fusion.2.after_ref.refs_1_), channel_id=1, source_target_pairs={{0,12},{1,19},{4,0},{5,23},{8,4},{9,27},{12,8},{13,31},{2,14},{3,1... | collective-permute-start | bytes 983048 | tf_op jit(solution)/shard_map/ppermute | solution.py:365
  30.5 0.5 collective-permute-start.5
  30.9 1.0 collective-permute-start.4
  31.9 4.9 %shard_map.104 = (bf16[128,29568]{1,0:T(8,128)(2,1)S(1)}, bf16[128,8192]{1,0:T(8,128)(2,1)S(1)}, bf16[128,8192]{1,0:T(8,128)(2,1)S(1)}) custom-call(bf16[16,16,640]{2,1,0:T(8,128)(2,1)S(1)} %constant_dynamic-update-slice_fusion.2.after_ref.refs_1_, s32[4]{0:T(128)S(1)} %pad_add_fusion.place_ref, bf16[128,29568]{1,0:T(8,128)(2,1)} %bitcast.25, ...), custom_call_target="tpu_custom_call" | custom-call | bytes 23527424 | tf_op jit(solution)/shard_map/pallas_call | solution.py:269
  36.9 2.7 %collective-permute-start.13 = (bf16[16,16,640]{2,1,0:T(8,128)(2,1)S(1)}, bf16[16,16,640]{2,1,0:T(8,128)(2,1)S(1)}, u32[]{:S(2)}, u32[]{:S(2)}) collective-permute-start(bf16[16,16,640]{2,1,0:T(8,128)(2,1)S(1)} %collective-permute-done.6.refs_7_), channel_id=1, source_target_pairs={{0,12},{1,19},{4,0},{5,23},{8,4},{9,27},{12,8},{13,31},{2,14},{3,1... | collective-permute-start | bytes 983048 | tf_op jit(solution)/shard_map/ppermute | solution.py:365
  39.6 7.3 %collective-permute-start.7 = (bf16[16,16,640]{2,1,0:T(8,128)(2,1)S(1)}, bf16[16,16,640]{2,1,0:T(8,128)(2,1)S(1)}, u32[]{:S(2)}, u32[]{:S(2)}) collective-permute-start(bf16[16,16,640]{2,1,0:T(8,128)(2,1)S(1)} %constant_dynamic-update-slice_fusion.refs_0_), channel_id=1, source_target_pairs={{0,1},{1,0},{2,3},{3,2},{4,5},{5,4},{6,7},{7,6},{8,9},{9,8},{10,11... | collective-permute-start | bytes 983048 | tf_op jit(solution)/shard_map/ppermute | solution.py:369
  47.0 0.4 collective-permute-start.9
  47.4 4.4 %collective-permute-start.10 = (bf16[16,16,640]{2,1,0:T(8,128)(2,1)S(1)}, bf16[16,16,640]{2,1,0:T(8,128)(2,1)S(1)}, u32[]{:S(2)}, u32[]{:S(2)}) collective-permute-start(bf16[16,16,640]{2,1,0:T(8,128)(2,1)S(1)} %collective-permute-done.4.refs_3_), channel_id=1, source_target_pairs={{0,1},{1,0},{2,3},{3,2},{4,5},{5,4},{6,7},{7,6},{8,9},{9,8},{10,11... | collective-permute-start | bytes 983048 | tf_op jit(solution)/shard_map/ppermute | solution.py:369
  51.8 0.5 collective-permute-start.16
  52.5 0.4 collective-permute-start.14
  52.9 3.6 %shard_map.105 = (bf16[32,8192]{1,0:T(8,128)(2,1)S(1)}, f32[128,32]{1,0:T(8,128)S(1)}, f32[2,64,128]{2,1,0:T(8,128)S(1)}, f32[8,128]{1,0:T(8,128)S(1)}) custom-call(s32[4]{0:T(128)S(1)} %pad_add_fusion.place_ref, bf16[16,16,640]{2,1,0:T(8,128)(2,1)S(1)} %constant_dynamic-update-slice_fusion.refs_0_, ...), custom_call_target="tpu_custom_call" | custom-call | flops 242221056 | bytes 12812288 | tf_op jit(solution)/shard_map/pallas_call | solution.py:290
  56.6 11.3 %shard_map.106 = (bf16[64,16,640]{2,1,0:T(8,128)(2,1)S(1)}, bf16[64,16,640]{2,1,0:T(8,128)(2,1)S(1)}, bf16[64,4096]{1,0:T(8,128)(2,1)S(1)}, bf16[64,128]{1,0:T(8,128)(2,1)S(1)}, f32[8,128]{1,0:T(8,128)S(1)}) custom-call(s32[4]{0:T(128)S(1)} %pad_add_fusion.place_ref, s32[1,2]{1,0:T(1,128)S(1)} %copy-done, ...), custom_call_target="tpu_custom_call" | custom-call | flops 1505755136 | bytes 22249472 | tf_op jit(solution)/shard_map/pallas_call | solution.py:312
  67.8 0.4 collective-permute-start.17
  68.2 1.7 %shard_map.107 = (bf16[64,16,640]{2,1,0:T(8,128)(2,1)S(1)}, bf16[64,16,640]{2,1,0:T(8,128)(2,1)S(1)}) custom-call(s32[4]{0:T(128)S(1)} %pad_add_fusion.place_ref, bf16[64,128]{1,0:T(8,128)(2,1)S(1)} %get-tuple-element.47.low_ref, bf16[64,4096]{1,0:T(8,128)(2,1)S(1)} %get-tuple-element.48.up_rest, bf16[128,29568]{1,0:T(8,128)(2,1)S(1)} %get-tuple-element.37.refs_8_.hid), custom_call_target="tpu_custom_call" | custom-call | flops 242221056 | bytes 6406144 | tf_op jit(solution)/shard_map/pallas_call | solution.py:339
  69.8 0.3 collective-permute-start.21
  70.2 0.8 collective-permute-done.17
  71.0 0.3 add_convert_fusion.8
  71.2 0.3 collective-permute-start.18
  71.5 2.7 %collective-permute-start.20 = (bf16[16,16,640]{2,1,0:T(8,128)(2,1)S(1)}, bf16[16,16,640]{2,1,0:T(8,128)(2,1)S(1)}, u32[]{:S(2)}, u32[]{:S(2)}) collective-permute-start(bf16[16,16,640]{2,1,0:T(8,128)(2,1)S(1)} %get-tuple-element.54), channel_id=1, source_target_pairs={{0,12},{1,19},{4,0},{5,23},{8,4},{9,27},{12,8},{13,31},{2,14},{3,1... | collective-permute-start | bytes 983048 | tf_op jit(solution)/shard_map/ppermute | solution.py:365
  74.2 0.5 collective-permute-start.19
  74.7 0.3 add_convert_fusion.3
  75.1 2.6 %collective-permute-start.24 = (bf16[16,16,640]{2,1,0:T(8,128)(2,1)S(1)}, bf16[16,16,640]{2,1,0:T(8,128)(2,1)S(1)}, u32[]{:S(2)}, u32[]{:S(2)}) collective-permute-start(bf16[16,16,640]{2,1,0:T(8,128)(2,1)S(1)} %get-tuple-element.57), channel_id=1, source_target_pairs={{0,12},{1,19},{4,0},{5,23},{8,4},{9,27},{12,8},{13,31},{2,14},{3,1... | collective-permute-start | bytes 983048 | tf_op jit(solution)/shard_map/ppermute | solution.py:365
  77.7 4.8 %collective-permute-done.18 = bf16[16,16,640]{2,1,0:T(8,128)(2,1)S(1)} collective-permute-done((bf16[16,16,640]{2,1,0:T(8,128)(2,1)S(1)}, bf16[16,16,640]{2,1,0:T(8,128)(2,1)S(1)}, u32[]{:S(2)}, u32[]{:S(2)}) %collective-permute-start.18) | collective-permute-done | bytes 327712 | tf_op jit(solution)/shard_map/ppermute | solution.py:365
  82.5 0.5 collective-permute-start.23
  82.9 0.2 add_convert_fusion.5
  83.2 2.8 %collective-permute-done.22 = bf16[16,16,640]{2,1,0:T(8,128)(2,1)S(1)} collective-permute-done((bf16[16,16,640]{2,1,0:T(8,128)(2,1)S(1)}, bf16[16,16,640]{2,1,0:T(8,128)(2,1)S(1)}, u32[]{:S(2)}, u32[]{:S(2)}) %collective-permute-start.22) | collective-permute-done | bytes 327712 | tf_op jit(solution)/shard_map/ppermute | solution.py:365
  86.0 2.8 %collective-permute-done.24 = bf16[16,16,640]{2,1,0:T(8,128)(2,1)S(1)} collective-permute-done((bf16[16,16,640]{2,1,0:T(8,128)(2,1)S(1)}, bf16[16,16,640]{2,1,0:T(8,128)(2,1)S(1)}, u32[]{:S(2)}, u32[]{:S(2)}) %collective-permute-start.24) | collective-permute-done | bytes 327712 | tf_op jit(solution)/shard_map/ppermute | solution.py:365
  88.8 1.4 %collective-permute-done.23 = bf16[16,16,640]{2,1,0:T(8,128)(2,1)S(1)} collective-permute-done((bf16[16,16,640]{2,1,0:T(8,128)(2,1)S(1)}, bf16[16,16,640]{2,1,0:T(8,128)(2,1)S(1)}, u32[]{:S(2)}, u32[]{:S(2)}) %collective-permute-start.23) | collective-permute-done | bytes 327712 | tf_op jit(solution)/shard_map/ppermute | solution.py:365
  90.2 0.2 add_convert_fusion
  90.6 2.7 %collective-permute-start.27 = (bf16[8,16,640]{2,1,0:T(8,128)(2,1)S(1)}, bf16[8,16,640]{2,1,0:T(8,128)(2,1)S(1)}, u32[]{:S(2)}, u32[]{:S(2)}) collective-permute-start(bf16[8,16,640]{2,1,0:T(8,128)(2,1)S(1)} %get-tuple-element.60), channel_id=1, source_target_pairs={{0,18},{1,13},{4,22},{5,1},{8,26},{9,5},{12,30},{13,9},{2,0},{3,15... | collective-permute-start | bytes 491528 | tf_op jit(solution)/shard_map/ppermute | solution.py:365
  93.2 0.9 collective-permute-start.26
  94.2 1.8 %collective-permute-done.25 = bf16[8,16,640]{2,1,0:T(8,128)(2,1)S(1)} collective-permute-done((bf16[8,16,640]{2,1,0:T(8,128)(2,1)S(1)}, bf16[8,16,640]{2,1,0:T(8,128)(2,1)S(1)}, u32[]{:S(2)}, u32[]{:S(2)}) %collective-permute-start.25) | collective-permute-done | bytes 163872 | tf_op jit(solution)/shard_map/ppermute | solution.py:365
  96.0 3.0 %collective-permute-done.26 = bf16[8,16,640]{2,1,0:T(8,128)(2,1)S(1)} collective-permute-done((bf16[8,16,640]{2,1,0:T(8,128)(2,1)S(1)}, bf16[8,16,640]{2,1,0:T(8,128)(2,1)S(1)}, u32[]{:S(2)}, u32[]{:S(2)}) %collective-permute-start.26) | collective-permute-done | bytes 163872 | tf_op jit(solution)/shard_map/ppermute | solution.py:365
  99.0 10.8 %all_to_all.11 = bf16[8,16,640]{2,1,0:T(8,128)(2,1)S(1)} all-to-all(bf16[8,16,640]{2,1,0:T(8,128)(2,1)S(1)} %fusion.2), channel_id=1, replica_groups=mesh['z'=8,'yh'=2,'x'=4,'yl'=2,'c'=2] {'z'}, dimensions={0} | all-to-all | bytes 327680 | tf_op jit(solution)/shard_map/all_to_all | solution.py:430
  109.8 3.2 %collective-permute-start.30 = (f32[16,640]{1,0:T(8,128)S(1)}, f32[16,640]{1,0:T(8,128)S(1)}, u32[]{:S(2)}, u32[]{:S(2)}) collective-permute-start(f32[16,640]{1,0:T(8,128)S(1)} %convert_reduce_fusion.refs_0_), channel_id=1, source_target_pairs={{0,3},{1,2},{2,1},{3,0},{4,7},{5,6},{6,5},{7,4},{8,11},{9,10},{10,... | collective-permute-start | bytes 122888 | tf_op jit(solution)/shard_map/ppermute | solution.py:432
  113.0 1.4 %collective-permute-start.29 = (f32[16,640]{1,0:T(8,128)S(1)}, f32[16,640]{1,0:T(8,128)S(1)}, u32[]{:S(2)}, u32[]{:S(2)}) collective-permute-start(f32[16,640]{1,0:T(8,128)S(1)} %convert_reduce_fusion.refs_0_), channel_id=1, source_target_pairs={{0,1},{1,0},{2,3},{3,2},{4,5},{5,4},{6,7},{7,6},{8,9},{9,8},{10,11... | collective-permute-start | bytes 122888 | tf_op jit(solution)/shard_map/ppermute | solution.py:432
  114.4 1.3 %collective-permute-start.28 = (f32[16,640]{1,0:T(8,128)S(1)}, f32[16,640]{1,0:T(8,128)S(1)}, u32[]{:S(2)}, u32[]{:S(2)}) collective-permute-start(f32[16,640]{1,0:T(8,128)S(1)} %convert_reduce_fusion.refs_0_), channel_id=1, source_target_pairs={{0,2},{1,3},{2,0},{3,1},{4,6},{5,7},{6,4},{7,5},{8,10},{9,11},{10,... | collective-permute-start | bytes 122888 | tf_op jit(solution)/shard_map/ppermute | solution.py:432
  115.7 0.5 slice.63
  116.9 1.0 collective-permute-done.28.refs_1_
  117.9 1.2 %shard_map.108 = (f32[64,462]{1,0:T(8,128)}, f32[64,128]{1,0:T(8,128)}) custom-call(s32[4]{0:T(128)S(1)} %pad_add_fusion.place_ref, f32[16,640]{1,0:T(8,128)S(1)} %convert_reduce_fusion.refs_0_, f32[16,640]{1,0:T(8,128)S(1)} %collective-permute-done.28.refs_1_, f32[16,640]{1,0:T(8,128)S(1)} %collective-permute-done.29.refs_2_, ...), custom_call_target="tpu_custom_call" | custom-call | tf_op jit(solution)/shard_map/pallas_call | solution.py:245
  (37 shorter events, 1.0 us)
Async XLA Ops:
  19.2 5.4 %collective-permute-start = (bf16[8,16,640]{2,1,0:T(8,128)(2,1)S(1)}, bf16[8,16,640]{2,1,0:T(8,128)(2,1)S(1)}, u32[]{:S(2)}, u32[]{:S(2)}) collective-permute-start(bf16[8,16,640]{2,1,0:T(8,128)(2,1)S(1)} %all_to_all.10), channel_id=1, source_target_pairs={{0,2},{1,5},{4,6},{5,9},{8,10},{9,13},{12,14},{13,1},{2,16},{3,7},... | collective-permute-start | bytes 491528 | tf_op jit(solution)/shard_map/ppermute | solution.py:365
  20.4 7.2 %collective-permute-start.2 = (bf16[8,16,640]{2,1,0:T(8,128)(2,1)S(1)}, bf16[8,16,640]{2,1,0:T(8,128)(2,1)S(1)}, u32[]{:S(2)}, u32[]{:S(2)}) collective-permute-start(bf16[8,16,640]{2,1,0:T(8,128)(2,1)S(1)} %all_to_all.10), channel_id=1, source_target_pairs={{0,18},{1,13},{4,22},{5,1},{8,26},{9,5},{12,30},{13,9},{2,0},{3,15... | collective-permute-start | bytes 491528 | tf_op jit(solution)/shard_map/ppermute | solution.py:365
  21.9 5.7 %collective-permute-start.1 = (bf16[8,16,640]{2,1,0:T(8,128)(2,1)S(1)}, bf16[8,16,640]{2,1,0:T(8,128)(2,1)S(1)}, u32[]{:S(2)}, u32[]{:S(2)}) collective-permute-start(bf16[8,16,640]{2,1,0:T(8,128)(2,1)S(1)} %all_to_all.10), channel_id=1, source_target_pairs={{0,16},{1,9},{4,20},{5,13},{8,24},{9,1},{12,28},{13,5},{2,18},{3,1... | collective-permute-start | bytes 491528 | tf_op jit(solution)/shard_map/ppermute | solution.py:365
  24.6 12.2 %collective-permute-start.3 = (bf16[16,16,640]{2,1,0:T(8,128)(2,1)S(1)}, bf16[16,16,640]{2,1,0:T(8,128)(2,1)S(1)}, u32[]{:S(2)}, u32[]{:S(2)}) collective-permute-start(bf16[16,16,640]{2,1,0:T(8,128)(2,1)S(1)} %constant_dynamic-update-slice_fusion.refs_0_), channel_id=1, source_target_pairs={{0,4},{1,3},{4,8},{5,7},{8,12},{9,11},{12,0},{13,15},{2,6},{3,17},... | collective-permute-start | bytes 983048 | tf_op jit(solution)/shard_map/ppermute | solution.py:365
  27.6 9.3 %collective-permute-start.6 = (bf16[16,16,640]{2,1,0:T(8,128)(2,1)S(1)}, bf16[16,16,640]{2,1,0:T(8,128)(2,1)S(1)}, u32[]{:S(2)}, u32[]{:S(2)}) collective-permute-start(bf16[16,16,640]{2,1,0:T(8,128)(2,1)S(1)} %constant_dynamic-update-slice_fusion.2.after_ref.refs_1_), channel_id=1, source_target_pairs={{0,12},{1,19},{4,0},{5,23},{8,4},{9,27},{12,8},{13,31},{2,14},{3,1... | collective-permute-start | bytes 983048 | tf_op jit(solution)/shard_map/ppermute | solution.py:365
  30.5 9.2 %collective-permute-start.5 = (bf16[16,16,640]{2,1,0:T(8,128)(2,1)S(1)}, bf16[16,16,640]{2,1,0:T(8,128)(2,1)S(1)}, u32[]{:S(2)}, u32[]{:S(2)}) collective-permute-start(bf16[16,16,640]{2,1,0:T(8,128)(2,1)S(1)} %constant_dynamic-update-slice_fusion.refs_0_), channel_id=1, source_target_pairs={{0,12},{1,19},{4,0},{5,23},{8,4},{9,27},{12,8},{13,31},{2,14},{3,1... | collective-permute-start | bytes 983048 | tf_op jit(solution)/shard_map/ppermute | solution.py:365
  30.9 8.7 %collective-permute-start.4 = (bf16[16,16,640]{2,1,0:T(8,128)(2,1)S(1)}, bf16[16,16,640]{2,1,0:T(8,128)(2,1)S(1)}, u32[]{:S(2)}, u32[]{:S(2)}) collective-permute-start(bf16[16,16,640]{2,1,0:T(8,128)(2,1)S(1)} %constant_dynamic-update-slice_fusion.2.after_ref.refs_1_), channel_id=1, source_target_pairs={{0,4},{1,3},{4,8},{5,7},{8,12},{9,11},{12,0},{13,15},{2,6},{3,17},... | collective-permute-start | bytes 983048 | tf_op jit(solution)/shard_map/ppermute | solution.py:365
  36.8 10.6 %collective-permute-start.11 = (bf16[16,16,640]{2,1,0:T(8,128)(2,1)S(1)}, bf16[16,16,640]{2,1,0:T(8,128)(2,1)S(1)}, u32[]{:S(2)}, u32[]{:S(2)}) collective-permute-start(bf16[16,16,640]{2,1,0:T(8,128)(2,1)S(1)} %collective-permute-done.3.refs_2_), channel_id=1, source_target_pairs={{0,4},{1,3},{4,8},{5,7},{8,12},{9,11},{12,0},{13,15},{2,6},{3,17},... | collective-permute-start | bytes 983048 | tf_op jit(solution)/shard_map/ppermute | solution.py:365
  36.9 14.9 %collective-permute-start.13 = (bf16[16,16,640]{2,1,0:T(8,128)(2,1)S(1)}, bf16[16,16,640]{2,1,0:T(8,128)(2,1)S(1)}, u32[]{:S(2)}, u32[]{:S(2)}) collective-permute-start(bf16[16,16,640]{2,1,0:T(8,128)(2,1)S(1)} %collective-permute-done.6.refs_7_), channel_id=1, source_target_pairs={{0,12},{1,19},{4,0},{5,23},{8,4},{9,27},{12,8},{13,31},{2,14},{3,1... | collective-permute-start | bytes 983048 | tf_op jit(solution)/shard_map/ppermute | solution.py:365
  39.6 17.0 %copy-start = (s32[1,2]{1,0:T(1,128)S(1)}, s32[1,2]{1,0:T(1,128)}, u32[]{:S(2)}) copy-start(s32[1,2]{1,0:T(1,128)} %starts_ref.1) | copy-start | bytes 28
  39.6 12.2 %collective-permute-start.7 = (bf16[16,16,640]{2,1,0:T(8,128)(2,1)S(1)}, bf16[16,16,640]{2,1,0:T(8,128)(2,1)S(1)}, u32[]{:S(2)}, u32[]{:S(2)}) collective-permute-start(bf16[16,16,640]{2,1,0:T(8,128)(2,1)S(1)} %constant_dynamic-update-slice_fusion.refs_0_), channel_id=1, source_target_pairs={{0,1},{1,0},{2,3},{3,2},{4,5},{5,4},{6,7},{7,6},{8,9},{9,8},{10,11... | collective-permute-start | bytes 983048 | tf_op jit(solution)/shard_map/ppermute | solution.py:369
  46.9 5.5 %collective-permute-start.8 = (bf16[16,16,640]{2,1,0:T(8,128)(2,1)S(1)}, bf16[16,16,640]{2,1,0:T(8,128)(2,1)S(1)}, u32[]{:S(2)}, u32[]{:S(2)}) collective-permute-start(bf16[16,16,640]{2,1,0:T(8,128)(2,1)S(1)} %constant_dynamic-update-slice_fusion.2.after_ref.refs_1_), channel_id=1, source_target_pairs={{0,1},{1,0},{2,3},{3,2},{4,5},{5,4},{6,7},{7,6},{8,9},{9,8},{10,11... | collective-permute-start | bytes 983048 | tf_op jit(solution)/shard_map/ppermute | solution.py:369
  47.0 5.5 %collective-permute-start.9 = (bf16[16,16,640]{2,1,0:T(8,128)(2,1)S(1)}, bf16[16,16,640]{2,1,0:T(8,128)(2,1)S(1)}, u32[]{:S(2)}, u32[]{:S(2)}) collective-permute-start(bf16[16,16,640]{2,1,0:T(8,128)(2,1)S(1)} %collective-permute-done.3.refs_2_), channel_id=1, source_target_pairs={{0,1},{1,0},{2,3},{3,2},{4,5},{5,4},{6,7},{7,6},{8,9},{9,8},{10,11... | collective-permute-start | bytes 983048 | tf_op jit(solution)/shard_map/ppermute | solution.py:369
  47.4 9.1 %collective-permute-start.10 = (bf16[16,16,640]{2,1,0:T(8,128)(2,1)S(1)}, bf16[16,16,640]{2,1,0:T(8,128)(2,1)S(1)}, u32[]{:S(2)}, u32[]{:S(2)}) collective-permute-start(bf16[16,16,640]{2,1,0:T(8,128)(2,1)S(1)} %collective-permute-done.4.refs_3_), channel_id=1, source_target_pairs={{0,1},{1,0},{2,3},{3,2},{4,5},{5,4},{6,7},{7,6},{8,9},{9,8},{10,11... | collective-permute-start | bytes 983048 | tf_op jit(solution)/shard_map/ppermute | solution.py:369
  51.8 4.7 %collective-permute-start.15 = (bf16[16,16,640]{2,1,0:T(8,128)(2,1)S(1)}, bf16[16,16,640]{2,1,0:T(8,128)(2,1)S(1)}, u32[]{:S(2)}, u32[]{:S(2)}) collective-permute-start(bf16[16,16,640]{2,1,0:T(8,128)(2,1)S(1)} %collective-permute-done.5.refs_6_), channel_id=1, source_target_pairs={{0,1},{1,0},{2,3},{3,2},{4,5},{5,4},{6,7},{7,6},{8,9},{9,8},{10,11... | collective-permute-start | bytes 983048 | tf_op jit(solution)/shard_map/ppermute | solution.py:369
  51.8 4.7 %collective-permute-start.16 = (bf16[16,16,640]{2,1,0:T(8,128)(2,1)S(1)}, bf16[16,16,640]{2,1,0:T(8,128)(2,1)S(1)}, u32[]{:S(2)}, u32[]{:S(2)}) collective-permute-start(bf16[16,16,640]{2,1,0:T(8,128)(2,1)S(1)} %collective-permute-done.6.refs_7_), channel_id=1, source_target_pairs={{0,1},{1,0},{2,3},{3,2},{4,5},{5,4},{6,7},{7,6},{8,9},{9,8},{10,11... | collective-permute-start | bytes 983048 | tf_op jit(solution)/shard_map/ppermute | solution.py:369
  52.4 4.2 %collective-permute-start.12 = (bf16[16,16,640]{2,1,0:T(8,128)(2,1)S(1)}, bf16[16,16,640]{2,1,0:T(8,128)(2,1)S(1)}, u32[]{:S(2)}, u32[]{:S(2)}) collective-permute-start(bf16[16,16,640]{2,1,0:T(8,128)(2,1)S(1)} %collective-permute-done.11.refs_4_), channel_id=1, source_target_pairs={{0,1},{1,0},{2,3},{3,2},{4,5},{5,4},{6,7},{7,6},{8,9},{9,8},{10,11... | collective-permute-start | bytes 983048 | tf_op jit(solution)/shard_map/ppermute | solution.py:369
  52.5 4.1 %collective-permute-start.14 = (bf16[16,16,640]{2,1,0:T(8,128)(2,1)S(1)}, bf16[16,16,640]{2,1,0:T(8,128)(2,1)S(1)}, u32[]{:S(2)}, u32[]{:S(2)}) collective-permute-start(bf16[16,16,640]{2,1,0:T(8,128)(2,1)S(1)} %collective-permute-done.13.refs_5_), channel_id=1, source_target_pairs={{0,1},{1,0},{2,3},{3,2},{4,5},{5,4},{6,7},{7,6},{8,9},{9,8},{10,11... | collective-permute-start | bytes 983048 | tf_op jit(solution)/shard_map/ppermute | solution.py:369
  67.8 3.1 %collective-permute-start.17 = (bf16[64,16,640]{2,1,0:T(8,128)(2,1)S(1)}, bf16[64,16,640]{2,1,0:T(8,128)(2,1)S(1)}, u32[]{:S(2)}, u32[]{:S(2)}) collective-permute-start(bf16[64,16,640]{2,1,0:T(8,128)(2,1)S(1)} %get-tuple-element.46), channel_id=1, source_target_pairs={{0,1},{1,0},{2,3},{3,2},{4,5},{5,4},{6,7},{7,6},{8,9},{9,8},{10,11... | collective-permute-start | bytes 3932168 | tf_op jit(solution)/shard_map/ppermute | solution.py:369
  69.8 4.8 %collective-permute-start.21 = (bf16[64,16,640]{2,1,0:T(8,128)(2,1)S(1)}, bf16[64,16,640]{2,1,0:T(8,128)(2,1)S(1)}, u32[]{:S(2)}, u32[]{:S(2)}) collective-permute-start(bf16[64,16,640]{2,1,0:T(8,128)(2,1)S(1)} %get-tuple-element.50), channel_id=1, source_target_pairs={{0,1},{1,0},{2,3},{3,2},{4,5},{5,4},{6,7},{7,6},{8,9},{9,8},{10,11... | collective-permute-start | bytes 3932168 | tf_op jit(solution)/shard_map/ppermute | solution.py:369
  71.2 11.2 %collective-permute-start.18 = (bf16[16,16,640]{2,1,0:T(8,128)(2,1)S(1)}, bf16[16,16,640]{2,1,0:T(8,128)(2,1)S(1)}, u32[]{:S(2)}, u32[]{:S(2)}) collective-permute-start(bf16[16,16,640]{2,1,0:T(8,128)(2,1)S(1)} %get-tuple-element.53), channel_id=1, source_target_pairs={{0,4},{1,3},{4,8},{5,7},{8,12},{9,11},{12,0},{13,15},{2,6},{3,17},... | collective-permute-start | bytes 983048 | tf_op jit(solution)/shard_map/ppermute | solution.py:365
  71.5 11.4 %collective-permute-start.20 = (bf16[16,16,640]{2,1,0:T(8,128)(2,1)S(1)}, bf16[16,16,640]{2,1,0:T(8,128)(2,1)S(1)}, u32[]{:S(2)}, u32[]{:S(2)}) collective-permute-start(bf16[16,16,640]{2,1,0:T(8,128)(2,1)S(1)} %get-tuple-element.54), channel_id=1, source_target_pairs={{0,12},{1,19},{4,0},{5,23},{8,4},{9,27},{12,8},{13,31},{2,14},{3,1... | collective-permute-start | bytes 983048 | tf_op jit(solution)/shard_map/ppermute | solution.py:365
  74.2 8.7 %collective-permute-start.19 = (bf16[16,16,640]{2,1,0:T(8,128)(2,1)S(1)}, bf16[16,16,640]{2,1,0:T(8,128)(2,1)S(1)}, u32[]{:S(2)}, u32[]{:S(2)}) collective-permute-start(bf16[16,16,640]{2,1,0:T(8,128)(2,1)S(1)} %get-tuple-element.55), channel_id=1, source_target_pairs={{0,8},{1,17},{4,12},{5,21},{8,0},{9,25},{12,4},{13,29},{2,10},{3,1... | collective-permute-start | bytes 983048 | tf_op jit(solution)/shard_map/ppermute | solution.py:365
  74.9 11.0 %collective-permute-start.22 = (bf16[16,16,640]{2,1,0:T(8,128)(2,1)S(1)}, bf16[16,16,640]{2,1,0:T(8,128)(2,1)S(1)}, u32[]{:S(2)}, u32[]{:S(2)}) collective-permute-start(bf16[16,16,640]{2,1,0:T(8,128)(2,1)S(1)} %get-tuple-element.56), channel_id=1, source_target_pairs={{0,4},{1,3},{4,8},{5,7},{8,12},{9,11},{12,0},{13,15},{2,6},{3,17},... | collective-permute-start | bytes 983048 | tf_op jit(solution)/shard_map/ppermute | solution.py:365
  75.1 13.6 %collective-permute-start.24 = (bf16[16,16,640]{2,1,0:T(8,128)(2,1)S(1)}, bf16[16,16,640]{2,1,0:T(8,128)(2,1)S(1)}, u32[]{:S(2)}, u32[]{:S(2)}) collective-permute-start(bf16[16,16,640]{2,1,0:T(8,128)(2,1)S(1)} %get-tuple-element.57), channel_id=1, source_target_pairs={{0,12},{1,19},{4,0},{5,23},{8,4},{9,27},{12,8},{13,31},{2,14},{3,1... | collective-permute-start | bytes 983048 | tf_op jit(solution)/shard_map/ppermute | solution.py:365
  82.5 7.7 %collective-permute-start.23 = (bf16[16,16,640]{2,1,0:T(8,128)(2,1)S(1)}, bf16[16,16,640]{2,1,0:T(8,128)(2,1)S(1)}, u32[]{:S(2)}, u32[]{:S(2)}) collective-permute-start(bf16[16,16,640]{2,1,0:T(8,128)(2,1)S(1)} %get-tuple-element.58), channel_id=1, source_target_pairs={{0,8},{1,17},{4,12},{5,21},{8,0},{9,25},{12,4},{13,29},{2,10},{3,1... | collective-permute-start | bytes 983048 | tf_op jit(solution)/shard_map/ppermute | solution.py:365
  90.5 5.5 %collective-permute-start.25 = (bf16[8,16,640]{2,1,0:T(8,128)(2,1)S(1)}, bf16[8,16,640]{2,1,0:T(8,128)(2,1)S(1)}, u32[]{:S(2)}, u32[]{:S(2)}) collective-permute-start(bf16[8,16,640]{2,1,0:T(8,128)(2,1)S(1)} %get-tuple-element.59), channel_id=1, source_target_pairs={{0,2},{1,5},{4,6},{5,9},{8,10},{9,13},{12,14},{13,1},{2,16},{3,7},... | collective-permute-start | bytes 491528 | tf_op jit(solution)/shard_map/ppermute | solution.py:365
  90.6 5.4 %collective-permute-start.27 = (bf16[8,16,640]{2,1,0:T(8,128)(2,1)S(1)}, bf16[8,16,640]{2,1,0:T(8,128)(2,1)S(1)}, u32[]{:S(2)}, u32[]{:S(2)}) collective-permute-start(bf16[8,16,640]{2,1,0:T(8,128)(2,1)S(1)} %get-tuple-element.60), channel_id=1, source_target_pairs={{0,18},{1,13},{4,22},{5,1},{8,26},{9,5},{12,30},{13,9},{2,0},{3,15... | collective-permute-start | bytes 491528 | tf_op jit(solution)/shard_map/ppermute | solution.py:365
  93.2 5.7 %collective-permute-start.26 = (bf16[8,16,640]{2,1,0:T(8,128)(2,1)S(1)}, bf16[8,16,640]{2,1,0:T(8,128)(2,1)S(1)}, u32[]{:S(2)}, u32[]{:S(2)}) collective-permute-start(bf16[8,16,640]{2,1,0:T(8,128)(2,1)S(1)} %get-tuple-element.61), channel_id=1, source_target_pairs={{0,16},{1,9},{4,20},{5,13},{8,24},{9,1},{12,28},{13,5},{2,18},{3,1... | collective-permute-start | bytes 491528 | tf_op jit(solution)/shard_map/ppermute | solution.py:365
  109.8 7.1 %collective-permute-start.30 = (f32[16,640]{1,0:T(8,128)S(1)}, f32[16,640]{1,0:T(8,128)S(1)}, u32[]{:S(2)}, u32[]{:S(2)}) collective-permute-start(f32[16,640]{1,0:T(8,128)S(1)} %convert_reduce_fusion.refs_0_), channel_id=1, source_target_pairs={{0,3},{1,2},{2,1},{3,0},{4,7},{5,6},{6,5},{7,4},{8,11},{9,10},{10,... | collective-permute-start | bytes 122888 | tf_op jit(solution)/shard_map/ppermute | solution.py:432
  113.0 3.9 %collective-permute-start.29 = (f32[16,640]{1,0:T(8,128)S(1)}, f32[16,640]{1,0:T(8,128)S(1)}, u32[]{:S(2)}, u32[]{:S(2)}) collective-permute-start(f32[16,640]{1,0:T(8,128)S(1)} %convert_reduce_fusion.refs_0_), channel_id=1, source_target_pairs={{0,1},{1,0},{2,3},{3,2},{4,5},{5,4},{6,7},{7,6},{8,9},{9,8},{10,11... | collective-permute-start | bytes 122888 | tf_op jit(solution)/shard_map/ppermute | solution.py:432
  114.4 3.5 %collective-permute-start.28 = (f32[16,640]{1,0:T(8,128)S(1)}, f32[16,640]{1,0:T(8,128)S(1)}, u32[]{:S(2)}, u32[]{:S(2)}) collective-permute-start(f32[16,640]{1,0:T(8,128)S(1)} %convert_reduce_fusion.refs_0_), channel_id=1, source_target_pairs={{0,2},{1,3},{2,0},{3,1},{4,6},{5,7},{6,4},{7,5},{8,10},{9,11},{10,... | collective-permute-start | bytes 122888 | tf_op jit(solution)/shard_map/ppermute | solution.py:432

commit v10 on v7

--- a/solution.py
+++ b/solution.py
@@ -57,13 +57,13 @@
 
 
 def kernel(place_ref, starts_ref, *refs):
-    parts, (hid, fro, hea) = refs[:8], refs[8:11]
-    outs, up_rest, low_ref, margin_ref = refs[11:13], refs[13], refs[14], refs[15]
-    wt, up, gains, gain, pol, block, sems = refs[16:]
+    parts, (hid, fro, hea) = refs[:16], refs[16:19]
+    outs, up_rest, low_ref, margin_ref = refs[19:21], refs[21], refs[22], refs[23]
+    wt, up, gains, gain, pol, block, sems = refs[24:]
     width = fro.shape[1]
 
     loads = [
-        pltpu.make_async_copy(parts[i], block.at[pl.ds(32 * i, 32)], sems.at[i]) for i in range(8)
+        pltpu.make_async_copy(parts[i], block.at[pl.ds(16 * i, 16)], sems.at[i]) for i in range(16)
     ]
     for copy in loads:
         copy.start()
@@ -202,7 +202,7 @@
     arrays = [starts, *arrays]
     return pl.pallas_call(
         pack,
-        out_shape=jax.ShapeDtypeStruct((8, 16, LANES), BF),
+        out_shape=pltpu.VMEM((8, 16, LANES), BF),
         in_specs=[pl.BlockSpec(memory_space=pltpu.SMEM)]
         + [pl.BlockSpec(memory_space=pl.ANY)] * 5,
         out_specs=pl.BlockSpec(memory_space=pltpu.VMEM),
@@ -233,7 +233,7 @@
         in_specs=[pl.BlockSpec(memory_space=pltpu.SMEM)] + [vmem] * 4,
         out_specs=[vmem] * 2,
         compiler_params=pltpu.CompilerParams(vmem_limit_bytes=4 * 1024 * 1024),
-    )(place, *shares_)
+    )(place, *near_vmem(*shares_))
 
 
 def bring(after_ref, place_ref, *refs):
@@ -277,7 +277,7 @@
             pltpu.VMEM((ORDER, rows), BF),
             jax.ShapeDtypeStruct((8, 128), F32),
         ],
-        in_specs=[smem, smem] + [any_space] * 8 + [vmem] * 3,
+        in_specs=[smem, smem] + [any_space] * 16 + [vmem] * 3,
         out_specs=[vmem] * 5,
         scratch_shapes=[
             pltpu.VMEM((ORDER, units), BF),
@@ -286,7 +286,7 @@
             pltpu.VMEM((CHUNKS, 128), F32),
             pltpu.VMEM((rows, width), F32),
             pltpu.VMEM((256, 16, LANES), BF),
-            pltpu.SemaphoreType.DMA((8,)),
+            pltpu.SemaphoreType.DMA((16,)),
         ],
         compiler_params=pltpu.CompilerParams(vmem_limit_bytes=20 * 1024 * 1024),
         cost_estimate=pl.CostEstimate(
@@ -354,18 +354,23 @@
         final_norm_gain[None],
     )
     held = lax.all_to_all(quarter, "z", 0, 0, tiled=True)
-    line = jnp.concatenate([held] + [ring(held, step, 1) for step in (1, 2, 3)])
-    own = [line] + [ring(line, step) for step in (1, 2, 3)]
+    side = [ring(held, step, 1) for step in (1, 2, 3)]
+    line = [jnp.concatenate([held, side[0]]), jnp.concatenate(side[1:])]
+    behind = [ring(line[0], 1), ring(line[1], 1)]
+    ahead = [ring(line[0], 3), ring(line[1], 3)]
+    opposite = [ring(behind[0], 1), ring(ahead[1], 3)]
     width = frozen.shape[3]
     near = brought(
-        line,
+        line[1],
         place,
         gated_hidden_input.reshape(-1, gated_hidden_input.shape[3]),
         frozen.reshape(-1, width),
         head_gradient_rows.reshape(-1, width),
     )
-    line, *near = lax.optimization_barrier((line, *near))
-    other = [other_core(v) for v in (line, *own[1:])]
+    own = line + behind + opposite + ahead
+    *early, near_0, near_1, near_2 = lax.optimization_barrier((*line, *behind, *ahead, *near))
+    other = [other_core(v) for v in early[:4] + opposite + early[4:]]
+    near = (near_0, near_1, near_2)
 
     first, second, margin = shares(place, starts, [*own, *other], *near)
 

time: 119 us -> 120 us (level)
  starting transfers between devices: 36.7 us -> 42.2 us
  waiting for transfers between devices: 28.1 us -> 23.3 us
    ppermute x15 -> x18, waiting for transfers between devices: 25.1 us -> 19.5 us  [ring(): return lax.ppermute(values, FINE_AXES, pairs)]
    ppermute x15 -> x18, starting transfers between devices: 17.8 us -> 22.5 us  [ring(): return lax.ppermute(values, FINE_AXES, pairs)]
    ppermute x3, starting transfers between devices: 4.36 us -> 5.76 us  [local(): lax.ppermute(share, CTX, [(i, i ^ step) for i in range(4)])]
    ppermute x6 -> x10, starting transfers between devices: 14.6 us -> 13.9 us  [other_core(): return lax.ppermute(values, 'c', [(0, 1), (1, 0)])]
    ppermute x6 -> x10, waiting for transfers between devices: 2.46 us -> 2.84 us  [other_core(): return lax.ppermute(values, 'c', [(0, 1), (1, 0)])]
  transfers between devices with their start and end apart: 24 -> 31, of which waited for: 15 -> 16; matrix products, arithmetic and copies ran while one was open for 1% -> 1% of each run, Pallas kernels for 6% -> 6%
where the time goes in v10:
time: 120 us; the launch traced here: 119 us
  starting transfers between devices  42.2 us (35%)
  blocking collectives  27.7 us (23%)
  waiting for transfers between devices  23.3 us (19%)
  Pallas kernels  21.6 us (18%)
  between operations  2.68 us (2%)
  other arithmetic  1.23 us (1%)
    ppermute x18, starting transfers between devices, ring(): return lax.ppermute(values, FINE_AXES, pairs)  22.5 us
    ppermute x18, waiting for transfers between devices, ring(): return lax.ppermute(values, FINE_AXES, pairs)  19.5 us
    all_to_all x1, blocking collectives, local(): held = lax.all_to_all(quarter, 'z', 0, 0, tiled=True)  17 us
    ppermute x10, starting transfers between devices, other_core(): return lax.ppermute(values, 'c', [(0, 1), (1, 0)])  13.9 us
    pallas_call x1, Pallas kernels, shares(): pl.pallas_call(kernel, out_shape=[pltpu.VMEM((64, 16, LANES), BF)] * 2 +...  12.2 us
    all_to_all x1, blocking collectives, local(): lax.all_to_all(plane, 'z', 0, 0, tiled=True).astype(F32)  10.8 us
    ppermute x3, starting transfers between devices, local(): lax.ppermute(share, CTX, [(i, i ^ step) for i in range(4)])  5.76 us
    pallas_call x1, Pallas kernels, brought(): pl.pallas_call(bring, out_shape=[pltpu.VMEM(v.shape, v.dtype) for v in ar...  4.91 us
  transfers between devices with their start and end apart: 31, of which 16 were waited for; matrix products, arithmetic and copies ran while one was open for 1% of the time, Pallas kernels for 6%

profile of v10, /device:TPU:1, one launch (start us, length us, event | category | flops | bytes accessed | tf_op | source)
XLA Modules:
  0.0 119.3 jit_solution(17692498129182389068)
XLA Ops:
  0.7 1.5 %shard_map.103 = bf16[8,16,640]{2,1,0:T(8,128)(2,1)S(1)} custom-call(s32[4]{0:T(128)S(1)} %pad_add_fusion.place_ref, s32[1,2]{1,0:T(1,128)} %starts_ref.1, f32[2,64]{1,0:T(2,128)} %bitcast.33, bf16[64,462]{1,0:T(8,128)(2,1)} %bitcast.32, bf16[64,128]{1,0:T(8,128)(2,1)} %refs_3_.1, bf16[1,128]{1,0:T(2,128)(2,1)} %bitcast.34), custom_call_target="tpu_custom_call" | custom-call | tf_op jit(solution)/shard_map/pallas_call | solution.py:203
  2.3 17.0 %all_to_all.10 = bf16[8,16,640]{2,1,0:T(8,128)(2,1)S(1)} all-to-all(bf16[8,16,640]{2,1,0:T(8,128)(2,1)S(1)} %shard_map.103), channel_id=1, replica_groups=mesh['z'=8,'yh'=2,'x'=4,'yl'=2,'c'=2] {'z'}, dimensions={0} | all-to-all | bytes 327680 | tf_op jit(solution)/shard_map/all_to_all | solution.py:356
  19.2 1.2 %collective-permute-start = (bf16[8,16,640]{2,1,0:T(8,128)(2,1)S(1)}, bf16[8,16,640]{2,1,0:T(8,128)(2,1)S(1)}, u32[]{:S(2)}, u32[]{:S(2)}) collective-permute-start(bf16[8,16,640]{2,1,0:T(8,128)(2,1)S(1)} %all_to_all.10), channel_id=1, source_target_pairs={{0,2},{1,5},{4,6},{5,9},{8,10},{9,13},{12,14},{13,1},{2,16},{3,7},... | collective-permute-start | bytes 491528 | tf_op jit(solution)/shard_map/ppermute | solution.py:324
  20.4 1.5 %collective-permute-start.2 = (bf16[8,16,640]{2,1,0:T(8,128)(2,1)S(1)}, bf16[8,16,640]{2,1,0:T(8,128)(2,1)S(1)}, u32[]{:S(2)}, u32[]{:S(2)}) collective-permute-start(bf16[8,16,640]{2,1,0:T(8,128)(2,1)S(1)} %all_to_all.10), channel_id=1, source_target_pairs={{0,18},{1,13},{4,22},{5,1},{8,26},{9,5},{12,30},{13,9},{2,0},{3,15... | collective-permute-start | bytes 491528 | tf_op jit(solution)/shard_map/ppermute | solution.py:324
  21.9 1.5 %collective-permute-start.1 = (bf16[8,16,640]{2,1,0:T(8,128)(2,1)S(1)}, bf16[8,16,640]{2,1,0:T(8,128)(2,1)S(1)}, u32[]{:S(2)}, u32[]{:S(2)}) collective-permute-start(bf16[8,16,640]{2,1,0:T(8,128)(2,1)S(1)} %all_to_all.10), channel_id=1, source_target_pairs={{0,16},{1,9},{4,20},{5,13},{8,24},{9,1},{12,28},{13,5},{2,18},{3,1... | collective-permute-start | bytes 491528 | tf_op jit(solution)/shard_map/ppermute | solution.py:324
  23.5 1.2 collective-permute-done
  24.6 1.4 %collective-permute-start.3 = (bf16[16,16,640]{2,1,0:T(8,128)(2,1)S(1)}, bf16[16,16,640]{2,1,0:T(8,128)(2,1)S(1)}, u32[]{:S(2)}, u32[]{:S(2)}) collective-permute-start(bf16[16,16,640]{2,1,0:T(8,128)(2,1)S(1)} %constant_dynamic-update-slice_fusion.refs_0_), channel_id=1, source_target_pairs={{0,4},{1,3},{4,8},{5,7},{8,12},{9,11},{12,0},{13,15},{2,6},{3,17},... | collective-permute-start | bytes 983048 | tf_op jit(solution)/shard_map/ppermute | solution.py:324
  26.0 1.6 %collective-permute-done.1 = bf16[8,16,640]{2,1,0:T(8,128)(2,1)S(1)} collective-permute-done((bf16[8,16,640]{2,1,0:T(8,128)(2,1)S(1)}, bf16[8,16,640]{2,1,0:T(8,128)(2,1)S(1)}, u32[]{:S(2)}, u32[]{:S(2)}) %collective-permute-start.1) | collective-permute-done | bytes 163872 | tf_op jit(solution)/shard_map/ppermute | solution.py:324
  27.6 2.8 %collective-permute-start.6 = (bf16[16,16,640]{2,1,0:T(8,128)(2,1)S(1)}, bf16[16,16,640]{2,1,0:T(8,128)(2,1)S(1)}, u32[]{:S(2)}, u32[]{:S(2)}) collective-permute-start(bf16[16,16,640]{2,1,0:T(8,128)(2,1)S(1)} %constant_dynamic-update-slice_fusion.2.after_ref.refs_1_), channel_id=1, source_target_pairs={{0,12},{1,19},{4,0},{5,23},{8,4},{9,27},{12,8},{13,31},{2,14},{3,1... | collective-permute-start | bytes 983048 | tf_op jit(solution)/shard_map/ppermute | solution.py:324
  30.5 0.5 collective-permute-start.8
  30.9 1.0 collective-permute-start.4
  31.9 4.9 %shard_map.104 = (bf16[128,29568]{1,0:T(8,128)(2,1)S(1)}, bf16[128,8192]{1,0:T(8,128)(2,1)S(1)}, bf16[128,8192]{1,0:T(8,128)(2,1)S(1)}) custom-call(bf16[16,16,640]{2,1,0:T(8,128)(2,1)S(1)} %constant_dynamic-update-slice_fusion.2.after_ref.refs_1_, s32[4]{0:T(128)S(1)} %pad_add_fusion.place_ref, bf16[128,29568]{1,0:T(8,128)(2,1)} %bitcast.25, ...), custom_call_target="tpu_custom_call" | custom-call | bytes 23527424 | tf_op jit(solution)/shard_map/pallas_call | solution.py:251
  36.9 2.7 %collective-permute-start.7 = (bf16[16,16,640]{2,1,0:T(8,128)(2,1)S(1)}, bf16[16,16,640]{2,1,0:T(8,128)(2,1)S(1)}, u32[]{:S(2)}, u32[]{:S(2)}) collective-permute-start(bf16[16,16,640]{2,1,0:T(8,128)(2,1)S(1)} %collective-permute-done.6.refs_7_), channel_id=1, source_target_pairs={{0,12},{1,19},{4,0},{5,23},{8,4},{9,27},{12,8},{13,31},{2,14},{3,1... | collective-permute-start | bytes 983048 | tf_op jit(solution)/shard_map/ppermute | solution.py:324
  39.6 7.2 %collective-permute-start.9 = (bf16[16,16,640]{2,1,0:T(8,128)(2,1)S(1)}, bf16[16,16,640]{2,1,0:T(8,128)(2,1)S(1)}, u32[]{:S(2)}, u32[]{:S(2)}) collective-permute-start(bf16[16,16,640]{2,1,0:T(8,128)(2,1)S(1)} %constant_dynamic-update-slice_fusion.refs_0_), channel_id=1, source_target_pairs={{0,1},{1,0},{2,3},{3,2},{4,5},{5,4},{6,7},{7,6},{8,9},{9,8},{10,11... | collective-permute-start | bytes 983048 | tf_op jit(solution)/shard_map/ppermute | solution.py:328
  46.9 0.4 collective-permute-start.11
  47.3 4.5 %collective-permute-start.12 = (bf16[16,16,640]{2,1,0:T(8,128)(2,1)S(1)}, bf16[16,16,640]{2,1,0:T(8,128)(2,1)S(1)}, u32[]{:S(2)}, u32[]{:S(2)}) collective-permute-start(bf16[16,16,640]{2,1,0:T(8,128)(2,1)S(1)} %collective-permute-done.4.refs_3_), channel_id=1, source_target_pairs={{0,1},{1,0},{2,3},{3,2},{4,5},{5,4},{6,7},{7,6},{8,9},{9,8},{10,11... | collective-permute-start | bytes 983048 | tf_op jit(solution)/shard_map/ppermute | solution.py:328
  51.9 0.5 collective-permute-start.16
  52.5 0.4 collective-permute-start.14
  53.1 0.5 collective-permute-done.15.refs_14_
  53.6 0.5 collective-permute-done.16.refs_15_
  54.0 0.5 collective-permute-done.13.refs_12_
  54.5 0.5 collective-permute-done.14.refs_13_
  55.0 12.2 %shard_map.105 = (bf16[64,16,640]{2,1,0:T(8,128)(2,1)S(1)}, bf16[64,16,640]{2,1,0:T(8,128)(2,1)S(1)}, bf16[64,4096]{1,0:T(8,128)(2,1)S(1)}, bf16[64,128]{1,0:T(8,128)(2,1)S(1)}, f32[8,128]{1,0:T(8,128)S(1)}) custom-call(s32[4]{0:T(128)S(1)} %pad_add_fusion.place_ref, s32[1,2]{1,0:T(1,128)S(1)} %copy-done, ...), custom_call_target="tpu_custom_call" | custom-call | flops 1505755136 | bytes 22249472 | tf_op jit(solution)/shard_map/pallas_call | solution.py:272
  67.2 0.5 collective-permute-start.17
  67.7 1.7 %shard_map.106 = (bf16[64,16,640]{2,1,0:T(8,128)(2,1)S(1)}, bf16[64,16,640]{2,1,0:T(8,128)(2,1)S(1)}) custom-call(s32[4]{0:T(128)S(1)} %pad_add_fusion.place_ref, bf16[64,128]{1,0:T(8,128)(2,1)S(1)} %get-tuple-element.39.low_ref, bf16[64,4096]{1,0:T(8,128)(2,1)S(1)} %get-tuple-element.40.up_rest, bf16[128,29568]{1,0:T(8,128)(2,1)S(1)} %get-tuple-element.33.refs_16_.hid), custom_call_target="tpu_custom_call" | custom-call | flops 242221056 | bytes 6406144 | tf_op jit(solution)/shard_map/pallas_call | solution.py:298
  69.6 0.7 collective-permute-done.17
  70.3 0.3 add_convert_fusion.8
  70.7 2.7 %collective-permute-start.20 = (bf16[16,16,640]{2,1,0:T(8,128)(2,1)S(1)}, bf16[16,16,640]{2,1,0:T(8,128)(2,1)S(1)}, u32[]{:S(2)}, u32[]{:S(2)}) collective-permute-start(bf16[16,16,640]{2,1,0:T(8,128)(2,1)S(1)} %get-tuple-element.46), channel_id=1, source_target_pairs={{0,12},{1,19},{4,0},{5,23},{8,4},{9,27},{12,8},{13,31},{2,14},{3,1... | collective-permute-start | bytes 983048 | tf_op jit(solution)/shard_map/ppermute | solution.py:324
  73.3 0.5 collective-permute-start.19
  73.8 0.3 add_convert_fusion.3
  74.3 2.6 %collective-permute-start.24 = (bf16[16,16,640]{2,1,0:T(8,128)(2,1)S(1)}, bf16[16,16,640]{2,1,0:T(8,128)(2,1)S(1)}, u32[]{:S(2)}, u32[]{:S(2)}) collective-permute-start(bf16[16,16,640]{2,1,0:T(8,128)(2,1)S(1)} %get-tuple-element.49), channel_id=1, source_target_pairs={{0,12},{1,19},{4,0},{5,23},{8,4},{9,27},{12,8},{13,31},{2,14},{3,1... | collective-permute-start | bytes 983048 | tf_op jit(solution)/shard_map/ppermute | solution.py:324
  76.8 4.8 %collective-permute-done.18 = bf16[16,16,640]{2,1,0:T(8,128)(2,1)S(1)} collective-permute-done((bf16[16,16,640]{2,1,0:T(8,128)(2,1)S(1)}, bf16[16,16,640]{2,1,0:T(8,128)(2,1)S(1)}, u32[]{:S(2)}, u32[]{:S(2)}) %collective-permute-start.18) | collective-permute-done | bytes 327712 | tf_op jit(solution)/shard_map/ppermute | solution.py:324
  81.6 0.5 collective-permute-start.23
  82.3 2.8 %collective-permute-done.22 = bf16[16,16,640]{2,1,0:T(8,128)(2,1)S(1)} collective-permute-done((bf16[16,16,640]{2,1,0:T(8,128)(2,1)S(1)}, bf16[16,16,640]{2,1,0:T(8,128)(2,1)S(1)}, u32[]{:S(2)}, u32[]{:S(2)}) %collective-permute-start.22) | collective-permute-done | bytes 327712 | tf_op jit(solution)/shard_map/ppermute | solution.py:324
  85.1 2.8 %collective-permute-done.24 = bf16[16,16,640]{2,1,0:T(8,128)(2,1)S(1)} collective-permute-done((bf16[16,16,640]{2,1,0:T(8,128)(2,1)S(1)}, bf16[16,16,640]{2,1,0:T(8,128)(2,1)S(1)}, u32[]{:S(2)}, u32[]{:S(2)}) %collective-permute-start.24) | collective-permute-done | bytes 327712 | tf_op jit(solution)/shard_map/ppermute | solution.py:324
  87.9 1.4 %collective-permute-done.23 = bf16[16,16,640]{2,1,0:T(8,128)(2,1)S(1)} collective-permute-done((bf16[16,16,640]{2,1,0:T(8,128)(2,1)S(1)}, bf16[16,16,640]{2,1,0:T(8,128)(2,1)S(1)}, u32[]{:S(2)}, u32[]{:S(2)}) %collective-permute-start.23) | collective-permute-done | bytes 327712 | tf_op jit(solution)/shard_map/ppermute | solution.py:324
  89.7 2.7 %collective-permute-start.27 = (bf16[8,16,640]{2,1,0:T(8,128)(2,1)S(1)}, bf16[8,16,640]{2,1,0:T(8,128)(2,1)S(1)}, u32[]{:S(2)}, u32[]{:S(2)}) collective-permute-start(bf16[8,16,640]{2,1,0:T(8,128)(2,1)S(1)} %get-tuple-element.52), channel_id=1, source_target_pairs={{0,18},{1,13},{4,22},{5,1},{8,26},{9,5},{12,30},{13,9},{2,0},{3,15... | collective-permute-start | bytes 491528 | tf_op jit(solution)/shard_map/ppermute | solution.py:324
  92.4 0.7 collective-permute-start.26
  93.1 2.0 %collective-permute-done.25 = bf16[8,16,640]{2,1,0:T(8,128)(2,1)S(1)} collective-permute-done((bf16[8,16,640]{2,1,0:T(8,128)(2,1)S(1)}, bf16[8,16,640]{2,1,0:T(8,128)(2,1)S(1)}, u32[]{:S(2)}, u32[]{:S(2)}) %collective-permute-start.25) | collective-permute-done | bytes 163872 | tf_op jit(solution)/shard_map/ppermute | solution.py:324
  95.1 1.3 %collective-permute-done.27 = bf16[8,16,640]{2,1,0:T(8,128)(2,1)S(1)} collective-permute-done((bf16[8,16,640]{2,1,0:T(8,128)(2,1)S(1)}, bf16[8,16,640]{2,1,0:T(8,128)(2,1)S(1)}, u32[]{:S(2)}, u32[]{:S(2)}) %collective-permute-start.27) | collective-permute-done | bytes 163872 | tf_op jit(solution)/shard_map/ppermute | solution.py:324
  96.4 1.7 %collective-permute-done.26 = bf16[8,16,640]{2,1,0:T(8,128)(2,1)S(1)} collective-permute-done((bf16[8,16,640]{2,1,0:T(8,128)(2,1)S(1)}, bf16[8,16,640]{2,1,0:T(8,128)(2,1)S(1)}, u32[]{:S(2)}, u32[]{:S(2)}) %collective-permute-start.26) | collective-permute-done | bytes 163872 | tf_op jit(solution)/shard_map/ppermute | solution.py:324
  98.1 10.8 %all_to_all.11 = bf16[8,16,640]{2,1,0:T(8,128)(2,1)S(1)} all-to-all(bf16[8,16,640]{2,1,0:T(8,128)(2,1)S(1)} %fusion.2), channel_id=1, replica_groups=mesh['z'=8,'yh'=2,'x'=4,'yl'=2,'c'=2] {'z'}, dimensions={0} | all-to-all | bytes 327680 | tf_op jit(solution)/shard_map/all_to_all | solution.py:389
  108.9 3.1 %collective-permute-start.30 = (f32[16,640]{1,0:T(8,128)S(1)}, f32[16,640]{1,0:T(8,128)S(1)}, u32[]{:S(2)}, u32[]{:S(2)}) collective-permute-start(f32[16,640]{1,0:T(8,128)S(1)} %convert_reduce_fusion.refs_0_), channel_id=1, source_target_pairs={{0,3},{1,2},{2,1},{3,0},{4,7},{5,6},{6,5},{7,4},{8,11},{9,10},{10,... | collective-permute-start | bytes 122888 | tf_op jit(solution)/shard_map/ppermute | solution.py:391
  112.0 1.4 %collective-permute-start.29 = (f32[16,640]{1,0:T(8,128)S(1)}, f32[16,640]{1,0:T(8,128)S(1)}, u32[]{:S(2)}, u32[]{:S(2)}) collective-permute-start(f32[16,640]{1,0:T(8,128)S(1)} %convert_reduce_fusion.refs_0_), channel_id=1, source_target_pairs={{0,1},{1,0},{2,3},{3,2},{4,5},{5,4},{6,7},{7,6},{8,9},{9,8},{10,11... | collective-permute-start | bytes 122888 | tf_op jit(solution)/shard_map/ppermute | solution.py:391
  113.5 1.3 %collective-permute-start.28 = (f32[16,640]{1,0:T(8,128)S(1)}, f32[16,640]{1,0:T(8,128)S(1)}, u32[]{:S(2)}, u32[]{:S(2)}) collective-permute-start(f32[16,640]{1,0:T(8,128)S(1)} %convert_reduce_fusion.refs_0_), channel_id=1, source_target_pairs={{0,2},{1,3},{2,0},{3,1},{4,6},{5,7},{6,4},{7,5},{8,10},{9,11},{10,... | collective-permute-start | bytes 122888 | tf_op jit(solution)/shard_map/ppermute | solution.py:391
  114.7 0.5 slice.63
  116.0 1.0 collective-permute-done.28.refs_1_
  117.0 1.2 %shard_map.107 = (f32[64,462]{1,0:T(8,128)}, f32[64,128]{1,0:T(8,128)}) custom-call(s32[4]{0:T(128)S(1)} %pad_add_fusion.place_ref, f32[16,640]{1,0:T(8,128)S(1)} %convert_reduce_fusion.refs_0_, f32[16,640]{1,0:T(8,128)S(1)} %collective-permute-done.28.refs_1_, f32[16,640]{1,0:T(8,128)S(1)} %collective-permute-done.29.refs_2_, ...), custom_call_target="tpu_custom_call" | custom-call | tf_op jit(solution)/shard_map/pallas_call | solution.py:227
  (36 shorter events, 1.9 us)
Async XLA Ops:
  19.2 5.4 %collective-permute-start = (bf16[8,16,640]{2,1,0:T(8,128)(2,1)S(1)}, bf16[8,16,640]{2,1,0:T(8,128)(2,1)S(1)}, u32[]{:S(2)}, u32[]{:S(2)}) collective-permute-start(bf16[8,16,640]{2,1,0:T(8,128)(2,1)S(1)} %all_to_all.10), channel_id=1, source_target_pairs={{0,2},{1,5},{4,6},{5,9},{8,10},{9,13},{12,14},{13,1},{2,16},{3,7},... | collective-permute-start | bytes 491528 | tf_op jit(solution)/shard_map/ppermute | solution.py:324
  20.4 7.2 %collective-permute-start.2 = (bf16[8,16,640]{2,1,0:T(8,128)(2,1)S(1)}, bf16[8,16,640]{2,1,0:T(8,128)(2,1)S(1)}, u32[]{:S(2)}, u32[]{:S(2)}) collective-permute-start(bf16[8,16,640]{2,1,0:T(8,128)(2,1)S(1)} %all_to_all.10), channel_id=1, source_target_pairs={{0,18},{1,13},{4,22},{5,1},{8,26},{9,5},{12,30},{13,9},{2,0},{3,15... | collective-permute-start | bytes 491528 | tf_op jit(solution)/shard_map/ppermute | solution.py:324
  21.9 5.7 %collective-permute-start.1 = (bf16[8,16,640]{2,1,0:T(8,128)(2,1)S(1)}, bf16[8,16,640]{2,1,0:T(8,128)(2,1)S(1)}, u32[]{:S(2)}, u32[]{:S(2)}) collective-permute-start(bf16[8,16,640]{2,1,0:T(8,128)(2,1)S(1)} %all_to_all.10), channel_id=1, source_target_pairs={{0,16},{1,9},{4,20},{5,13},{8,24},{9,1},{12,28},{13,5},{2,18},{3,1... | collective-permute-start | bytes 491528 | tf_op jit(solution)/shard_map/ppermute | solution.py:324
  24.6 12.2 %collective-permute-start.3 = (bf16[16,16,640]{2,1,0:T(8,128)(2,1)S(1)}, bf16[16,16,640]{2,1,0:T(8,128)(2,1)S(1)}, u32[]{:S(2)}, u32[]{:S(2)}) collective-permute-start(bf16[16,16,640]{2,1,0:T(8,128)(2,1)S(1)} %constant_dynamic-update-slice_fusion.refs_0_), channel_id=1, source_target_pairs={{0,4},{1,3},{4,8},{5,7},{8,12},{9,11},{12,0},{13,15},{2,6},{3,17},... | collective-permute-start | bytes 983048 | tf_op jit(solution)/shard_map/ppermute | solution.py:324
  27.6 9.3 %collective-permute-start.6 = (bf16[16,16,640]{2,1,0:T(8,128)(2,1)S(1)}, bf16[16,16,640]{2,1,0:T(8,128)(2,1)S(1)}, u32[]{:S(2)}, u32[]{:S(2)}) collective-permute-start(bf16[16,16,640]{2,1,0:T(8,128)(2,1)S(1)} %constant_dynamic-update-slice_fusion.2.after_ref.refs_1_), channel_id=1, source_target_pairs={{0,12},{1,19},{4,0},{5,23},{8,4},{9,27},{12,8},{13,31},{2,14},{3,1... | collective-permute-start | bytes 983048 | tf_op jit(solution)/shard_map/ppermute | solution.py:324
  30.5 9.2 %collective-permute-start.8 = (bf16[16,16,640]{2,1,0:T(8,128)(2,1)S(1)}, bf16[16,16,640]{2,1,0:T(8,128)(2,1)S(1)}, u32[]{:S(2)}, u32[]{:S(2)}) collective-permute-start(bf16[16,16,640]{2,1,0:T(8,128)(2,1)S(1)} %constant_dynamic-update-slice_fusion.refs_0_), channel_id=1, source_target_pairs={{0,12},{1,19},{4,0},{5,23},{8,4},{9,27},{12,8},{13,31},{2,14},{3,1... | collective-permute-start | bytes 983048 | tf_op jit(solution)/shard_map/ppermute | solution.py:324
  30.9 8.7 %collective-permute-start.4 = (bf16[16,16,640]{2,1,0:T(8,128)(2,1)S(1)}, bf16[16,16,640]{2,1,0:T(8,128)(2,1)S(1)}, u32[]{:S(2)}, u32[]{:S(2)}) collective-permute-start(bf16[16,16,640]{2,1,0:T(8,128)(2,1)S(1)} %constant_dynamic-update-slice_fusion.2.after_ref.refs_1_), channel_id=1, source_target_pairs={{0,4},{1,3},{4,8},{5,7},{8,12},{9,11},{12,0},{13,15},{2,6},{3,17},... | collective-permute-start | bytes 983048 | tf_op jit(solution)/shard_map/ppermute | solution.py:324
  31.9 23.1 %copy-start = (s32[1,2]{1,0:T(1,128)S(1)}, s32[1,2]{1,0:T(1,128)}, u32[]{:S(2)}) copy-start(s32[1,2]{1,0:T(1,128)} %starts_ref.1) | copy-start | bytes 28
  36.8 10.5 %collective-permute-start.5 = (bf16[16,16,640]{2,1,0:T(8,128)(2,1)S(1)}, bf16[16,16,640]{2,1,0:T(8,128)(2,1)S(1)}, u32[]{:S(2)}, u32[]{:S(2)}) collective-permute-start(bf16[16,16,640]{2,1,0:T(8,128)(2,1)S(1)} %collective-permute-done.3.refs_2_), channel_id=1, source_target_pairs={{0,4},{1,3},{4,8},{5,7},{8,12},{9,11},{12,0},{13,15},{2,6},{3,17},... | collective-permute-start | bytes 983048 | tf_op jit(solution)/shard_map/ppermute | solution.py:324
  36.9 14.9 %collective-permute-start.7 = (bf16[16,16,640]{2,1,0:T(8,128)(2,1)S(1)}, bf16[16,16,640]{2,1,0:T(8,128)(2,1)S(1)}, u32[]{:S(2)}, u32[]{:S(2)}) collective-permute-start(bf16[16,16,640]{2,1,0:T(8,128)(2,1)S(1)} %collective-permute-done.6.refs_7_), channel_id=1, source_target_pairs={{0,12},{1,19},{4,0},{5,23},{8,4},{9,27},{12,8},{13,31},{2,14},{3,1... | collective-permute-start | bytes 983048 | tf_op jit(solution)/shard_map/ppermute | solution.py:324
  39.6 12.2 %collective-permute-start.9 = (bf16[16,16,640]{2,1,0:T(8,128)(2,1)S(1)}, bf16[16,16,640]{2,1,0:T(8,128)(2,1)S(1)}, u32[]{:S(2)}, u32[]{:S(2)}) collective-permute-start(bf16[16,16,640]{2,1,0:T(8,128)(2,1)S(1)} %constant_dynamic-update-slice_fusion.refs_0_), channel_id=1, source_target_pairs={{0,1},{1,0},{2,3},{3,2},{4,5},{5,4},{6,7},{7,6},{8,9},{9,8},{10,11... | collective-permute-start | bytes 983048 | tf_op jit(solution)/shard_map/ppermute | solution.py:328
  46.8 5.6 %collective-permute-start.10 = (bf16[16,16,640]{2,1,0:T(8,128)(2,1)S(1)}, bf16[16,16,640]{2,1,0:T(8,128)(2,1)S(1)}, u32[]{:S(2)}, u32[]{:S(2)}) collective-permute-start(bf16[16,16,640]{2,1,0:T(8,128)(2,1)S(1)} %constant_dynamic-update-slice_fusion.2.after_ref.refs_1_), channel_id=1, source_target_pairs={{0,1},{1,0},{2,3},{3,2},{4,5},{5,4},{6,7},{7,6},{8,9},{9,8},{10,11... | collective-permute-start | bytes 983048 | tf_op jit(solution)/shard_map/ppermute | solution.py:328
  46.9 5.6 %collective-permute-start.11 = (bf16[16,16,640]{2,1,0:T(8,128)(2,1)S(1)}, bf16[16,16,640]{2,1,0:T(8,128)(2,1)S(1)}, u32[]{:S(2)}, u32[]{:S(2)}) collective-permute-start(bf16[16,16,640]{2,1,0:T(8,128)(2,1)S(1)} %collective-permute-done.3.refs_2_), channel_id=1, source_target_pairs={{0,1},{1,0},{2,3},{3,2},{4,5},{5,4},{6,7},{7,6},{8,9},{9,8},{10,11... | collective-permute-start | bytes 983048 | tf_op jit(solution)/shard_map/ppermute | solution.py:328
  47.3 5.8 %collective-permute-start.12 = (bf16[16,16,640]{2,1,0:T(8,128)(2,1)S(1)}, bf16[16,16,640]{2,1,0:T(8,128)(2,1)S(1)}, u32[]{:S(2)}, u32[]{:S(2)}) collective-permute-start(bf16[16,16,640]{2,1,0:T(8,128)(2,1)S(1)} %collective-permute-done.4.refs_3_), channel_id=1, source_target_pairs={{0,1},{1,0},{2,3},{3,2},{4,5},{5,4},{6,7},{7,6},{8,9},{9,8},{10,11... | collective-permute-start | bytes 983048 | tf_op jit(solution)/shard_map/ppermute | solution.py:328
  51.8 1.7 %collective-permute-start.15 = (bf16[16,16,640]{2,1,0:T(8,128)(2,1)S(1)}, bf16[16,16,640]{2,1,0:T(8,128)(2,1)S(1)}, u32[]{:S(2)}, u32[]{:S(2)}) collective-permute-start(bf16[16,16,640]{2,1,0:T(8,128)(2,1)S(1)} %collective-permute-done.8.refs_6_), channel_id=1, source_target_pairs={{0,1},{1,0},{2,3},{3,2},{4,5},{5,4},{6,7},{7,6},{8,9},{9,8},{10,11... | collective-permute-start | bytes 983048 | tf_op jit(solution)/shard_map/ppermute | solution.py:328
  51.9 2.2 %collective-permute-start.16 = (bf16[16,16,640]{2,1,0:T(8,128)(2,1)S(1)}, bf16[16,16,640]{2,1,0:T(8,128)(2,1)S(1)}, u32[]{:S(2)}, u32[]{:S(2)}) collective-permute-start(bf16[16,16,640]{2,1,0:T(8,128)(2,1)S(1)} %collective-permute-done.6.refs_7_), channel_id=1, source_target_pairs={{0,1},{1,0},{2,3},{3,2},{4,5},{5,4},{6,7},{7,6},{8,9},{9,8},{10,11... | collective-permute-start | bytes 983048 | tf_op jit(solution)/shard_map/ppermute | solution.py:328
  52.4 2.1 %collective-permute-start.13 = (bf16[16,16,640]{2,1,0:T(8,128)(2,1)S(1)}, bf16[16,16,640]{2,1,0:T(8,128)(2,1)S(1)}, u32[]{:S(2)}, u32[]{:S(2)}) collective-permute-start(bf16[16,16,640]{2,1,0:T(8,128)(2,1)S(1)} %collective-permute-done.5.refs_4_), channel_id=1, source_target_pairs={{0,1},{1,0},{2,3},{3,2},{4,5},{5,4},{6,7},{7,6},{8,9},{9,8},{10,11... | collective-permute-start | bytes 983048 | tf_op jit(solution)/shard_map/ppermute | solution.py:328
  52.5 2.5 %collective-permute-start.14 = (bf16[16,16,640]{2,1,0:T(8,128)(2,1)S(1)}, bf16[16,16,640]{2,1,0:T(8,128)(2,1)S(1)}, u32[]{:S(2)}, u32[]{:S(2)}) collective-permute-start(bf16[16,16,640]{2,1,0:T(8,128)(2,1)S(1)} %collective-permute-done.7.refs_5_), channel_id=1, source_target_pairs={{0,1},{1,0},{2,3},{3,2},{4,5},{5,4},{6,7},{7,6},{8,9},{9,8},{10,11... | collective-permute-start | bytes 983048 | tf_op jit(solution)/shard_map/ppermute | solution.py:328
  67.2 3.1 %collective-permute-start.17 = (bf16[64,16,640]{2,1,0:T(8,128)(2,1)S(1)}, bf16[64,16,640]{2,1,0:T(8,128)(2,1)S(1)}, u32[]{:S(2)}, u32[]{:S(2)}) collective-permute-start(bf16[64,16,640]{2,1,0:T(8,128)(2,1)S(1)} %get-tuple-element.38), channel_id=1, source_target_pairs={{0,1},{1,0},{2,3},{3,2},{4,5},{5,4},{6,7},{7,6},{8,9},{9,8},{10,11... | collective-permute-start | bytes 3932168 | tf_op jit(solution)/shard_map/ppermute | solution.py:328
  69.4 4.4 %collective-permute-start.21 = (bf16[64,16,640]{2,1,0:T(8,128)(2,1)S(1)}, bf16[64,16,640]{2,1,0:T(8,128)(2,1)S(1)}, u32[]{:S(2)}, u32[]{:S(2)}) collective-permute-start(bf16[64,16,640]{2,1,0:T(8,128)(2,1)S(1)} %get-tuple-element.42), channel_id=1, source_target_pairs={{0,1},{1,0},{2,3},{3,2},{4,5},{5,4},{6,7},{7,6},{8,9},{9,8},{10,11... | collective-permute-start | bytes 3932168 | tf_op jit(solution)/shard_map/ppermute | solution.py:328
  70.6 11.0 %collective-permute-start.18 = (bf16[16,16,640]{2,1,0:T(8,128)(2,1)S(1)}, bf16[16,16,640]{2,1,0:T(8,128)(2,1)S(1)}, u32[]{:S(2)}, u32[]{:S(2)}) collective-permute-start(bf16[16,16,640]{2,1,0:T(8,128)(2,1)S(1)} %get-tuple-element.45), channel_id=1, source_target_pairs={{0,4},{1,3},{4,8},{5,7},{8,12},{9,11},{12,0},{13,15},{2,6},{3,17},... | collective-permute-start | bytes 983048 | tf_op jit(solution)/shard_map/ppermute | solution.py:324
  70.7 11.4 %collective-permute-start.20 = (bf16[16,16,640]{2,1,0:T(8,128)(2,1)S(1)}, bf16[16,16,640]{2,1,0:T(8,128)(2,1)S(1)}, u32[]{:S(2)}, u32[]{:S(2)}) collective-permute-start(bf16[16,16,640]{2,1,0:T(8,128)(2,1)S(1)} %get-tuple-element.46), channel_id=1, source_target_pairs={{0,12},{1,19},{4,0},{5,23},{8,4},{9,27},{12,8},{13,31},{2,14},{3,1... | collective-permute-start | bytes 983048 | tf_op jit(solution)/shard_map/ppermute | solution.py:324
  73.3 8.7 %collective-permute-start.19 = (bf16[16,16,640]{2,1,0:T(8,128)(2,1)S(1)}, bf16[16,16,640]{2,1,0:T(8,128)(2,1)S(1)}, u32[]{:S(2)}, u32[]{:S(2)}) collective-permute-start(bf16[16,16,640]{2,1,0:T(8,128)(2,1)S(1)} %get-tuple-element.47), channel_id=1, source_target_pairs={{0,8},{1,17},{4,12},{5,21},{8,0},{9,25},{12,4},{13,29},{2,10},{3,1... | collective-permute-start | bytes 983048 | tf_op jit(solution)/shard_map/ppermute | solution.py:324
  74.1 11.0 %collective-permute-start.22 = (bf16[16,16,640]{2,1,0:T(8,128)(2,1)S(1)}, bf16[16,16,640]{2,1,0:T(8,128)(2,1)S(1)}, u32[]{:S(2)}, u32[]{:S(2)}) collective-permute-start(bf16[16,16,640]{2,1,0:T(8,128)(2,1)S(1)} %get-tuple-element.48), channel_id=1, source_target_pairs={{0,4},{1,3},{4,8},{5,7},{8,12},{9,11},{12,0},{13,15},{2,6},{3,17},... | collective-permute-start | bytes 983048 | tf_op jit(solution)/shard_map/ppermute | solution.py:324
  74.3 13.6 %collective-permute-start.24 = (bf16[16,16,640]{2,1,0:T(8,128)(2,1)S(1)}, bf16[16,16,640]{2,1,0:T(8,128)(2,1)S(1)}, u32[]{:S(2)}, u32[]{:S(2)}) collective-permute-start(bf16[16,16,640]{2,1,0:T(8,128)(2,1)S(1)} %get-tuple-element.49), channel_id=1, source_target_pairs={{0,12},{1,19},{4,0},{5,23},{8,4},{9,27},{12,8},{13,31},{2,14},{3,1... | collective-permute-start | bytes 983048 | tf_op jit(solution)/shard_map/ppermute | solution.py:324
  81.6 7.7 %collective-permute-start.23 = (bf16[16,16,640]{2,1,0:T(8,128)(2,1)S(1)}, bf16[16,16,640]{2,1,0:T(8,128)(2,1)S(1)}, u32[]{:S(2)}, u32[]{:S(2)}) collective-permute-start(bf16[16,16,640]{2,1,0:T(8,128)(2,1)S(1)} %get-tuple-element.50), channel_id=1, source_target_pairs={{0,8},{1,17},{4,12},{5,21},{8,0},{9,25},{12,4},{13,29},{2,10},{3,1... | collective-permute-start | bytes 983048 | tf_op jit(solution)/shard_map/ppermute | solution.py:324
  89.6 5.5 %collective-permute-start.25 = (bf16[8,16,640]{2,1,0:T(8,128)(2,1)S(1)}, bf16[8,16,640]{2,1,0:T(8,128)(2,1)S(1)}, u32[]{:S(2)}, u32[]{:S(2)}) collective-permute-start(bf16[8,16,640]{2,1,0:T(8,128)(2,1)S(1)} %get-tuple-element.51), channel_id=1, source_target_pairs={{0,2},{1,5},{4,6},{5,9},{8,10},{9,13},{12,14},{13,1},{2,16},{3,7},... | collective-permute-start | bytes 491528 | tf_op jit(solution)/shard_map/ppermute | solution.py:324
  89.7 6.7 %collective-permute-start.27 = (bf16[8,16,640]{2,1,0:T(8,128)(2,1)S(1)}, bf16[8,16,640]{2,1,0:T(8,128)(2,1)S(1)}, u32[]{:S(2)}, u32[]{:S(2)}) collective-permute-start(bf16[8,16,640]{2,1,0:T(8,128)(2,1)S(1)} %get-tuple-element.52), channel_id=1, source_target_pairs={{0,18},{1,13},{4,22},{5,1},{8,26},{9,5},{12,30},{13,9},{2,0},{3,15... | collective-permute-start | bytes 491528 | tf_op jit(solution)/shard_map/ppermute | solution.py:324
  92.4 5.7 %collective-permute-start.26 = (bf16[8,16,640]{2,1,0:T(8,128)(2,1)S(1)}, bf16[8,16,640]{2,1,0:T(8,128)(2,1)S(1)}, u32[]{:S(2)}, u32[]{:S(2)}) collective-permute-start(bf16[8,16,640]{2,1,0:T(8,128)(2,1)S(1)} %get-tuple-element.53), channel_id=1, source_target_pairs={{0,16},{1,9},{4,20},{5,13},{8,24},{9,1},{12,28},{13,5},{2,18},{3,1... | collective-permute-start | bytes 491528 | tf_op jit(solution)/shard_map/ppermute | solution.py:324
  108.9 7.0 %collective-permute-start.30 = (f32[16,640]{1,0:T(8,128)S(1)}, f32[16,640]{1,0:T(8,128)S(1)}, u32[]{:S(2)}, u32[]{:S(2)}) collective-permute-start(f32[16,640]{1,0:T(8,128)S(1)} %convert_reduce_fusion.refs_0_), channel_id=1, source_target_pairs={{0,3},{1,2},{2,1},{3,0},{4,7},{5,6},{6,5},{7,4},{8,11},{9,10},{10,... | collective-permute-start | bytes 122888 | tf_op jit(solution)/shard_map/ppermute | solution.py:391
  112.0 3.9 %collective-permute-start.29 = (f32[16,640]{1,0:T(8,128)S(1)}, f32[16,640]{1,0:T(8,128)S(1)}, u32[]{:S(2)}, u32[]{:S(2)}) collective-permute-start(f32[16,640]{1,0:T(8,128)S(1)} %convert_reduce_fusion.refs_0_), channel_id=1, source_target_pairs={{0,1},{1,0},{2,3},{3,2},{4,5},{5,4},{6,7},{7,6},{8,9},{9,8},{10,11... | collective-permute-start | bytes 122888 | tf_op jit(solution)/shard_map/ppermute | solution.py:391
  113.5 3.5 %collective-permute-start.28 = (f32[16,640]{1,0:T(8,128)S(1)}, f32[16,640]{1,0:T(8,128)S(1)}, u32[]{:S(2)}, u32[]{:S(2)}) collective-permute-start(f32[16,640]{1,0:T(8,128)S(1)} %convert_reduce_fusion.refs_0_), channel_id=1, source_target_pairs={{0,2},{1,3},{2,0},{3,1},{4,6},{5,7},{6,4},{7,5},{8,10},{9,11},{10,... | collective-permute-start | bytes 122888 | tf_op jit(solution)/shard_map/ppermute | solution.py:391

commit v11 on v7

--- a/solution.py
+++ b/solution.py
@@ -23,6 +23,7 @@
 SUMS_AT = GAIN_AT + 32
 CHUNKS = 64
 ORDER = 64
+PLANES = 3
 BF, F32 = jnp.bfloat16, jnp.float32
 NT = (((1,), (1,)), ((), ()))
 NN = (((1,), (0,)), ((), ()))
@@ -41,15 +42,15 @@
         yield x, yh, other, yl, jnp.where(pc == other, dx * 4 + dy, dy * 4 + dx)
 
 
-def to_blocks(place, outs, first, up_share, grad_low, hid, held):
+def to_blocks(place, outs, first, planes, up_share, grad_low, hid, held):
     origin = first * DOWN // 128 * 128
-    stop = -(-(first + 32) * DOWN // 128) * 128
+    stop = -(-(first + 8 * planes) * DOWN // 128) * 128
     for begin in range(origin, stop, 1024):
         end = min(begin + 1024, stop)
         held[:, begin - origin : end - origin] = dot(grad_low, hid[:, begin:end], NN).astype(BF)
-    for x, yh, other, yl, base in slots(place, -1, 4):
+    for x, yh, other, yl, base in slots(place, -1, planes):
         rows = slice(32 * other + 16 * yl, 32 * other + 16 * yl + 16)
-        for z in range(4):
+        for z in range(planes):
             chunk = z * 8 + yh * 4 + x
             begin = (first + chunk) * DOWN - origin
             outs[other][base + z, :, :UP] = up_share[rows, chunk * UP : chunk * UP + UP]
@@ -142,6 +143,7 @@
     first = slope / rms
     second = inner / (width * rms * rms * rms)
 
+    packed_here = PLANES * 8 * UP
     total = jnp.zeros((128, ORDER), F32)
     for i in range(width // step):
         at = slice(i * step, (i + 1) * step)
@@ -150,18 +152,20 @@
         rest = (grad - high.astype(F32)).astype(BF)
         total += dot(high, up[:, at], NT) + dot(rest, up[:, at], NT)
         share = (SCALE * dot(low_t, high, NN)).astype(BF)
-        if i * step < width // 2:
+        if i * step < packed_here:
             up[:, at] = share
         else:
-            up_rest[:, i * step - width // 2 : (i + 1) * step - width // 2] = share
+            up_rest[:, i * step - packed_here : (i + 1) * step - packed_here] = share
     grad_low = (SCALE * total).T.astype(BF)
 
     low_ref[...] = grad_low
-    to_blocks(place_ref, outs, 0, up, grad_low, hid, wt)
+    to_blocks(place_ref, outs, 0, PLANES, up, grad_low, hid, wt)
 
 
 def second_kernel(place_ref, low_ref, up_rest, hid, *refs):
-    to_blocks(place_ref, refs[:2], CHUNKS // 2, up_rest, low_ref[...], hid, refs[2])
+    to_blocks(
+        place_ref, refs[:2], 8 * PLANES, 8 - PLANES, up_rest, low_ref[...], hid, refs[2]
+    )
 
 
 def pack(place_ref, *refs):
@@ -271,9 +275,9 @@
     vmem = pl.BlockSpec(memory_space=pltpu.VMEM)
     *outs, up_rest, grad_low, margin = pl.pallas_call(
         kernel,
-        out_shape=[pltpu.VMEM((64, 16, LANES), BF)] * 2
+        out_shape=[pltpu.VMEM((16 * PLANES, 16, LANES), BF)] * 2
         + [
-            pltpu.VMEM((ORDER, width // 2), BF),
+            pltpu.VMEM((ORDER, width - PLANES * 8 * UP), BF),
             pltpu.VMEM((ORDER, rows), BF),
             jax.ShapeDtypeStruct((8, 128), F32),
         ],
@@ -297,11 +301,11 @@
     )(place, starts, *parts, *near_vmem(hidden, frozen, head))
     rest = pl.pallas_call(
         second_kernel,
-        out_shape=[pltpu.VMEM((64, 16, LANES), BF)] * 2,
+        out_shape=[pltpu.VMEM((16 * (8 - PLANES), 16, LANES), BF)] * 2,
         in_specs=[smem] + [vmem] * 3,
         out_specs=[vmem] * 2,
-        scratch_shapes=[pltpu.VMEM((ORDER, (units // 256 + 1) * 128), BF)],
-        compiler_params=pltpu.CompilerParams(vmem_limit_bytes=4 * 1024 * 1024),
+        scratch_shapes=[pltpu.VMEM((ORDER, (8 - PLANES) * 8 * DOWN // 128 * 128 + 256), BF)],
+        compiler_params=pltpu.CompilerParams(vmem_limit_bytes=8 * 1024 * 1024),
         cost_estimate=pl.CostEstimate(
             flops=rows * ORDER * units,
             bytes_accessed=rows * units + 2 * 128 * 16 * LANES,
@@ -372,12 +376,13 @@
     lines = []
     for own, other in (first, second):
         came = other_core(other)
+        each = own.shape[0] // 4
         chip = [
-            total_of(own[16 * i : 16 * i + 16], came[16 * i : 16 * i + 16]).astype(BF)
+            total_of(own[each * i : each * i + each], came[each * i : each * i + each]).astype(BF)
             for i in range(4)
         ]
         came = [ring(chip[step], step) for step in (1, 2, 3)]
-        lines.append(total_of(chip[0], *came).astype(BF).reshape(4, 4, 16, LANES))
+        lines.append(total_of(chip[0], *came).astype(BF).reshape(4, each // 4, 16, LANES))
     line = jnp.concatenate(lines, axis=1)
     came = [ring(line[step], step, 1) for step in (1, 2, 3)]
     plane = total_of(line[0], *came).astype(BF)

time: 119 us -> 123 us (1.034)
  waiting for transfers between devices: 28.1 us -> 31.3 us
    ppermute x6, waiting for transfers between devices: 2.46 us -> 6.12 us  [other_core(): return lax.ppermute(values, 'c', [(0, 1), (1, 0)])]
  transfers between devices with their start and end apart: 24 -> 24, of which waited for: 15 -> 14; matrix products, arithmetic and copies ran while one was open for 1% -> 1% of each run, Pallas kernels for 6% -> 4%
where the time goes in v11:
time: 123 us
  starting transfers between devices  37.9 us (31%)
  waiting for transfers between devices  31.3 us (25%)
  blocking collectives  27.7 us (23%)
  Pallas kernels  21.3 us (17%)
  between operations  2.65 us (2%)
  other arithmetic  1.24 us (1%)
    ppermute x15, waiting for transfers between devices, ring(): return lax.ppermute(values, FINE_AXES, pairs)  24.6 us
    ppermute x15, starting transfers between devices, ring(): return lax.ppermute(values, FINE_AXES, pairs)  18.1 us
    all_to_all x1, blocking collectives, local(): held = lax.all_to_all(quarter, 'z', 0, 0, tiled=True)  17 us
    ppermute x6, starting transfers between devices, other_core(): return lax.ppermute(values, 'c', [(0, 1), (1, 0)])  14.5 us
    pallas_call x1, Pallas kernels, shares(): pl.pallas_call(kernel, out_shape=[pltpu.VMEM((16 * PLANES, 16, LANES), BF...  11.7 us
    all_to_all x1, blocking collectives, local(): lax.all_to_all(plane, 'z', 0, 0, tiled=True).astype(F32)  10.8 us
    ppermute x6, waiting for transfers between devices, other_core(): return lax.ppermute(values, 'c', [(0, 1), (1, 0)])  6.12 us
    ppermute x3, starting transfers between devices, local(): lax.ppermute(share, CTX, [(i, i ^ step) for i in range(4)])  5.34 us
  transfers between devices with their start and end apart: 24, of which 14 were waited for; matrix products, arithmetic and copies ran while one was open for 1% of the time, Pallas kernels for 4%

profile of v11, /device:TPU:1, one launch (start us, length us, event | category | flops | bytes accessed | tf_op | source)
XLA Modules:
  0.0 122.7 jit_solution(6106416364944879969)
XLA Ops:
  0.7 1.5 %shard_map.103 = bf16[8,16,640]{2,1,0:T(8,128)(2,1)S(1)} custom-call(s32[4]{0:T(128)S(1)} %pad_add_fusion.place_ref, s32[1,2]{1,0:T(1,128)} %starts_ref.1, f32[2,64]{1,0:T(2,128)} %bitcast.33, bf16[64,462]{1,0:T(8,128)(2,1)} %bitcast.32, bf16[64,128]{1,0:T(8,128)(2,1)} %refs_3_.1, bf16[1,128]{1,0:T(2,128)(2,1)} %bitcast.34), custom_call_target="tpu_custom_call" | custom-call | tf_op jit(solution)/shard_map/pallas_call | solution.py:207
  2.3 17.0 %all_to_all.10 = bf16[8,16,640]{2,1,0:T(8,128)(2,1)S(1)} all-to-all(bf16[8,16,640]{2,1,0:T(8,128)(2,1)S(1)} %shard_map.103), channel_id=1, replica_groups=mesh['z'=8,'yh'=2,'x'=4,'yl'=2,'c'=2] {'z'}, dimensions={0} | all-to-all | bytes 327680 | tf_op jit(solution)/shard_map/all_to_all | solution.py:360
  19.2 1.2 collective-permute-start
  20.4 1.5 %collective-permute-start.2 = (bf16[8,16,640]{2,1,0:T(8,128)(2,1)S(1)}, bf16[8,16,640]{2,1,0:T(8,128)(2,1)S(1)}, u32[]{:S(2)}, u32[]{:S(2)}) collective-permute-start(bf16[8,16,640]{2,1,0:T(8,128)(2,1)S(1)} %all_to_all.10), channel_id=1, source_target_pairs={{0,18},{1,13},{4,22},{5,1},{8,26},{9,5},{12,30},{13,9},{2,0},{3,15... | collective-permute-start | bytes 491528 | tf_op jit(solution)/shard_map/ppermute | solution.py:328
  21.9 1.5 %collective-permute-start.1 = (bf16[8,16,640]{2,1,0:T(8,128)(2,1)S(1)}, bf16[8,16,640]{2,1,0:T(8,128)(2,1)S(1)}, u32[]{:S(2)}, u32[]{:S(2)}) collective-permute-start(bf16[8,16,640]{2,1,0:T(8,128)(2,1)S(1)} %all_to_all.10), channel_id=1, source_target_pairs={{0,16},{1,9},{4,20},{5,13},{8,24},{9,1},{12,28},{13,5},{2,18},{3,1... | collective-permute-start | bytes 491528 | tf_op jit(solution)/shard_map/ppermute | solution.py:328
  23.5 1.2 collective-permute-done
  24.6 2.9 %collective-permute-done.1 = bf16[8,16,640]{2,1,0:T(8,128)(2,1)S(1)} collective-permute-done((bf16[8,16,640]{2,1,0:T(8,128)(2,1)S(1)}, bf16[8,16,640]{2,1,0:T(8,128)(2,1)S(1)}, u32[]{:S(2)}, u32[]{:S(2)}) %collective-permute-start.1) | collective-permute-done | bytes 163872 | tf_op jit(solution)/shard_map/ppermute | solution.py:328
  27.7 2.8 %collective-permute-start.5 = (bf16[32,16,640]{2,1,0:T(8,128)(2,1)S(1)}, bf16[32,16,640]{2,1,0:T(8,128)(2,1)S(1)}, u32[]{:S(2)}, u32[]{:S(2)}) collective-permute-start(bf16[32,16,640]{2,1,0:T(8,128)(2,1)S(1)} %constant_dynamic-update-slice_fusion.after_ref.refs_0_), channel_id=1, source_target_pairs={{0,12},{1,19},{4,0},{5,23},{8,4},{9,27},{12,8},{13,31},{2,14},{3,1... | collective-permute-start | bytes 1966088 | tf_op jit(solution)/shard_map/ppermute | solution.py:328
  30.5 0.3 collective-permute-start.4
  30.8 0.7 collective-permute-start.3
  31.5 4.9 %shard_map.104 = (bf16[128,29568]{1,0:T(8,128)(2,1)S(1)}, bf16[128,8192]{1,0:T(8,128)(2,1)S(1)}, bf16[128,8192]{1,0:T(8,128)(2,1)S(1)}) custom-call(bf16[32,16,640]{2,1,0:T(8,128)(2,1)S(1)} %constant_dynamic-update-slice_fusion.after_ref.refs_0_, s32[4]{0:T(128)S(1)} %pad_add_fusion.place_ref, bf16[128,29568]{1,0:T(8,128)(2,1)} %bitcast.25, ...), custom_call_target="tpu_custom_call" | custom-call | bytes 23527424 | tf_op jit(solution)/shard_map/pallas_call | solution.py:255
  36.4 5.0 %collective-permute-start.6 = (bf16[32,16,640]{2,1,0:T(8,128)(2,1)S(1)}, bf16[32,16,640]{2,1,0:T(8,128)(2,1)S(1)}, u32[]{:S(2)}, u32[]{:S(2)}) collective-permute-start(bf16[32,16,640]{2,1,0:T(8,128)(2,1)S(1)} %constant_dynamic-update-slice_fusion.after_ref.refs_0_), channel_id=1, source_target_pairs={{0,1},{1,0},{2,3},{3,2},{4,5},{5,4},{6,7},{7,6},{8,9},{9,8},{10,11... | collective-permute-start | bytes 1966088 | tf_op jit(solution)/shard_map/ppermute | solution.py:332
  41.5 3.6 %collective-permute-done.5.refs_3_ = bf16[32,16,640]{2,1,0:T(8,128)(2,1)S(1)} collective-permute-done((bf16[32,16,640]{2,1,0:T(8,128)(2,1)S(1)}, bf16[32,16,640]{2,1,0:T(8,128)(2,1)S(1)}, u32[]{:S(2)}, u32[]{:S(2)}) %collective-permute-start.5) | collective-permute-done | bytes 655392 | tf_op jit(solution)/shard_map/ppermute | solution.py:328
  45.0 4.9 %collective-permute-start.9 = (bf16[32,16,640]{2,1,0:T(8,128)(2,1)S(1)}, bf16[32,16,640]{2,1,0:T(8,128)(2,1)S(1)}, u32[]{:S(2)}, u32[]{:S(2)}) collective-permute-start(bf16[32,16,640]{2,1,0:T(8,128)(2,1)S(1)} %collective-permute-done.5.refs_3_), channel_id=1, source_target_pairs={{0,1},{1,0},{2,3},{3,2},{4,5},{5,4},{6,7},{7,6},{8,9},{9,8},{10,11... | collective-permute-start | bytes 1966088 | tf_op jit(solution)/shard_map/ppermute | solution.py:332
  49.9 3.9 %collective-permute-start.7 = (bf16[32,16,640]{2,1,0:T(8,128)(2,1)S(1)}, bf16[32,16,640]{2,1,0:T(8,128)(2,1)S(1)}, u32[]{:S(2)}, u32[]{:S(2)}) collective-permute-start(bf16[32,16,640]{2,1,0:T(8,128)(2,1)S(1)} %collective-permute-done.3.refs_1_), channel_id=1, source_target_pairs={{0,1},{1,0},{2,3},{3,2},{4,5},{5,4},{6,7},{7,6},{8,9},{9,8},{10,11... | collective-permute-start | bytes 1966088 | tf_op jit(solution)/shard_map/ppermute | solution.py:332
  53.9 1.7 %collective-permute-done.7.refs_5_ = bf16[32,16,640]{2,1,0:T(8,128)(2,1)S(1)} collective-permute-done((bf16[32,16,640]{2,1,0:T(8,128)(2,1)S(1)}, bf16[32,16,640]{2,1,0:T(8,128)(2,1)S(1)}, u32[]{:S(2)}, u32[]{:S(2)}) %collective-permute-start.7) | collective-permute-done | bytes 655392 | tf_op jit(solution)/shard_map/ppermute | solution.py:332
  55.6 11.7 %shard_map.105 = (bf16[48,16,640]{2,1,0:T(8,128)(2,1)S(1)}, bf16[48,16,640]{2,1,0:T(8,128)(2,1)S(1)}, bf16[64,5120]{1,0:T(8,128)(2,1)S(1)}, bf16[64,128]{1,0:T(8,128)(2,1)S(1)}, f32[8,128]{1,0:T(8,128)S(1)}) custom-call(s32[4]{0:T(128)S(1)} %pad_add_fusion.place_ref, s32[1,2]{1,0:T(1,128)S(1)} %copy-done, ...), custom_call_target="tpu_custom_call" | custom-call | flops 1505755136 | bytes 22249472 | tf_op jit(solution)/shard_map/pallas_call | solution.py:276
  67.3 1.9 %shard_map.106 = (bf16[80,16,640]{2,1,0:T(8,128)(2,1)S(1)}, bf16[80,16,640]{2,1,0:T(8,128)(2,1)S(1)}) custom-call(s32[4]{0:T(128)S(1)} %pad_add_fusion.place_ref, bf16[64,128]{1,0:T(8,128)(2,1)S(1)} %get-tuple-element.29.low_ref, bf16[64,5120]{1,0:T(8,128)(2,1)S(1)} %get-tuple-element.30.up_rest, bf16[128,29568]{1,0:T(8,128)(2,1)S(1)} %get-tuple-element.23.refs_8_.hid), custom_call_target="tpu_custom_call" | custom-call | flops 242221056 | bytes 6406144 | tf_op jit(solution)/shard_map/pallas_call | solution.py:302
  69.3 0.5 collective-permute-start.14
  69.7 0.1 collective-permute-start.10
  69.9 4.4 %collective-permute-done.10 = bf16[48,16,640]{2,1,0:T(8,128)(2,1)S(1)} collective-permute-done((bf16[48,16,640]{2,1,0:T(8,128)(2,1)S(1)}, bf16[48,16,640]{2,1,0:T(8,128)(2,1)S(1)}, u32[]{:S(2)}, u32[]{:S(2)}) %collective-permute-start.10) | collective-permute-done | bytes 983072 | tf_op jit(solution)/shard_map/ppermute | solution.py:332
  74.3 0.2 add_convert_fusion.8
  74.5 1.0 collective-permute-start.11
  75.5 1.8 %collective-permute-start.13 = (bf16[12,16,640]{2,1,0:T(8,128)(2,1)S(1)}, bf16[12,16,640]{2,1,0:T(8,128)(2,1)S(1)}, u32[]{:S(2)}, u32[]{:S(2)}) collective-permute-start(bf16[12,16,640]{2,1,0:T(8,128)(2,1)S(1)} %get-tuple-element.39), channel_id=1, source_target_pairs={{0,12},{1,19},{4,0},{5,23},{8,4},{9,27},{12,8},{13,31},{2,14},{3,1... | collective-permute-start | bytes 737288 | tf_op jit(solution)/shard_map/ppermute | solution.py:328
  77.2 1.0 collective-permute-start.12
  78.2 0.3 add_convert_fusion.3
  78.5 0.9 collective-permute-start.15
  79.5 1.8 %collective-permute-start.17 = (bf16[20,16,640]{2,1,0:T(8,128)(2,1)S(1)}, bf16[20,16,640]{2,1,0:T(8,128)(2,1)S(1)}, u32[]{:S(2)}, u32[]{:S(2)}) collective-permute-start(bf16[20,16,640]{2,1,0:T(8,128)(2,1)S(1)} %get-tuple-element.36), channel_id=1, source_target_pairs={{0,12},{1,19},{4,0},{5,23},{8,4},{9,27},{12,8},{13,31},{2,14},{3,1... | collective-permute-start | bytes 1228808 | tf_op jit(solution)/shard_map/ppermute | solution.py:328
  81.3 0.8 collective-permute-start.16
  82.1 0.9 collective-permute-done.13
  83.0 1.8 %collective-permute-done.12 = bf16[12,16,640]{2,1,0:T(8,128)(2,1)S(1)} collective-permute-done((bf16[12,16,640]{2,1,0:T(8,128)(2,1)S(1)}, bf16[12,16,640]{2,1,0:T(8,128)(2,1)S(1)}, u32[]{:S(2)}, u32[]{:S(2)}) %collective-permute-start.12) | collective-permute-done | bytes 245792 | tf_op jit(solution)/shard_map/ppermute | solution.py:328
  84.8 0.2 add_convert_fusion.5
  84.9 4.2 %collective-permute-done.15 = bf16[20,16,640]{2,1,0:T(8,128)(2,1)S(1)} collective-permute-done((bf16[20,16,640]{2,1,0:T(8,128)(2,1)S(1)}, bf16[20,16,640]{2,1,0:T(8,128)(2,1)S(1)}, u32[]{:S(2)}, u32[]{:S(2)}) %collective-permute-start.15) | collective-permute-done | bytes 409632 | tf_op jit(solution)/shard_map/ppermute | solution.py:328
  89.1 2.7 %collective-permute-done.17 = bf16[20,16,640]{2,1,0:T(8,128)(2,1)S(1)} collective-permute-done((bf16[20,16,640]{2,1,0:T(8,128)(2,1)S(1)}, bf16[20,16,640]{2,1,0:T(8,128)(2,1)S(1)}, u32[]{:S(2)}, u32[]{:S(2)}) %collective-permute-start.17) | collective-permute-done | bytes 409632 | tf_op jit(solution)/shard_map/ppermute | solution.py:328
  91.8 1.8 %collective-permute-done.16 = bf16[20,16,640]{2,1,0:T(8,128)(2,1)S(1)} collective-permute-done((bf16[20,16,640]{2,1,0:T(8,128)(2,1)S(1)}, bf16[20,16,640]{2,1,0:T(8,128)(2,1)S(1)}, u32[]{:S(2)}, u32[]{:S(2)}) %collective-permute-start.16) | collective-permute-done | bytes 409632 | tf_op jit(solution)/shard_map/ppermute | solution.py:328
  93.5 0.3 add_convert_fusion
  93.9 0.1 collective-permute-start.18
  94.0 2.7 %collective-permute-start.20 = (bf16[8,16,640]{2,1,0:T(8,128)(2,1)S(1)}, bf16[8,16,640]{2,1,0:T(8,128)(2,1)S(1)}, u32[]{:S(2)}, u32[]{:S(2)}) collective-permute-start(bf16[8,16,640]{2,1,0:T(8,128)(2,1)S(1)} %get-tuple-element.42), channel_id=1, source_target_pairs={{0,18},{1,13},{4,22},{5,1},{8,26},{9,5},{12,30},{13,9},{2,0},{3,15... | collective-permute-start | bytes 491528 | tf_op jit(solution)/shard_map/ppermute | solution.py:328
  96.7 3.0 %collective-permute-done.18 = bf16[8,16,640]{2,1,0:T(8,128)(2,1)S(1)} collective-permute-done((bf16[8,16,640]{2,1,0:T(8,128)(2,1)S(1)}, bf16[8,16,640]{2,1,0:T(8,128)(2,1)S(1)}, u32[]{:S(2)}, u32[]{:S(2)}) %collective-permute-start.18) | collective-permute-done | bytes 163872 | tf_op jit(solution)/shard_map/ppermute | solution.py:328
  99.6 1.0 collective-permute-done.20
  100.7 1.7 %collective-permute-done.19 = bf16[8,16,640]{2,1,0:T(8,128)(2,1)S(1)} collective-permute-done((bf16[8,16,640]{2,1,0:T(8,128)(2,1)S(1)}, bf16[8,16,640]{2,1,0:T(8,128)(2,1)S(1)}, u32[]{:S(2)}, u32[]{:S(2)}) %collective-permute-start.19) | collective-permute-done | bytes 163872 | tf_op jit(solution)/shard_map/ppermute | solution.py:328
  102.3 0.1 fusion.2
  102.4 10.8 %all_to_all.11 = bf16[8,16,640]{2,1,0:T(8,128)(2,1)S(1)} all-to-all(bf16[8,16,640]{2,1,0:T(8,128)(2,1)S(1)} %fusion.2), channel_id=1, replica_groups=mesh['z'=8,'yh'=2,'x'=4,'yl'=2,'c'=2] {'z'}, dimensions={0} | all-to-all | bytes 327680 | tf_op jit(solution)/shard_map/all_to_all | solution.py:389
  113.2 4.2 %collective-permute-start.23 = (f32[16,640]{1,0:T(8,128)S(1)}, f32[16,640]{1,0:T(8,128)S(1)}, u32[]{:S(2)}, u32[]{:S(2)}) collective-permute-start(f32[16,640]{1,0:T(8,128)S(1)} %convert_reduce_fusion.refs_0_), channel_id=1, source_target_pairs={{0,3},{1,2},{2,1},{3,0},{4,7},{5,6},{6,5},{7,4},{8,11},{9,10},{10,... | collective-permute-start | bytes 122888 | tf_op jit(solution)/shard_map/ppermute | solution.py:391
  117.4 1.1 collective-permute-start.21
  118.6 0.5 slice.63
  119.8 0.5 collective-permute-done.21.refs_1_
  120.4 1.2 shard_map.107
  (22 shorter events, 0.3 us)
Async XLA Ops:
  19.2 5.4 %collective-permute-start = (bf16[8,16,640]{2,1,0:T(8,128)(2,1)S(1)}, bf16[8,16,640]{2,1,0:T(8,128)(2,1)S(1)}, u32[]{:S(2)}, u32[]{:S(2)}) collective-permute-start(bf16[8,16,640]{2,1,0:T(8,128)(2,1)S(1)} %all_to_all.10), channel_id=1, source_target_pairs={{0,2},{1,5},{4,6},{5,9},{8,10},{9,13},{12,14},{13,1},{2,16},{3,7},... | collective-permute-start | bytes 491528 | tf_op jit(solution)/shard_map/ppermute | solution.py:328
  20.4 7.2 %collective-permute-start.2 = (bf16[8,16,640]{2,1,0:T(8,128)(2,1)S(1)}, bf16[8,16,640]{2,1,0:T(8,128)(2,1)S(1)}, u32[]{:S(2)}, u32[]{:S(2)}) collective-permute-start(bf16[8,16,640]{2,1,0:T(8,128)(2,1)S(1)} %all_to_all.10), channel_id=1, source_target_pairs={{0,18},{1,13},{4,22},{5,1},{8,26},{9,5},{12,30},{13,9},{2,0},{3,15... | collective-permute-start | bytes 491528 | tf_op jit(solution)/shard_map/ppermute | solution.py:328
  21.9 5.7 %collective-permute-start.1 = (bf16[8,16,640]{2,1,0:T(8,128)(2,1)S(1)}, bf16[8,16,640]{2,1,0:T(8,128)(2,1)S(1)}, u32[]{:S(2)}, u32[]{:S(2)}) collective-permute-start(bf16[8,16,640]{2,1,0:T(8,128)(2,1)S(1)} %all_to_all.10), channel_id=1, source_target_pairs={{0,16},{1,9},{4,20},{5,13},{8,24},{9,1},{12,28},{13,5},{2,18},{3,1... | collective-permute-start | bytes 491528 | tf_op jit(solution)/shard_map/ppermute | solution.py:328
  27.7 17.4 %collective-permute-start.5 = (bf16[32,16,640]{2,1,0:T(8,128)(2,1)S(1)}, bf16[32,16,640]{2,1,0:T(8,128)(2,1)S(1)}, u32[]{:S(2)}, u32[]{:S(2)}) collective-permute-start(bf16[32,16,640]{2,1,0:T(8,128)(2,1)S(1)} %constant_dynamic-update-slice_fusion.after_ref.refs_0_), channel_id=1, source_target_pairs={{0,12},{1,19},{4,0},{5,23},{8,4},{9,27},{12,8},{13,31},{2,14},{3,1... | collective-permute-start | bytes 1966088 | tf_op jit(solution)/shard_map/ppermute | solution.py:328
  30.5 19.5 %collective-permute-start.4 = (bf16[32,16,640]{2,1,0:T(8,128)(2,1)S(1)}, bf16[32,16,640]{2,1,0:T(8,128)(2,1)S(1)}, u32[]{:S(2)}, u32[]{:S(2)}) collective-permute-start(bf16[32,16,640]{2,1,0:T(8,128)(2,1)S(1)} %constant_dynamic-update-slice_fusion.after_ref.refs_0_), channel_id=1, source_target_pairs={{0,8},{1,17},{4,12},{5,21},{8,0},{9,25},{12,4},{13,29},{2,10},{3,1... | collective-permute-start | bytes 1966088 | tf_op jit(solution)/shard_map/ppermute | solution.py:328
  30.8 19.1 %collective-permute-start.3 = (bf16[32,16,640]{2,1,0:T(8,128)(2,1)S(1)}, bf16[32,16,640]{2,1,0:T(8,128)(2,1)S(1)}, u32[]{:S(2)}, u32[]{:S(2)}) collective-permute-start(bf16[32,16,640]{2,1,0:T(8,128)(2,1)S(1)} %constant_dynamic-update-slice_fusion.after_ref.refs_0_), channel_id=1, source_target_pairs={{0,4},{1,3},{4,8},{5,7},{8,12},{9,11},{12,0},{13,15},{2,6},{3,17},... | collective-permute-start | bytes 1966088 | tf_op jit(solution)/shard_map/ppermute | solution.py:328
  31.5 24.1 %copy-start = (s32[1,2]{1,0:T(1,128)S(1)}, s32[1,2]{1,0:T(1,128)}, u32[]{:S(2)}) copy-start(s32[1,2]{1,0:T(1,128)} %starts_ref.1) | copy-start | bytes 28
  36.4 17.5 %collective-permute-start.6 = (bf16[32,16,640]{2,1,0:T(8,128)(2,1)S(1)}, bf16[32,16,640]{2,1,0:T(8,128)(2,1)S(1)}, u32[]{:S(2)}, u32[]{:S(2)}) collective-permute-start(bf16[32,16,640]{2,1,0:T(8,128)(2,1)S(1)} %constant_dynamic-update-slice_fusion.after_ref.refs_0_), channel_id=1, source_target_pairs={{0,1},{1,0},{2,3},{3,2},{4,5},{5,4},{6,7},{7,6},{8,9},{9,8},{10,11... | collective-permute-start | bytes 1966088 | tf_op jit(solution)/shard_map/ppermute | solution.py:332
  45.0 8.9 %collective-permute-start.9 = (bf16[32,16,640]{2,1,0:T(8,128)(2,1)S(1)}, bf16[32,16,640]{2,1,0:T(8,128)(2,1)S(1)}, u32[]{:S(2)}, u32[]{:S(2)}) collective-permute-start(bf16[32,16,640]{2,1,0:T(8,128)(2,1)S(1)} %collective-permute-done.5.refs_3_), channel_id=1, source_target_pairs={{0,1},{1,0},{2,3},{3,2},{4,5},{5,4},{6,7},{7,6},{8,9},{9,8},{10,11... | collective-permute-start | bytes 1966088 | tf_op jit(solution)/shard_map/ppermute | solution.py:332
  49.9 4.0 %collective-permute-start.8 = (bf16[32,16,640]{2,1,0:T(8,128)(2,1)S(1)}, bf16[32,16,640]{2,1,0:T(8,128)(2,1)S(1)}, u32[]{:S(2)}, u32[]{:S(2)}) collective-permute-start(bf16[32,16,640]{2,1,0:T(8,128)(2,1)S(1)} %collective-permute-done.4.refs_2_), channel_id=1, source_target_pairs={{0,1},{1,0},{2,3},{3,2},{4,5},{5,4},{6,7},{7,6},{8,9},{9,8},{10,11... | collective-permute-start | bytes 1966088 | tf_op jit(solution)/shard_map/ppermute | solution.py:332
  49.9 5.7 %collective-permute-start.7 = (bf16[32,16,640]{2,1,0:T(8,128)(2,1)S(1)}, bf16[32,16,640]{2,1,0:T(8,128)(2,1)S(1)}, u32[]{:S(2)}, u32[]{:S(2)}) collective-permute-start(bf16[32,16,640]{2,1,0:T(8,128)(2,1)S(1)} %collective-permute-done.3.refs_1_), channel_id=1, source_target_pairs={{0,1},{1,0},{2,3},{3,2},{4,5},{5,4},{6,7},{7,6},{8,9},{9,8},{10,11... | collective-permute-start | bytes 1966088 | tf_op jit(solution)/shard_map/ppermute | solution.py:332
  69.3 9.0 %collective-permute-start.14 = (bf16[80,16,640]{2,1,0:T(8,128)(2,1)S(1)}, bf16[80,16,640]{2,1,0:T(8,128)(2,1)S(1)}, u32[]{:S(2)}, u32[]{:S(2)}) collective-permute-start(bf16[80,16,640]{2,1,0:T(8,128)(2,1)S(1)} %get-tuple-element.32), channel_id=1, source_target_pairs={{0,1},{1,0},{2,3},{3,2},{4,5},{5,4},{6,7},{7,6},{8,9},{9,8},{10,11... | collective-permute-start | bytes 4915208 | tf_op jit(solution)/shard_map/ppermute | solution.py:332
  69.7 4.5 %collective-permute-start.10 = (bf16[48,16,640]{2,1,0:T(8,128)(2,1)S(1)}, bf16[48,16,640]{2,1,0:T(8,128)(2,1)S(1)}, u32[]{:S(2)}, u32[]{:S(2)}) collective-permute-start(bf16[48,16,640]{2,1,0:T(8,128)(2,1)S(1)} %get-tuple-element.28), channel_id=1, source_target_pairs={{0,1},{1,0},{2,3},{3,2},{4,5},{5,4},{6,7},{7,6},{8,9},{9,8},{10,11... | collective-permute-start | bytes 2949128 | tf_op jit(solution)/shard_map/ppermute | solution.py:332
  74.5 6.8 %collective-permute-start.11 = (bf16[12,16,640]{2,1,0:T(8,128)(2,1)S(1)}, bf16[12,16,640]{2,1,0:T(8,128)(2,1)S(1)}, u32[]{:S(2)}, u32[]{:S(2)}) collective-permute-start(bf16[12,16,640]{2,1,0:T(8,128)(2,1)S(1)} %get-tuple-element.38), channel_id=1, source_target_pairs={{0,4},{1,3},{4,8},{5,7},{8,12},{9,11},{12,0},{13,15},{2,6},{3,17},... | collective-permute-start | bytes 737288 | tf_op jit(solution)/shard_map/ppermute | solution.py:328
  75.5 7.5 %collective-permute-start.13 = (bf16[12,16,640]{2,1,0:T(8,128)(2,1)S(1)}, bf16[12,16,640]{2,1,0:T(8,128)(2,1)S(1)}, u32[]{:S(2)}, u32[]{:S(2)}) collective-permute-start(bf16[12,16,640]{2,1,0:T(8,128)(2,1)S(1)} %get-tuple-element.39), channel_id=1, source_target_pairs={{0,12},{1,19},{4,0},{5,23},{8,4},{9,27},{12,8},{13,31},{2,14},{3,1... | collective-permute-start | bytes 737288 | tf_op jit(solution)/shard_map/ppermute | solution.py:328
  77.2 7.5 %collective-permute-start.12 = (bf16[12,16,640]{2,1,0:T(8,128)(2,1)S(1)}, bf16[12,16,640]{2,1,0:T(8,128)(2,1)S(1)}, u32[]{:S(2)}, u32[]{:S(2)}) collective-permute-start(bf16[12,16,640]{2,1,0:T(8,128)(2,1)S(1)} %get-tuple-element.40), channel_id=1, source_target_pairs={{0,8},{1,17},{4,12},{5,21},{8,0},{9,25},{12,4},{13,29},{2,10},{3,1... | collective-permute-start | bytes 737288 | tf_op jit(solution)/shard_map/ppermute | solution.py:328
  78.5 10.6 %collective-permute-start.15 = (bf16[20,16,640]{2,1,0:T(8,128)(2,1)S(1)}, bf16[20,16,640]{2,1,0:T(8,128)(2,1)S(1)}, u32[]{:S(2)}, u32[]{:S(2)}) collective-permute-start(bf16[20,16,640]{2,1,0:T(8,128)(2,1)S(1)} %get-tuple-element.35), channel_id=1, source_target_pairs={{0,4},{1,3},{4,8},{5,7},{8,12},{9,11},{12,0},{13,15},{2,6},{3,17},... | collective-permute-start | bytes 1228808 | tf_op jit(solution)/shard_map/ppermute | solution.py:328
  79.5 12.3 %collective-permute-start.17 = (bf16[20,16,640]{2,1,0:T(8,128)(2,1)S(1)}, bf16[20,16,640]{2,1,0:T(8,128)(2,1)S(1)}, u32[]{:S(2)}, u32[]{:S(2)}) collective-permute-start(bf16[20,16,640]{2,1,0:T(8,128)(2,1)S(1)} %get-tuple-element.36), channel_id=1, source_target_pairs={{0,12},{1,19},{4,0},{5,23},{8,4},{9,27},{12,8},{13,31},{2,14},{3,1... | collective-permute-start | bytes 1228808 | tf_op jit(solution)/shard_map/ppermute | solution.py:328
  81.3 12.2 %collective-permute-start.16 = (bf16[20,16,640]{2,1,0:T(8,128)(2,1)S(1)}, bf16[20,16,640]{2,1,0:T(8,128)(2,1)S(1)}, u32[]{:S(2)}, u32[]{:S(2)}) collective-permute-start(bf16[20,16,640]{2,1,0:T(8,128)(2,1)S(1)} %get-tuple-element.37), channel_id=1, source_target_pairs={{0,8},{1,17},{4,12},{5,21},{8,0},{9,25},{12,4},{13,29},{2,10},{3,1... | collective-permute-start | bytes 1228808 | tf_op jit(solution)/shard_map/ppermute | solution.py:328
  93.9 5.8 %collective-permute-start.18 = (bf16[8,16,640]{2,1,0:T(8,128)(2,1)S(1)}, bf16[8,16,640]{2,1,0:T(8,128)(2,1)S(1)}, u32[]{:S(2)}, u32[]{:S(2)}) collective-permute-start(bf16[8,16,640]{2,1,0:T(8,128)(2,1)S(1)} %get-tuple-element.41), channel_id=1, source_target_pairs={{0,2},{1,5},{4,6},{5,9},{8,10},{9,13},{12,14},{13,1},{2,16},{3,7},... | collective-permute-start | bytes 491528 | tf_op jit(solution)/shard_map/ppermute | solution.py:328
  94.0 6.7 %collective-permute-start.20 = (bf16[8,16,640]{2,1,0:T(8,128)(2,1)S(1)}, bf16[8,16,640]{2,1,0:T(8,128)(2,1)S(1)}, u32[]{:S(2)}, u32[]{:S(2)}) collective-permute-start(bf16[8,16,640]{2,1,0:T(8,128)(2,1)S(1)} %get-tuple-element.42), channel_id=1, source_target_pairs={{0,18},{1,13},{4,22},{5,1},{8,26},{9,5},{12,30},{13,9},{2,0},{3,15... | collective-permute-start | bytes 491528 | tf_op jit(solution)/shard_map/ppermute | solution.py:328
  96.6 5.7 %collective-permute-start.19 = (bf16[8,16,640]{2,1,0:T(8,128)(2,1)S(1)}, bf16[8,16,640]{2,1,0:T(8,128)(2,1)S(1)}, u32[]{:S(2)}, u32[]{:S(2)}) collective-permute-start(bf16[8,16,640]{2,1,0:T(8,128)(2,1)S(1)} %get-tuple-element.43), channel_id=1, source_target_pairs={{0,16},{1,9},{4,20},{5,13},{8,24},{9,1},{12,28},{13,5},{2,18},{3,1... | collective-permute-start | bytes 491528 | tf_op jit(solution)/shard_map/ppermute | solution.py:328
  113.2 6.6 %collective-permute-start.23 = (f32[16,640]{1,0:T(8,128)S(1)}, f32[16,640]{1,0:T(8,128)S(1)}, u32[]{:S(2)}, u32[]{:S(2)}) collective-permute-start(f32[16,640]{1,0:T(8,128)S(1)} %convert_reduce_fusion.refs_0_), channel_id=1, source_target_pairs={{0,3},{1,2},{2,1},{3,0},{4,7},{5,6},{6,5},{7,4},{8,11},{9,10},{10,... | collective-permute-start | bytes 122888 | tf_op jit(solution)/shard_map/ppermute | solution.py:391
  117.4 2.4 %collective-permute-start.22 = (f32[16,640]{1,0:T(8,128)S(1)}, f32[16,640]{1,0:T(8,128)S(1)}, u32[]{:S(2)}, u32[]{:S(2)}) collective-permute-start(f32[16,640]{1,0:T(8,128)S(1)} %convert_reduce_fusion.refs_0_), channel_id=1, source_target_pairs={{0,1},{1,0},{2,3},{3,2},{4,5},{5,4},{6,7},{7,6},{8,9},{9,8},{10,11... | collective-permute-start | bytes 122888 | tf_op jit(solution)/shard_map/ppermute | solution.py:391
  117.4 2.9 %collective-permute-start.21 = (f32[16,640]{1,0:T(8,128)S(1)}, f32[16,640]{1,0:T(8,128)S(1)}, u32[]{:S(2)}, u32[]{:S(2)}) collective-permute-start(f32[16,640]{1,0:T(8,128)S(1)} %convert_reduce_fusion.refs_0_), channel_id=1, source_target_pairs={{0,2},{1,3},{2,0},{3,1},{4,6},{5,7},{6,4},{7,5},{8,10},{9,11},{10,... | collective-permute-start | bytes 122888 | tf_op jit(solution)/shard_map/ppermute | solution.py:391

commit v12 on v11

--- a/solution.py
+++ b/solution.py
@@ -374,8 +374,9 @@
     first, second, margin = shares(place, starts, [*own, *other], *near)
 
     lines = []
-    for own, other in (first, second):
-        came = other_core(other)
+    came_first = other_core(first[1])
+    came_first, other = lax.optimization_barrier((came_first, second[1]))
+    for own, came in ((first[0], came_first), (second[0], other_core(other))):
         each = own.shape[0] // 4
         chip = [
             total_of(own[each * i : each * i + each], came[each * i : each * i + each]).astype(BF)

time: 123 us -> 119 us (0.967)
  waiting for transfers between devices: 31.3 us -> 27.2 us
    ppermute x6, waiting for transfers between devices: 6.12 us -> 1.98 us  [other_core(): return lax.ppermute(values, 'c', [(0, 1), (1, 0)])]
  transfers between devices with their start and end apart: 24 -> 24, of which waited for: 14 -> 14; matrix products, arithmetic and copies ran while one was open for 1% -> 1% of each run, Pallas kernels for 4% -> 6%
where the time goes in v12:
time: 119 us
  starting transfers between devices  37.9 us (32%)
  blocking collectives  27.7 us (23%)
  waiting for transfers between devices  27.2 us (23%)
  Pallas kernels  21.3 us (18%)
  between operations  2.65 us (2%)
  other arithmetic  1.22 us (1%)
    ppermute x15, waiting for transfers between devices, ring(): return lax.ppermute(values, FINE_AXES, pairs)  24.6 us
    ppermute x15, starting transfers between devices, ring(): return lax.ppermute(values, FINE_AXES, pairs)  18.1 us
    all_to_all x1, blocking collectives, local(): held = lax.all_to_all(quarter, 'z', 0, 0, tiled=True)  17 us
    ppermute x6, starting transfers between devices, other_core(): return lax.ppermute(values, 'c', [(0, 1), (1, 0)])  14.7 us
    pallas_call x1, Pallas kernels, shares(): pl.pallas_call(kernel, out_shape=[pltpu.VMEM((16 * PLANES, 16, LANES), BF...  11.7 us
    all_to_all x1, blocking collectives, local(): lax.all_to_all(plane, 'z', 0, 0, tiled=True).astype(F32)  10.8 us
    ppermute x3, starting transfers between devices, local(): lax.ppermute(share, CTX, [(i, i ^ step) for i in range(4)])  5.11 us
    pallas_call x1, Pallas kernels, brought(): pl.pallas_call(bring, out_shape=[pltpu.VMEM(v.shape, v.dtype) for v in ar...  4.91 us
  transfers between devices with their start and end apart: 24, of which 14 were waited for; matrix products, arithmetic and copies ran while one was open for 1% of the time, Pallas kernels for 6%

profile of v12, /device:TPU:1, one launch (start us, length us, event | category | flops | bytes accessed | tf_op | source)
XLA Modules:
  0.0 118.6 jit_solution(1100644074421595901)
XLA Ops:
  0.7 1.5 %shard_map.103 = bf16[8,16,640]{2,1,0:T(8,128)(2,1)S(1)} custom-call(s32[4]{0:T(128)S(1)} %pad_add_fusion.place_ref, s32[1,2]{1,0:T(1,128)} %starts_ref.1, f32[2,64]{1,0:T(2,128)} %bitcast.33, bf16[64,462]{1,0:T(8,128)(2,1)} %bitcast.32, bf16[64,128]{1,0:T(8,128)(2,1)} %refs_3_.1, bf16[1,128]{1,0:T(2,128)(2,1)} %bitcast.34), custom_call_target="tpu_custom_call" | custom-call | tf_op jit(solution)/shard_map/pallas_call | solution.py:207
  2.3 17.0 %all_to_all.10 = bf16[8,16,640]{2,1,0:T(8,128)(2,1)S(1)} all-to-all(bf16[8,16,640]{2,1,0:T(8,128)(2,1)S(1)} %shard_map.103), channel_id=1, replica_groups=mesh['z'=8,'yh'=2,'x'=4,'yl'=2,'c'=2] {'z'}, dimensions={0} | all-to-all | bytes 327680 | tf_op jit(solution)/shard_map/all_to_all | solution.py:360
  19.2 1.2 %collective-permute-start = (bf16[8,16,640]{2,1,0:T(8,128)(2,1)S(1)}, bf16[8,16,640]{2,1,0:T(8,128)(2,1)S(1)}, u32[]{:S(2)}, u32[]{:S(2)}) collective-permute-start(bf16[8,16,640]{2,1,0:T(8,128)(2,1)S(1)} %all_to_all.10), channel_id=1, source_target_pairs={{0,2},{1,5},{4,6},{5,9},{8,10},{9,13},{12,14},{13,1},{2,16},{3,7},... | collective-permute-start | bytes 491528 | tf_op jit(solution)/shard_map/ppermute | solution.py:328
  20.4 1.5 %collective-permute-start.2 = (bf16[8,16,640]{2,1,0:T(8,128)(2,1)S(1)}, bf16[8,16,640]{2,1,0:T(8,128)(2,1)S(1)}, u32[]{:S(2)}, u32[]{:S(2)}) collective-permute-start(bf16[8,16,640]{2,1,0:T(8,128)(2,1)S(1)} %all_to_all.10), channel_id=1, source_target_pairs={{0,18},{1,13},{4,22},{5,1},{8,26},{9,5},{12,30},{13,9},{2,0},{3,15... | collective-permute-start | bytes 491528 | tf_op jit(solution)/shard_map/ppermute | solution.py:328
  21.9 1.5 %collective-permute-start.1 = (bf16[8,16,640]{2,1,0:T(8,128)(2,1)S(1)}, bf16[8,16,640]{2,1,0:T(8,128)(2,1)S(1)}, u32[]{:S(2)}, u32[]{:S(2)}) collective-permute-start(bf16[8,16,640]{2,1,0:T(8,128)(2,1)S(1)} %all_to_all.10), channel_id=1, source_target_pairs={{0,16},{1,9},{4,20},{5,13},{8,24},{9,1},{12,28},{13,5},{2,18},{3,1... | collective-permute-start | bytes 491528 | tf_op jit(solution)/shard_map/ppermute | solution.py:328
  23.5 1.2 collective-permute-done
  24.6 2.9 %collective-permute-done.1 = bf16[8,16,640]{2,1,0:T(8,128)(2,1)S(1)} collective-permute-done((bf16[8,16,640]{2,1,0:T(8,128)(2,1)S(1)}, bf16[8,16,640]{2,1,0:T(8,128)(2,1)S(1)}, u32[]{:S(2)}, u32[]{:S(2)}) %collective-permute-start.1) | collective-permute-done | bytes 163872 | tf_op jit(solution)/shard_map/ppermute | solution.py:328
  27.7 2.8 %collective-permute-start.5 = (bf16[32,16,640]{2,1,0:T(8,128)(2,1)S(1)}, bf16[32,16,640]{2,1,0:T(8,128)(2,1)S(1)}, u32[]{:S(2)}, u32[]{:S(2)}) collective-permute-start(bf16[32,16,640]{2,1,0:T(8,128)(2,1)S(1)} %constant_dynamic-update-slice_fusion.after_ref.refs_0_), channel_id=1, source_target_pairs={{0,12},{1,19},{4,0},{5,23},{8,4},{9,27},{12,8},{13,31},{2,14},{3,1... | collective-permute-start | bytes 1966088 | tf_op jit(solution)/shard_map/ppermute | solution.py:328
  30.5 0.3 collective-permute-start.4
  30.8 0.7 collective-permute-start.3
  31.5 4.9 %shard_map.104 = (bf16[128,29568]{1,0:T(8,128)(2,1)S(1)}, bf16[128,8192]{1,0:T(8,128)(2,1)S(1)}, bf16[128,8192]{1,0:T(8,128)(2,1)S(1)}) custom-call(bf16[32,16,640]{2,1,0:T(8,128)(2,1)S(1)} %constant_dynamic-update-slice_fusion.after_ref.refs_0_, s32[4]{0:T(128)S(1)} %pad_add_fusion.place_ref, bf16[128,29568]{1,0:T(8,128)(2,1)} %bitcast.25, ...), custom_call_target="tpu_custom_call" | custom-call | bytes 23527424 | tf_op jit(solution)/shard_map/pallas_call | solution.py:255
  36.4 5.0 %collective-permute-start.6 = (bf16[32,16,640]{2,1,0:T(8,128)(2,1)S(1)}, bf16[32,16,640]{2,1,0:T(8,128)(2,1)S(1)}, u32[]{:S(2)}, u32[]{:S(2)}) collective-permute-start(bf16[32,16,640]{2,1,0:T(8,128)(2,1)S(1)} %constant_dynamic-update-slice_fusion.after_ref.refs_0_), channel_id=1, source_target_pairs={{0,1},{1,0},{2,3},{3,2},{4,5},{5,4},{6,7},{7,6},{8,9},{9,8},{10,11... | collective-permute-start | bytes 1966088 | tf_op jit(solution)/shard_map/ppermute | solution.py:332
  41.5 3.6 %collective-permute-done.5.refs_3_ = bf16[32,16,640]{2,1,0:T(8,128)(2,1)S(1)} collective-permute-done((bf16[32,16,640]{2,1,0:T(8,128)(2,1)S(1)}, bf16[32,16,640]{2,1,0:T(8,128)(2,1)S(1)}, u32[]{:S(2)}, u32[]{:S(2)}) %collective-permute-start.5) | collective-permute-done | bytes 655392 | tf_op jit(solution)/shard_map/ppermute | solution.py:328
  45.0 4.9 %collective-permute-start.9 = (bf16[32,16,640]{2,1,0:T(8,128)(2,1)S(1)}, bf16[32,16,640]{2,1,0:T(8,128)(2,1)S(1)}, u32[]{:S(2)}, u32[]{:S(2)}) collective-permute-start(bf16[32,16,640]{2,1,0:T(8,128)(2,1)S(1)} %collective-permute-done.5.refs_3_), channel_id=1, source_target_pairs={{0,1},{1,0},{2,3},{3,2},{4,5},{5,4},{6,7},{7,6},{8,9},{9,8},{10,11... | collective-permute-start | bytes 1966088 | tf_op jit(solution)/shard_map/ppermute | solution.py:332
  49.9 3.9 %collective-permute-start.7 = (bf16[32,16,640]{2,1,0:T(8,128)(2,1)S(1)}, bf16[32,16,640]{2,1,0:T(8,128)(2,1)S(1)}, u32[]{:S(2)}, u32[]{:S(2)}) collective-permute-start(bf16[32,16,640]{2,1,0:T(8,128)(2,1)S(1)} %collective-permute-done.3.refs_1_), channel_id=1, source_target_pairs={{0,1},{1,0},{2,3},{3,2},{4,5},{5,4},{6,7},{7,6},{8,9},{9,8},{10,11... | collective-permute-start | bytes 1966088 | tf_op jit(solution)/shard_map/ppermute | solution.py:332
  53.9 1.7 %collective-permute-done.7.refs_5_ = bf16[32,16,640]{2,1,0:T(8,128)(2,1)S(1)} collective-permute-done((bf16[32,16,640]{2,1,0:T(8,128)(2,1)S(1)}, bf16[32,16,640]{2,1,0:T(8,128)(2,1)S(1)}, u32[]{:S(2)}, u32[]{:S(2)}) %collective-permute-start.7) | collective-permute-done | bytes 655392 | tf_op jit(solution)/shard_map/ppermute | solution.py:332
  55.6 11.7 %shard_map.105 = (bf16[48,16,640]{2,1,0:T(8,128)(2,1)S(1)}, bf16[48,16,640]{2,1,0:T(8,128)(2,1)S(1)}, bf16[64,5120]{1,0:T(8,128)(2,1)S(1)}, bf16[64,128]{1,0:T(8,128)(2,1)S(1)}, f32[8,128]{1,0:T(8,128)S(1)}) custom-call(s32[4]{0:T(128)S(1)} %pad_add_fusion.place_ref, s32[1,2]{1,0:T(1,128)S(1)} %copy-done, ...), custom_call_target="tpu_custom_call" | custom-call | flops 1505755136 | bytes 22249472 | tf_op jit(solution)/shard_map/pallas_call | solution.py:276
  67.3 0.5 collective-permute-start.10
  67.8 1.9 %shard_map.106 = (bf16[80,16,640]{2,1,0:T(8,128)(2,1)S(1)}, bf16[80,16,640]{2,1,0:T(8,128)(2,1)S(1)}) custom-call(s32[4]{0:T(128)S(1)} %pad_add_fusion.place_ref, bf16[64,128]{1,0:T(8,128)(2,1)S(1)} %get-tuple-element.31.low_ref, bf16[64,5120]{1,0:T(8,128)(2,1)S(1)} %get-tuple-element.32.up_rest, bf16[128,29568]{1,0:T(8,128)(2,1)S(1)} %get-tuple-element.25.refs_8_.hid), custom_call_target="tpu_custom_call" | custom-call | flops 242221056 | bytes 6406144 | tf_op jit(solution)/shard_map/pallas_call | solution.py:302
  69.7 0.3 collective-permute-done.10
  70.0 0.4 collective-permute-start.14
  70.3 0.2 add_convert_fusion.8
  70.5 1.0 collective-permute-start.11
  71.5 1.8 %collective-permute-start.13 = (bf16[12,16,640]{2,1,0:T(8,128)(2,1)S(1)}, bf16[12,16,640]{2,1,0:T(8,128)(2,1)S(1)}, u32[]{:S(2)}, u32[]{:S(2)}) collective-permute-start(bf16[12,16,640]{2,1,0:T(8,128)(2,1)S(1)} %get-tuple-element.43), channel_id=1, source_target_pairs={{0,12},{1,19},{4,0},{5,23},{8,4},{9,27},{12,8},{13,31},{2,14},{3,1... | collective-permute-start | bytes 737288 | tf_op jit(solution)/shard_map/ppermute | solution.py:328
  73.3 1.0 collective-permute-start.12
  74.3 0.3 add_convert_fusion.3
  74.6 0.9 collective-permute-start.15
  75.5 1.8 %collective-permute-start.17 = (bf16[20,16,640]{2,1,0:T(8,128)(2,1)S(1)}, bf16[20,16,640]{2,1,0:T(8,128)(2,1)S(1)}, u32[]{:S(2)}, u32[]{:S(2)}) collective-permute-start(bf16[20,16,640]{2,1,0:T(8,128)(2,1)S(1)} %get-tuple-element.40), channel_id=1, source_target_pairs={{0,12},{1,19},{4,0},{5,23},{8,4},{9,27},{12,8},{13,31},{2,14},{3,1... | collective-permute-start | bytes 1228808 | tf_op jit(solution)/shard_map/ppermute | solution.py:328
  77.4 0.8 collective-permute-start.16
  78.1 0.9 collective-permute-done.13
  79.1 1.8 %collective-permute-done.12 = bf16[12,16,640]{2,1,0:T(8,128)(2,1)S(1)} collective-permute-done((bf16[12,16,640]{2,1,0:T(8,128)(2,1)S(1)}, bf16[12,16,640]{2,1,0:T(8,128)(2,1)S(1)}, u32[]{:S(2)}, u32[]{:S(2)}) %collective-permute-start.12) | collective-permute-done | bytes 245792 | tf_op jit(solution)/shard_map/ppermute | solution.py:328
  80.8 0.2 add_convert_fusion.5
  81.0 4.2 %collective-permute-done.15 = bf16[20,16,640]{2,1,0:T(8,128)(2,1)S(1)} collective-permute-done((bf16[20,16,640]{2,1,0:T(8,128)(2,1)S(1)}, bf16[20,16,640]{2,1,0:T(8,128)(2,1)S(1)}, u32[]{:S(2)}, u32[]{:S(2)}) %collective-permute-start.15) | collective-permute-done | bytes 409632 | tf_op jit(solution)/shard_map/ppermute | solution.py:328
  85.2 2.7 %collective-permute-done.17 = bf16[20,16,640]{2,1,0:T(8,128)(2,1)S(1)} collective-permute-done((bf16[20,16,640]{2,1,0:T(8,128)(2,1)S(1)}, bf16[20,16,640]{2,1,0:T(8,128)(2,1)S(1)}, u32[]{:S(2)}, u32[]{:S(2)}) %collective-permute-start.17) | collective-permute-done | bytes 409632 | tf_op jit(solution)/shard_map/ppermute | solution.py:328
  87.8 1.8 %collective-permute-done.16 = bf16[20,16,640]{2,1,0:T(8,128)(2,1)S(1)} collective-permute-done((bf16[20,16,640]{2,1,0:T(8,128)(2,1)S(1)}, bf16[20,16,640]{2,1,0:T(8,128)(2,1)S(1)}, u32[]{:S(2)}, u32[]{:S(2)}) %collective-permute-start.16) | collective-permute-done | bytes 409632 | tf_op jit(solution)/shard_map/ppermute | solution.py:328
  89.6 0.3 add_convert_fusion
  90.0 0.1 collective-permute-start.18
  90.1 2.7 %collective-permute-start.20 = (bf16[8,16,640]{2,1,0:T(8,128)(2,1)S(1)}, bf16[8,16,640]{2,1,0:T(8,128)(2,1)S(1)}, u32[]{:S(2)}, u32[]{:S(2)}) collective-permute-start(bf16[8,16,640]{2,1,0:T(8,128)(2,1)S(1)} %get-tuple-element.46), channel_id=1, source_target_pairs={{0,18},{1,13},{4,22},{5,1},{8,26},{9,5},{12,30},{13,9},{2,0},{3,15... | collective-permute-start | bytes 491528 | tf_op jit(solution)/shard_map/ppermute | solution.py:328
  92.7 3.0 %collective-permute-done.18 = bf16[8,16,640]{2,1,0:T(8,128)(2,1)S(1)} collective-permute-done((bf16[8,16,640]{2,1,0:T(8,128)(2,1)S(1)}, bf16[8,16,640]{2,1,0:T(8,128)(2,1)S(1)}, u32[]{:S(2)}, u32[]{:S(2)}) %collective-permute-start.18) | collective-permute-done | bytes 163872 | tf_op jit(solution)/shard_map/ppermute | solution.py:328
  95.7 1.0 collective-permute-done.20
  96.7 1.7 %collective-permute-done.19 = bf16[8,16,640]{2,1,0:T(8,128)(2,1)S(1)} collective-permute-done((bf16[8,16,640]{2,1,0:T(8,128)(2,1)S(1)}, bf16[8,16,640]{2,1,0:T(8,128)(2,1)S(1)}, u32[]{:S(2)}, u32[]{:S(2)}) %collective-permute-start.19) | collective-permute-done | bytes 163872 | tf_op jit(solution)/shard_map/ppermute | solution.py:328
  98.4 0.1 fusion.2
  98.5 10.8 %all_to_all.11 = bf16[8,16,640]{2,1,0:T(8,128)(2,1)S(1)} all-to-all(bf16[8,16,640]{2,1,0:T(8,128)(2,1)S(1)} %fusion.2), channel_id=1, replica_groups=mesh['z'=8,'yh'=2,'x'=4,'yl'=2,'c'=2] {'z'}, dimensions={0} | all-to-all | bytes 327680 | tf_op jit(solution)/shard_map/all_to_all | solution.py:390
  109.3 4.0 %collective-permute-start.23 = (f32[16,640]{1,0:T(8,128)S(1)}, f32[16,640]{1,0:T(8,128)S(1)}, u32[]{:S(2)}, u32[]{:S(2)}) collective-permute-start(f32[16,640]{1,0:T(8,128)S(1)} %convert_reduce_fusion.refs_0_), channel_id=1, source_target_pairs={{0,3},{1,2},{2,1},{3,0},{4,7},{5,6},{6,5},{7,4},{8,11},{9,10},{10,... | collective-permute-start | bytes 122888 | tf_op jit(solution)/shard_map/ppermute | solution.py:392
  113.3 1.1 collective-permute-start.21
  114.4 0.5 slice.63
  115.7 0.5 collective-permute-done.21.refs_1_
  116.2 1.2 %shard_map.107 = (f32[64,462]{1,0:T(8,128)}, f32[64,128]{1,0:T(8,128)}) custom-call(s32[4]{0:T(128)S(1)} %pad_add_fusion.place_ref, f32[16,640]{1,0:T(8,128)S(1)} %convert_reduce_fusion.refs_0_, f32[16,640]{1,0:T(8,128)S(1)} %collective-permute-done.21.refs_1_, f32[16,640]{1,0:T(8,128)S(1)} %collective-permute-done.22.refs_2_, ...), custom_call_target="tpu_custom_call" | custom-call | tf_op jit(solution)/shard_map/pallas_call | solution.py:231
  (22 shorter events, 0.3 us)
Async XLA Ops:
  19.2 5.4 %collective-permute-start = (bf16[8,16,640]{2,1,0:T(8,128)(2,1)S(1)}, bf16[8,16,640]{2,1,0:T(8,128)(2,1)S(1)}, u32[]{:S(2)}, u32[]{:S(2)}) collective-permute-start(bf16[8,16,640]{2,1,0:T(8,128)(2,1)S(1)} %all_to_all.10), channel_id=1, source_target_pairs={{0,2},{1,5},{4,6},{5,9},{8,10},{9,13},{12,14},{13,1},{2,16},{3,7},... | collective-permute-start | bytes 491528 | tf_op jit(solution)/shard_map/ppermute | solution.py:328
  20.4 7.2 %collective-permute-start.2 = (bf16[8,16,640]{2,1,0:T(8,128)(2,1)S(1)}, bf16[8,16,640]{2,1,0:T(8,128)(2,1)S(1)}, u32[]{:S(2)}, u32[]{:S(2)}) collective-permute-start(bf16[8,16,640]{2,1,0:T(8,128)(2,1)S(1)} %all_to_all.10), channel_id=1, source_target_pairs={{0,18},{1,13},{4,22},{5,1},{8,26},{9,5},{12,30},{13,9},{2,0},{3,15... | collective-permute-start | bytes 491528 | tf_op jit(solution)/shard_map/ppermute | solution.py:328
  21.9 5.7 %collective-permute-start.1 = (bf16[8,16,640]{2,1,0:T(8,128)(2,1)S(1)}, bf16[8,16,640]{2,1,0:T(8,128)(2,1)S(1)}, u32[]{:S(2)}, u32[]{:S(2)}) collective-permute-start(bf16[8,16,640]{2,1,0:T(8,128)(2,1)S(1)} %all_to_all.10), channel_id=1, source_target_pairs={{0,16},{1,9},{4,20},{5,13},{8,24},{9,1},{12,28},{13,5},{2,18},{3,1... | collective-permute-start | bytes 491528 | tf_op jit(solution)/shard_map/ppermute | solution.py:328
  27.7 17.4 %collective-permute-start.5 = (bf16[32,16,640]{2,1,0:T(8,128)(2,1)S(1)}, bf16[32,16,640]{2,1,0:T(8,128)(2,1)S(1)}, u32[]{:S(2)}, u32[]{:S(2)}) collective-permute-start(bf16[32,16,640]{2,1,0:T(8,128)(2,1)S(1)} %constant_dynamic-update-slice_fusion.after_ref.refs_0_), channel_id=1, source_target_pairs={{0,12},{1,19},{4,0},{5,23},{8,4},{9,27},{12,8},{13,31},{2,14},{3,1... | collective-permute-start | bytes 1966088 | tf_op jit(solution)/shard_map/ppermute | solution.py:328
  30.5 19.5 %collective-permute-start.4 = (bf16[32,16,640]{2,1,0:T(8,128)(2,1)S(1)}, bf16[32,16,640]{2,1,0:T(8,128)(2,1)S(1)}, u32[]{:S(2)}, u32[]{:S(2)}) collective-permute-start(bf16[32,16,640]{2,1,0:T(8,128)(2,1)S(1)} %constant_dynamic-update-slice_fusion.after_ref.refs_0_), channel_id=1, source_target_pairs={{0,8},{1,17},{4,12},{5,21},{8,0},{9,25},{12,4},{13,29},{2,10},{3,1... | collective-permute-start | bytes 1966088 | tf_op jit(solution)/shard_map/ppermute | solution.py:328
  30.8 19.1 %collective-permute-start.3 = (bf16[32,16,640]{2,1,0:T(8,128)(2,1)S(1)}, bf16[32,16,640]{2,1,0:T(8,128)(2,1)S(1)}, u32[]{:S(2)}, u32[]{:S(2)}) collective-permute-start(bf16[32,16,640]{2,1,0:T(8,128)(2,1)S(1)} %constant_dynamic-update-slice_fusion.after_ref.refs_0_), channel_id=1, source_target_pairs={{0,4},{1,3},{4,8},{5,7},{8,12},{9,11},{12,0},{13,15},{2,6},{3,17},... | collective-permute-start | bytes 1966088 | tf_op jit(solution)/shard_map/ppermute | solution.py:328
  31.5 24.1 %copy-start = (s32[1,2]{1,0:T(1,128)S(1)}, s32[1,2]{1,0:T(1,128)}, u32[]{:S(2)}) copy-start(s32[1,2]{1,0:T(1,128)} %starts_ref.1) | copy-start | bytes 28
  36.4 17.5 %collective-permute-start.6 = (bf16[32,16,640]{2,1,0:T(8,128)(2,1)S(1)}, bf16[32,16,640]{2,1,0:T(8,128)(2,1)S(1)}, u32[]{:S(2)}, u32[]{:S(2)}) collective-permute-start(bf16[32,16,640]{2,1,0:T(8,128)(2,1)S(1)} %constant_dynamic-update-slice_fusion.after_ref.refs_0_), channel_id=1, source_target_pairs={{0,1},{1,0},{2,3},{3,2},{4,5},{5,4},{6,7},{7,6},{8,9},{9,8},{10,11... | collective-permute-start | bytes 1966088 | tf_op jit(solution)/shard_map/ppermute | solution.py:332
  45.0 8.9 %collective-permute-start.9 = (bf16[32,16,640]{2,1,0:T(8,128)(2,1)S(1)}, bf16[32,16,640]{2,1,0:T(8,128)(2,1)S(1)}, u32[]{:S(2)}, u32[]{:S(2)}) collective-permute-start(bf16[32,16,640]{2,1,0:T(8,128)(2,1)S(1)} %collective-permute-done.5.refs_3_), channel_id=1, source_target_pairs={{0,1},{1,0},{2,3},{3,2},{4,5},{5,4},{6,7},{7,6},{8,9},{9,8},{10,11... | collective-permute-start | bytes 1966088 | tf_op jit(solution)/shard_map/ppermute | solution.py:332
  49.9 4.0 %collective-permute-start.8 = (bf16[32,16,640]{2,1,0:T(8,128)(2,1)S(1)}, bf16[32,16,640]{2,1,0:T(8,128)(2,1)S(1)}, u32[]{:S(2)}, u32[]{:S(2)}) collective-permute-start(bf16[32,16,640]{2,1,0:T(8,128)(2,1)S(1)} %collective-permute-done.4.refs_2_), channel_id=1, source_target_pairs={{0,1},{1,0},{2,3},{3,2},{4,5},{5,4},{6,7},{7,6},{8,9},{9,8},{10,11... | collective-permute-start | bytes 1966088 | tf_op jit(solution)/shard_map/ppermute | solution.py:332
  49.9 5.7 %collective-permute-start.7 = (bf16[32,16,640]{2,1,0:T(8,128)(2,1)S(1)}, bf16[32,16,640]{2,1,0:T(8,128)(2,1)S(1)}, u32[]{:S(2)}, u32[]{:S(2)}) collective-permute-start(bf16[32,16,640]{2,1,0:T(8,128)(2,1)S(1)} %collective-permute-done.3.refs_1_), channel_id=1, source_target_pairs={{0,1},{1,0},{2,3},{3,2},{4,5},{5,4},{6,7},{7,6},{8,9},{9,8},{10,11... | collective-permute-start | bytes 1966088 | tf_op jit(solution)/shard_map/ppermute | solution.py:332
  67.3 2.7 %collective-permute-start.10 = (bf16[48,16,640]{2,1,0:T(8,128)(2,1)S(1)}, bf16[48,16,640]{2,1,0:T(8,128)(2,1)S(1)}, u32[]{:S(2)}, u32[]{:S(2)}) collective-permute-start(bf16[48,16,640]{2,1,0:T(8,128)(2,1)S(1)} %get-tuple-element.30), channel_id=1, source_target_pairs={{0,1},{1,0},{2,3},{3,2},{4,5},{5,4},{6,7},{7,6},{8,9},{9,8},{10,11... | collective-permute-start | bytes 2949128 | tf_op jit(solution)/shard_map/ppermute | solution.py:332
  70.0 4.3 %collective-permute-start.14 = (bf16[80,16,640]{2,1,0:T(8,128)(2,1)S(1)}, bf16[80,16,640]{2,1,0:T(8,128)(2,1)S(1)}, u32[]{:S(2)}, u32[]{:S(2)}) collective-permute-start(bf16[80,16,640]{2,1,0:T(8,128)(2,1)S(1)} %get-tuple-element.36), channel_id=1, source_target_pairs={{0,1},{1,0},{2,3},{3,2},{4,5},{5,4},{6,7},{7,6},{8,9},{9,8},{10,11... | collective-permute-start | bytes 4915208 | tf_op jit(solution)/shard_map/ppermute | solution.py:332
  70.5 6.8 %collective-permute-start.11 = (bf16[12,16,640]{2,1,0:T(8,128)(2,1)S(1)}, bf16[12,16,640]{2,1,0:T(8,128)(2,1)S(1)}, u32[]{:S(2)}, u32[]{:S(2)}) collective-permute-start(bf16[12,16,640]{2,1,0:T(8,128)(2,1)S(1)} %get-tuple-element.42), channel_id=1, source_target_pairs={{0,4},{1,3},{4,8},{5,7},{8,12},{9,11},{12,0},{13,15},{2,6},{3,17},... | collective-permute-start | bytes 737288 | tf_op jit(solution)/shard_map/ppermute | solution.py:328
  71.5 7.5 %collective-permute-start.13 = (bf16[12,16,640]{2,1,0:T(8,128)(2,1)S(1)}, bf16[12,16,640]{2,1,0:T(8,128)(2,1)S(1)}, u32[]{:S(2)}, u32[]{:S(2)}) collective-permute-start(bf16[12,16,640]{2,1,0:T(8,128)(2,1)S(1)} %get-tuple-element.43), channel_id=1, source_target_pairs={{0,12},{1,19},{4,0},{5,23},{8,4},{9,27},{12,8},{13,31},{2,14},{3,1... | collective-permute-start | bytes 737288 | tf_op jit(solution)/shard_map/ppermute | solution.py:328
  73.3 7.5 %collective-permute-start.12 = (bf16[12,16,640]{2,1,0:T(8,128)(2,1)S(1)}, bf16[12,16,640]{2,1,0:T(8,128)(2,1)S(1)}, u32[]{:S(2)}, u32[]{:S(2)}) collective-permute-start(bf16[12,16,640]{2,1,0:T(8,128)(2,1)S(1)} %get-tuple-element.44), channel_id=1, source_target_pairs={{0,8},{1,17},{4,12},{5,21},{8,0},{9,25},{12,4},{13,29},{2,10},{3,1... | collective-permute-start | bytes 737288 | tf_op jit(solution)/shard_map/ppermute | solution.py:328
  74.6 10.6 %collective-permute-start.15 = (bf16[20,16,640]{2,1,0:T(8,128)(2,1)S(1)}, bf16[20,16,640]{2,1,0:T(8,128)(2,1)S(1)}, u32[]{:S(2)}, u32[]{:S(2)}) collective-permute-start(bf16[20,16,640]{2,1,0:T(8,128)(2,1)S(1)} %get-tuple-element.39), channel_id=1, source_target_pairs={{0,4},{1,3},{4,8},{5,7},{8,12},{9,11},{12,0},{13,15},{2,6},{3,17},... | collective-permute-start | bytes 1228808 | tf_op jit(solution)/shard_map/ppermute | solution.py:328
  75.5 12.3 %collective-permute-start.17 = (bf16[20,16,640]{2,1,0:T(8,128)(2,1)S(1)}, bf16[20,16,640]{2,1,0:T(8,128)(2,1)S(1)}, u32[]{:S(2)}, u32[]{:S(2)}) collective-permute-start(bf16[20,16,640]{2,1,0:T(8,128)(2,1)S(1)} %get-tuple-element.40), channel_id=1, source_target_pairs={{0,12},{1,19},{4,0},{5,23},{8,4},{9,27},{12,8},{13,31},{2,14},{3,1... | collective-permute-start | bytes 1228808 | tf_op jit(solution)/shard_map/ppermute | solution.py:328
  77.4 12.2 %collective-permute-start.16 = (bf16[20,16,640]{2,1,0:T(8,128)(2,1)S(1)}, bf16[20,16,640]{2,1,0:T(8,128)(2,1)S(1)}, u32[]{:S(2)}, u32[]{:S(2)}) collective-permute-start(bf16[20,16,640]{2,1,0:T(8,128)(2,1)S(1)} %get-tuple-element.41), channel_id=1, source_target_pairs={{0,8},{1,17},{4,12},{5,21},{8,0},{9,25},{12,4},{13,29},{2,10},{3,1... | collective-permute-start | bytes 1228808 | tf_op jit(solution)/shard_map/ppermute | solution.py:328
  90.0 5.8 %collective-permute-start.18 = (bf16[8,16,640]{2,1,0:T(8,128)(2,1)S(1)}, bf16[8,16,640]{2,1,0:T(8,128)(2,1)S(1)}, u32[]{:S(2)}, u32[]{:S(2)}) collective-permute-start(bf16[8,16,640]{2,1,0:T(8,128)(2,1)S(1)} %get-tuple-element.45), channel_id=1, source_target_pairs={{0,2},{1,5},{4,6},{5,9},{8,10},{9,13},{12,14},{13,1},{2,16},{3,7},... | collective-permute-start | bytes 491528 | tf_op jit(solution)/shard_map/ppermute | solution.py:328
  90.1 6.7 %collective-permute-start.20 = (bf16[8,16,640]{2,1,0:T(8,128)(2,1)S(1)}, bf16[8,16,640]{2,1,0:T(8,128)(2,1)S(1)}, u32[]{:S(2)}, u32[]{:S(2)}) collective-permute-start(bf16[8,16,640]{2,1,0:T(8,128)(2,1)S(1)} %get-tuple-element.46), channel_id=1, source_target_pairs={{0,18},{1,13},{4,22},{5,1},{8,26},{9,5},{12,30},{13,9},{2,0},{3,15... | collective-permute-start | bytes 491528 | tf_op jit(solution)/shard_map/ppermute | solution.py:328
  92.7 5.7 %collective-permute-start.19 = (bf16[8,16,640]{2,1,0:T(8,128)(2,1)S(1)}, bf16[8,16,640]{2,1,0:T(8,128)(2,1)S(1)}, u32[]{:S(2)}, u32[]{:S(2)}) collective-permute-start(bf16[8,16,640]{2,1,0:T(8,128)(2,1)S(1)} %get-tuple-element.47), channel_id=1, source_target_pairs={{0,16},{1,9},{4,20},{5,13},{8,24},{9,1},{12,28},{13,5},{2,18},{3,1... | collective-permute-start | bytes 491528 | tf_op jit(solution)/shard_map/ppermute | solution.py:328
  109.3 6.4 %collective-permute-start.23 = (f32[16,640]{1,0:T(8,128)S(1)}, f32[16,640]{1,0:T(8,128)S(1)}, u32[]{:S(2)}, u32[]{:S(2)}) collective-permute-start(f32[16,640]{1,0:T(8,128)S(1)} %convert_reduce_fusion.refs_0_), channel_id=1, source_target_pairs={{0,3},{1,2},{2,1},{3,0},{4,7},{5,6},{6,5},{7,4},{8,11},{9,10},{10,... | collective-permute-start | bytes 122888 | tf_op jit(solution)/shard_map/ppermute | solution.py:392
  113.3 2.4 %collective-permute-start.22 = (f32[16,640]{1,0:T(8,128)S(1)}, f32[16,640]{1,0:T(8,128)S(1)}, u32[]{:S(2)}, u32[]{:S(2)}) collective-permute-start(f32[16,640]{1,0:T(8,128)S(1)} %convert_reduce_fusion.refs_0_), channel_id=1, source_target_pairs={{0,1},{1,0},{2,3},{3,2},{4,5},{5,4},{6,7},{7,6},{8,9},{9,8},{10,11... | collective-permute-start | bytes 122888 | tf_op jit(solution)/shard_map/ppermute | solution.py:392
  113.3 2.9 %collective-permute-start.21 = (f32[16,640]{1,0:T(8,128)S(1)}, f32[16,640]{1,0:T(8,128)S(1)}, u32[]{:S(2)}, u32[]{:S(2)}) collective-permute-start(f32[16,640]{1,0:T(8,128)S(1)} %convert_reduce_fusion.refs_0_), channel_id=1, source_target_pairs={{0,2},{1,3},{2,0},{3,1},{4,6},{5,7},{6,4},{7,5},{8,10},{9,11},{10,... | collective-permute-start | bytes 122888 | tf_op jit(solution)/shard_map/ppermute | solution.py:392
